TPU v7x, 32 devices: a whole 2x2x4 slice. The times are simulated.
32 devices in a mesh: dp: 8 (over y, x, core), copy: 4 (over z).
Axes of the slice: x: 2, y: 2, z: 4, core: 2. Of those that a mesh axis runs over, the one named last changes fastest.
Arguments:
- block_input: bfloat16 [2, 8, 384, 768], P(None, 'dp', 'copy'), may hold values from -6 to 6
- image_ids: int32 [2, 8, 384], P(None, 'dp'), may hold values from -1 to 3, as said below
- latents: float32 [2, 8, 384, 16], P(None, 'dp'), may hold values from -6 to 6
- noise: float32 [2, 4, 8, 384, 16], P(None, 'copy', 'dp'), may hold values from -6 to 6
- timesteps: int32 [2, 4, 8, 4], P(None, 'copy', 'dp'), may hold values from 0 to 999
- norm_gains: bfloat16 [2, 768], P(None, ('dp', 'copy')), may hold values from 0.5 to 1.5
- block_biases: bfloat16 [6, 768], P(None, ('dp', 'copy')), may hold values from -1.75 to 1.75
- w_qkv: bfloat16 [768, 2304], P(('dp', 'copy')), may hold values from -0.21875 to 0.21875
- w_proj: bfloat16 [768, 768], P(('dp', 'copy')), may hold values from -2.5 to 2.5
- w_up: bfloat16 [768, 3072], P(('dp', 'copy')), may hold values from -0.21875 to 0.21875
- up_bias: bfloat16 [3072], P(('dp', 'copy')), may hold values from -1.75 to 1.75
- w_down: bfloat16 [3072, 768], P(('dp', 'copy')), may hold values from -0.109375 to 0.109375
- head_gain: bfloat16 [1024], P(('dp', 'copy')), may hold values from 0.5 to 1.5
- head_biases: bfloat16 [12, 1024], P(None, ('dp', 'copy')), may hold values from -1.75 to 1.75
- w_cond: bfloat16 [768, 1024], P(('dp', 'copy')), may hold values from -0.21875 to 0.21875
- w_time1: bfloat16 [256, 1024], P(('dp', 'copy')), may hold values from -0.375 to 0.375
- w_time2: bfloat16 [1024, 1024], P(('dp', 'copy')), may hold values from -0.1875 to 0.1875
- w_input: bfloat16 [16, 1024], P(None, ('dp', 'copy')), may hold values from -1.5 to 1.5
- w_ada: bfloat16 [1024, 3072], P(('dp', 'copy')), may hold values from -0.1875 to 0.1875
- w_mlp1: bfloat16 [1024, 1024], P(('dp', 'copy')), may hold values from -0.1875 to 0.1875
- w_mlp2: bfloat16 [1024, 1024], P(('dp', 'copy')), may hold values from -0.1875 to 0.1875
- w_final: bfloat16 [1024, 2048], P(('dp', 'copy')), may hold values from -0.1875 to 0.1875
- w_output: bfloat16 [1024, 16], P(('dp', 'copy')), may hold values from -0.1875 to 0.1875
- output_bias: bfloat16 [16], replicated, may hold values from -1.75 to 1.75
Outputs:
- block_output: bfloat16 [2, 8, 384, 768], P(None, 'dp', 'copy')
- input_grad: float32 [2, 8, 384, 768], P(None, 'dp', 'copy')
- grad_norm_gains: float32 [2, 768], P(None, ('dp', 'copy'))
- grad_block_biases: float32 [6, 768], P(None, ('dp', 'copy'))
- grad_w_qkv: float32 [768, 2304], P(('dp', 'copy'))
- grad_w_proj: float32 [768, 768], P(('dp', 'copy'))
- grad_w_up: float32 [768, 3072], P(('dp', 'copy'))
- grad_up_bias: float32 [3072], P(('dp', 'copy'))
- grad_w_down: float32 [3072, 768], P(('dp', 'copy'))
- grad_head_gain: float32 [1024], P(('dp', 'copy'))
- grad_head_biases: float32 [12, 1024], P(None, ('dp', 'copy'))
- grad_w_cond: float32 [768, 1024], P(('dp', 'copy'))
- grad_w_time1: float32 [256, 1024], P(('dp', 'copy'))
- grad_w_time2: float32 [1024, 1024], P(('dp', 'copy'))
- grad_w_input: float32 [16, 1024], P(None, ('dp', 'copy'))
- grad_w_ada: float32 [1024, 3072], P(('dp', 'copy'))
- grad_w_mlp1: float32 [1024, 1024], P(('dp', 'copy'))
- grad_w_mlp2: float32 [1024, 1024], P(('dp', 'copy'))
- grad_w_final: float32 [1024, 2048], P(('dp', 'copy'))
- grad_w_output: float32 [1024, 16], P(('dp', 'copy'))
- grad_output_bias: float32 [16], replicated
Inputs may be any that keep to these rules, and one draw needn't show every extreme that they name: `image_ids`: along a sequence the ids never fall; -1 marks padding, which comes only at a sequence's end.
All inputs are finite; a program needn't handle non-finite values.
Results may differ from a plain program's by a relative error of at most 0.013.
Values may be sent and summed in bfloat16 or wider, within the bound.
No kernel may reach another device: no remote copies, remote signals or barrier semaphores. Data moves between devices by JAX's collectives and lax.ppermute only.
A program may use at most 128 MiB of HBM per device.

v0:
```python
import math

import jax
import jax.numpy as jnp
from jax import lax
from jax.sharding import PartitionSpec as P

D = 768
HEADS = 12
HEAD_DIM = 64
WIDTH = 1024
FREQ = 256
CHANNELS = 16
IMAGES = 4


epsilon = 1e-06
highest = lax.Precision.HIGHEST


def product(left_side, right_side):
    return jnp.dot(left_side, right_side, preferred_element_type=jnp.float32)


def weight_grad(left_side, right_side):
    return lax.dot_general(
        left_side, right_side, (((0,), (0,)), ((), ())), preferred_element_type=jnp.float32
    )


def input_back(gradient, weight):
    return lax.dot_general(
        gradient, weight, (((1,), (1,)), ((), ())), preferred_element_type=jnp.float32
    )


def column_sum(values):
    return jnp.sum(values.astype(jnp.float32), axis=0)


def normalize(values):
    center = values - jnp.mean(values, axis=-1, keepdims=True)
    inverse = lax.rsqrt(jnp.mean(center * center, axis=-1, keepdims=True) + epsilon)
    return (center * inverse, inverse)


def norm_back(gradient, normed, inverse):
    return inverse * (
        gradient
        - jnp.mean(gradient, axis=-1, keepdims=True)
        - normed * jnp.mean(gradient * normed, axis=-1, keepdims=True)
    )


def silu_slope(values):
    sigma = jax.nn.sigmoid(values)
    return sigma * (1.0 + values * (1.0 - sigma))


def gelu_slope(values):
    return 0.5 * (1.0 + lax.erf(values * 2.0 ** (-0.5))) + values * jnp.exp(
        -0.5 * values * values
    ) * (2.0 * math.pi) ** (-0.5)


def sinusoid(step_vals):
    half_width = FREQ // 2
    rates = jnp.exp(-math.log(10000.0) * jnp.arange(half_width, dtype=jnp.float32) / half_width)
    angles = step_vals[:, None] * rates[None, :]
    return jnp.concatenate([jnp.cos(angles), jnp.sin(angles)], axis=1)


def plan(step_vals):
    anchor = math.cos(0.008 / 1.008 * math.pi / 2.0) ** 2
    angle_now = ((step_vals + 1.0) / 1000.0 + 0.008) / 1.008 * (math.pi / 2.0)
    signal = jnp.cos(angle_now) ** 2 / anchor
    return jnp.stack([jnp.sqrt(signal), jnp.sqrt(1.0 - signal)], axis=1)


def attention_scores(queries, key_rows, same_image, score_scale):
    scores = (
        jnp.einsum("qhd,khd->hqk", queries, key_rows, preferred_element_type=jnp.float32)
        * score_scale
    )
    return jnp.where(same_image[None], scores, -1e30)


def micro_batch(rows_in, image_row, latent_rows, noise_rows, step_row, full, bias_out):
    (
        norm_gains,
        block_biases,
        w_qkv,
        w_proj,
        w_up,
        up_bias,
        w_down,
        head_gain,
        head_biases,
        w_cond,
        w_time1,
        w_time2,
        w_input,
        w_ada,
        w_mlp1,
        w_mlp2,
        w_final,
        w_output,
    ) = full
    local_rows = rows_in.shape[0]
    length = image_row.shape[0]
    score_scale = HEAD_DIM ** (-0.5)
    gains = norm_gains.astype(jnp.float32)
    biases = block_biases.astype(jnp.float32)
    head_bias = head_biases.astype(jnp.float32)
    head_gain_f = head_gain.astype(jnp.float32)
    own_ids = lax.dynamic_slice_in_dim(image_row, lax.axis_index("copy") * local_rows, local_rows)
    rows = rows_in.astype(jnp.float32)
    norm_one, inv_one = normalize(rows)
    first_in = (norm_one * gains[0] + biases[0]).astype(jnp.bfloat16)
    zeros_key = jnp.zeros((D,), jnp.float32)
    projected = product(first_in, w_qkv) + jnp.concatenate([biases[1], zeros_key, biases[2]])
    projected = projected.astype(jnp.bfloat16)
    queries = projected[:, :D].reshape(local_rows, HEADS, HEAD_DIM)
    keys_vals = lax.all_gather(projected[:, D:], "copy", axis=0, tiled=True)
    key_rows = keys_vals[:, :D].reshape(length, HEADS, HEAD_DIM)
    value_rows = keys_vals[:, D:].reshape(length, HEADS, HEAD_DIM)
    same_image = own_ids[:, None] == image_row[None, :]
    scores = attention_scores(queries, key_rows, same_image, score_scale)
    row_max = jnp.max(scores, axis=-1, keepdims=True)
    exp_scores = jnp.exp(scores - row_max)
    row_total = jnp.sum(exp_scores, axis=-1, keepdims=True)
    log_total = row_max + jnp.log(row_total)
    attn_weights = (exp_scores / row_total).astype(jnp.bfloat16)
    mixed = jnp.einsum("hqk,khd->qhd", attn_weights, value_rows, preferred_element_type=jnp.float32)
    mixed = mixed.reshape(local_rows, D).astype(jnp.bfloat16)
    middle = rows + product(mixed, w_proj) + biases[3]
    norm_two, inv_two = normalize(middle)
    second_in = (norm_two * gains[1] + biases[4]).astype(jnp.bfloat16)
    hidden = product(second_in, w_up) + up_bias.astype(jnp.float32)
    active = jax.nn.gelu(hidden, approximate=False).astype(jnp.bfloat16)
    output = middle + product(active, w_down) + biases[5]
    out_low = output.astype(jnp.bfloat16)
    condition = lax.all_gather(out_low, "copy", axis=0, tiled=True)
    valid_rows = (image_row >= 0).astype(jnp.float32)[:, None]
    image_onehot = (image_row[:, None] == jnp.arange(IMAGES, dtype=jnp.int32)[None, :]).astype(
        jnp.float32
    )
    step_vals = step_row.astype(jnp.float32)
    sinusoid_in = sinusoid(step_vals).astype(jnp.bfloat16)
    time_one = product(sinusoid_in, w_time1) + head_bias[1]
    time_act = jax.nn.silu(time_one).astype(jnp.bfloat16)
    embedded = product(time_act, w_time2) + head_bias[2]
    cond_all = (
        product(condition, w_cond)
        + head_bias[0]
        + jnp.dot(image_onehot, embedded, precision=highest, preferred_element_type=jnp.float32)
    )
    gated = jax.nn.silu(cond_all).astype(jnp.bfloat16)
    modulation = product(gated, w_ada) + head_bias[7:10].reshape(3 * WIDTH)
    shift_rows = modulation[:, :WIDTH]
    scale_rows = modulation[:, WIDTH : 2 * WIDTH]
    gate_rows = modulation[:, 2 * WIDTH :]
    mixing = jnp.dot(
        image_onehot, plan(step_vals), precision=highest, preferred_element_type=jnp.float32
    )
    noisy = (latent_rows * mixing[:, 0:1] + noise_rows * mixing[:, 1:2]).astype(jnp.bfloat16)
    entry_rows = product(noisy, w_input) + head_bias[3]
    norm_head, inv_head = normalize(entry_rows)
    affine = norm_head * head_gain_f + head_bias[4]
    mlp_in = (affine * (1.0 + scale_rows) + shift_rows).astype(jnp.bfloat16)
    inner_one = product(mlp_in, w_mlp1) + head_bias[5]
    inner_act = jax.nn.silu(inner_one).astype(jnp.bfloat16)
    inner_two = product(inner_act, w_mlp2) + head_bias[6]
    residual = entry_rows + gate_rows * inner_two
    final_mod = product(gated, w_final) + head_bias[10:12].reshape(2 * WIDTH)
    norm_final, inv_final = normalize(residual)
    final_in = (norm_final * (1.0 + final_mod[:, WIDTH:]) + final_mod[:, :WIDTH]).astype(
        jnp.bfloat16
    )
    predicted = product(final_in, w_output) + bias_out
    grad_pred = ((predicted - noise_rows) * valid_rows).astype(jnp.bfloat16)
    grad_w_output = weight_grad(final_in, grad_pred)
    grad_out_bias = column_sum(grad_pred)
    grad_final_in = input_back(grad_pred, w_output)
    grad_final_mod = jnp.concatenate([grad_final_in, grad_final_in * norm_final], axis=1).astype(
        jnp.bfloat16
    )
    grad_residual = norm_back(grad_final_in * (1.0 + final_mod[:, WIDTH:]), norm_final, inv_final)
    grad_w_final = weight_grad(gated, grad_final_mod)
    grad_gated = input_back(grad_final_mod, w_final)
    grad_inner_two = (grad_residual * gate_rows).astype(jnp.bfloat16)
    grad_w_mlp2 = weight_grad(inner_act, grad_inner_two)
    grad_inner_one = (input_back(grad_inner_two, w_mlp2) * silu_slope(inner_one)).astype(
        jnp.bfloat16
    )
    grad_w_mlp1 = weight_grad(mlp_in, grad_inner_one)
    grad_mlp_in = input_back(grad_inner_one, w_mlp1)
    grad_modulation = jnp.concatenate(
        [grad_mlp_in, grad_mlp_in * affine, grad_residual * inner_two], axis=1
    ).astype(jnp.bfloat16)
    grad_affine = grad_mlp_in * (1.0 + scale_rows)
    grad_head_gain = jnp.sum(grad_affine * norm_head, axis=0)
    grad_entry = (grad_residual + norm_back(grad_affine * head_gain_f, norm_head, inv_head)).astype(
        jnp.bfloat16
    )
    grad_w_input = weight_grad(noisy, grad_entry)
    grad_w_ada = weight_grad(gated, grad_modulation)
    grad_gated = grad_gated + input_back(grad_modulation, w_ada)
    grad_cond = grad_gated * silu_slope(cond_all)
    grad_cond_low = grad_cond.astype(jnp.bfloat16)
    grad_w_cond = weight_grad(condition, grad_cond_low)
    grad_condition = input_back(grad_cond_low, w_cond)
    grad_embedded = lax.dot_general(
        image_onehot,
        grad_cond,
        (((0,), (0,)), ((), ())),
        precision=highest,
        preferred_element_type=jnp.float32,
    ).astype(jnp.bfloat16)
    grad_w_time2 = weight_grad(time_act, grad_embedded)
    grad_time_one = (input_back(grad_embedded, w_time2) * silu_slope(time_one)).astype(jnp.bfloat16)
    grad_w_time1 = weight_grad(sinusoid_in, grad_time_one)
    grad_head_biases = jnp.concatenate(
        [
            jnp.stack(
                [
                    column_sum(grad_cond_low),
                    column_sum(grad_time_one),
                    column_sum(grad_embedded),
                    column_sum(grad_entry),
                    jnp.sum(grad_affine, axis=0),
                    column_sum(grad_inner_one),
                    column_sum(grad_inner_two),
                ]
            ),
            column_sum(grad_modulation).reshape(3, WIDTH),
            column_sum(grad_final_mod).reshape(2, WIDTH),
        ],
        axis=0,
    )
    grad_z = lax.psum_scatter(
        grad_condition.astype(jnp.bfloat16), "copy", scatter_dimension=0, tiled=True
    ).astype(jnp.float32)
    grad_down = grad_z.astype(jnp.bfloat16)
    grad_w_down = weight_grad(active, grad_down)
    grad_hidden = (input_back(grad_down, w_down) * gelu_slope(hidden)).astype(jnp.bfloat16)
    grad_w_up = weight_grad(second_in, grad_hidden)
    grad_second = input_back(grad_hidden, w_up)
    grad_middle = grad_z + norm_back(grad_second * gains[1], norm_two, inv_two)
    grad_branch = grad_middle.astype(jnp.bfloat16)
    grad_w_proj = weight_grad(mixed, grad_branch)
    grad_mixed = (
        input_back(grad_branch, w_proj).astype(jnp.bfloat16).reshape(local_rows, HEADS, HEAD_DIM)
    )
    probs = jnp.exp(attention_scores(queries, key_rows, same_image, score_scale) - log_total)
    grad_probs = jnp.einsum(
        "qhd,khd->hqk", grad_mixed, value_rows, preferred_element_type=jnp.float32
    )
    delta = jnp.sum(grad_probs * probs, axis=-1, keepdims=True)
    grad_scores = (probs * (grad_probs - delta)).astype(jnp.bfloat16)
    grad_queries = (
        jnp.einsum("hqk,khd->qhd", grad_scores, key_rows, preferred_element_type=jnp.float32)
        * score_scale
    )
    grad_keys = (
        jnp.einsum("hqk,qhd->khd", grad_scores, queries, preferred_element_type=jnp.float32)
        * score_scale
    )
    grad_values = jnp.einsum(
        "hqk,qhd->khd", probs.astype(jnp.bfloat16), grad_mixed, preferred_element_type=jnp.float32
    )
    grad_kv = lax.psum_scatter(
        jnp.concatenate(
            [grad_keys.reshape(length, D), grad_values.reshape(length, D)], axis=1
        ).astype(jnp.bfloat16),
        "copy",
        scatter_dimension=0,
        tiled=True,
    ).astype(jnp.float32)
    grad_projected = jnp.concatenate([grad_queries.reshape(local_rows, D), grad_kv], axis=1).astype(
        jnp.bfloat16
    )
    grad_w_qkv = weight_grad(first_in, grad_projected)
    grad_first = input_back(grad_projected, w_qkv)
    grad_rows = grad_middle + norm_back(grad_first * gains[0], norm_one, inv_one)
    grad_norm_gains = jnp.stack(
        [jnp.sum(grad_first * norm_one, axis=0), jnp.sum(grad_second * norm_two, axis=0)]
    )
    grad_block_biases = jnp.stack(
        [
            jnp.sum(grad_first, axis=0),
            column_sum(grad_projected[:, :D]),
            column_sum(grad_projected[:, 2 * D :]),
            column_sum(grad_branch),
            jnp.sum(grad_second, axis=0),
            column_sum(grad_down),
        ]
    )
    grads = (
        grad_norm_gains,
        grad_block_biases,
        grad_w_qkv,
        grad_w_proj,
        grad_w_up,
        column_sum(grad_hidden),
        grad_w_down,
        grad_head_gain,
        grad_head_biases,
        grad_w_cond,
        grad_w_time1,
        grad_w_time2,
        grad_w_input,
        grad_w_ada,
        grad_w_mlp1,
        grad_w_mlp2,
        grad_w_final,
        grad_w_output,
    )
    return (out_low, grad_rows, grads, grad_out_bias)


def shards(
    block_input,
    image_ids,
    latents,
    noise,
    timesteps,
    norm_gains,
    block_biases,
    w_qkv,
    w_proj,
    w_up,
    up_bias,
    w_down,
    head_gain,
    head_biases,
    w_cond,
    w_time1,
    w_time2,
    w_input,
    w_ada,
    w_mlp1,
    w_mlp2,
    w_final,
    w_output,
    output_bias,
):
    bias_out = output_bias.astype(jnp.float32)
    outputs = []
    row_grads = []
    owned = None
    bias_sum = jnp.zeros((CHANNELS,), jnp.float32)
    for micro in range(block_input.shape[0]):
        full = (
            lax.all_gather(norm_gains, ("dp", "copy"), axis=1, tiled=True),
            lax.all_gather(block_biases, ("dp", "copy"), axis=1, tiled=True),
            lax.all_gather(w_qkv, ("dp", "copy"), axis=0, tiled=True),
            lax.all_gather(w_proj, ("dp", "copy"), axis=0, tiled=True),
            lax.all_gather(w_up, ("dp", "copy"), axis=0, tiled=True),
            lax.all_gather(up_bias, ("dp", "copy"), axis=0, tiled=True),
            lax.all_gather(w_down, ("dp", "copy"), axis=0, tiled=True),
            lax.all_gather(head_gain, ("dp", "copy"), axis=0, tiled=True),
            lax.all_gather(head_biases, ("dp", "copy"), axis=1, tiled=True),
            lax.all_gather(w_cond, ("dp", "copy"), axis=0, tiled=True),
            lax.all_gather(w_time1, ("dp", "copy"), axis=0, tiled=True),
            lax.all_gather(w_time2, ("dp", "copy"), axis=0, tiled=True),
            lax.all_gather(w_input, ("dp", "copy"), axis=1, tiled=True),
            lax.all_gather(w_ada, ("dp", "copy"), axis=0, tiled=True),
            lax.all_gather(w_mlp1, ("dp", "copy"), axis=0, tiled=True),
            lax.all_gather(w_mlp2, ("dp", "copy"), axis=0, tiled=True),
            lax.all_gather(w_final, ("dp", "copy"), axis=0, tiled=True),
            lax.all_gather(w_output, ("dp", "copy"), axis=0, tiled=True),
        )
        out_low, grad_rows, grads, grad_out_bias = micro_batch(
            block_input[micro, 0],
            image_ids[micro, 0],
            latents[micro, 0],
            noise[micro, 0, 0],
            timesteps[micro, 0, 0],
            full,
            bias_out,
        )
        outputs.append(out_low)
        row_grads.append(grad_rows)
        bias_sum = bias_sum + grad_out_bias
        piece = (
            lax.psum_scatter(grads[0], ("dp", "copy"), scatter_dimension=1, tiled=True),
            lax.psum_scatter(grads[1], ("dp", "copy"), scatter_dimension=1, tiled=True),
            lax.psum_scatter(grads[2], ("dp", "copy"), scatter_dimension=0, tiled=True),
            lax.psum_scatter(grads[3], ("dp", "copy"), scatter_dimension=0, tiled=True),
            lax.psum_scatter(grads[4], ("dp", "copy"), scatter_dimension=0, tiled=True),
            lax.psum_scatter(grads[5], ("dp", "copy"), scatter_dimension=0, tiled=True),
            lax.psum_scatter(grads[6], ("dp", "copy"), scatter_dimension=0, tiled=True),
            lax.psum_scatter(grads[7], ("dp", "copy"), scatter_dimension=0, tiled=True),
            lax.psum_scatter(grads[8], ("dp", "copy"), scatter_dimension=1, tiled=True),
            lax.psum_scatter(grads[9], ("dp", "copy"), scatter_dimension=0, tiled=True),
            lax.psum_scatter(grads[10], ("dp", "copy"), scatter_dimension=0, tiled=True),
            lax.psum_scatter(grads[11], ("dp", "copy"), scatter_dimension=0, tiled=True),
            lax.psum_scatter(grads[12], ("dp", "copy"), scatter_dimension=1, tiled=True),
            lax.psum_scatter(grads[13], ("dp", "copy"), scatter_dimension=0, tiled=True),
            lax.psum_scatter(grads[14], ("dp", "copy"), scatter_dimension=0, tiled=True),
            lax.psum_scatter(grads[15], ("dp", "copy"), scatter_dimension=0, tiled=True),
            lax.psum_scatter(grads[16], ("dp", "copy"), scatter_dimension=0, tiled=True),
            lax.psum_scatter(grads[17], ("dp", "copy"), scatter_dimension=0, tiled=True),
        )
        owned = (
            piece
            if owned is None
            else tuple((first + second for first, second in zip(owned, piece)))
        )
    bias_total = lax.psum(bias_sum, ("dp", "copy"))
    block_output = jnp.stack(outputs)[:, None]
    input_grad = jnp.stack(row_grads)[:, None]
    return (block_output, input_grad) + tuple(owned) + (bias_total,)


def solution(mesh):
    in_specs = (
        P(None, "dp", "copy", None),
        P(None, "dp", None),
        P(None, "dp", None, None),
        P(None, "copy", "dp", None, None),
        P(None, "copy", "dp", None),
        P(None, ("dp", "copy")),
        P(None, ("dp", "copy")),
        P(("dp", "copy"), None),
        P(("dp", "copy"), None),
        P(("dp", "copy"), None),
        P(("dp", "copy")),
        P(("dp", "copy"), None),
        P(("dp", "copy")),
        P(None, ("dp", "copy")),
        P(("dp", "copy"), None),
        P(("dp", "copy"), None),
        P(("dp", "copy"), None),
        P(None, ("dp", "copy")),
        P(("dp", "copy"), None),
        P(("dp", "copy"), None),
        P(("dp", "copy"), None),
        P(("dp", "copy"), None),
        P(("dp", "copy"), None),
        P(),
    )
    out_specs = (
        P(None, "dp", "copy", None),
        P(None, "dp", "copy", None),
        P(None, ("dp", "copy")),
        P(None, ("dp", "copy")),
        P(("dp", "copy"), None),
        P(("dp", "copy"), None),
        P(("dp", "copy"), None),
        P(("dp", "copy")),
        P(("dp", "copy"), None),
        P(("dp", "copy")),
        P(None, ("dp", "copy")),
        P(("dp", "copy"), None),
        P(("dp", "copy"), None),
        P(("dp", "copy"), None),
        P(None, ("dp", "copy")),
        P(("dp", "copy"), None),
        P(("dp", "copy"), None),
        P(("dp", "copy"), None),
        P(("dp", "copy"), None),
        P(("dp", "copy"), None),
        P(),
    )
    return jax.shard_map(shards, mesh=mesh, in_specs=in_specs, out_specs=out_specs, check_vma=False)
```

profile of v0, /device:TPU:9, one launch (start us, length us, event | category | flops | bytes accessed | tf_op | source)
XLA Modules:
  0.0 2837.7 jit_solution(12453353598706552528)
XLA Ops:
  8.7 58.6 %all-gather = bf16[32,24,2]{1,2,0:T(2,128)(2,1)S(1)} all-gather(bf16[1,24,2]{1,2,0:T(2,128)(2,1)} %bitcast.434), channel_id=1, replica_groups=mesh['dp'=8,'copy'=4] {'dp','copy'}, dimensions={0}, use_global_device_ids=true | all-gather | bytes 3168 | tf_op jit(solution)/shard_map/all_gather | solution.py:355
  67.6 68.8 %all-gather.1 = bf16[32,24,6]{1,2,0:T(8,128)(2,1)S(1)} all-gather(bf16[1,24,6]{1,2,0:T(8,128)(2,1)} %bitcast.433), channel_id=1, replica_groups=mesh['dp'=8,'copy'=4] {'dp','copy'}, dimensions={0}, use_global_device_ids=true | all-gather | bytes 9504 | tf_op jit(solution)/shard_map/all_gather | solution.py:356
  142.1 2.9 fusion.1
  156.1 66.1 %all-gather.3 = bf16[32,32,12]{1,2,0:T(8,128)(2,1)S(1)} all-gather(bf16[1,32,12]{1,2,0:T(8,128)(2,1)S(1)} %bitcast.426), channel_id=1, replica_groups=mesh['dp'=8,'copy'=4] {'dp','copy'}, dimensions={0}, use_global_device_ids=true | all-gather | bytes 25344 | tf_op jit(solution)/shard_map/all_gather | solution.py:363
  224.0 44.4 %all-reduce.7 = (bf16[3072]{0:T(1024)(128)(2,1)S(1)}, bf16[1024]{0:T(1024)(128)(2,1)S(1)}) all-reduce(bf16[3072]{0:T(1024)(128)(2,1)S(1)} %dynamic-update-slice, bf16[1024]{0:T(1024)(128)(2,1)S(1)} %dynamic-update-slice.1), channel_id=1, replica_groups=mesh['dp'=8,'copy'=4] {'dp','copy'}, use_global_device_ids=true, to_apply=%add | all-reduce | flops 4096 | bytes 16384
  272.3 61.3 %all-gather.2 = bf16[32,32,16]{1,2,0:T(8,128)(2,1)S(1)} all-gather(bf16[1,32,16]{1,2,0:T(8,128)(2,1)S(1)} %bitcast.427), channel_id=1, replica_groups=mesh['dp'=8,'copy'=4] {'dp','copy'}, dimensions={0}, use_global_device_ids=true | all-gather | bytes 33792 | tf_op jit(solution)/shard_map/all_gather | solution.py:367
  333.7 66.1 %all-gather.4 = bf16[32,32,16]{1,2,0:T(8,128)(2,1)S(1)} all-gather(bf16[1,32,16]{1,2,0:T(8,128)(2,1)S(1)} %bitcast.428), channel_id=1, replica_groups=mesh['dp'=8,'copy'=4] {'dp','copy'}, dimensions={0}, use_global_device_ids=true | all-gather | bytes 33792 | tf_op jit(solution)/shard_map/all_gather | solution.py:372
  400.7 70.6 %all_gather.97 = bf16[256,1024]{1,0:T(8,128)(2,1)S(1)} all-gather(bf16[8,1024]{1,0:T(8,128)(2,1)S(1)} %copy-done.172), channel_id=1, replica_groups=mesh['dp'=8,'copy'=4] {'dp','copy'}, dimensions={0}, use_global_device_ids=true | all-gather | bytes 540672 | tf_op jit(solution)/shard_map/all_gather | solution.py:365
  498.8 4.4 convolution_add_fusion.9
  503.2 6.2 fusion.53
  510.1 16.0 all_gather.105
  526.2 4.9 fusion.20
  532.6 15.7 all_gather.95
  557.1 6.0 convolution_add_fusion.12
  563.1 3.5 convolution_add_fusion.11
  566.5 32.1 %all-gather.34.cloned.1.call-done = bf16[1024,3072]{1,0:T(8,128)(2,1)} async-done(((bf16[32,3072]{1,0:T(8,128)(2,1)}), bf16[1024,3072]{1,0:T(8,128)(2,1)}) %all-gather.34.cloned.1.call-update) | async-done | bytes 6291472 | tf_op jit(solution)/shard_map/all_gather | solution.py:368
  598.6 5.1 convolution_add_fusion.6
  610.9 44.7 %all-gather.36.cloned.1.call-done = bf16[1024,1024]{1,0:T(8,128)(2,1)} async-done(((bf16[32,1024]{1,0:T(8,128)(2,1)}), bf16[1024,1024]{1,0:T(8,128)(2,1)}) %all-gather.36.cloned.1.call-update) | async-done | bytes 2097168 | tf_op jit(solution)/shard_map/all_gather | solution.py:369
  655.7 3.9 convolution_add_fusion.19
  659.6 54.2 %all-gather.38.cloned.1.call-done = bf16[1024,1024]{1,0:T(8,128)(2,1)} async-done(((bf16[32,1024]{1,0:T(8,128)(2,1)}), bf16[1024,1024]{1,0:T(8,128)(2,1)}) %all-gather.38.cloned.1.call-update) | async-done | bytes 2097168 | tf_op jit(solution)/shard_map/all_gather | solution.py:370
  713.8 4.3 fusion.166
  733.4 4.1 convert_reduce_fusion.5
  742.4 6.9 multiply_reduce_fusion.2
  749.3 3.2 convert_reduce_fusion.6
  752.5 5.9 fusion.157
  758.5 2.8 convert_reduce_fusion.11
  764.2 7.8 fusion.155
  772.0 2.8 convert_reduce_fusion.7
  777.8 4.2 reduce-scatter.31.cloned.1.call-done
  782.0 5.0 convert_reduce_fusion.13
  787.0 5.5 multiply_reduce_fusion.15
  793.5 11.0 reduce-scatter.33.cloned.1.call-done
  804.5 5.0 convert_reduce_fusion.12
  809.6 5.6 convert_reduce_fusion.23
  841.8 2.7 convert_reduce_fusion.26
  846.3 4.2 concatenate.62
  850.6 2.7 convert_reduce_fusion.28
  867.1 2.7 fusion.144
  877.1 2.9 fusion.160
  880.0 3.3 convolution_add_fusion.13
  886.9 3.3 convolution_add_fusion.14
  891.7 2.7 convolution_add_fusion.15
  901.8 4.2 convolution_add_fusion.1
  908.8 5.1 convolution_add_fusion.3
  916.4 6.2 convolution_add_fusion.2
  924.0 3.7 fusion.66
  927.7 5.8 convolution_add_fusion.4
  933.8 5.5 fusion.156
  939.3 7.2 convolution_add_fusion
  950.8 60.9 %reduce-scatter.61.cloned.1.call-done = f32[32,12]{1,0:T(8,128)} async-done(((f32[1024,12]{1,0:T(8,128)}), f32[32,12]{1,0:T(8,128)}) %reduce-scatter.61.cloned.1.call-update) | async-done | bytes 1552
  1013.1 131.3 %reduce-scatter.63.cloned.1.call-done = f32[32,16]{1,0:T(8,128)} async-done(((f32[1024,16]{1,0:T(8,128)}), f32[32,16]{1,0:T(8,128)}) %reduce-scatter.63.cloned.1.call-update) | async-done | bytes 2064
  1145.8 131.3 %reduce-scatter.65.cloned.1.call-done = f32[32,16]{1,0:T(8,128)} async-done(((f32[1024,16]{1,0:T(8,128)}), f32[32,16]{1,0:T(8,128)}) %reduce-scatter.65.cloned.1.call-update) | async-done | bytes 2064
  1302.5 49.2 %all-reduce.6 = (f32[2,768]{1,0:T(2,128)S(1)}, f32[6,768]{1,0:T(8,128)S(1)}, f32[3072]{0:T(1024)S(1)}, f32[1024]{0:T(1024)S(1)}, f32[16]{0:T(128)}) all-reduce(f32[2,768]{1,0:T(2,128)S(1)} %maximum_add_fusion, f32[6,768]{1,0:T(8,128)S(1)} %add.815, f32[3072]{0:T(1024)} %add.819, ...), channel_id=24, replica_groups=mesh['dp'=8,'copy'=4] {'dp','copy'}, use_global_device_ids=true, to_apply=%region_40.41.clone | all-reduce | flops 10256 | bytes 82048
  1359.1 52.9 %reduce-scatter.45.cloned.1.call-done = f32[8,1024]{1,0:T(8,128)} async-done(((f32[256,1024]{1,0:T(8,128)}), f32[8,1024]{1,0:T(8,128)}) %reduce-scatter.45.cloned.1.call-update) | async-done | bytes 32784 | tf_op jit(solution)/shard_map/reduce_scatter | solution.py:397
  1411.9 111.6 %reduce-scatter.43.cloned.1.call-done = f32[24,1024]{1,0:T(8,128)} async-done(((f32[768,1024]{1,0:T(8,128)}), f32[24,1024]{1,0:T(8,128)}) %reduce-scatter.43.cloned.1.call-update) | async-done | bytes 98320 | tf_op jit(solution)/shard_map/reduce_scatter | solution.py:396
  1523.5 104.0 %reduce-scatter.37.cloned.1.call-done = f32[24,768]{1,0:T(8,128)} async-done(((f32[768,768]{1,0:T(8,128)}), f32[24,768]{1,0:T(8,128)}) %reduce-scatter.37.cloned.1.call-update) | async-done | bytes 73744 | tf_op jit(solution)/shard_map/reduce_scatter | solution.py:390
  1627.5 144.3 %reduce-scatter.53.cloned.1.call-done = f32[32,1024]{1,0:T(8,128)} async-done(((f32[1024,1024]{1,0:T(8,128)}), f32[32,1024]{1,0:T(8,128)}) %reduce-scatter.53.cloned.1.call-update) | async-done | bytes 131088 | tf_op jit(solution)/shard_map/reduce_scatter | solution.py:402
  1771.8 148.6 %reduce-scatter.51.cloned.1.call-done = f32[32,1024]{1,0:T(8,128)} async-done(((f32[1024,1024]{1,0:T(8,128)}), f32[32,1024]{1,0:T(8,128)}) %reduce-scatter.51.cloned.1.call-update) | async-done | bytes 131088 | tf_op jit(solution)/shard_map/reduce_scatter | solution.py:401
  1920.5 149.7 %reduce-scatter.47.cloned.1.call-done = f32[32,1024]{1,0:T(8,128)} async-done(((f32[1024,1024]{1,0:T(8,128)}), f32[32,1024]{1,0:T(8,128)}) %reduce-scatter.47.cloned.1.call-update) | async-done | bytes 131088 | tf_op jit(solution)/shard_map/reduce_scatter | solution.py:398
  2070.1 130.0 %reduce-scatter.35.cloned.1.call-done = f32[24,2304]{1,0:T(8,128)} async-done(((f32[768,2304]{1,0:T(8,128)}), f32[24,2304]{1,0:T(8,128)}) %reduce-scatter.35.cloned.1.call-update) | async-done | bytes 221200 | tf_op jit(solution)/shard_map/reduce_scatter | solution.py:389
  2200.1 141.0 %reduce-scatter.39.cloned.1.call-done = f32[24,3072]{1,0:T(8,128)} async-done(((f32[768,3072]{1,0:T(8,128)}), f32[24,3072]{1,0:T(8,128)}) %reduce-scatter.39.cloned.1.call-update) | async-done | bytes 294928 | tf_op jit(solution)/shard_map/reduce_scatter | solution.py:391
  2341.1 142.1 %reduce-scatter.41.cloned.1.call-done = f32[96,768]{1,0:T(8,128)} async-done(((f32[3072,768]{1,0:T(8,128)}), f32[96,768]{1,0:T(8,128)}) %reduce-scatter.41.cloned.1.call-update) | async-done | bytes 294928 | tf_op jit(solution)/shard_map/reduce_scatter | solution.py:393
  2483.2 186.4 %reduce-scatter.55.cloned.1.call-done = f32[32,2048]{1,0:T(8,128)} async-done(((f32[1024,2048]{1,0:T(8,128)}), f32[32,2048]{1,0:T(8,128)}) %reduce-scatter.55.cloned.1.call-update) | async-done | bytes 262160 | tf_op jit(solution)/shard_map/reduce_scatter | solution.py:403
  2669.7 161.0 %reduce-scatter.49.cloned.1.call-done = f32[32,3072]{1,0:T(8,128)} async-done(((f32[1024,3072]{1,0:T(8,128)}), f32[32,3072]{1,0:T(8,128)}) %reduce-scatter.49.cloned.1.call-update) | async-done | bytes 393232 | tf_op jit(solution)/shard_map/reduce_scatter | solution.py:400
  (789 shorter events, 204.4 us)
Async XLA Ops:
  7.2 134.9 %all-gather.18.cloned.1.call-start = ((), (), s32[]{:S(2)}) async-start(), calls=%async_computation.18 | async-start | bytes 3649536 | tf_op jit(solution)/shard_map/all_gather | solution.py:357
  7.9 468.8 %all-gather.32.cloned.1.call-start = ((), (), s32[]{:S(2)}) async-start(), calls=%async_computation.25 | async-start | bytes 2162688 | tf_op jit(solution)/shard_map/all_gather | solution.py:366
  8.7 473.9 %all-gather.28.cloned.1.call-start = ((), (), s32[]{:S(2)}) async-start(), calls=%async_computation.23 | async-start | bytes 1474560 | tf_op jit(solution)/shard_map/all_gather | solution.py:124
  137.4 9.9 copy-start.121
  137.4 388.7 %copy-start.123 = (f32[768]{0:T(1024)}, f32[768]{0:T(1024)S(1)}, u32[]{:S(2)}) copy-start(f32[768]{0:T(1024)S(1)} %get-tuple-element.139) | copy-start | bytes 9220
  138.0 9.3 copy-start.115
  146.5 338.5 %all-gather.20.cloned.1.call-start = ((), (), s32[]{:S(2)}) async-start(), calls=%async_computation.19 | async-start | bytes 1474560 | tf_op jit(solution)/shard_map/all_gather | solution.py:124
  149.7 73.2 %copy-start.233 = (bf16[16]{0:T(256)(128)(2,1)S(1)}, bf16[16]{0:T(256)(128)(2,1)}, u32[]{:S(2)}) copy-start(bf16[16]{0:T(256)(128)(2,1)} %param.47) | copy-start | bytes 100
  149.8 73.8 %copy-start.234 = (bf16[32]{0:T(256)(128)(2,1)S(1)}, bf16[32]{0:T(256)(128)(2,1)}, u32[]{:S(2)}) copy-start(bf16[32]{0:T(256)(128)(2,1)} %param.36) | copy-start | bytes 196
  149.8 74.0 %copy-start.235 = (bf16[96]{0:T(256)(128)(2,1)S(1)}, bf16[96]{0:T(256)(128)(2,1)}, u32[]{:S(2)}) copy-start(bf16[96]{0:T(256)(128)(2,1)} %param.34) | copy-start | bytes 580
  149.8 119.8 %copy-start.218 = (s32[2,1,384]{2,1,0:T(1,128)S(1)}, s32[2,1,384]{2,1,0:T(1,128)}, u32[]{:S(2)}) copy-start(s32[2,1,384]{2,1,0:T(1,128)} %param.25) | copy-start | bytes 9220
  149.8 122.5 %copy-start.215 = (bf16[16,32]{1,0:T(8,128)(2,1)S(1)}, bf16[16,32]{1,0:T(8,128)(2,1)}, u32[]{:S(2)}) copy-start(bf16[16,32]{1,0:T(8,128)(2,1)} %param.41) | copy-start | bytes 3076
  150.5 183.2 %copy-start.216 = (bf16[32,16]{0,1:T(8,128)(2,1)S(1)}, bf16[32,16]{0,1:T(8,128)(2,1)}, u32[]{:S(2)}) copy-start(bf16[32,16]{0,1:T(8,128)(2,1)} %param.46) | copy-start | bytes 3076
  150.6 250.1 %copy-start.172 = (bf16[8,1024]{1,0:T(8,128)(2,1)S(1)}, bf16[8,1024]{1,0:T(8,128)(2,1)}, u32[]{:S(2)}) copy-start(bf16[8,1024]{1,0:T(8,128)(2,1)} %param.39) | copy-start | bytes 49156
  150.6 340.9 %all-gather.22.cloned.1.call-start = ((), (), s32[]{:S(2)}) async-start(), calls=%async_computation.20 | async-start | bytes 1216512 | tf_op jit(solution)/shard_map/all_gather | solution.py:358
  151.2 347.6 %all-gather.24.cloned.1.call-start = ((), (), s32[]{:S(2)}) async-start(), calls=%async_computation.21 | async-start | bytes 4866048 | tf_op jit(solution)/shard_map/all_gather | solution.py:359
  151.7 351.4 %all-gather.26.cloned.1.call-start = ((), (), s32[]{:S(2)}) async-start(), calls=%async_computation.22 | async-start | bytes 4866048 | tf_op jit(solution)/shard_map/all_gather | solution.py:361
  152.5 395.9 %all-gather.30.cloned.1.call-start = ((), (), s32[]{:S(2)}) async-start(), calls=%async_computation.24 | async-start | bytes 1622016 | tf_op jit(solution)/shard_map/all_gather | solution.py:364
  153.2 403.9 %all-gather.40.cloned.1.call-start = ((), (), s32[]{:S(2)}) async-start(), calls=%async_computation.29 | async-start | bytes 4325376 | tf_op jit(solution)/shard_map/all_gather | solution.py:371
  154.0 317.3 %copy-start.125 = (f32[2,1,1,384,16]{3,4,2,1,0:T(8,128)S(1)}, f32[2,1,1,384,16]{3,4,2,1,0:T(8,128)}, u32[]{:S(2)}) copy-start(f32[2,1,1,384,16]{3,4,2,1,0:T(8,128)} %param.27) | copy-start | bytes 147460
  154.0 317.3 %copy-start.147 = (f32[2,1,384,16]{2,3,1,0:T(8,128)S(1)}, f32[2,1,384,16]{2,3,1,0:T(8,128)}, u32[]{:S(2)}) copy-start(f32[2,1,384,16]{2,3,1,0:T(8,128)} %param.26) | copy-start | bytes 147460
  154.0 444.7 %all-gather.34.cloned.1.call-start = ((), (), s32[]{:S(2)}) async-start(), calls=%async_computation.26 | async-start | bytes 6488064 | tf_op jit(solution)/shard_map/all_gather | solution.py:368
  154.6 501.1 %all-gather.36.cloned.1.call-start = ((), (), s32[]{:S(2)}) async-start(), calls=%async_computation.27 | async-start | bytes 2162688 | tf_op jit(solution)/shard_map/all_gather | solution.py:369
  155.3 558.5 %all-gather.38.cloned.1.call-start = ((), (), s32[]{:S(2)}) async-start(), calls=%async_computation.28 | async-start | bytes 2162688 | tf_op jit(solution)/shard_map/all_gather | solution.py:370
  155.9 626.1 %reduce-scatter.31.cloned.1.call-start = ((), (), s32[]{:S(2)}) async-start(), calls=%async_computation.30 | async-start | bytes 737280 | tf_op jit(solution)/shard_map/reduce_scatter | solution.py:241
  269.6 205.8 %copy-start.155 = (s32[384]{0:T(512)}, s32[384]{0:T(512)S(1)}, u32[]{:S(2)}) copy-start(s32[384]{0:T(512)S(1)} %get-tuple-element.155) | copy-start | bytes 4612
  269.6 205.8 %copy-start.158 = (s32[384]{0:T(512)}, s32[384]{0:T(512)S(1)}, u32[]{:S(2)}) copy-start(s32[384]{0:T(512)S(1)} %get-tuple-element.156) | copy-start | bytes 4612
  503.1 23.0 copy-start
  503.1 23.0 copy-start.17
  503.1 23.0 copy-start.148
  503.2 23.0 copy-start.181
  503.2 23.0 copy-start.202
  510.1 21.0 slice-start.4
  733.1 25.3 copy-start.43
  733.1 25.3 copy-start.45
  764.1 40.4 %reduce-scatter.33.cloned.1.call-start = ((), (), s32[]{:S(2)}) async-start(), calls=%async_computation.31 | async-start | bytes 737280 | tf_op jit(solution)/shard_map/reduce_scatter | solution.py:241
  764.1 7.8 copy-start.47
  764.1 7.8 copy-start.49
  764.1 7.8 copy-start.227
  764.1 7.8 copy-start.238
  777.6 120.3 %reduce-scatter.57.cloned.1.call-start = ((), (), s32[]{:S(2)}) async-start(), calls=%async_computation.43 | async-start | bytes 1474560
  793.5 16.1 copy-start.178
  824.7 74.5 %reduce-scatter.59.cloned.1.call-start = ((), (), s32[]{:S(2)}) async-start(), calls=%async_computation.44 | async-start | bytes 1474560
  826.6 47.4 %copy-start.66 = (f32[96,768]{1,0:T(8,128)}, f32[96,768]{1,0:T(8,128)S(1)}, u32[]{:S(2)}) copy-start(f32[96,768]{1,0:T(8,128)S(1)} %get-tuple-element.177) | copy-start | bytes 884740
  834.2 177.5 %reduce-scatter.61.cloned.1.call-start = ((), (), s32[]{:S(2)}) async-start(), calls=%async_computation.45 | async-start | bytes 540672
  841.8 8.8 copy-start.157
  844.5 8.8 copy-start.120
  853.3 7.6 copy-start.133
  862.5 281.9 %reduce-scatter.63.cloned.1.call-start = ((), (), s32[]{:S(2)}) async-start(), calls=%async_computation.46 | async-start | bytes 540672
  864.9 412.2 %reduce-scatter.65.cloned.1.call-start = ((), (), s32[]{:S(2)}) async-start(), calls=%async_computation.47 | async-start | bytes 540672
  865.6 546.3 %reduce-scatter.45.cloned.1.call-start = ((), (), s32[]{:S(2)}) async-start(), calls=%async_computation.37 | async-start | bytes 1081344 | tf_op jit(solution)/shard_map/reduce_scatter | solution.py:397
  867.0 656.5 %reduce-scatter.43.cloned.1.call-start = ((), (), s32[]{:S(2)}) async-start(), calls=%async_computation.36 | async-start | bytes 3244032 | tf_op jit(solution)/shard_map/reduce_scatter | solution.py:396
  872.6 754.9 %reduce-scatter.37.cloned.1.call-start = ((), (), s32[]{:S(2)}) async-start(), calls=%async_computation.33 | async-start | bytes 2433024 | tf_op jit(solution)/shard_map/reduce_scatter | solution.py:390
  876.0 895.8 %reduce-scatter.53.cloned.1.call-start = ((), (), s32[]{:S(2)}) async-start(), calls=%async_computation.41 | async-start | bytes 4325376 | tf_op jit(solution)/shard_map/reduce_scatter | solution.py:402
  883.3 1037.1 %reduce-scatter.51.cloned.1.call-start = ((), (), s32[]{:S(2)}) async-start(), calls=%async_computation.40 | async-start | bytes 4325376 | tf_op jit(solution)/shard_map/reduce_scatter | solution.py:401
  890.3 1179.8 %reduce-scatter.47.cloned.1.call-start = ((), (), s32[]{:S(2)}) async-start(), calls=%async_computation.38 | async-start | bytes 4325376 | tf_op jit(solution)/shard_map/reduce_scatter | solution.py:398
  894.5 1305.6 %reduce-scatter.35.cloned.1.call-start = ((), (), s32[]{:S(2)}) async-start(), calls=%async_computation.32 | async-start | bytes 7299072 | tf_op jit(solution)/shard_map/reduce_scatter | solution.py:389
  906.1 1435.0 %reduce-scatter.39.cloned.1.call-start = ((), (), s32[]{:S(2)}) async-start(), calls=%async_computation.34 | async-start | bytes 9732096 | tf_op jit(solution)/shard_map/reduce_scatter | solution.py:391
  913.9 1569.4 %reduce-scatter.41.cloned.1.call-start = ((), (), s32[]{:S(2)}) async-start(), calls=%async_computation.35 | async-start | bytes 9732096 | tf_op jit(solution)/shard_map/reduce_scatter | solution.py:393
  922.6 1747.0 %reduce-scatter.55.cloned.1.call-start = ((), (), s32[]{:S(2)}) async-start(), calls=%async_computation.42 | async-start | bytes 8650752 | tf_op jit(solution)/shard_map/reduce_scatter | solution.py:403
  933.6 1897.1 %reduce-scatter.49.cloned.1.call-start = ((), (), s32[]{:S(2)}) async-start(), calls=%async_computation.39 | async-start | bytes 12976128 | tf_op jit(solution)/shard_map/reduce_scatter | solution.py:400
  946.5 332.0 %copy-start.170 = (f32[768]{0:T(1024)S(1)}, f32[768]{0:T(1024)}, u32[]{:S(2)}) copy-start(f32[768]{0:T(1024)} %get-tuple-element.123) | copy-start | bytes 9220
  946.5 337.6 %copy-start.169 = (f32[768]{0:T(1024)S(1)}, f32[768]{0:T(1024)}, u32[]{:S(2)}) copy-start(f32[768]{0:T(1024)} %get-tuple-element.133) | copy-start | bytes 9220
  946.5 348.7 %copy-start.10 = (bf16[768,2304]{1,0:T(8,128)(2,1)S(1)}, bf16[768,2304]{1,0:T(8,128)(2,1)}, u32[]{:S(2)}) copy-start(bf16[768,2304]{1,0:T(8,128)(2,1)} %all-gather.18.cloned.1.call-done) | copy-start | bytes 10616836
  (214 other events, 612.5 us)
Sparse Core Ops, SparseCore 0:
  10.8 61.1 all-gather.17
  75.0 54.9 all-gather.31
  146.7 33.4 all-gather.27
  182.2 30.2 all-gather.19
  215.1 53.5 all-gather.21
  271.4 64.2 all-gather.23
  338.4 62.6 all-gather.25
  404.0 52.8 all-gather.29
  459.8 64.0 all-gather.39
  526.6 71.9 all-gather.33
  601.6 54.0 all-gather.35
  658.5 55.3 all-gather.37
  764.2 17.7 reduce-scatter.30
  784.1 20.2 reduce-scatter.32
  824.8 29.0 reduce-scatter.56
  856.0 28.0 reduce-scatter.58
  886.8 124.8 reduce-scatter.60
  1013.9 130.5 reduce-scatter.62
  1146.6 130.3 reduce-scatter.64
  1279.8 132.0 reduce-scatter.44
  1417.9 105.5 reduce-scatter.42
  1529.4 98.0 reduce-scatter.36
  1630.4 141.3 reduce-scatter.52
  1774.6 145.7 reduce-scatter.50
  1923.4 146.6 reduce-scatter.46
  2077.2 122.9 reduce-scatter.34
  2206.5 134.6 reduce-scatter.38
  2348.6 134.5 reduce-scatter.40
  2486.1 183.4 reduce-scatter.54
  2676.1 154.4 reduce-scatter.48
where the time goes:
time: 2850 us; the launch traced here: 2840 us
  waiting for transfers between devices  1950 us (68%)
  blocking collectives  517 us (18%)
  matrix products  223 us (8%)
  local copies, waits for them, and re-layouts  78.9 us (3%)
  other arithmetic  50.5 us (2%)
    unnamed x35, waiting for transfers between devices  330 us
    reduce_scatter x1, waiting for transfers between devices, shards(): lax.psum_scatter(grads[16], ('dp', 'copy'), scatter_dimension=0, tiled=True)  186 us
    reduce_scatter x1, waiting for transfers between devices, shards(): lax.psum_scatter(grads[13], ('dp', 'copy'), scatter_dimension=0, tiled=True)  161 us
    reduce_scatter x1, waiting for transfers between devices, shards(): lax.psum_scatter(grads[11], ('dp', 'copy'), scatter_dimension=0, tiled=True)  150 us
    reduce_scatter x1, waiting for transfers between devices, shards(): lax.psum_scatter(grads[14], ('dp', 'copy'), scatter_dimension=0, tiled=True)  149 us
    reduce_scatter x1, waiting for transfers between devices, shards(): lax.psum_scatter(grads[15], ('dp', 'copy'), scatter_dimension=0, tiled=True)  144 us
    reduce_scatter x1, waiting for transfers between devices, shards(): lax.psum_scatter(grads[6], ('dp', 'copy'), scatter_dimension=0, tiled=True)  142 us
    reduce_scatter x1, waiting for transfers between devices, shards(): lax.psum_scatter(grads[4], ('dp', 'copy'), scatter_dimension=0, tiled=True)  141 us
  transfers between devices with their start and end apart: 30, of which 19 were waited for; matrix products, arithmetic and copies ran while one was open for 9% of the time, Pallas kernels for 0%

commit v1 on v0

v1 whole, which is shorter than its diff:
```python
import math

import jax
import jax.numpy as jnp
from jax import lax
from jax.sharding import PartitionSpec as P

D = 768
HEADS = 12
HEAD_DIM = 64
WIDTH = 1024
FREQ = 256
CHANNELS = 16
IMAGES = 4


epsilon = 1e-06
highest = lax.Precision.HIGHEST


def product(left_side, right_side):
    return jnp.dot(left_side, right_side, preferred_element_type=jnp.float32)


def weight_grad(left_side, right_side):
    return lax.dot_general(
        left_side, right_side, (((0,), (0,)), ((), ())), preferred_element_type=jnp.float32
    )


def input_back(gradient, weight):
    return lax.dot_general(
        gradient, weight, (((1,), (1,)), ((), ())), preferred_element_type=jnp.float32
    )


def column_sum(values):
    return jnp.sum(values.astype(jnp.float32), axis=0)


def normalize(values):
    center = values - jnp.mean(values, axis=-1, keepdims=True)
    inverse = lax.rsqrt(jnp.mean(center * center, axis=-1, keepdims=True) + epsilon)
    return (center * inverse, inverse)


def norm_back(gradient, normed, inverse):
    return inverse * (
        gradient
        - jnp.mean(gradient, axis=-1, keepdims=True)
        - normed * jnp.mean(gradient * normed, axis=-1, keepdims=True)
    )


def silu_slope(values):
    sigma = jax.nn.sigmoid(values)
    return sigma * (1.0 + values * (1.0 - sigma))


def gelu_slope(values):
    return 0.5 * (1.0 + lax.erf(values * 2.0 ** (-0.5))) + values * jnp.exp(
        -0.5 * values * values
    ) * (2.0 * math.pi) ** (-0.5)


def sinusoid(step_vals):
    half_width = FREQ // 2
    rates = jnp.exp(-math.log(10000.0) * jnp.arange(half_width, dtype=jnp.float32) / half_width)
    angles = step_vals[:, None] * rates[None, :]
    return jnp.concatenate([jnp.cos(angles), jnp.sin(angles)], axis=1)


def plan(step_vals):
    anchor = math.cos(0.008 / 1.008 * math.pi / 2.0) ** 2
    angle_now = ((step_vals + 1.0) / 1000.0 + 0.008) / 1.008 * (math.pi / 2.0)
    signal = jnp.cos(angle_now) ** 2 / anchor
    return jnp.stack([jnp.sqrt(signal), jnp.sqrt(1.0 - signal)], axis=1)


def tdot(left_side, right_side):
    return lax.dot_general(
        left_side, right_side, (((0,), (0,)), ((), ())), preferred_element_type=jnp.float32
    )


def swap_bit(values, size, bit):
    return lax.ppermute(values, "dp", [(i, i ^ (1 << bit)) for i in range(size)])


def shift_copy(values, size, shift):
    return lax.ppermute(values, "copy", [(i, (i + shift) % size) for i in range(size)])


def copy_gather(values, size):
    parts = [values] + [shift_copy(values, size, size - j) for j in range(1, size)]
    return jnp.stack(parts)


def copy_reduce(chunks, size):
    total = chunks[0].astype(jnp.float32)
    for j in range(1, size):
        total = total + shift_copy(chunks[j], size, j).astype(jnp.float32)
    return total


def pick(values, index, axis):
    return lax.dynamic_index_in_dim(values, index, axis, keepdims=False)


def scatter_bits(values, me, size, bits):
    for bit in bits:
        mine = (me >> bit) & 1
        send = pick(values, 1 - mine, 0).astype(jnp.bfloat16)
        keep = pick(values, mine, 0)
        got = swap_bit(send, size, bit)
        values = (keep.astype(jnp.float32) + got.astype(jnp.float32)).astype(jnp.bfloat16)
    return values


def reduce_dp(values, size):
    me = lax.axis_index("dp")
    levels = size.bit_length() - 1
    rows, width = values.shape[1:]
    cube = values.reshape((2,) * levels + (rows, width))
    cube = jnp.moveaxis(cube, levels - 1, 0)
    cube = scatter_bits(cube, me, size, [0])
    rest = list(range(levels - 1, 0, -1))
    half = rows // 2 // 8 * 8
    first = scatter_bits(cube[..., :half, :], me, size, rest)
    second_cube = cube[..., half:, :]
    second_cube = jnp.transpose(
        second_cube, tuple(range(levels - 1))[::-1] + (levels - 1, levels)
    )
    second = scatter_bits(second_cube, me, size, rest[::-1])
    return jnp.concatenate([first, second], axis=0)


def reduce_all(values, dp_size, copy_size):
    rows, width = values.shape[2:]
    got = reduce_dp(values.reshape(dp_size, copy_size * rows, width), dp_size)
    got = got.reshape(copy_size, rows, width)
    me = lax.axis_index("copy")
    chunks = [pick(got, lax.rem(me + j, copy_size), 0) for j in range(copy_size)]
    return copy_reduce(chunks, copy_size)


def shards(
    block_input,
    image_ids,
    latents,
    noise,
    timesteps,
    norm_gains,
    block_biases,
    w_qkv,
    w_proj,
    w_up,
    up_bias,
    w_down,
    head_gain,
    head_biases,
    w_cond,
    w_time1,
    w_time2,
    w_input,
    w_ada,
    w_mlp1,
    w_mlp2,
    w_final,
    w_output,
    output_bias,
):
    bf16, f32 = jnp.bfloat16, jnp.float32
    dp_size, copy_size = lax.axis_size("dp"), lax.axis_size("copy")
    world = dp_size * copy_size
    place = lax.axis_index("copy")
    micros, _, own, _ = block_input.shape
    length = image_ids.shape[2]
    total = micros * length
    k_d, k_ff, k_w, k_t = D // world, w_down.shape[0], WIDTH // world, w_time1.shape[0]
    ff = k_ff * world
    score_scale = HEAD_DIM ** (-0.5)

    def cut(matrix, width):
        return [matrix[:, i : i + width] for i in range(0, matrix.shape[1], width)]

    def pad_flat(parts, width):
        flat = jnp.concatenate([p.reshape(-1) for p in parts])
        count = -(-flat.shape[0] // (8 * width)) * 8 * width
        return jnp.pad(flat, (0, count - flat.shape[0])).reshape(-1, width)

    block_parts = (
        cut(w_qkv, D)
        + [w_proj]
        + cut(w_up, D)
        + [w_down, pad_flat([norm_gains, block_biases, up_bias], D)]
    )
    head_parts = (
        [w_cond]
        + cut(w_ada, WIDTH)
        + [w_mlp1, w_mlp2]
        + cut(w_final, WIDTH)
        + [w_time1, w_time2, pad_flat([w_input, w_output, head_gain, head_biases], WIDTH)]
    )
    block_pack = lax.all_gather(jnp.concatenate(block_parts, 0), ("dp", "copy"), axis=0)
    head_pack = lax.all_gather(jnp.concatenate(head_parts, 0), ("dp", "copy"), axis=0)

    rows = jnp.moveaxis(copy_gather(block_input[:, 0], copy_size), 0, 1)
    rows = rows.reshape(total, D).astype(f32)

    def turned(values):
        twice = jnp.concatenate([values, values], axis=1)
        return lax.dynamic_slice_in_dim(twice, place * own, length, 1)

    ids = turned(image_ids[:, 0])
    latent_rows = turned(latents[:, 0]).reshape(total, CHANNELS)
    noise_rows = turned(noise[:, 0, 0]).reshape(total, CHANNELS)

    def unpack(pack, parts):
        out, at = [], 0
        for part in parts:
            out.append(pack[:, at : at + part.shape[0]].reshape(-1, pack.shape[2]))
            at += part.shape[0]
        return out

    block_full = unpack(block_pack, block_parts)
    w_q, w_k, w_v, w_proj_full = block_full[:4]
    w_up_full = jnp.concatenate(block_full[4:8], axis=1)
    w_down_full = block_full[8]
    small = block_full[9].reshape(world, -1)
    gains = small[:, : 2 * k_d].reshape(world, 2, k_d)
    gains = jnp.moveaxis(gains, 0, 1).reshape(2, D).astype(f32)
    biases = small[:, 2 * k_d : 8 * k_d].reshape(world, 6, k_d)
    biases = jnp.moveaxis(biases, 0, 1).reshape(6, D).astype(f32)
    up_bias_full = small[:, 8 * k_d : 8 * k_d + k_ff].reshape(ff).astype(f32)

    norm_one, inv_one = normalize(rows)
    first_in = (norm_one * gains[0] + biases[0]).astype(bf16)
    queries = (product(first_in, w_q) + biases[1]).astype(bf16)
    key_rows = product(first_in, w_k).astype(bf16)
    value_rows = (product(first_in, w_v) + biases[2]).astype(bf16)
    queries = queries.reshape(micros, length, HEADS, HEAD_DIM)
    key_rows = key_rows.reshape(micros, length, HEADS, HEAD_DIM)
    value_rows = value_rows.reshape(micros, length, HEADS, HEAD_DIM)
    same_image = (ids[:, :, None] == ids[:, None, :])[:, None]

    def attention_scores():
        scores = jnp.einsum("bqhd,bkhd->bhqk", queries, key_rows, preferred_element_type=f32)
        return jnp.where(same_image, scores * score_scale, -1e30)

    scores = attention_scores()
    row_max = jnp.max(scores, axis=-1, keepdims=True)
    exp_scores = jnp.exp(scores - row_max)
    row_total = jnp.sum(exp_scores, axis=-1, keepdims=True)
    log_total = row_max + jnp.log(row_total)
    attn_weights = (exp_scores / row_total).astype(bf16)
    mixed = jnp.einsum("bhqk,bkhd->bqhd", attn_weights, value_rows, preferred_element_type=f32)
    mixed = mixed.reshape(total, D).astype(bf16)
    middle = rows + product(mixed, w_proj_full) + biases[3]
    norm_two, inv_two = normalize(middle)
    second_in = (norm_two * gains[1] + biases[4]).astype(bf16)
    hidden = product(second_in, w_up_full) + up_bias_full
    active = jax.nn.gelu(hidden, approximate=False).astype(bf16)
    output = middle + product(active, w_down_full) + biases[5]
    condition = output.astype(bf16)

    head_full = unpack(head_pack, head_parts)
    w_cond_full, w_shift, w_scale, w_gate, w_one, w_two, w_fshift, w_fscale = head_full[:8]
    w_time1_full, w_time2_full = head_full[8:10]
    small = head_full[10].reshape(world, -1)
    at = CHANNELS * k_w
    w_input_full = small[:, :at].reshape(world, CHANNELS, k_w)
    w_input_full = jnp.moveaxis(w_input_full, 0, 1).reshape(CHANNELS, WIDTH)
    w_output_full = small[:, at : 2 * at].reshape(WIDTH, CHANNELS)
    head_gain_f = small[:, 2 * at : 2 * at + k_w].reshape(WIDTH).astype(f32)
    head_bias = small[:, 2 * at + k_w : 2 * at + 13 * k_w].reshape(world, 12, k_w)
    head_bias = jnp.moveaxis(head_bias, 0, 1).reshape(12, WIDTH).astype(f32)

    valid_rows = (ids >= 0).astype(f32).reshape(total, 1)
    slots = jnp.arange(micros * IMAGES, dtype=jnp.int32)
    row_slot = ids + IMAGES * jnp.arange(micros, dtype=jnp.int32)[:, None]
    row_slot = jnp.where(ids >= 0, row_slot, -1).reshape(total, 1)
    image_onehot = (row_slot == slots[None, :]).astype(f32)
    step_vals = timesteps[:, 0, 0].reshape(micros * IMAGES).astype(f32)
    sinusoid_in = sinusoid(step_vals).astype(bf16)
    time_one = product(sinusoid_in, w_time1_full) + head_bias[1]
    time_act = jax.nn.silu(time_one).astype(bf16)
    embedded = product(time_act, w_time2_full) + head_bias[2]
    cond_all = (
        product(condition, w_cond_full)
        + head_bias[0]
        + jnp.dot(image_onehot, embedded, precision=highest, preferred_element_type=f32)
    )
    gated = jax.nn.silu(cond_all).astype(bf16)
    shift_rows = product(gated, w_shift) + head_bias[7]
    scale_rows = product(gated, w_scale) + head_bias[8]
    gate_rows = product(gated, w_gate) + head_bias[9]
    mixing = jnp.dot(image_onehot, plan(step_vals), precision=highest, preferred_element_type=f32)
    noisy = (latent_rows * mixing[:, 0:1] + noise_rows * mixing[:, 1:2]).astype(bf16)
    entry_rows = product(noisy, w_input_full) + head_bias[3]
    norm_head, inv_head = normalize(entry_rows)
    affine = norm_head * head_gain_f + head_bias[4]
    mlp_in = (affine * (1.0 + scale_rows) + shift_rows).astype(bf16)
    inner_one = product(mlp_in, w_one) + head_bias[5]
    inner_act = jax.nn.silu(inner_one).astype(bf16)
    inner_two = product(inner_act, w_two) + head_bias[6]
    residual = entry_rows + gate_rows * inner_two
    fshift_rows = product(gated, w_fshift) + head_bias[10]
    fscale_rows = product(gated, w_fscale) + head_bias[11]
    norm_final, inv_final = normalize(residual)
    final_in = (norm_final * (1.0 + fscale_rows) + fshift_rows).astype(bf16)
    predicted = product(final_in, w_output_full) + output_bias.astype(f32)

    grad_pred = ((predicted - noise_rows) * valid_rows).astype(bf16)
    grad_out_bias = lax.psum(column_sum(grad_pred), ("dp", "copy"))
    grad_w_output = weight_grad(final_in, grad_pred)
    grad_final_in = input_back(grad_pred, w_output_full)
    grad_fshift = grad_final_in.astype(bf16)
    grad_fscale = (grad_final_in * norm_final).astype(bf16)
    grad_residual = norm_back(grad_final_in * (1.0 + fscale_rows), norm_final, inv_final)
    grad_gated = input_back(grad_fshift, w_fshift) + input_back(grad_fscale, w_fscale)
    grad_inner_two = (grad_residual * gate_rows).astype(bf16)
    grad_inner_one = (input_back(grad_inner_two, w_two) * silu_slope(inner_one)).astype(bf16)
    grad_mlp_in = input_back(grad_inner_one, w_one)
    grad_shift = grad_mlp_in.astype(bf16)
    grad_scale = (grad_mlp_in * affine).astype(bf16)
    grad_gate = (grad_residual * inner_two).astype(bf16)
    grad_affine = grad_mlp_in * (1.0 + scale_rows)
    grad_head_gain = jnp.sum(grad_affine * norm_head, axis=0)
    grad_entry = grad_residual + norm_back(grad_affine * head_gain_f, norm_head, inv_head)
    grad_entry = grad_entry.astype(bf16)
    grad_w_input = weight_grad(noisy, grad_entry)
    grad_gated = (
        grad_gated
        + input_back(grad_shift, w_shift)
        + input_back(grad_scale, w_scale)
        + input_back(grad_gate, w_gate)
    )
    grad_cond = grad_gated * silu_slope(cond_all)
    grad_cond_low = grad_cond.astype(bf16)
    grad_condition = input_back(grad_cond_low, w_cond_full).astype(bf16)

    chunks = grad_condition.reshape(micros, copy_size, own, D)
    grad_z_own = copy_reduce([chunks[:, j] for j in range(copy_size)], copy_size).astype(bf16)

    grad_embedded = lax.dot_general(
        image_onehot,
        grad_cond,
        (((0,), (0,)), ((), ())),
        precision=highest,
        preferred_element_type=f32,
    ).astype(bf16)
    grad_time_one = (input_back(grad_embedded, w_time2_full) * silu_slope(time_one)).astype(bf16)

    def grad_pack(pieces, width):
        split = [p.astype(bf16).reshape(dp_size, copy_size, -1, width) for p in pieces]
        return jnp.concatenate(split, axis=2)

    def split_pack(pack, parts):
        out, at = [], 0
        for rows_of in parts:
            out.append(pack[at : at + rows_of])
            at += rows_of
        return out

    pack_one = grad_pack(
        [
            weight_grad(gated, grad_fshift),
            weight_grad(gated, grad_fscale),
            weight_grad(inner_act, grad_inner_two),
            weight_grad(mlp_in, grad_inner_one),
        ],
        WIDTH,
    )
    own_fshift, own_fscale, own_two, own_one = split_pack(
        reduce_all(pack_one, dp_size, copy_size), [k_w] * 4
    )
    head_bias_grad = jnp.stack(
        [
            column_sum(grad_cond_low),
            column_sum(grad_time_one),
            column_sum(grad_embedded),
            column_sum(grad_entry),
            jnp.sum(grad_affine, axis=0),
            column_sum(grad_inner_one),
            column_sum(grad_inner_two),
            column_sum(grad_shift),
            column_sum(grad_scale),
            column_sum(grad_gate),
            column_sum(grad_fshift),
            column_sum(grad_fscale),
        ]
    )

    def owned(values, count):
        return jnp.moveaxis(values.reshape(count, world, -1), 1, 0).reshape(world, -1)

    small_grads = jnp.concatenate(
        [
            owned(grad_w_input, CHANNELS),
            grad_w_output.reshape(world, -1),
            owned(grad_head_gain[None], 1),
            owned(head_bias_grad, 12),
        ],
        axis=1,
    )
    small_rows = -(-small_grads.shape[1] // (8 * WIDTH)) * 8
    small_grads = jnp.pad(
        small_grads, ((0, 0), (0, small_rows * WIDTH - small_grads.shape[1]))
    ).reshape(world * small_rows, WIDTH)
    pack_two = grad_pack(
        [
            weight_grad(gated, grad_shift),
            weight_grad(gated, grad_scale),
            weight_grad(gated, grad_gate),
            weight_grad(condition, grad_cond_low),
            weight_grad(time_act, grad_embedded),
            weight_grad(sinusoid_in, grad_time_one),
            small_grads,
        ],
        WIDTH,
    )
    own_shift, own_scale, own_gate, own_cond, own_time2, own_time1, own_small = split_pack(
        reduce_all(pack_two, dp_size, copy_size), [k_w] * 3 + [k_d, k_w, k_t, small_rows]
    )
    own_small = own_small.reshape(-1)
    own_w_input = own_small[:at].reshape(CHANNELS, k_w)
    own_w_output = own_small[at : 2 * at].reshape(k_w, CHANNELS)
    own_head_gain = own_small[2 * at : 2 * at + k_w]
    own_head_biases = own_small[2 * at + k_w : 2 * at + 13 * k_w].reshape(12, k_w)

    grad_z = jnp.moveaxis(copy_gather(grad_z_own, copy_size), 0, 1).reshape(total, D)
    grad_down = grad_z
    grad_hidden = (input_back(grad_down, w_down_full) * gelu_slope(hidden)).astype(bf16)
    grad_second = input_back(grad_hidden, w_up_full)
    grad_middle = grad_z.astype(f32) + norm_back(grad_second * gains[1], norm_two, inv_two)
    grad_branch = grad_middle.astype(bf16)
    grad_mixed = input_back(grad_branch, w_proj_full).astype(bf16)
    grad_mixed = grad_mixed.reshape(micros, length, HEADS, HEAD_DIM)
    probs = jnp.exp(attention_scores() - log_total)
    grad_probs = jnp.einsum("bqhd,bkhd->bhqk", grad_mixed, value_rows, preferred_element_type=f32)
    delta = jnp.sum(grad_probs * probs, axis=-1, keepdims=True)
    grad_scores = (probs * (grad_probs - delta)).astype(bf16)
    grad_queries = (
        jnp.einsum("bhqk,bkhd->bqhd", grad_scores, key_rows, preferred_element_type=f32)
        * score_scale
    )
    grad_keys = (
        jnp.einsum("bhqk,bqhd->bkhd", grad_scores, queries, preferred_element_type=f32)
        * score_scale
    )
    grad_values = jnp.einsum(
        "bhqk,bqhd->bkhd", probs.astype(bf16), grad_mixed, preferred_element_type=f32
    )
    grad_q = grad_queries.astype(bf16).reshape(total, D)
    grad_k = grad_keys.astype(bf16).reshape(total, D)
    grad_v = grad_values.astype(bf16).reshape(total, D)
    grad_first = input_back(grad_q, w_q) + input_back(grad_k, w_k) + input_back(grad_v, w_v)

    def chosen(values):
        width = values.shape[1]
        k = width // world
        source = jnp.arange(width, dtype=jnp.int32)[:, None]
        target = jnp.arange(dp_size * k, dtype=jnp.int32)[None, :]
        wanted = (target // k * copy_size + place) * k + target % k
        return product(values, (source == wanted).astype(bf16)).astype(bf16)

    def block_pack_of(pieces, width):
        split = [p.astype(bf16).reshape(dp_size, -1, width) for p in pieces]
        return jnp.concatenate(split, axis=1)

    second_z = chosen(second_in)
    grads_up = [weight_grad(second_z, g) for g in cut(grad_hidden, D)]
    pack_three = block_pack_of(grads_up + [weight_grad(chosen(active), grad_down)], D)
    own_up_down = reduce_dp(pack_three, dp_size).astype(f32)
    own_up = jnp.concatenate(split_pack(own_up_down, [k_d] * 4), axis=1)
    own_down = own_up_down[4 * k_d :]

    first_z = chosen(first_in)
    mixed_z = chosen(mixed)
    block_small = jnp.concatenate(
        [
            owned(
                jnp.stack(
                    [jnp.sum(grad_first * norm_one, axis=0), jnp.sum(grad_second * norm_two, axis=0)]
                ),
                2,
            ),
            owned(
                jnp.stack(
                    [
                        jnp.sum(grad_first, axis=0),
                        column_sum(grad_q),
                        column_sum(grad_v),
                        column_sum(grad_branch),
                        jnp.sum(grad_second, axis=0),
                        column_sum(grad_down),
                    ]
                ),
                6,
            ),
            owned(column_sum(grad_hidden)[None], 1),
        ],
        axis=1,
    )
    block_small = pick(block_small.reshape(dp_size, copy_size, -1), place, 1)
    block_rows = -(-block_small.shape[1] // (8 * D)) * 8
    block_small = jnp.pad(
        block_small, ((0, 0), (0, block_rows * D - block_small.shape[1]))
    ).reshape(dp_size * block_rows, D)
    pack_four = block_pack_of(
        [
            weight_grad(first_z, grad_q),
            weight_grad(first_z, grad_k),
            weight_grad(first_z, grad_v),
            weight_grad(mixed_z, grad_branch),
            block_small,
        ],
        D,
    )
    own_four = reduce_dp(pack_four, dp_size).astype(f32)
    own_q, own_k, own_v, own_proj, own_rest = split_pack(own_four, [k_d] * 4 + [block_rows])
    own_rest = own_rest.reshape(-1)
    own_gains = own_rest[: 2 * k_d].reshape(2, k_d)
    own_biases = own_rest[2 * k_d : 8 * k_d].reshape(6, k_d)
    own_up_bias = own_rest[8 * k_d : 8 * k_d + k_ff]

    mine = grad_first.reshape(micros, length, D)[:, :own].reshape(micros * own, D)
    mine_norm = norm_one.reshape(micros, length, D)[:, :own].reshape(micros * own, D)
    mine_inv = inv_one.reshape(micros, length, 1)[:, :own].reshape(micros * own, 1)
    mine_middle = grad_middle.reshape(micros, length, D)[:, :own].reshape(micros * own, D)
    input_grad = mine_middle + norm_back(mine * gains[0], mine_norm, mine_inv)
    input_grad = input_grad.reshape(micros, 1, own, D)
    block_output = condition.reshape(micros, length, D)[:, :own].reshape(micros, 1, own, D)
    return (
        block_output,
        input_grad,
        own_gains,
        own_biases,
        jnp.concatenate([own_q, own_k, own_v], axis=1),
        own_proj,
        own_up,
        own_up_bias,
        own_down,
        own_head_gain,
        own_head_biases,
        own_cond,
        own_time1,
        own_time2,
        own_w_input,
        jnp.concatenate([own_shift, own_scale, own_gate], axis=1),
        own_one,
        own_two,
        jnp.concatenate([own_fshift, own_fscale], axis=1),
        own_w_output,
        grad_out_bias,
    )


def solution(mesh):
    in_specs = (
        P(None, "dp", "copy", None),
        P(None, "dp", None),
        P(None, "dp", None, None),
        P(None, "copy", "dp", None, None),
        P(None, "copy", "dp", None),
        P(None, ("dp", "copy")),
        P(None, ("dp", "copy")),
        P(("dp", "copy"), None),
        P(("dp", "copy"), None),
        P(("dp", "copy"), None),
        P(("dp", "copy")),
        P(("dp", "copy"), None),
        P(("dp", "copy")),
        P(None, ("dp", "copy")),
        P(("dp", "copy"), None),
        P(("dp", "copy"), None),
        P(("dp", "copy"), None),
        P(None, ("dp", "copy")),
        P(("dp", "copy"), None),
        P(("dp", "copy"), None),
        P(("dp", "copy"), None),
        P(("dp", "copy"), None),
        P(("dp", "copy"), None),
        P(),
    )
    out_specs = (
        P(None, "dp", "copy", None),
        P(None, "dp", "copy", None),
        P(None, ("dp", "copy")),
        P(None, ("dp", "copy")),
        P(("dp", "copy"), None),
        P(("dp", "copy"), None),
        P(("dp", "copy"), None),
        P(("dp", "copy")),
        P(("dp", "copy"), None),
        P(("dp", "copy")),
        P(None, ("dp", "copy")),
        P(("dp", "copy"), None),
        P(("dp", "copy"), None),
        P(("dp", "copy"), None),
        P(None, ("dp", "copy")),
        P(("dp", "copy"), None),
        P(("dp", "copy"), None),
        P(("dp", "copy"), None),
        P(("dp", "copy"), None),
        P(("dp", "copy"), None),
        P(),
    )
    return jax.shard_map(shards, mesh=mesh, in_specs=in_specs, out_specs=out_specs, check_vma=False)
```

time: 2850 us -> 769 us (0.27)
  waiting for transfers between devices: 1950 us -> 234 us
  blocking collectives: 517 us -> 38.6 us
  local copies, waits for them, and re-layouts: 78.9 us -> 160 us
  starting transfers between devices: 2.39 us -> 35.4 us
    reduce_scatter x13 -> x0, waiting for transfers between devices: 1490 us -> none  [the longest x1 186 us: shards(): lax.psum_scatter(grads[16], ('dp', 'copy'), scatter_dimension=0, tiled=True)]
    all_gather x8 -> x0, blocking collectives: 423 us -> none  [the longest x1 70.6 us: shards(): lax.all_gather(w_time1, ('dp', 'copy'), axis=0, tiled=True)]
    unnamed x35 -> x2, waiting for transfers between devices: 330 us -> 0.03 us
    ppermute x0 -> x35, waiting for transfers between devices: none -> 137 us  [the longest x15 69 us: shift_copy(): lax.ppermute(values, 'copy', [(i, (i + shift) % size) for i in range(size)])]
    unnamed x2 -> x0, blocking collectives: 93.6 us -> none
    psum x0 -> x1, blocking collectives: none -> 38.6 us  [shards(): grad_out_bias = lax.psum(column_sum(grad_pred), ('dp', 'copy'))]
    slice x21 -> x40, local copies, waits for them, and re-layouts: 9.89 us -> 48 us  [the longest x6 37.8 us: unpack(): out.append(pack[:, at:at + part.shape[0]].reshape(-1, pack.shape[2]))]
    ppermute x0 -> x35, starting transfers between devices: none -> 35.3 us  [the longest x20 17.9 us: swap_bit(): return lax.ppermute(values, 'dp', [(i, i ^ 1 << bit) for i in range(size)])]
  transfers between devices with their start and end apart: 30 -> 37, of which waited for: 19 -> 21; matrix products, arithmetic and copies ran while one was open for 9% -> 37% of each run, Pallas kernels for 0% -> 0%
where the time goes in v1:
time: 769 us; the launch traced here: 756 us
  waiting for transfers between devices  234 us (30%)
  matrix products  208 us (27%)
  local copies, waits for them, and re-layouts  160 us (21%)
  other arithmetic  63 us (8%)
  blocking collectives  38.6 us (5%)
  starting transfers between devices  35.4 us (5%)
  between operations  16.8 us (2%)
    all_gather x1, waiting for transfers between devices, shards(): lax.all_gather(jnp.concatenate(block_parts, 0), ('dp', 'copy'), axis=0)  69.9 us
    ppermute x15, waiting for transfers between devices, shift_copy(): lax.ppermute(values, 'copy', [(i, (i + shift) % size) for i in range(size)])  69 us
    ppermute x20, waiting for transfers between devices, swap_bit(): return lax.ppermute(values, 'dp', [(i, i ^ 1 << bit) for i in range(size)])  68.1 us
    dot_general x20, matrix products, product(): return jnp.dot(left_side, right_side, preferred_element_type=jnp.float32)  62.5 us
    dot_general x16, matrix products, input_back(): lax.dot_general(gradient, weight, (((1,), (1,)), ((), ())), preferred_ele...  52.2 us
    dot_general x21, matrix products, weight_grad(): lax.dot_general(left_side, right_side, (((0,), (0,)), ((), ())), preferre...  49.5 us
    unnamed x322, local copies, waits for them, and re-layouts  45.9 us
    psum x1, blocking collectives, shards(): grad_out_bias = lax.psum(column_sum(grad_pred), ('dp', 'copy'))  38.6 us
  transfers between devices with their start and end apart: 37, of which 21 were waited for; matrix products, arithmetic and copies ran while one was open for 37% of the time, Pallas kernels for 0%

profile of v1, /device:TPU:9, one launch (start us, length us, event | category | flops | bytes accessed | tf_op | source)
XLA Modules:
  0.0 756.4 jit_solution(11557644165368711527)
XLA Ops:
  38.6 8.1 %collective-permute-done.2 = bf16[2,96,768]{2,1,0:T(8,128)(2,1)S(1)} collective-permute-done((bf16[2,96,768]{2,1,0:T(8,128)(2,1)S(1)}, bf16[2,96,768]{2,1,0:T(8,128)(2,1)S(1)}, u32[]{:S(2)}, u32[]{:S(2)}) %collective-permute-start.2) | collective-permute-done | bytes 294944 | tf_op jit(solution)/shard_map/ppermute | solution.py:91
  46.7 16.8 %collective-permute-done.1 = bf16[2,96,768]{2,1,0:T(8,128)(2,1)S(1)} collective-permute-done((bf16[2,96,768]{2,1,0:T(8,128)(2,1)S(1)}, bf16[2,96,768]{2,1,0:T(8,128)(2,1)S(1)}, u32[]{:S(2)}, u32[]{:S(2)}) %collective-permute-start.1) | collective-permute-done | bytes 294944 | tf_op jit(solution)/shard_map/ppermute | solution.py:91
  63.5 2.4 collective-permute-done
  71.6 69.9 %all-gather.5.cloned.1.call-done = bf16[9472,768]{1,0:T(8,128)(2,1)} async-done(((bf16[296,768]{1,0:T(8,128)(2,1)}), bf16[9472,768]{1,0:T(8,128)(2,1)}) %all-gather.5.cloned.1.call-update) | async-done | bytes 14549008 | tf_op jit(solution)/shard_map/all_gather | solution.py:205
  142.5 4.8 slice.499
  150.9 7.9 %fusion.176 = (bf16[32,24,768]{2,1,0:T(8,128)(2,1)}, bf16[32,24,768]{2,1,0:T(8,128)(2,1)}, bf16[32,24,768]{2,1,0:T(8,128)(2,1)}, bf16[32,24,768]{2,1,0:T(8,128)(...) fusion(bf16[32,296,768]{2,1,0:T(8,128)(2,1)} %bitcast.458), kind=kLoop, calls=%fused_computation.495 | loop fusion | bytes 18874368 | tf_op jit(solution)/shard_map/slice | solution.py:222
  161.9 3.1 convolution_convert_fusion.12
  166.5 2.8 reshape.969
  169.3 4.2 add_convert_fusion.6
  173.5 2.4 copy.216
  175.8 3.6 reshape.965
  179.4 7.5 fusion.186
  186.9 7.4 fusion
  194.3 7.7 %fusion.51 = bf16[2,384,12,64]{1,3,2,0:T(8,128)(2,1)S(1)} fusion(f32[2,12,384,384]{2,3,1,0:T(8,128)} %get-tuple-element.220, f32[2,12,384]{2,1,0:T(8,128)S(1)} %fusion, f32[2,12,384]{2,1,0:T(8,128)S(1)} %get-tuple-element.219, bf16[2,384,12,64]{1,0,3,2:T(2,128)(2,1)S(1)} %copy-done.13), kind=kOutput, calls=%fused_computation.141 | convolution fusion | flops 464191488 | bytes 16588800 | tf_op jit(solution)/shard_map/bhqk,bkhd->bqhd/dot_general | solution.py:257
  207.8 27.2 %fusion.5 = (bf16[768,3072]{1,0:T(8,128)(2,1)S(1)}, f32[768,3072]{1,0:T(8,128)}) fusion(f32[3072]{0:T(1024)S(1)} %copy-done.92, bf16[768,768]{1,0:T(8,128)(2,1)S(1)} %add_convert_fusion.4, bf16[768,768]{1,0:T(8,128)(2,1)S(1)} %bitcast.530, bf16[768,768]{1,0:T(8,128)(2,1)S(1)} %bitcast.532, bf16[768,768]{1,0:T(8,128)(2,1)S(1)} %bitcast.534, ...), kind=kOutput, calls=%fused_computation.14 | convolution fusion | flops 3798466560 | bytes 20066304 | tf_op jit(solution)/shard_map/dot_general | solution.py:22
  235.0 3.8 add_convert_fusion.3
  241.9 27.1 %all-gather.7.cloned.1.call-done = bf16[9472,1024]{1,0:T(8,128)(2,1)} async-done(((bf16[296,1024]{1,0:T(8,128)(2,1)}), bf16[9472,1024]{1,0:T(8,128)(2,1)}) %all-gather.7.cloned.1.call-update) | async-done | bytes 19398672 | tf_op jit(solution)/shard_map/all_gather | solution.py:206
  270.5 2.7 slice.508
  273.3 20.2 %fusion.175 = (bf16[32,32,1024]{2,1,0:T(8,128)(2,1)}, bf16[32,32,1024]{2,1,0:T(8,128)(2,1)}, bf16[32,32,1024]{2,1,0:T(8,128)(2,1)}, bf16[32,32,1024]{2,1,0:T(8,1...) fusion(bf16[32,296,1024]{2,1,0:T(8,128)(2,1)} %bitcast.452), kind=kLoop, calls=%fused_computation.494 | loop fusion | bytes 33554432 | tf_op jit(solution)/shard_map/slice | solution.py:222
  301.2 3.8 multiply_convert_fusion.7
  311.7 2.5 add_convert_fusion.2
  320.2 3.6 add_convert_fusion.1
  326.5 3.2 fusion.165
  332.2 2.5 fusion.190
  334.8 3.3 convolution_convert_fusion.2
  338.1 3.2 convolution_convert_fusion.1
  341.2 5.3 multiply_reduce_fusion.1
  346.6 3.3 fusion.169
  349.9 3.5 fusion.197
  353.4 3.2 convolution_convert_fusion.6
  358.5 3.2 convolution_convert_fusion.7
  361.7 3.5 fusion.196
  365.2 3.2 convolution_convert_fusion.3
  370.2 3.7 convolution_convert_fusion.4
  373.9 3.3 convolution_convert_fusion.5
  377.2 4.7 convert_reduce_fusion.7
  381.9 2.5 convolution_convert_fusion.11
  385.7 2.7 convolution_convert_fusion.8
  391.0 38.6 %psum.7 = f32[16]{0:T(128)} all-reduce(f32[16]{0:T(128)S(1)} %get-tuple-element.250), channel_id=1, replica_groups=mesh['dp'=8,'copy'=4] {'dp','copy'}, use_global_device_ids=true, to_apply=%region_42.43 | all-reduce | flops 16 | bytes 128 | tf_op jit(solution)/shard_map/psum | solution.py:315
  437.1 4.4 pad_maximum_fusion
  441.5 3.4 constant_dynamic-slice_fusion.2
  444.9 2.4 copy.350
  460.3 3.1 collective-permute-done.5
  466.3 9.5 %constant_dynamic-slice_fusion.4 = (bf16[2,2,1,672,1024]{4,3,2,1,0:T(8,128)(2,1)}, bf16[2,2,1,672,1024]{4,3,2,1,0:T(8,128)(2,1)}) fusion(bf16[2,2,2,672,1024]{4,3,2,1,0:T(8,128)(2,1)} %bitcast.109, s32[]{:T(128)S(6)} %select_n.157, s32[]{:T(128)S(6)} %select_n.158), kind=kLoop, calls=%fused_computation.385 | loop fusion | bytes 22020104 | tf_op jit(solution)/shard_map/dynamic-slice.8
  475.9 5.7 copy.349
  483.2 6.8 collective-permute-done.7
  492.0 10.8 %convert_reduce_fusion = (bf16[3072]{0:T(1024)(128)(2,1)}, bf16[768,3072]{1,0:T(8,128)(2,1)S(1)}) fusion(f32[768,3072]{1,0:T(8,128)} %get-tuple-element.224, f32[3072]{0:T(1024)S(1)} %copy-done.93, bf16[768,768]{1,0:T(8,128)(2,1)S(1)} %bitcast.489, bf16[3072,768]{1,0:T(8,128)(2,1)S(1)} %bitcast.478), kind=kOutput, calls=%fused_computation.22 | convolution fusion | flops 3654546432 | bytes 20072448 | tf_op jit(solution)/shard_map/dot_general | solution.py:32
  502.8 4.9 multiply_reduce_fusion.7
  510.9 2.5 convolution_convert_fusion.10
  519.7 2.8 reshape.999
  522.5 8.8 %convert_reduce_fusion.3 = (bf16[12,64]{1,0:T(8,128)(2,1)S(1)}, bf16[2,384,12,64]{1,3,2,0:T(8,128)(2,1)}) fusion(f32[2,12,384,384]{2,3,1,0:T(8,128)} %get-tuple-element.220, f32[2,12,384]{2,1,0:T(8,128)} %log_add_fusion, bf16[2,384,12,64]{1,0,3,2:T(2,128)(2,1)S(1)} %reshape.999), kind=kOutput, calls=%fused_computation.106 | convolution fusion | flops 461831424 | bytes 16553472 | tf_op jit(solution)/shard_map/bhqk,bqhd->bkhd/dot_general | solution.py:452
  531.3 10.4 %multiply_reduce_fusion = (f32[2,12,384]{2,1,0:T(8,128)S(1)}, f32[2,12,384,384]{2,3,1,0:T(8,128)}) fusion(f32[2,12,384,384]{2,3,1,0:T(8,128)} %get-tuple-element.220, f32[2,12,384]{2,1,0:T(8,128)S(1)} %copy-done.57, bf16[2,384,12,64]{1,0,3,2:T(2,128)(2,1)S(1)} %copy-done.14, bf16[2,384,12,64]{1,0,3,2:T(2,128)(2,1)S(1)} %reshape.999), kind=kOutput, calls=%fused_computation.1 | convolution fusion | flops 463592448 | bytes 30744576 | tf_op jit(solution)/shard_map/bqhd,bkhd->bhqk/dot_general | solution.py:441
  541.8 7.3 multiply_convert_fusion
  549.2 2.6 fusion.56
  560.4 3.8 fusion.39
  568.8 9.9 %convolution_convert_fusion.9 = bf16[768,768]{1,0:T(8,128)(2,1)} fusion(bf16[768,768]{1,0:T(8,128)(2,1)S(1)} %bitcast.490, bf16[768,3072]{1,0:T(8,128)(2,1)} %copy-done.118, s32[768]{0:T(1024)} %fusion.133), kind=kOutput, calls=%fused_computation.137 | convolution fusion | flops 4533387264 | bytes 7080960 | tf_op jit(solution)/shard_map/dot_general | solution.py:26
  612.5 4.3 fusion.20
  621.6 23.5 %collective-permute-done.18 = bf16[96,768]{1,0:T(8,128)(2,1)S(1)} collective-permute-done((bf16[96,768]{1,0:T(8,128)(2,1)S(1)}, bf16[96,768]{1,0:T(8,128)(2,1)S(1)}, u32[]{:S(2)}, u32[]{:S(2)}) %collective-permute-start.18) | collective-permute-done | bytes 147488 | tf_op jit(solution)/shard_map/ppermute | solution.py:87
  647.8 5.4 fusion.1
  658.6 35.3 %collective-permute-done.29 = bf16[256,1024]{1,0:T(8,128)(2,1)S(1)} collective-permute-done((bf16[256,1024]{1,0:T(8,128)(2,1)S(1)}, bf16[256,1024]{1,0:T(8,128)(2,1)S(1)}, u32[]{:S(2)}, u32[]{:S(2)}) %collective-permute-start.29) | collective-permute-done | bytes 524320 | tf_op jit(solution)/shard_map/ppermute | solution.py:87
  699.9 5.9 collective-permute-done.34
  710.6 3.8 collective-permute-start.24
  719.9 5.5 collective-permute-done.24
  726.1 17.7 %collective-permute-done.25 = bf16[168,1024]{1,0:T(8,128)(2,1)S(1)} collective-permute-done((bf16[168,1024]{1,0:T(8,128)(2,1)S(1)}, bf16[168,1024]{1,0:T(8,128)(2,1)S(1)}, u32[]{:S(2)}, u32[]{:S(2)}) %collective-permute-start.25) | collective-permute-done | bytes 344096 | tf_op jit(solution)/shard_map/ppermute | solution.py:91
  (668 shorter events, 206.5 us)
Async XLA Ops:
  7.2 19.6 %copy-start.65 = (bf16[32,2048]{1,0:T(8,128)(2,1)S(1)}, bf16[32,2048]{1,0:T(8,128)(2,1)}, u32[]{:S(2)}) copy-start(bf16[32,2048]{1,0:T(8,128)(2,1)} %param.45) | copy-start | bytes 393220
  7.2 19.6 %copy-start.91 = (bf16[8,1024]{1,0:T(8,128)(2,1)S(1)}, bf16[8,1024]{1,0:T(8,128)(2,1)}, u32[]{:S(2)}) copy-start(bf16[8,1024]{1,0:T(8,128)(2,1)} %param.39) | copy-start | bytes 49156
  7.2 19.6 %copy-start.75 = (bf16[32,1024]{1,0:T(8,128)(2,1)S(1)}, bf16[32,1024]{1,0:T(8,128)(2,1)}, u32[]{:S(2)}) copy-start(bf16[32,1024]{1,0:T(8,128)(2,1)} %param.40) | copy-start | bytes 196612
  7.2 20.5 %copy-start.60 = (bf16[2,1,96,768]{3,2,1,0:T(8,128)(2,1)S(1)}, bf16[2,1,96,768]{3,2,1,0:T(8,128)(2,1)}, u32[]{:S(2)}) copy-start(bf16[2,1,96,768]{3,2,1,0:T(8,128)(2,1)} %param.24) | copy-start | bytes 884740
  7.2 24.3 %copy-start.104 = (bf16[16]{0:T(256)(128)(2,1)S(1)}, bf16[16]{0:T(256)(128)(2,1)}, u32[]{:S(2)}) copy-start(bf16[16]{0:T(256)(128)(2,1)} %param.47) | copy-start | bytes 100
  7.2 24.8 %copy-start.102 = (s32[2,1,1,4]{3,2,1,0:T(1,128)S(1)}, s32[2,1,1,4]{3,2,1,0:T(1,128)}, u32[]{:S(2)}) copy-start(s32[2,1,1,4]{3,2,1,0:T(1,128)} %param.28) | copy-start | bytes 100
  7.3 25.1 %copy-start.98 = (s32[2,1,384]{2,1,0:T(1,128)S(1)}, s32[2,1,384]{2,1,0:T(1,128)}, u32[]{:S(2)}) copy-start(s32[2,1,384]{2,1,0:T(1,128)} %param.25) | copy-start | bytes 9220
  7.3 26.5 %copy-start.76 = (f32[2,1,1,384,16]{3,4,2,1,0:T(8,128)S(1)}, f32[2,1,1,384,16]{3,4,2,1,0:T(8,128)}, u32[]{:S(2)}) copy-start(f32[2,1,1,384,16]{3,4,2,1,0:T(8,128)} %param.27) | copy-start | bytes 147460
  7.3 26.5 %copy-start.77 = (f32[2,1,384,16]{2,3,1,0:T(8,128)S(1)}, f32[2,1,384,16]{2,3,1,0:T(8,128)}, u32[]{:S(2)}) copy-start(f32[2,1,384,16]{2,3,1,0:T(8,128)} %param.26) | copy-start | bytes 147460
  7.3 134.2 %all-gather.5.cloned.1.call-start = ((), (), s32[]{:S(2)}) async-start(), calls=%async_computation | async-start | bytes 15003648 | tf_op jit(solution)/shard_map/all_gather | solution.py:205
  17.7 251.4 %all-gather.7.cloned.1.call-start = ((), (), s32[]{:S(2)}) async-start(), calls=%async_computation.1 | async-start | bytes 20004864 | tf_op jit(solution)/shard_map/all_gather | solution.py:206
  27.7 19.0 %collective-permute-start.2 = (bf16[2,96,768]{2,1,0:T(8,128)(2,1)S(1)}, bf16[2,96,768]{2,1,0:T(8,128)(2,1)S(1)}, u32[]{:S(2)}, u32[]{:S(2)}) collective-permute-start(bf16[2,96,768]{2,1,0:T(8,128)(2,1)S(1)} %bitcast.558), channel_id=1, source_target_pairs={{0,1},{1,2},{2,3},{3,0},{4,5},{5,6},{6,7},{7,4},{8,9},{9,10},{10,1... | collective-permute-start | bytes 884744 | tf_op jit(solution)/shard_map/ppermute | solution.py:91
  29.0 34.4 %collective-permute-start.1 = (bf16[2,96,768]{2,1,0:T(8,128)(2,1)S(1)}, bf16[2,96,768]{2,1,0:T(8,128)(2,1)S(1)}, u32[]{:S(2)}, u32[]{:S(2)}) collective-permute-start(bf16[2,96,768]{2,1,0:T(8,128)(2,1)S(1)} %bitcast.559), channel_id=1, source_target_pairs={{0,2},{1,3},{2,0},{3,1},{4,6},{5,7},{6,4},{7,5},{8,10},{9,11},{10,... | collective-permute-start | bytes 884744 | tf_op jit(solution)/shard_map/ppermute | solution.py:91
  30.1 35.7 %collective-permute-start = (bf16[2,96,768]{2,1,0:T(8,128)(2,1)S(1)}, bf16[2,96,768]{2,1,0:T(8,128)(2,1)S(1)}, u32[]{:S(2)}, u32[]{:S(2)}) collective-permute-start(bf16[2,96,768]{2,1,0:T(8,128)(2,1)S(1)} %bitcast.560), channel_id=1, source_target_pairs={{0,3},{1,0},{2,1},{3,2},{4,7},{5,4},{6,5},{7,6},{8,11},{9,8},{10,9... | collective-permute-start | bytes 884744 | tf_op jit(solution)/shard_map/ppermute | solution.py:91
  67.5 136.0 %copy-start = (bf16[4,2,96,768]{3,2,0,1:T(8,128)(2,1)}, bf16[4,2,96,768]{3,2,0,1:T(8,128)(2,1)S(1)}, u32[]{:S(2)}) copy-start(bf16[4,2,96,768]{3,2,0,1:T(8,128)(2,1)S(1)} %get-tuple-element.131) | copy-start | bytes 3538948
  148.4 57.6 %copy-start.80 = (f32[768]{0:T(1024)}, f32[768]{0:T(1024)S(1)}, u32[]{:S(2)}) copy-start(f32[768]{0:T(1024)S(1)} %mul.491) | copy-start | bytes 9220
  161.9 17.5 %copy-start.5 = (bf16[2,384,12,64]{1,0,3,2:T(2,128)(2,1)}, bf16[2,384,12,64]{1,0,3,2:T(2,128)(2,1)S(1)}, u32[]{:S(2)}) copy-start(bf16[2,384,12,64]{1,0,3,2:T(2,128)(2,1)S(1)} %reshape.967) | copy-start | bytes 3538948
  204.9 30.1 %copy-start.2 = (f32[768,768]{1,0:T(8,128)}, f32[768,768]{1,0:T(8,128)S(1)}, u32[]{:S(2)}) copy-start(f32[768,768]{1,0:T(8,128)S(1)} %get-tuple-element.222) | copy-start | bytes 7077892
  204.9 30.1 %slice-start.6 = ((s8[4718592]{0:T(1024)(128)(4,1)}), s8[4194304]{0:T(1024)(128)(4,1)S(1)}, s32[]{:S(2)}) async-start(s8[4718592]{0:T(1024)(128)(4,1)} %bitcast.473), calls=%async_computation.8 | async-start | bytes 8388608
  205.4 29.6 %copy-start.82 = (f32[768]{0:T(1024)}, f32[768]{0:T(1024)S(1)}, u32[]{:S(2)}) copy-start(f32[768]{0:T(1024)S(1)} %add_rsqrt_fusion.2) | copy-start | bytes 9220
  207.8 27.2 %slice-start.7 = ((s8[4718592]{0:T(1024)(128)(4,1)}), s8[524288]{0:T(1024)(128)(4,1)S(1)}, s32[]{:S(2)}) async-start(s8[4718592]{0:T(1024)(128)(4,1)} %bitcast.473), calls=%async_computation.9 | async-start | bytes 1048576
  207.8 27.2 %copy-start.97 = (f32[768]{0:T(1024)S(1)}, f32[768]{0:T(1024)}, u32[]{:S(2)}) copy-start(f32[768]{0:T(1024)} %add.714) | copy-start | bytes 9220
  273.3 22.4 %copy-start.68 = (bf16[2,2,8,384]{3,2,0,1:T(8,128)(2,1)S(1)}, bf16[2,2,8,384]{3,2,0,1:T(8,128)(2,1)}, u32[]{:S(2)}) copy-start(bf16[2,2,8,384]{3,2,0,1:T(8,128)(2,1)} %copy.290) | copy-start | bytes 73732
  389.0 41.5 %copy-start.10 = (bf16[768,1024]{1,0:T(8,128)(2,1)S(1)}, bf16[768,1024]{1,0:T(8,128)(2,1)}, u32[]{:S(2)}) copy-start(bf16[768,1024]{1,0:T(8,128)(2,1)} %get-tuple-element.124) | copy-start | bytes 4718596
  391.0 40.2 %copy-start.69 = (bf16[768,16,1]{0,1,2:T(8,128)(2,1)S(1)}, bf16[768,16,1]{0,1,2:T(8,128)(2,1)}, u32[]{:S(2)}) copy-start(bf16[768,16,1]{0,1,2:T(8,128)(2,1)} %reshape.1064) | copy-start | bytes 73732
  434.4 25.9 %collective-permute-start.3 = (bf16[2,96,768]{2,1,0:T(8,128)(2,1)S(1)}, bf16[2,96,768]{2,1,0:T(8,128)(2,1)}, u32[]{:S(2)}, u32[]{:S(2)}) collective-permute-start(bf16[2,96,768]{2,1,0:T(8,128)(2,1)S(1)} %get-tuple-element.178), channel_id=1, source_target_pairs={{0,1},{1,2},{2,3},{3,0},{4,5},{5,6},{6,7},{7,4},{8,9},{9,10},{10,1... | collective-permute-start | bytes 884744 | tf_op jit(solution)/shard_map/ppermute | solution.py:91
  434.8 25.5 %collective-permute-start.4 = (bf16[2,96,768]{2,1,0:T(8,128)(2,1)S(1)}, bf16[2,96,768]{2,1,0:T(8,128)(2,1)}, u32[]{:S(2)}, u32[]{:S(2)}) collective-permute-start(bf16[2,96,768]{2,1,0:T(8,128)(2,1)S(1)} %get-tuple-element.179), channel_id=1, source_target_pairs={{0,2},{1,3},{2,0},{3,1},{4,6},{5,7},{6,4},{7,5},{8,10},{9,11},{10,... | collective-permute-start | bytes 884744 | tf_op jit(solution)/shard_map/ppermute | solution.py:91
  436.9 26.6 %collective-permute-start.5 = (bf16[2,96,768]{2,1,0:T(8,128)(2,1)S(1)}, bf16[2,96,768]{2,1,0:T(8,128)(2,1)}, u32[]{:S(2)}, u32[]{:S(2)}) collective-permute-start(bf16[2,96,768]{2,1,0:T(8,128)(2,1)S(1)} %get-tuple-element.180), channel_id=1, source_target_pairs={{0,3},{1,0},{2,1},{3,2},{4,7},{5,4},{6,5},{7,6},{8,11},{9,8},{10,9... | collective-permute-start | bytes 884744 | tf_op jit(solution)/shard_map/ppermute | solution.py:91
  447.3 165.2 %collective-permute-start.27 = (bf16[2,2,512,1024]{3,2,0,1:T(8,128)(2,1)}, bf16[2,2,512,1024]{3,2,0,1:T(8,128)(2,1)}, u32[]{:S(2)}, u32[]{:S(2)}) collective-permute-start(bf16[2,2,512,1024]{3,2,0,1:T(8,128)(2,1)} %bitcast.438), channel_id=1, source_target_pairs={{0,4},{4,0},{8,12},{12,8},{16,20},{20,16},{24,28},{28,24},{1,5},{5... | collective-permute-start | bytes 12582920 | tf_op jit(solution)/shard_map/ppermute | solution.py:87
  464.8 18.4 %collective-permute-start.8 = (bf16[2,96,768]{2,1,0:T(8,128)(2,1)S(1)}, bf16[2,96,768]{2,1,0:T(8,128)(2,1)S(1)}, u32[]{:S(2)}, u32[]{:S(2)}) collective-permute-start(bf16[2,96,768]{2,1,0:T(8,128)(2,1)S(1)} %fusion.90), channel_id=1, source_target_pairs={{0,1},{1,2},{2,3},{3,0},{4,5},{5,6},{6,7},{7,4},{8,9},{9,10},{10,1... | collective-permute-start | bytes 884744 | tf_op jit(solution)/shard_map/ppermute | solution.py:91
  464.9 25.2 %collective-permute-start.7 = (bf16[2,96,768]{2,1,0:T(8,128)(2,1)S(1)}, bf16[2,96,768]{2,1,0:T(8,128)(2,1)S(1)}, u32[]{:S(2)}, u32[]{:S(2)}) collective-permute-start(bf16[2,96,768]{2,1,0:T(8,128)(2,1)S(1)} %fusion.90), channel_id=1, source_target_pairs={{0,2},{1,3},{2,0},{3,1},{4,6},{5,7},{6,4},{7,5},{8,10},{9,11},{10,... | collective-permute-start | bytes 884744 | tf_op jit(solution)/shard_map/ppermute | solution.py:91
  465.1 26.5 %collective-permute-start.6 = (bf16[2,96,768]{2,1,0:T(8,128)(2,1)S(1)}, bf16[2,96,768]{2,1,0:T(8,128)(2,1)S(1)}, u32[]{:S(2)}, u32[]{:S(2)}) collective-permute-start(bf16[2,96,768]{2,1,0:T(8,128)(2,1)S(1)} %fusion.90), channel_id=1, source_target_pairs={{0,3},{1,0},{2,1},{3,2},{4,7},{5,4},{6,5},{7,6},{8,11},{9,8},{10,9... | collective-permute-start | bytes 884744 | tf_op jit(solution)/shard_map/ppermute | solution.py:91
  475.8 16.0 %slice-start.8 = ((s8[4718592]{0:T(1024)(128)(4,1)}), s8[4194304]{0:T(1024)(128)(4,1)S(1)}, s32[]{:S(2)}) async-start(s8[4718592]{0:T(1024)(128)(4,1)} %bitcast.476), calls=%async_computation.10 | async-start | bytes 8388608
  475.8 16.0 %slice-start.9 = ((s8[4718592]{0:T(1024)(128)(4,1)}), s8[524288]{0:T(1024)(128)(4,1)S(1)}, s32[]{:S(2)}) async-start(s8[4718592]{0:T(1024)(128)(4,1)} %bitcast.476), calls=%async_computation.11 | async-start | bytes 1048576
  481.6 166.2 %collective-permute-start.19 = (bf16[2,2,672,1024]{3,2,0,1:T(8,128)(2,1)}, bf16[2,2,672,1024]{3,2,0,1:T(8,128)(2,1)}, u32[]{:S(2)}, u32[]{:S(2)}) collective-permute-start(bf16[2,2,672,1024]{3,2,0,1:T(8,128)(2,1)} %bitcast.437), channel_id=1, source_target_pairs={{0,4},{4,0},{8,12},{12,8},{16,20},{20,16},{24,28},{28,24},{1,5},{5... | collective-permute-start | bytes 16515080 | tf_op jit(solution)/shard_map/ppermute | solution.py:87
  491.9 15.8 %copy-start.18 = (bf16[4,2,96,768]{3,2,0,1:T(8,128)(2,1)}, bf16[4,2,96,768]{3,2,0,1:T(8,128)(2,1)S(1)}, u32[]{:S(2)}) copy-start(bf16[4,2,96,768]{3,2,0,1:T(8,128)(2,1)S(1)} %get-tuple-element.127) | copy-start | bytes 3538948
  522.5 19.3 %slice-start = ((s8[14155776]{0:T(1024)(128)(4,1)}), s8[4194304]{0:T(1024)(128)(4,1)S(1)}, s32[]{:S(2)}) async-start(s8[14155776]{0:T(1024)(128)(4,1)} %bitcast.445), calls=%async_computation.2 | async-start | bytes 8388608
  522.5 19.3 %slice-start.1 = ((s8[14155776]{0:T(1024)(128)(4,1)}), s8[4194304]{0:T(1024)(128)(4,1)S(1)}, s32[]{:S(2)}) async-start(s8[14155776]{0:T(1024)(128)(4,1)} %bitcast.445), calls=%async_computation.3 | async-start | bytes 8388608
  588.2 5.2 collective-permute-start.9
  591.6 17.3 %collective-permute-start.14 = (bf16[2,2,192,768]{3,2,0,1:T(8,128)(2,1)}, bf16[2,2,192,768]{3,2,0,1:T(8,128)(2,1)}, u32[]{:S(2)}, u32[]{:S(2)}) collective-permute-start(bf16[2,2,192,768]{3,2,0,1:T(8,128)(2,1)} %bitcast.439), channel_id=1, source_target_pairs={{0,4},{4,0},{8,12},{12,8},{16,20},{20,16},{24,28},{28,24},{1,5},{5... | collective-permute-start | bytes 3538952 | tf_op jit(solution)/shard_map/ppermute | solution.py:87
  593.6 6.1 collective-permute-start.10
  597.0 5.2 collective-permute-start.12
  599.7 4.4 collective-permute-start.11
  602.3 3.4 collective-permute-start.13
  610.7 7.3 collective-permute-start.17
  612.0 7.9 %collective-permute-start.15 = (bf16[2,96,768]{2,1,0:T(8,128)(2,1)S(1)}, bf16[2,96,768]{2,1,0:T(8,128)(2,1)S(1)}, u32[]{:S(2)}, u32[]{:S(2)}) collective-permute-start(bf16[2,96,768]{2,1,0:T(8,128)(2,1)S(1)} %dynamic-slice_bitcast_fusion.12), channel_id=1, source_target_pairs={{0,16},{4,20},{8,24},{12,28},{16,0},{20,4},{24,8},{28,12},{1,17},{... | collective-permute-start | bytes 884744 | tf_op jit(solution)/shard_map/ppermute | solution.py:87
  616.7 31.1 %slice-start.4 = ((s8[5505024]{0:T(1024)(128)(4,1)}), s8[4194304]{0:T(1024)(128)(4,1)S(1)}, s32[]{:S(2)}) async-start(s8[5505024]{0:T(1024)(128)(4,1)} %bitcast.448), calls=%async_computation.6 | async-start | bytes 8388608
  617.5 30.3 %slice-start.5 = ((s8[5505024]{0:T(1024)(128)(4,1)}), s8[1310720]{0:T(1024)(128)(4,1)S(1)}, s32[]{:S(2)}) async-start(s8[5505024]{0:T(1024)(128)(4,1)} %bitcast.448), calls=%async_computation.7 | async-start | bytes 2621440
  617.5 27.7 %collective-permute-start.30 = (bf16[2,256,1024]{2,1,0:T(8,128)(2,1)S(1)}, bf16[2,256,1024]{2,1,0:T(8,128)(2,1)S(1)}, u32[]{:S(2)}, u32[]{:S(2)}) collective-permute-start(bf16[2,256,1024]{2,1,0:T(8,128)(2,1)S(1)} %dynamic-slice_bitcast_fusion.2), channel_id=1, source_target_pairs={{0,8},{4,12},{8,0},{12,4},{16,24},{20,28},{24,16},{28,20},{1,9},{5... | collective-permute-start | bytes 3145736 | tf_op jit(solution)/shard_map/ppermute | solution.py:87
  618.3 28.2 %collective-permute-start.28 = (bf16[2,256,1024]{2,1,0:T(8,128)(2,1)S(1)}, bf16[2,256,1024]{2,1,0:T(8,128)(2,1)S(1)}, u32[]{:S(2)}, u32[]{:S(2)}) collective-permute-start(bf16[2,256,1024]{2,1,0:T(8,128)(2,1)S(1)} %dynamic-slice_bitcast_fusion.3), channel_id=1, source_target_pairs={{0,16},{4,20},{8,24},{12,28},{16,0},{20,4},{24,8},{28,12},{1,17},{... | collective-permute-start | bytes 3145736 | tf_op jit(solution)/shard_map/ppermute | solution.py:87
  619.2 25.9 %collective-permute-start.18 = (bf16[96,768]{1,0:T(8,128)(2,1)S(1)}, bf16[96,768]{1,0:T(8,128)(2,1)S(1)}, u32[]{:S(2)}, u32[]{:S(2)}) collective-permute-start(bf16[96,768]{1,0:T(8,128)(2,1)S(1)} %dynamic-slice_bitcast_fusion.17), channel_id=1, source_target_pairs={{0,16},{4,20},{8,24},{12,28},{16,0},{20,4},{24,8},{28,12},{1,17},{... | collective-permute-start | bytes 442376 | tf_op jit(solution)/shard_map/ppermute | solution.py:87
  620.6 36.7 %collective-permute-start.16 = (bf16[96,768]{1,0:T(8,128)(2,1)}, bf16[96,768]{1,0:T(8,128)(2,1)}, u32[]{:S(2)}, u32[]{:S(2)}) collective-permute-start(bf16[96,768]{1,0:T(8,128)(2,1)} %dynamic-slice_bitcast_fusion.18), channel_id=1, source_target_pairs={{0,8},{4,12},{8,0},{12,4},{16,24},{20,28},{24,16},{28,20},{1,9},{5... | collective-permute-start | bytes 442376 | tf_op jit(solution)/shard_map/ppermute | solution.py:87
  646.4 11.9 %collective-permute-start.31 = (bf16[256,1024]{1,0:T(8,128)(2,1)}, bf16[256,1024]{1,0:T(8,128)(2,1)S(1)}, u32[]{:S(2)}, u32[]{:S(2)}) collective-permute-start(bf16[256,1024]{1,0:T(8,128)(2,1)} %dynamic-slice_bitcast_fusion.6), channel_id=1, source_target_pairs={{0,16},{4,20},{8,24},{12,28},{16,0},{20,4},{24,8},{28,12},{1,17},{... | collective-permute-start | bytes 1572872 | tf_op jit(solution)/shard_map/ppermute | solution.py:87
  654.1 41.7 %collective-permute-start.22 = (bf16[2,336,1024]{2,1,0:T(8,128)(2,1)S(1)}, bf16[2,336,1024]{2,1,0:T(8,128)(2,1)S(1)}, u32[]{:S(2)}, u32[]{:S(2)}) collective-permute-start(bf16[2,336,1024]{2,1,0:T(8,128)(2,1)S(1)} %dynamic-slice_bitcast_fusion), channel_id=1, source_target_pairs={{0,8},{4,12},{8,0},{12,4},{16,24},{20,28},{24,16},{28,20},{1,9},{5... | collective-permute-start | bytes 4128776 | tf_op jit(solution)/shard_map/ppermute | solution.py:87
  655.2 38.7 %collective-permute-start.29 = (bf16[256,1024]{1,0:T(8,128)(2,1)S(1)}, bf16[256,1024]{1,0:T(8,128)(2,1)S(1)}, u32[]{:S(2)}, u32[]{:S(2)}) collective-permute-start(bf16[256,1024]{1,0:T(8,128)(2,1)S(1)} %dynamic-slice_bitcast_fusion.7), channel_id=1, source_target_pairs={{0,8},{4,12},{8,0},{12,4},{16,24},{20,28},{24,16},{28,20},{1,9},{5... | collective-permute-start | bytes 1572872 | tf_op jit(solution)/shard_map/ppermute | solution.py:87
  655.8 41.9 %collective-permute-start.20 = (bf16[2,336,1024]{2,1,0:T(8,128)(2,1)S(1)}, bf16[2,336,1024]{2,1,0:T(8,128)(2,1)S(1)}, u32[]{:S(2)}, u32[]{:S(2)}) collective-permute-start(bf16[2,336,1024]{2,1,0:T(8,128)(2,1)S(1)} %dynamic-slice_bitcast_fusion.1), channel_id=1, source_target_pairs={{0,16},{4,20},{8,24},{12,28},{16,0},{20,4},{24,8},{28,12},{1,17},{... | collective-permute-start | bytes 4128776 | tf_op jit(solution)/shard_map/ppermute | solution.py:87
  694.3 5.7 collective-permute-start.32
  694.3 11.4 %collective-permute-start.34 = (bf16[128,1024]{1,0:T(8,128)(2,1)S(1)}, bf16[128,1024]{1,0:T(8,128)(2,1)S(1)}, u32[]{:S(2)}, u32[]{:S(2)}) collective-permute-start(bf16[128,1024]{1,0:T(8,128)(2,1)S(1)} %get-tuple-element.182), channel_id=1, source_target_pairs={{0,3},{1,0},{2,1},{3,2},{4,7},{5,4},{6,5},{7,6},{8,11},{9,8},{10,9... | collective-permute-start | bytes 786440 | tf_op jit(solution)/shard_map/ppermute | solution.py:91
  695.8 10.5 %collective-permute-start.33 = (bf16[128,1024]{1,0:T(8,128)(2,1)S(1)}, bf16[128,1024]{1,0:T(8,128)(2,1)S(1)}, u32[]{:S(2)}, u32[]{:S(2)}) collective-permute-start(bf16[128,1024]{1,0:T(8,128)(2,1)S(1)} %get-tuple-element.183), channel_id=1, source_target_pairs={{0,2},{1,3},{2,0},{3,1},{4,6},{5,7},{6,4},{7,5},{8,10},{9,11},{10,... | collective-permute-start | bytes 786440 | tf_op jit(solution)/shard_map/ppermute | solution.py:91
  696.4 11.9 %collective-permute-start.23 = (bf16[336,1024]{1,0:T(8,128)(2,1)S(1)}, bf16[336,1024]{1,0:T(8,128)(2,1)S(1)}, u32[]{:S(2)}, u32[]{:S(2)}) collective-permute-start(bf16[336,1024]{1,0:T(8,128)(2,1)S(1)} %dynamic-slice_bitcast_fusion.4), channel_id=1, source_target_pairs={{0,16},{4,20},{8,24},{12,28},{16,0},{20,4},{24,8},{28,12},{1,17},{... | collective-permute-start | bytes 2064392 | tf_op jit(solution)/shard_map/ppermute | solution.py:87
  698.4 11.8 %collective-permute-start.21 = (bf16[336,1024]{1,0:T(8,128)(2,1)S(1)}, bf16[336,1024]{1,0:T(8,128)(2,1)S(1)}, u32[]{:S(2)}, u32[]{:S(2)}) collective-permute-start(bf16[336,1024]{1,0:T(8,128)(2,1)S(1)} %dynamic-slice_bitcast_fusion.5), channel_id=1, source_target_pairs={{0,8},{4,12},{8,0},{12,4},{16,24},{20,28},{24,16},{28,20},{1,9},{5... | collective-permute-start | bytes 2064392 | tf_op jit(solution)/shard_map/ppermute | solution.py:87
  710.6 14.8 %collective-permute-start.24 = (bf16[168,1024]{1,0:T(8,128)(2,1)S(1)}, bf16[168,1024]{1,0:T(8,128)(2,1)S(1)}, u32[]{:S(2)}, u32[]{:S(2)}) collective-permute-start(bf16[168,1024]{1,0:T(8,128)(2,1)S(1)} %get-tuple-element.170), channel_id=1, source_target_pairs={{0,1},{1,2},{2,3},{3,0},{4,5},{5,6},{6,7},{7,4},{8,9},{9,10},{10,1... | collective-permute-start | bytes 1032200 | tf_op jit(solution)/shard_map/ppermute | solution.py:91
  714.4 11.7 %collective-permute-start.26 = (bf16[168,1024]{1,0:T(8,128)(2,1)S(1)}, bf16[168,1024]{1,0:T(8,128)(2,1)S(1)}, u32[]{:S(2)}, u32[]{:S(2)}) collective-permute-start(bf16[168,1024]{1,0:T(8,128)(2,1)S(1)} %get-tuple-element.171), channel_id=1, source_target_pairs={{0,3},{1,0},{2,1},{3,2},{4,7},{5,4},{6,5},{7,6},{8,11},{9,8},{10,9... | collective-permute-start | bytes 1032200 | tf_op jit(solution)/shard_map/ppermute | solution.py:91
  716.4 27.3 %collective-permute-start.25 = (bf16[168,1024]{1,0:T(8,128)(2,1)S(1)}, bf16[168,1024]{1,0:T(8,128)(2,1)S(1)}, u32[]{:S(2)}, u32[]{:S(2)}) collective-permute-start(bf16[168,1024]{1,0:T(8,128)(2,1)S(1)} %get-tuple-element.172), channel_id=1, source_target_pairs={{0,2},{1,3},{2,0},{3,1},{4,6},{5,7},{6,4},{7,5},{8,10},{9,11},{10,... | collective-permute-start | bytes 1032200 | tf_op jit(solution)/shard_map/ppermute | solution.py:91
  (102 other events, 405.2 us)
Sparse Core Ops, SparseCore 0:
  17.8 123.6 all-gather.4
  144.3 124.7 all-gather.6

commit v2 on v1

v2 whole, which is shorter than its diff:
```python
import functools
import math

import jax
import jax.numpy as jnp
from jax import lax
from jax.experimental import pallas as pl
from jax.experimental.pallas import tpu as pltpu
from jax.sharding import PartitionSpec as P

D = 768
HEADS = 12
HEAD_DIM = 64
WIDTH = 1024
FREQ = 256
CHANNELS = 16
IMAGES = 4


epsilon = 1e-06
highest = lax.Precision.HIGHEST


def product(left_side, right_side):
    return jnp.dot(left_side, right_side, preferred_element_type=jnp.float32)


def weight_grad(left_side, right_side):
    return lax.dot_general(
        left_side, right_side, (((0,), (0,)), ((), ())), preferred_element_type=jnp.float32
    )


def input_back(gradient, weight):
    return lax.dot_general(
        gradient, weight, (((1,), (1,)), ((), ())), preferred_element_type=jnp.float32
    )


def column_sum(values):
    return jnp.sum(values.astype(jnp.float32), axis=0)


def normalize(values):
    center = values - jnp.mean(values, axis=-1, keepdims=True)
    inverse = lax.rsqrt(jnp.mean(center * center, axis=-1, keepdims=True) + epsilon)
    return (center * inverse, inverse)


def norm_back(gradient, normed, inverse):
    return inverse * (
        gradient
        - jnp.mean(gradient, axis=-1, keepdims=True)
        - normed * jnp.mean(gradient * normed, axis=-1, keepdims=True)
    )


def silu_slope(values):
    sigma = jax.nn.sigmoid(values)
    return sigma * (1.0 + values * (1.0 - sigma))


def gelu_slope(values):
    return 0.5 * (1.0 + lax.erf(values * 2.0 ** (-0.5))) + values * jnp.exp(
        -0.5 * values * values
    ) * (2.0 * math.pi) ** (-0.5)


def sinusoid(step_vals):
    half_width = FREQ // 2
    rates = jnp.exp(-math.log(10000.0) * jnp.arange(half_width, dtype=jnp.float32) / half_width)
    angles = step_vals[:, None] * rates[None, :]
    return jnp.concatenate([jnp.cos(angles), jnp.sin(angles)], axis=1)


def plan(step_vals):
    anchor = math.cos(0.008 / 1.008 * math.pi / 2.0) ** 2
    angle_now = ((step_vals + 1.0) / 1000.0 + 0.008) / 1.008 * (math.pi / 2.0)
    signal = jnp.cos(angle_now) ** 2 / anchor
    return jnp.stack([jnp.sqrt(signal), jnp.sqrt(1.0 - signal)], axis=1)


def tdot(left_side, right_side):
    return lax.dot_general(
        left_side, right_side, (((0,), (0,)), ((), ())), preferred_element_type=jnp.float32
    )


def swap_bit(values, size, bit):
    return lax.ppermute(values, "dp", [(i, i ^ (1 << bit)) for i in range(size)])


def shift_copy(values, size, shift):
    return lax.ppermute(values, "copy", [(i, (i + shift) % size) for i in range(size)])


def swap_copy(values, size, shift):
    return lax.ppermute(values, "copy", [(i, i ^ shift) for i in range(size)])


def pick(values, index, axis):
    return lax.dynamic_index_in_dim(values, index, axis, keepdims=False)


def tie(*values):
    return lax.optimization_barrier(values)


MIB = 1 << 20
LIGHT = pl.CostEstimate(flops=10**6, bytes_accessed=10**5, transcendentals=0)


def dot0(left_side, right_side):
    return lax.dot_general(
        left_side, right_side, (((0,), (0,)), ((), ())), preferred_element_type=jnp.float32
    )


def dot1(left_side, right_side):
    return lax.dot_general(
        left_side, right_side, (((1,), (1,)), ((), ())), preferred_element_type=jnp.float32
    )


def small_call(body, outs, scalars, ins):
    size = sum(math.prod(o.shape) * o.dtype.itemsize for o in outs)
    size += sum(math.prod(v.shape) * v.dtype.itemsize for v in ins)
    return pl.pallas_call(
        body,
        out_shape=outs,
        in_specs=[pl.BlockSpec(memory_space=pltpu.SMEM)]
        + [pl.BlockSpec(memory_space=pltpu.VMEM)] * len(ins),
        out_specs=[pl.BlockSpec(memory_space=pltpu.VMEM)] * len(outs),
        compiler_params=pltpu.CompilerParams(vmem_limit_bytes=2 * size + 16 * MIB),
        cost_estimate=LIGHT,
    )(jnp.stack([jnp.asarray(v, jnp.int32) for v in scalars]), *ins)


def low_shape(*dims):
    return jax.ShapeDtypeStruct(dims, jnp.bfloat16)


def add_up(one, two):
    return one.astype(jnp.float32) + two.astype(jnp.float32)


def cut_first(keep, got, rows, bits, kernels):
    count, mids, total, width = keep.shape
    half = count // 2

    if not kernels:
        sums = add_up(keep, got).astype(jnp.bfloat16)
        first = sums[:, :, :rows].reshape(2, half, mids, rows, width)
        second = sums[:, :, rows:].reshape(half, 2, mids, total - rows, width)
        return [
            pick(first, 1 - bits[0], 0),
            pick(first, bits[0], 0),
            pick(second, 1 - bits[1], 1),
            pick(second, bits[1], 1),
        ]

    def body(at, keep_ref, got_ref, *outs):
        for out, bit, top in zip(outs, (1 - at[0], at[0], 1 - at[1], at[1]), (0, 0, 1, 1)):
            cut = pl.ds(rows, total - rows) if top else pl.ds(0, rows)
            for i in range(half):
                p = 2 * i + bit if top else bit * half + i
                out[i] = add_up(keep_ref[p, :, cut], got_ref[p, :, cut]).astype(jnp.bfloat16)

    outs = [low_shape(half, mids, n, width) for n in (rows, rows, total - rows, total - rows)]
    return small_call(body, outs, bits, [keep, got])


def cut_next(keeps, gots, bits, kernels):
    count, mids, _, width = keeps[0].shape
    half = count // 2
    sizes = [k.shape[2] for k in keeps]
    if not kernels:
        sums = [add_up(k, g).astype(jnp.bfloat16) for k, g in zip(keeps, gots)]
        first = sums[0].reshape(2, half, mids, sizes[0], width)
        second = sums[1].reshape(half, 2, mids, sizes[1], width)
        return [
            pick(first, 1 - bits[0], 0),
            pick(first, bits[0], 0),
            pick(second, 1 - bits[1], 1),
            pick(second, bits[1], 1),
        ]

    def body(at, keep_one, got_one, keep_two, got_two, *outs):
        for out, bit, top in zip(outs, (1 - at[0], at[0], 1 - at[1], at[1]), (0, 0, 1, 1)):
            keep, got = (keep_two, got_two) if top else (keep_one, got_one)
            for i in range(half):
                p = 2 * i + bit if top else bit * half + i
                out[i] = add_up(keep[p], got[p]).astype(jnp.bfloat16)

    outs = [low_shape(half, mids, n, width) for n in (sizes[0], sizes[0], sizes[1], sizes[1])]
    return small_call(body, outs, bits, [keeps[0], gots[0], keeps[1], gots[1]])


def cut_copies(keeps, gots, place, copy_size, kernels):
    _, mids, _, width = keeps[0].shape
    sizes = [k.shape[2] for k in keeps]
    total = sum(sizes)
    if not kernels:
        sums = jnp.concatenate([add_up(k, g)[0] for k, g in zip(keeps, gots)], axis=1)
        sums = sums.astype(jnp.bfloat16).reshape(2, copy_size, total, width)
        return [pick(sums, lax.rem(place + j, copy_size), 1) for j in range(copy_size)]

    def body(at, keep_one, got_one, keep_two, got_two, *outs):
        for j in range(copy_size):
            z = lax.rem(at[0] + j, copy_size)
            for c in range(2):
                m = c * copy_size + z
                top = add_up(keep_one[0, m], got_one[0, m]).astype(jnp.bfloat16)
                low = add_up(keep_two[0, m], got_two[0, m]).astype(jnp.bfloat16)
                outs[j][c, : sizes[0]] = top
                outs[j][c, sizes[0] :] = low

    outs = [low_shape(2, total, width)] * copy_size
    return small_call(body, outs, [place], [keeps[0], gots[0], keeps[1], gots[1]])


def own_and_other(parts, scalars, kernels):
    place, core = scalars
    count = len(parts)
    _, total, width = parts[0].shape
    if not kernels:
        stacked = jnp.stack(parts).astype(jnp.float32)
        sums = 0.0
        for i in range(count):
            sums = sums + pick(stacked, lax.rem(place + count - i, count), 0)
        sums = sums.astype(jnp.bfloat16)
        return [pick(sums, 1 - core, 0), pick(sums, core, 0)]

    def body(at, *refs):
        for out, c in zip(refs[count:], (1 - at[1], at[1])):
            values = [r[c].astype(jnp.float32) for r in refs[:count]]
            sums = None
            for i in range(count):
                turn = lax.rem(at[0] + count - i, count)
                value = values[0]
                for j in range(1, count):
                    value = jnp.where(turn == j, values[j], value)
                sums = value if sums is None else sums + value
            out[...] = sums.astype(jnp.bfloat16)

    return small_call(body, [low_shape(total, width)] * 2, scalars, parts)


class Reduction:
    def __init__(self, send, keep, rows, size, kernels):
        self.size, self.rows, self.kernels = size, rows, kernels
        self.left = size.bit_length() - 2
        self.me = lax.axis_index("dp")
        self.sent, self.kept, self.bits = [send], [keep], [0]

    def receive(self):
        self.got = [swap_bit(v, self.size, bit) for v, bit in zip(self.sent, self.bits)]
        return self

    def advance(self):
        if len(self.sent) == 1:
            self.bits = [self.left, 1]
            bits = [(self.me >> b) & 1 for b in self.bits]
            cuts = cut_first(self.kept[0], self.got[0], self.rows, bits, self.kernels)
        else:
            self.bits = [self.bits[0] - 1, self.bits[1] + 1]
            bits = [(self.me >> b) & 1 for b in self.bits]
            cuts = cut_next(self.kept, self.got, bits, self.kernels)
        self.left -= 1
        self.sent, self.kept = [cuts[0], cuts[2]], [cuts[1], cuts[3]]
        return self


def attend(ids_col, ids_row, q, k, lanes, head, scale):
    wanted = (lanes >= HEAD_DIM) if head else (lanes < HEAD_DIM)
    scores = dot1(jnp.where(wanted, q, 0), k) * scale
    scores = jnp.where(ids_col == ids_row, scores, -1e30)
    exps = jnp.exp(scores - jnp.max(scores, axis=-1, keepdims=True))
    return wanted, exps / jnp.sum(exps, axis=-1, keepdims=True)


def attention_specs(micros, length):
    wide = pl.BlockSpec((length, 2 * HEAD_DIM), lambda m, h: (m, h))
    col = pl.BlockSpec((length, 1), lambda m, h: (m, 0))
    row = pl.BlockSpec((1, 1, length), lambda m, h: (m, 0, 0))
    return wide, col, row


def attention(queries, key_rows, value_rows, ids):
    micros, length = ids.shape
    scale = HEAD_DIM ** (-0.5)
    wide, col, row = attention_specs(micros, length)

    def body(col_ref, row_ref, q_ref, k_ref, v_ref, out_ref):
        lanes = lax.broadcasted_iota(jnp.int32, (1, 2 * HEAD_DIM), 1)
        outs = []
        for head in range(2):
            _, probs = attend(
                col_ref[...], row_ref[0], q_ref[...], k_ref[...], lanes, head, scale
            )
            outs.append(
                jnp.dot(
                    probs.astype(jnp.bfloat16), v_ref[...], preferred_element_type=jnp.float32
                )
            )
        out_ref[...] = jnp.where(lanes < HEAD_DIM, outs[0], outs[1]).astype(jnp.bfloat16)

    return pl.pallas_call(
        body,
        grid=(micros, HEADS // 2),
        out_shape=low_shape(micros * length, D),
        in_specs=[col, row, wide, wide, wide],
        out_specs=wide,
        compiler_params=pltpu.CompilerParams(vmem_limit_bytes=24 * MIB),
        cost_estimate=LIGHT,
    )(ids.reshape(-1, 1), ids[:, None], queries, key_rows, value_rows)


def attention_back(queries, key_rows, value_rows, grad_mixed, ids):
    micros, length = ids.shape
    scale = HEAD_DIM ** (-0.5)
    wide, col, row = attention_specs(micros, length)

    def body(col_ref, row_ref, q_ref, k_ref, v_ref, g_ref, gq_ref, gk_ref, gv_ref):
        lanes = lax.broadcasted_iota(jnp.int32, (1, 2 * HEAD_DIM), 1)
        q, k, v, g = q_ref[...], k_ref[...], v_ref[...], g_ref[...]
        parts = []
        for head in range(2):
            wanted, probs = attend(col_ref[...], row_ref[0], q, k, lanes, head, scale)
            grad_probs = dot1(jnp.where(wanted, g, 0), v)
            delta = jnp.sum(grad_probs * probs, axis=-1, keepdims=True)
            grad_scores = (probs * (grad_probs - delta)).astype(jnp.bfloat16)
            parts.append(
                (
                    jnp.dot(grad_scores, k, preferred_element_type=jnp.float32) * scale,
                    dot0(grad_scores, q) * scale,
                    dot0(probs.astype(jnp.bfloat16), g),
                )
            )
        for out, one, two in zip((gq_ref, gk_ref, gv_ref), *parts):
            out[...] = jnp.where(lanes < HEAD_DIM, one, two).astype(jnp.bfloat16)

    return pl.pallas_call(
        body,
        grid=(micros, HEADS // 2),
        out_shape=[low_shape(micros * length, D)] * 3,
        in_specs=[col, row, wide, wide, wide, wide],
        out_specs=[wide] * 3,
        compiler_params=pltpu.CompilerParams(vmem_limit_bytes=32 * MIB),
        cost_estimate=LIGHT,
    )(ids.reshape(-1, 1), ids[:, None], queries, key_rows, value_rows, grad_mixed)


def pack_head_grads(pairs, core, dp_size, copy_size, kernels):
    world = dp_size * copy_size
    count, mids = dp_size // 2, 2 * copy_size
    width = pairs[0][1].shape[1]
    half = width // 2
    sizes = [p[0].shape[1] // world for p in pairs]
    total = sum(sizes)
    if not kernels:
        packs = []
        for c in (1 - core, core):
            parts = []
            for left_side, right_side in pairs:
                part = lax.dynamic_slice_in_dim(right_side, c * half, half, 1)
                part = weight_grad(left_side, part).astype(jnp.bfloat16)
                parts.append(part.reshape(count, mids, -1, half))
            packs.append(jnp.concatenate(parts, axis=2))
        return packs + [jnp.stack([column_sum(p[1]) for p in pairs])]

    lefts, which = [], []
    for left_side, _ in pairs:
        seen = [i for i, other in enumerate(lefts) if other is left_side]
        which.append(seen[0] if seen else len(lefts))
        lefts += [] if seen else [left_side]
    rights = [p[1] for p in pairs]
    narrow = [v.shape[1] // count % 128 == 0 for v in lefts]
    held = [i for i, w in enumerate(which) if not narrow[w]]

    def body(at, *refs):
        left_refs = refs[: len(lefts)]
        right_refs = refs[len(lefts) : len(lefts) + len(rights)]
        sent, kept, sums = refs[len(lefts) + len(rights) :][:3]
        scratch = refs[len(lefts) + len(rights) + 3 :]
        first = at[0] == 0
        step = pl.program_id(0)

        @pl.when(step == 0)
        def _():
            for i, right in enumerate(right_refs):
                ones = jnp.ones((8, right.shape[0]), jnp.bfloat16)
                row = jnp.dot(ones, right[...], preferred_element_type=jnp.float32)
                sums[i : i + 1] = row[:1]
            for i, buffer in zip(held, scratch):
                buffer[...] = dot0(left_refs[which[i]][...], right_refs[i][...])

        at_row = 0
        for i, n in enumerate(sizes):
            if i in held:
                rows = mids * n
                whole = scratch[held.index(i)][pl.ds(pl.multiple_of(step * rows, 8), rows)]
            else:
                whole = dot0(left_refs[which[i]][...], right_refs[i][...])
            left, right = whole[:, :half], whole[:, half:]
            for out, part in (
                (sent, jnp.where(first, right, left)),
                (kept, jnp.where(first, left, right)),
            ):
                out[0, :, at_row : at_row + n] = part.reshape(mids, n, half).astype(jnp.bfloat16)
            at_row += n

    in_specs = [pl.BlockSpec(memory_space=pltpu.SMEM)]
    for v, cut_up in zip(lefts, narrow):
        if cut_up:
            in_specs.append(pl.BlockSpec((v.shape[0], v.shape[1] // count), lambda p: (0, p)))
        else:
            in_specs.append(pl.BlockSpec(v.shape, lambda p: (0, 0)))
    in_specs += [pl.BlockSpec(v.shape, lambda p: (0, 0)) for v in rights]
    out_spec = pl.BlockSpec((1, mids, total, half), lambda p: (p, 0, 0, 0))
    return pl.pallas_call(
        body,
        grid=(count,),
        out_shape=[low_shape(count, mids, total, half)] * 2
        + [jax.ShapeDtypeStruct((len(pairs), width), jnp.float32)],
        in_specs=in_specs,
        out_specs=[out_spec] * 2 + [pl.BlockSpec((len(pairs), width), lambda p: (0, 0))],
        scratch_shapes=[
            pltpu.VMEM((lefts[which[i]].shape[1], width), jnp.float32) for i in held
        ],
        compiler_params=pltpu.CompilerParams(vmem_limit_bytes=44 * MIB),
        cost_estimate=LIGHT,
    )(jnp.asarray(core, jnp.int32)[None], *lefts, *rights)


def assemble(pieces, scalars, copy_size, rows):
    width = pieces[0][0].shape[-1]
    total = rows

    def body(at, *refs):
        ins, out, sems = refs[: len(pieces)], refs[len(pieces)], refs[len(pieces) + 1]
        copies = []
        for ref, (value, first, flip, vary) in zip(ins, pieces):
            for d in range(2):
                for j in range(copy_size):
                    dp = at[0] ^ (flip | (vary if d else 0))
                    owner = dp * copy_size + lax.rem(at[1] + j, copy_size)
                    copy = pltpu.make_async_copy(
                        ref.at[d, j],
                        out.at[owner, pl.ds(first, value.shape[2])],
                        sems.at[len(copies)],
                    )
                    copy.start()
                    copies.append(copy)
        for copy in copies:
            copy.wait()

    return pl.pallas_call(
        body,
        out_shape=low_shape(8 * copy_size, total, width),
        in_specs=[pl.BlockSpec(memory_space=pltpu.SMEM)]
        + [pl.BlockSpec(memory_space=pl.ANY)] * len(pieces),
        out_specs=pl.BlockSpec(memory_space=pl.ANY),
        scratch_shapes=[pltpu.SemaphoreType.DMA((len(pieces) * 2 * copy_size,))],
        compiler_params=pltpu.CompilerParams(vmem_limit_bytes=4 * MIB),
        cost_estimate=LIGHT,
    )(jnp.stack([jnp.asarray(v, jnp.int32) for v in scalars]), *[p[0] for p in pieces])


def gather(pack, rows, arrived):
    total = pack.shape[0]
    along = [pack, *arrived]
    pieces = []
    for first, last, bits in ((0, rows, (2, 1)), (rows, total, (1, 2))):
        held = jnp.stack([v[first:last] for v in along])
        held = jnp.stack([held, swap_bit(held, 8, bits[0])])
        got = swap_bit(held, 8, bits[1])
        vary = 1 << bits[0]
        other = 1 << bits[1]
        pieces += [(held, first, 0, vary), (got, first, other, vary)]
        pieces += [
            (swap_bit(held, 8, 0), first, 1, vary),
            (swap_bit(got, 8, 0), first, other | 1, vary),
        ]
    return assemble(pieces, (lax.axis_index("dp"), lax.axis_index("copy")), 4, total)


def spread(packed, count, k):
    world = packed.shape[0]
    width = world * k
    padded = -(-count // 8) * 8
    lanes = -(-count * k // 128) * 128
    if 128 % k or packed.shape[1] < lanes:
        values = packed[:, : count * k].reshape(world, count, k)
        return jnp.moveaxis(values, 0, 1).reshape(count, width).astype(jnp.float32)
    group = 128 // k

    def body(packed_ref, out_ref):
        column = lax.broadcasted_iota(jnp.int32, (128, width), 1)
        row = lax.broadcasted_iota(jnp.int32, (128, width), 0)
        owner = lax.broadcasted_iota(jnp.int32, (world, width), 0)
        own = owner == lax.broadcasted_iota(jnp.int32, (world, width), 1) // k
        for j in range(group):
            tile = (row == j * k + column % k).astype(jnp.bfloat16)
            for i in range(j, count, group):
                block = packed_ref[:, i // group * 128 : (i // group + 1) * 128]
                values = jnp.dot(block, tile, preferred_element_type=jnp.float32)
                out_ref[i : i + 1] = jnp.sum(jnp.where(own, values, 0.0), axis=0, keepdims=True)

    return pl.pallas_call(
        body,
        out_shape=jax.ShapeDtypeStruct((padded, width), jnp.float32),
        in_specs=[pl.BlockSpec(memory_space=pltpu.VMEM)],
        out_specs=pl.BlockSpec(memory_space=pltpu.VMEM),
        compiler_params=pltpu.CompilerParams(vmem_limit_bytes=16 * MIB),
        cost_estimate=LIGHT,
    )(packed[:, :lanes])[:count]


def entry_back(grad_affine, grad_residual, norm_head, inv_head, gain, noisy):
    rows, width = grad_affine.shape
    step = 256

    def body(ga_ref, gr_ref, norm_ref, inv_ref, gain_ref, noisy_ref, out_ref):
        grad, norm = ga_ref[...], norm_ref[...]
        back = norm_back(grad * gain_ref[...], norm, inv_ref[...])
        entry = (gr_ref[...] + back).astype(jnp.bfloat16)
        part = jnp.concatenate(
            [
                dot0(noisy_ref[...], entry),
                jnp.sum(grad * norm, axis=0, keepdims=True),
                jnp.sum(entry.astype(jnp.float32), axis=0, keepdims=True),
                jnp.sum(grad, axis=0, keepdims=True),
                jnp.zeros((5, width), jnp.float32),
            ],
            axis=0,
        )

        @pl.when(pl.program_id(0) == 0)
        def _():
            out_ref[...] = part

        @pl.when(pl.program_id(0) > 0)
        def _():
            out_ref[...] += part

    tall = pl.BlockSpec((step, width), lambda i: (i, 0))
    return pl.pallas_call(
        body,
        grid=(rows // step,),
        out_shape=jax.ShapeDtypeStruct((CHANNELS + 8, width), jnp.float32),
        in_specs=[
            tall,
            tall,
            tall,
            pl.BlockSpec((step, 1), lambda i: (i, 0)),
            pl.BlockSpec((1, width), lambda i: (0, 0)),
            pl.BlockSpec((step, CHANNELS), lambda i: (i, 0)),
        ],
        out_specs=pl.BlockSpec((CHANNELS + 8, width), lambda i: (0, 0)),
        compiler_params=pltpu.CompilerParams(vmem_limit_bytes=32 * MIB),
        cost_estimate=LIGHT,
    )(grad_affine, grad_residual, norm_head, inv_head, gain[None], noisy)


def feed_back(gradient, slope, w_up_full, w_down_full):
    rows, ff = slope.shape
    step = 512

    def body(g_ref, slope_ref, up_ref, down_ref, out_ref, sums_ref, second_ref):
        grad_hidden = dot1(g_ref[...], down_ref[...]) * slope_ref[...].astype(jnp.float32)
        grad_hidden = grad_hidden.astype(jnp.bfloat16)
        out_ref[...] = grad_hidden
        ones = jnp.ones((8, rows), jnp.bfloat16)
        sums_ref[...] = jnp.dot(ones, grad_hidden, preferred_element_type=jnp.float32)
        part = dot1(grad_hidden, up_ref[...])

        @pl.when(pl.program_id(0) == 0)
        def _():
            second_ref[...] = part

        @pl.when(pl.program_id(0) > 0)
        def _():
            second_ref[...] += part

    full = pl.BlockSpec((rows, D), lambda j: (0, 0))
    across = pl.BlockSpec((rows, step), lambda j: (0, j))
    grad_hidden, sums, second = pl.pallas_call(
        body,
        grid=(ff // step,),
        out_shape=[
            low_shape(rows, ff),
            jax.ShapeDtypeStruct((8, ff), jnp.float32),
            jax.ShapeDtypeStruct((rows, D), jnp.float32),
        ],
        in_specs=[
            full,
            across,
            pl.BlockSpec((D, step), lambda j: (0, j)),
            pl.BlockSpec((step, D), lambda j: (j, 0)),
        ],
        out_specs=[across, pl.BlockSpec((8, step), lambda j: (0, j)), full],
        compiler_params=pltpu.CompilerParams(vmem_limit_bytes=32 * MIB),
        cost_estimate=LIGHT,
    )(gradient, slope, w_up_full, w_down_full)
    return grad_hidden, sums[0], second


def pack_block_grads(pairs, ready, core, dp_size, kernels):
    count = dp_size // 2
    half = D // 2
    pieces = [(i, j) for i, p in enumerate(pairs) for j in range(p[1].shape[1] // D)]
    sizes = [pairs[i][0].shape[1] // dp_size for i, _ in pieces]
    sizes += [r.shape[0] // dp_size for r in ready]
    total = sum(sizes)

    if not kernels:
        packs = []
        for c in (1 - core, core):
            parts = []
            for i, j in pieces:
                part = lax.dynamic_slice_in_dim(pairs[i][1], j * D + c * half, half, 1)
                parts.append(weight_grad(pairs[i][0], part))
            for gradient in ready:
                parts.append(lax.dynamic_slice_in_dim(gradient, c * half, half, 1))
            parts = [p.astype(jnp.bfloat16).reshape(count, 2, -1, half) for p in parts]
            packs.append(jnp.concatenate(parts, axis=2))
        return packs

    def body(at, *refs):
        sent, kept = refs[-2:]
        first = at[0] == 0
        at_row = 0
        for piece, n in enumerate(sizes):
            if piece < len(pieces):
                i, j = pieces[piece]
                whole = dot0(refs[2 * i][...], refs[2 * i + 1][:, j * D : (j + 1) * D])
            else:
                whole = refs[2 * len(pairs) + piece - len(pieces)][...].astype(jnp.float32)
            left, right = whole[:, :half], whole[:, half:]
            for out, part in (
                (sent, jnp.where(first, right, left)),
                (kept, jnp.where(first, left, right)),
            ):
                part = part.reshape(count, 2, n, half).astype(jnp.bfloat16)
                out[:, :, at_row : at_row + n] = part
            at_row += n

    flat = [v for p in pairs for v in p] + list(ready)
    return small_call(body, [low_shape(count, 2, total, half)] * 2, [core], flat)


def shards(
    block_input,
    image_ids,
    latents,
    noise,
    timesteps,
    norm_gains,
    block_biases,
    w_qkv,
    w_proj,
    w_up,
    up_bias,
    w_down,
    head_gain,
    head_biases,
    w_cond,
    w_time1,
    w_time2,
    w_input,
    w_ada,
    w_mlp1,
    w_mlp2,
    w_final,
    w_output,
    output_bias,
):
    bf16, f32 = jnp.bfloat16, jnp.float32
    dp_size, copy_size = lax.axis_size("dp"), lax.axis_size("copy")
    world = dp_size * copy_size
    place = lax.axis_index("copy")
    micros, _, own, _ = block_input.shape
    length = image_ids.shape[2]
    total = micros * length
    k_d, k_ff, k_w, k_t = D // world, w_down.shape[0], WIDTH // world, w_time1.shape[0]
    ff = k_ff * world
    kernels = k_d % 8 == 0 and k_w % 16 == 0 and k_t % 8 == 0
    score_scale = HEAD_DIM ** (-0.5)

    def cut(matrix, width):
        return [matrix[:, i : i + width] for i in range(0, matrix.shape[1], width)]

    def pad_flat(parts, width):
        flat = jnp.concatenate([p.reshape(-1) for p in parts])
        count = -(-flat.shape[0] // (16 * width)) * 16 * width
        return jnp.pad(flat, (0, count - flat.shape[0])).reshape(-1, width)

    groups = [
        (cut(w_qkv, D) + [w_proj, pad_flat([norm_gains, block_biases, up_bias], D)], 2),
        (cut(w_up, D) + [w_down], 4),
        (
            cut(w_ada, WIDTH)
            + [w_time2, w_cond, w_time1]
            + [pad_flat([w_input, w_output.T, head_gain, head_biases], WIDTH)],
            3,
        ),
        ([w_mlp1, w_mlp2] + cut(w_final, WIDTH), 2),
    ]

    def everyone(pack):
        return [shift_copy(pack, copy_size, copy_size - j) for j in range(1, copy_size)]

    def unpack(pack, parts):
        out, at = [], 0
        for part in parts:
            out.append(pack[:, at : at + part.shape[0]].reshape(-1, pack.shape[2]))
            at += part.shape[0]
        return out

    own_rows = block_input[:, 0]
    packs = [jnp.concatenate(parts, 0) for parts, _ in groups]
    if kernels and dp_size == 8 and copy_size == 4:
        head_own = jnp.concatenate(packs[2:])
        arrived = [everyone(packs[0])]
        *arrived[0], packs[1] = tie(*arrived[0], packs[1])
        arrived.append(everyone(packs[1]))
        *arrived[1], own_rows, head_own = tie(*arrived[1], own_rows, head_own)
        rows_arrived = everyone(own_rows)
        full = [
            gather(pack, sum(p.shape[0] for p in parts[:n]), got)
            for pack, (parts, n), got in zip(packs[:2], groups[:2], arrived[:2])
        ]
        head = lax.all_gather(head_own, ("dp", "copy"), axis=0)
        full += [head[:, : packs[2].shape[0]], head[:, packs[2].shape[0] :]]
    else:
        rows_arrived = everyone(own_rows)
        full = [lax.all_gather(pack, ("dp", "copy"), axis=0) for pack in packs]
    full = [unpack(pack, parts) for pack, (parts, _) in zip(full, groups)]

    rows = jnp.stack([own_rows, *rows_arrived], axis=1).reshape(total, D).astype(f32)

    def turned(values):
        twice = jnp.concatenate([values, values], axis=1)
        return lax.dynamic_slice_in_dim(twice, place * own, length, 1)

    ids = turned(image_ids[:, 0])
    latent_rows = turned(latents[:, 0]).reshape(total, CHANNELS)
    noise_rows = turned(noise[:, 0, 0]).reshape(total, CHANNELS)

    w_q, w_k, w_v, w_proj_full, small = full[0]
    w_up_full = jnp.concatenate(full[1][:4], axis=1)
    w_down_full = full[1][4]
    small = small.reshape(world, -1)
    up_bias_full = small[:, 8 * k_d : 8 * k_d + k_ff].reshape(ff).astype(f32)
    gains = small[:, : 2 * k_d].reshape(world, 2, k_d)
    gains = jnp.moveaxis(gains, 0, 1).reshape(2, D).astype(f32)
    biases = small[:, 2 * k_d : 8 * k_d].reshape(world, 6, k_d)
    biases = jnp.moveaxis(biases, 0, 1).reshape(6, D).astype(f32)

    norm_one, inv_one = normalize(rows)
    first_in = (norm_one * gains[0] + biases[0]).astype(bf16)
    queries = (product(first_in, w_q) + biases[1]).astype(bf16)
    key_rows = product(first_in, w_k).astype(bf16)
    value_rows = (product(first_in, w_v) + biases[2]).astype(bf16)
    mixed = attention(queries, key_rows, value_rows, ids)
    middle = rows + product(mixed, w_proj_full) + biases[3]
    norm_two, inv_two = normalize(middle)
    second_in = (norm_two * gains[1] + biases[4]).astype(bf16)
    hidden = product(second_in, w_up_full) + up_bias_full
    active = jax.nn.gelu(hidden, approximate=False).astype(bf16)
    slope = gelu_slope(hidden).astype(bf16)
    output = middle + product(active, w_down_full) + biases[5]
    condition = output.astype(bf16)

    def chosen(values):
        width = values.shape[1]
        k = width // world
        source = jnp.arange(width, dtype=jnp.int32)[:, None]
        target = jnp.arange(dp_size * k, dtype=jnp.int32)[None, :]
        wanted = (target // k * copy_size + place) * k + target % k
        return product(values, (source == wanted).astype(bf16)).astype(bf16)

    condition, first_z, mixed_z, second_z, active_z, slope = tie(
        condition, chosen(first_in), chosen(mixed), chosen(second_in), chosen(active), slope
    )
    core = lax.axis_index("dp") & 1

    def split_pack(pack, parts):
        out, at = [], 0
        for rows_of in parts:
            out.append(pack[at : at + rows_of])
            at += rows_of
        return out

    def advance(reduction, others):
        tied = tie(*reduction.got, *others)
        reduction.got = list(tied[: len(reduction.got)])
        others = tied[len(reduction.got) :]
        reduction.advance()
        count = len(reduction.sent)
        tied = tie(*reduction.sent, *reduction.kept, *others)
        reduction.sent = list(tied[:count])
        reduction.kept = list(tied[count : 2 * count])
        reduction.receive()
        return tied[2 * count :]

    def to_copies(reduction, others):
        tied = tie(*reduction.got, *others)
        reduction.got = list(tied[: len(reduction.got)])
        others = tied[len(reduction.got) :]
        chunks = cut_copies(reduction.kept, reduction.got, place, copy_size, kernels)
        tied = tie(*chunks, *others)
        chunks = list(tied[:copy_size])
        arriving = [shift_copy(chunks[j], copy_size, j) for j in range(1, copy_size)]
        return [chunks[0], *arriving], tied[copy_size:]

    def whole(other, mine):
        got = swap_bit(other, dp_size, 0)
        left = jnp.where(core == 0, mine, got)
        right = jnp.where(core == 0, got, mine)
        return jnp.concatenate([left, right], axis=1).astype(f32)

    def landed(parts):
        return whole(*own_and_other(parts, (place, core), kernels))

    def finish(reduction):
        while reduction.left:
            reduction.advance().receive()
        parts = [
            jnp.concatenate([v[0] for v in values], axis=1)
            for values in (reduction.kept, reduction.got)
        ]
        return whole(*own_and_other(parts, (0, core), kernels))

    w_shift, w_scale, w_gate, w_time2_full, w_cond_full, w_time1_full, small = full[2]
    w_one, w_two, w_fshift, w_fscale = full[3]
    small = small.reshape(world, -1)
    small = spread(small, 2 * CHANNELS + 13, k_w)
    w_input_full = small[:CHANNELS].astype(bf16)
    w_output_t = small[CHANNELS : 2 * CHANNELS].astype(bf16)
    head_gain_f = small[2 * CHANNELS]
    head_bias = small[2 * CHANNELS + 1 :]

    valid_rows = (ids >= 0).astype(f32).reshape(total, 1)
    slots = jnp.arange(micros * IMAGES, dtype=jnp.int32)
    row_slot = ids + IMAGES * jnp.arange(micros, dtype=jnp.int32)[:, None]
    row_slot = jnp.where(ids >= 0, row_slot, -1).reshape(total, 1)
    image_onehot = (row_slot == slots[None, :]).astype(f32)
    step_vals = timesteps[:, 0, 0].reshape(micros * IMAGES).astype(f32)
    sinusoid_in = sinusoid(step_vals).astype(bf16)
    time_one = product(sinusoid_in, w_time1_full) + head_bias[1]
    time_act = jax.nn.silu(time_one).astype(bf16)
    embedded = product(time_act, w_time2_full) + head_bias[2]
    cond_all = (
        product(condition, w_cond_full)
        + head_bias[0]
        + jnp.dot(image_onehot, embedded, precision=highest, preferred_element_type=f32)
    )
    gated = jax.nn.silu(cond_all).astype(bf16)
    shift_rows = product(gated, w_shift) + head_bias[7]
    scale_rows = product(gated, w_scale) + head_bias[8]
    gate_rows = product(gated, w_gate) + head_bias[9]
    mixing = jnp.dot(image_onehot, plan(step_vals), precision=highest, preferred_element_type=f32)
    noisy = (latent_rows * mixing[:, 0:1] + noise_rows * mixing[:, 1:2]).astype(bf16)
    entry_rows = product(noisy, w_input_full) + head_bias[3]
    norm_head, inv_head = normalize(entry_rows)
    affine = norm_head * head_gain_f + head_bias[4]
    mlp_in = (affine * (1.0 + scale_rows) + shift_rows).astype(bf16)
    inner_one = product(mlp_in, w_one) + head_bias[5]
    inner_act = jax.nn.silu(inner_one).astype(bf16)
    inner_two = product(inner_act, w_two) + head_bias[6]
    residual = entry_rows + gate_rows * inner_two
    fshift_rows = product(gated, w_fshift) + head_bias[10]
    fscale_rows = product(gated, w_fscale) + head_bias[11]
    norm_final, inv_final = normalize(residual)
    final_in = (norm_final * (1.0 + fscale_rows) + fshift_rows).astype(bf16)
    predicted = input_back(final_in, w_output_t) + output_bias.astype(f32)

    grad_pred = ((predicted - noise_rows) * valid_rows).astype(bf16)
    grad_out_bias = column_sum(grad_pred)
    grad_w_output = weight_grad(grad_pred, final_in)
    grad_final_in = product(grad_pred, w_output_t)
    grad_fshift = grad_final_in.astype(bf16)
    grad_fscale = (grad_final_in * norm_final).astype(bf16)
    grad_residual = norm_back(grad_final_in * (1.0 + fscale_rows), norm_final, inv_final)
    grad_gated = input_back(grad_fshift, w_fshift) + input_back(grad_fscale, w_fscale)
    grad_inner_two = (grad_residual * gate_rows).astype(bf16)
    grad_inner_one = (input_back(grad_inner_two, w_two) * silu_slope(inner_one)).astype(bf16)
    send, keep, sums_one = pack_head_grads(
        [
            (gated, grad_fshift),
            (gated, grad_fscale),
            (inner_act, grad_inner_two),
            (mlp_in, grad_inner_one),
        ],
        core,
        dp_size,
        copy_size,
        kernels,
    )
    grad_inner_one, send, keep = tie(grad_inner_one, send, keep)
    pack_one = Reduction(send, keep, 2 * k_w, dp_size, kernels).receive()
    grad_mlp_in = input_back(grad_inner_one, w_one)
    (grad_mlp_in,) = advance(pack_one, [grad_mlp_in])
    grad_shift = grad_mlp_in.astype(bf16)
    grad_scale = (grad_mlp_in * affine).astype(bf16)
    grad_gate = (grad_residual * inner_two).astype(bf16)
    grad_affine = grad_mlp_in * (1.0 + scale_rows)
    grad_gated = (
        grad_gated
        + input_back(grad_shift, w_shift)
        + input_back(grad_scale, w_scale)
        + input_back(grad_gate, w_gate)
    )
    grad_cond = grad_gated * silu_slope(cond_all)
    grad_cond_low = grad_cond.astype(bf16)
    grad_condition = input_back(grad_cond_low, w_cond_full).astype(bf16)

    chunks = grad_condition.reshape(micros, copy_size, own, D)
    chunks = [chunks[:, j] for j in range(copy_size)]
    tied = advance(pack_one, [*chunks, grad_affine, grad_cond, grad_cond_low])
    chunks = tied[:copy_size]
    grad_affine, grad_cond, grad_cond_low = tied[copy_size:]
    arriving = [shift_copy(chunks[j], copy_size, j) for j in range(1, copy_size)]
    grad_embedded = lax.dot_general(
        image_onehot,
        grad_cond,
        (((0,), (0,)), ((), ())),
        precision=highest,
        preferred_element_type=f32,
    ).astype(bf16)
    grad_time_one = (input_back(grad_embedded, w_time2_full) * silu_slope(time_one)).astype(bf16)
    send, keep, sums_two = pack_head_grads(
        [
            (gated, grad_shift),
            (gated, grad_scale),
            (gated, grad_gate),
            (time_act, grad_embedded),
            (condition, grad_cond_low),
            (sinusoid_in, grad_time_one),
        ],
        core,
        dp_size,
        copy_size,
        kernels,
    )
    send, keep, *arriving = tie(send, keep, *arriving)
    pack_two = Reduction(send, keep, 3 * k_w, dp_size, kernels).receive()
    grad_z_own = chunks[0].astype(f32)
    for part in arriving:
        grad_z_own = grad_z_own + part.astype(f32)
    grad_z_own = grad_z_own.astype(bf16)
    (grad_z_own,) = advance(pack_two, [grad_z_own])
    arriving = [shift_copy(grad_z_own, copy_size, copy_size - j) for j in range(1, copy_size)]
    grad_affine, grad_z_own = tie(grad_affine, grad_z_own)
    if kernels:
        from_entry = entry_back(
            grad_affine, grad_residual, norm_head, inv_head, head_gain_f, noisy
        )
    else:
        grad_entry = grad_residual + norm_back(grad_affine * head_gain_f, norm_head, inv_head)
        grad_entry = grad_entry.astype(bf16)
        from_entry = jnp.concatenate(
            [
                weight_grad(noisy, grad_entry),
                jnp.sum(grad_affine * norm_head, axis=0)[None],
                column_sum(grad_entry)[None],
                jnp.sum(grad_affine, axis=0)[None],
            ]
        )
    from_entry, *arriving = tie(from_entry, *arriving)
    one_parts, (grad_z_own, *arriving) = to_copies(pack_one, [grad_z_own, *arriving])

    grad_z = jnp.stack([grad_z_own, *arriving], axis=1).reshape(total, D)
    grad_down = grad_z
    if kernels:
        grad_hidden, sums_hidden, grad_second = feed_back(grad_down, slope, w_up_full, w_down_full)
    else:
        grad_hidden = input_back(grad_down, w_down_full) * slope.astype(f32)
        grad_hidden = grad_hidden.astype(bf16)
        sums_hidden = column_sum(grad_hidden)
        grad_second = input_back(grad_hidden, w_up_full)
    grad_middle = grad_z.astype(f32) + norm_back(grad_second * gains[1], norm_two, inv_two)
    grad_branch = grad_middle.astype(bf16)
    grad_mixed = input_back(grad_branch, w_proj_full).astype(bf16)
    send, keep = pack_block_grads(
        [(second_z, grad_hidden), (active_z, grad_down)], [], core, dp_size, kernels
    )
    pack_three = Reduction(send, keep, 4 * k_d, dp_size, kernels)
    grad_mixed, pack_three.sent[0], pack_three.kept[0] = tie(grad_mixed, send, keep)
    pack_three.receive()
    (grad_mixed,) = advance(pack_two, [grad_mixed])
    small_grads = jnp.concatenate(
        [
            from_entry[:CHANNELS],
            grad_w_output,
            from_entry[CHANNELS : CHANNELS + 1],
            sums_two[4:6],
            sums_two[3:4],
            from_entry[CHANNELS + 1 : CHANNELS + 3],
            sums_one[3:4],
            sums_one[2:3],
            sums_two[:3],
            sums_one[:2],
            jnp.pad(grad_out_bias, (0, WIDTH - CHANNELS))[None],
            jnp.zeros((2, WIDTH), f32),
        ],
        axis=0,
    )
    swaps = [functools.partial(swap_bit, size=dp_size, bit=b) for b in range(dp_size.bit_length() - 1)]
    swaps += [functools.partial(swap_copy, size=copy_size, shift=n) for n in (1, 2)]

    def add_swapped(values, swap, *others):
        return tie(values + swap(values), *others)

    small_grads, grad_mixed = tie(small_grads, grad_mixed)
    small_grads, grad_mixed = add_swapped(small_grads, swaps[0], grad_mixed)
    grad_q, grad_k, grad_v = attention_back(queries, key_rows, value_rows, grad_mixed, ids)
    small_grads, grad_q = add_swapped(small_grads, swaps[1], grad_q)
    send, keep = pack_block_grads(
        [(first_z, grad_q), (first_z, grad_k), (first_z, grad_v), (mixed_z, grad_branch)],
        [],
        core,
        dp_size,
        kernels,
    )
    pack_four = Reduction(send, keep, 2 * k_d, dp_size, kernels)
    grad_q, pack_four.sent[0], pack_four.kept[0] = tie(grad_q, send, keep)
    pack_four.receive()
    two_parts, (grad_q,) = to_copies(pack_two, [grad_q])
    (grad_q,) = advance(pack_three, [grad_q])
    (grad_q,) = advance(pack_four, [grad_q])
    own_one_parts = own_and_other(one_parts, (place, core), kernels)
    small_grads, grad_q, *own_one_parts = add_swapped(small_grads, swaps[2], grad_q, *own_one_parts)
    for swap in swaps[3:]:
        small_grads = small_grads + swap(small_grads)

    grad_first = input_back(grad_q, w_q) + input_back(grad_k, w_k) + input_back(grad_v, w_v)

    own_up_down = finish(pack_three)
    own_up = jnp.concatenate(split_pack(own_up_down, [k_d] * 4), axis=1)
    own_down = own_up_down[4 * k_d :]

    block_small = jnp.concatenate(
        [
            jnp.stack(
                [
                    jnp.sum(grad_first * norm_one, axis=0),
                    jnp.sum(grad_second * norm_two, axis=0),
                    jnp.sum(grad_first, axis=0),
                    column_sum(grad_q),
                    column_sum(grad_v),
                    column_sum(grad_branch),
                    jnp.sum(grad_second, axis=0),
                    column_sum(grad_down),
                ]
            ),
            sums_hidden.reshape(-1, D),
        ],
        axis=0,
    )
    for bit in range(dp_size.bit_length() - 1):
        block_small = block_small + swap_bit(block_small, dp_size, bit)
    own_four = finish(pack_four)
    own_q, own_k, own_v, own_proj = split_pack(own_four, [k_d] * 4)
    own_fshift, own_fscale, own_two, own_one = split_pack(
        whole(*own_one_parts), [k_w] * 4
    )
    own_shift, own_scale, own_gate, own_time2, own_cond, own_time1 = split_pack(
        landed(two_parts), [k_w] * 4 + [k_d, k_t]
    )
    me = lax.axis_index("dp") * copy_size + place
    own_rest = lax.dynamic_slice_in_dim(block_small[:8], me * k_d, k_d, 1)
    own_gains, own_biases = own_rest[:2], own_rest[2:]
    own_up_bias = lax.dynamic_slice_in_dim(block_small[8:].reshape(ff), me * k_ff, k_ff)
    own_small = lax.dynamic_slice_in_dim(small_grads, me * k_w, k_w, 1)
    own_w_input = own_small[:CHANNELS]
    own_w_output = own_small[CHANNELS : 2 * CHANNELS].T
    own_head_gain = own_small[2 * CHANNELS]
    own_head_biases = own_small[2 * CHANNELS + 1 : 2 * CHANNELS + 13]
    grad_out_bias = small_grads[2 * CHANNELS + 13, :CHANNELS]

    mine = grad_first.reshape(micros, length, D)[:, :own].reshape(micros * own, D)
    mine_norm = norm_one.reshape(micros, length, D)[:, :own].reshape(micros * own, D)
    mine_inv = inv_one.reshape(micros, length, 1)[:, :own].reshape(micros * own, 1)
    mine_middle = grad_middle.reshape(micros, length, D)[:, :own].reshape(micros * own, D)
    input_grad = mine_middle + norm_back(mine * gains[0], mine_norm, mine_inv)
    input_grad = input_grad.reshape(micros, 1, own, D)
    block_output = condition.reshape(micros, length, D)[:, :own].reshape(micros, 1, own, D)
    return (
        block_output,
        input_grad,
        own_gains,
        own_biases,
        jnp.concatenate([own_q, own_k, own_v], axis=1),
        own_proj,
        own_up,
        own_up_bias,
        own_down,
        own_head_gain,
        own_head_biases,
        own_cond,
        own_time1,
        own_time2,
        own_w_input,
        jnp.concatenate([own_shift, own_scale, own_gate], axis=1),
        own_one,
        own_two,
        jnp.concatenate([own_fshift, own_fscale], axis=1),
        own_w_output,
        grad_out_bias,
    )


def solution(mesh):
    in_specs = (
        P(None, "dp", "copy", None),
        P(None, "dp", None),
        P(None, "dp", None, None),
        P(None, "copy", "dp", None, None),
        P(None, "copy", "dp", None),
        P(None, ("dp", "copy")),
        P(None, ("dp", "copy")),
        P(("dp", "copy"), None),
        P(("dp", "copy"), None),
        P(("dp", "copy"), None),
        P(("dp", "copy")),
        P(("dp", "copy"), None),
        P(("dp", "copy")),
        P(None, ("dp", "copy")),
        P(("dp", "copy"), None),
        P(("dp", "copy"), None),
        P(("dp", "copy"), None),
        P(None, ("dp", "copy")),
        P(("dp", "copy"), None),
        P(("dp", "copy"), None),
        P(("dp", "copy"), None),
        P(("dp", "copy"), None),
        P(("dp", "copy"), None),
        P(),
    )
    out_specs = (
        P(None, "dp", "copy", None),
        P(None, "dp", "copy", None),
        P(None, ("dp", "copy")),
        P(None, ("dp", "copy")),
        P(("dp", "copy"), None),
        P(("dp", "copy"), None),
        P(("dp", "copy"), None),
        P(("dp", "copy")),
        P(("dp", "copy"), None),
        P(("dp", "copy")),
        P(None, ("dp", "copy")),
        P(("dp", "copy"), None),
        P(("dp", "copy"), None),
        P(("dp", "copy"), None),
        P(None, ("dp", "copy")),
        P(("dp", "copy"), None),
        P(("dp", "copy"), None),
        P(("dp", "copy"), None),
        P(("dp", "copy"), None),
        P(("dp", "copy"), None),
        P(),
    )
    return jax.shard_map(shards, mesh=mesh, in_specs=in_specs, out_specs=out_specs, check_vma=False)
```

time: 769 us -> 603 us (0.78)
  waiting for transfers between devices: 234 us -> 112 us
  Pallas kernels: 0 us -> 120 us
  matrix products: 208 us -> 116 us
  local copies, waits for them, and re-layouts: 160 us -> 93.4 us
  starting transfers between devices: 35.4 us -> 79.4 us
  blocking collectives: 38.6 us -> 0 us
    pallas_call x0 -> x25, Pallas kernels: none -> 120 us  [the longest x16 32.5 us: small_call(): pl.pallas_call(body, out_shape=outs, in_specs=[pl.BlockSpec(memory_space=...]
    all_gather x2 -> x1, waiting for transfers between devices: 97.1 us -> 8.6 us  [shards(): head = lax.all_gather(head_own, ('dp', 'copy'), axis=0)]
    dot_general x21 -> x1, matrix products: 49.5 us -> 0.97 us  [weight_grad(): lax.dot_general(left_side, right_side, (((0,), (0,)), ((), ())), preferre...]
    psum x1 -> x0, blocking collectives: 38.6 us -> none  [shards(): grad_out_bias = lax.psum(column_sum(grad_pred), ('dp', 'copy'))]
    dot_general x6 -> x0, matrix products: 38.5 us -> none  [the longest x1 10.4 us: shards(): jnp.einsum('bqhd,bkhd->bhqk', grad_mixed, value_rows, preferred_element_t...]
    ppermute x20 -> x46, waiting for transfers between devices: 68.1 us -> 31 us  [swap_bit(): return lax.ppermute(values, 'dp', [(i, i ^ 1 << bit) for i in range(size)])]
    ppermute x20 -> x46, starting transfers between devices: 17.9 us -> 43.1 us  [swap_bit(): return lax.ppermute(values, 'dp', [(i, i ^ 1 << bit) for i in range(size)])]
    another operation x28 -> x8, local copies, waits for them, and re-layouts: 25.1 us -> 2.25 us  [the longest x7 2.23 us: gather(): held = jnp.stack([v[first:last] for v in along])]
  transfers between devices with their start and end apart: 37 -> 70, of which waited for: 21 -> 22; matrix products, arithmetic and copies ran while one was open for 37% -> 29% of each run, Pallas kernels for 0% -> 17%
where the time goes in v2:
time: 603 us; the launch traced here: 592 us
  Pallas kernels  120 us (20%)
  matrix products  116 us (19%)
  waiting for transfers between devices  112 us (19%)
  local copies, waits for them, and re-layouts  93.4 us (15%)
  starting transfers between devices  79.4 us (13%)
  other arithmetic  55.6 us (9%)
  between operations  17.3 us (3%)
    ppermute x21, waiting for transfers between devices, shift_copy(): lax.ppermute(values, 'copy', [(i, (i + shift) % size) for i in range(size)])  71.8 us
    dot_general x22, matrix products, product(): return jnp.dot(left_side, right_side, preferred_element_type=jnp.float32)  67.4 us
    unnamed x398, local copies, waits for them, and re-layouts  44.2 us
    ppermute x46, starting transfers between devices, swap_bit(): return lax.ppermute(values, 'dp', [(i, i ^ 1 << bit) for i in range(size)])  43.1 us
    dot_general x14, matrix products, input_back(): lax.dot_general(gradient, weight, (((1,), (1,)), ((), ())), preferred_ele...  41.8 us
    ppermute x21, starting transfers between devices, shift_copy(): lax.ppermute(values, 'copy', [(i, (i + shift) % size) for i in range(size)])  32.7 us
    pallas_call x16, Pallas kernels, small_call(): pl.pallas_call(body, out_shape=outs, in_specs=[pl.BlockSpec(memory_space=...  32.5 us
    ppermute x46, waiting for transfers between devices, swap_bit(): return lax.ppermute(values, 'dp', [(i, i ^ 1 << bit) for i in range(size)])  31 us
  transfers between devices with their start and end apart: 70, of which 22 were waited for; matrix products, arithmetic and copies ran while one was open for 29% of the time, Pallas kernels for 17%

profile of v2, /device:TPU:9, one launch (start us, length us, event | category | flops | bytes accessed | tf_op | source)
XLA Modules:
  0.0 592.4 jit_solution(936200843811976282)
XLA Ops:
  12.8 2.5 collective-permute-start.1
  15.3 2.2 collective-permute-start.2
  35.4 2.8 collective-permute-done.3
  38.2 14.2 %collective-permute-done.4 = bf16[192,768]{1,0:T(8,128)(2,1)S(1)} collective-permute-done((bf16[192,768]{1,0:T(8,128)(2,1)S(1)}, bf16[192,768]{1,0:T(8,128)(2,1)S(1)}, u32[]{:S(2)}, u32[]{:S(2)}) %collective-permute-start.4) | collective-permute-done | bytes 294944 | tf_op jit(solution)/shard_map/ppermute | solution.py:94
  52.5 6.3 %collective-permute-done.5 = bf16[192,768]{1,0:T(8,128)(2,1)S(1)} collective-permute-done((bf16[192,768]{1,0:T(8,128)(2,1)S(1)}, bf16[192,768]{1,0:T(8,128)(2,1)S(1)}, u32[]{:S(2)}, u32[]{:S(2)}) %collective-permute-start.5) | collective-permute-done | bytes 294944 | tf_op jit(solution)/shard_map/ppermute | solution.py:94
  67.4 3.4 collective-permute-start.7
  72.9 3.7 collective-permute-done.13
  79.1 4.1 collective-permute-done.6
  84.4 15.1 %collective-permute-done.7 = bf16[2,96,768]{2,1,0:T(8,128)(2,1)S(1)} collective-permute-done((bf16[2,96,768]{2,1,0:T(8,128)(2,1)}, bf16[2,96,768]{2,1,0:T(8,128)(2,1)S(1)}, u32[]{:S(2)}, u32[]{:S(2)}) %collective-permute-start.7) | collective-permute-done | bytes 294944 | tf_op jit(solution)/shard_map/ppermute | solution.py:94
  99.6 6.4 %collective-permute-done.8 = bf16[2,96,768]{2,1,0:T(8,128)(2,1)S(1)} collective-permute-done((bf16[2,96,768]{2,1,0:T(8,128)(2,1)}, bf16[2,96,768]{2,1,0:T(8,128)(2,1)S(1)}, u32[]{:S(2)}, u32[]{:S(2)}) %collective-permute-start.8) | collective-permute-done | bytes 294944 | tf_op jit(solution)/shard_map/ppermute | solution.py:94
  117.9 4.9 collective-permute-start.23
  122.9 4.1 shard_map.391
  127.0 2.4 copy-done
  133.5 2.8 fusion.100
  140.0 15.2 %shard_map.392 = bf16[768,768]{1,0:T(8,128)(2,1)S(1)} custom-call(s32[768,1]{1,0:T(8,128)S(1)} %bitcast.275, s32[2,1,384]{2,1,0:T(1,128)S(1)} %broadcast_in_dim.11.row_ref, bf16[768,768]{1,0:T(8,128)(2,1)S(1)} %add_convert_fusion.5.q_ref, bf16[768,768]{1,0:T(8,128)(2,1)S(1)} %convolution_convert_fusion.2.k_ref, bf16[768,768]{1,0:T(8,128)(2,1)S(1)} %add_convert_fusion.4.v_ref), custom_call_target="tpu_custom_call" | custom-call | flops 1000000 | bytes 100000 | tf_op jit(solution)/shard_map/pallas_call | solution.py:308
  165.2 6.4 %shard_map.393 = bf16[32,192,768]{2,1,0:T(8,128)(2,1)S(1)} custom-call(s32[2]{0:T(128)S(1)} %pad_add_fusion.at, bf16[2,4,96,768]{3,2,1,0:T(8,128)(2,1)S(1)} %pad_maximum_fusion.2.refs_0_, bf16[2,4,96,768]{3,2,1,0:T(8,128)(2,1)} %collective-permute-done.18.refs_1_, bf16[2,4,96,768]{3,2,1,0:T(8,128)(2,1)} %collective-permute-done.19.refs_2_, ...), custom_call_target="tpu_custom_call" | custom-call | flops 1000000 | bytes 100000 | tf_op jit(solution)/shard_map/pallas_call | solution.py:458
  174.1 30.9 %fusion.7 = (bf16[768,3072]{1,0:T(8,128)(2,1)}, bf16[768,3072]{1,0:T(8,128)(2,1)S(1)}) fusion(f32[3072]{0:T(1024)S(1)} %reshape.848, bf16[768,768]{1,0:T(8,128)(2,1)S(1)} %copy-done.114, bf16[768,768]{1,0:T(8,128)(2,1)S(1)} %bitcast.295, bf16[768,768]{1,0:T(8,128)(2,1)S(1)} %bitcast.297, bf16[768,768]{1,0:T(8,128)(2,1)S(1)} %bitcast.299, ...), kind=kOutput, calls=%fused_computation.9 | convolution fusion | flops 3819700224 | bytes 15347712 | tf_op jit(solution)/shard_map/dot_general | solution.py:25
  205.0 4.9 fusion.32.refs_2_
  209.9 3.9 add_convert_fusion.2.refs_2_
  213.8 8.6 %all-gather.3.cloned.1.call-done = bf16[9728,1024]{1,0:T(8,128)(2,1)} async-done(((bf16[304,1024]{1,0:T(8,128)(2,1)}), bf16[9728,1024]{1,0:T(8,128)(2,1)}) %all-gather.3.cloned.1.call-update) | async-done | bytes 19922960 | tf_op jit(solution)/shard_map/all_gather | solution.py:734
  225.8 9.2 %fusion.98 = (bf16[32,32,1024]{2,1,0:T(8,128)(2,1)}, bf16[32,32,1024]{2,1,0:T(8,128)(2,1)S(1)}, bf16[32,32,1024]{2,1,0:T(8,128)(2,1)}, bf16[32,32,1024]{2,1,0:T(...) fusion(bf16[32,304,1024]{2,1,0:T(8,128)(2,1)} %bitcast.287), kind=kLoop, calls=%fused_computation.315 | loop fusion | bytes 33554432 | tf_op jit(solution)/shard_map/slice | solution.py:717
  240.5 3.8 multiply_convert_fusion.6
  251.3 2.3 add_convert_fusion.1.refs_2_
  253.6 2.1 multiply_convert_fusion.5
  255.8 2.2 fusion.97
  266.6 3.6 multiply_convert_fusion.3.refs_6_
  270.2 12.1 %shard_map.395 = (bf16[4,8,128,512]{3,2,1,0:T(8,128)(2,1)}, bf16[4,8,128,512]{3,2,1,0:T(8,128)(2,1)}, f32[4,1024]{1,0:T(4,128)S(1)}) custom-call(s32[1]{0:T(128)} %bitcast.84.at, bf16[768,1024]{1,0:T(8,128)(2,1)S(1)} %get-tuple-element.530.refs_0_, bf16[768,1024]{1,0:T(8,128)(2,1)S(1)} %get-tuple-element.532.refs_1_, ...), custom_call_target="tpu_custom_call" | custom-call | flops 1000000 | bytes 100000 | tf_op jit(solution)/shard_map/pallas_call | solution.py:421
  282.6 5.7 fusion.115
  288.3 3.5 fusion.116
  291.8 3.5 fusion.114
  295.3 3.3 shard_map.396
  299.4 5.7 fusion.17
  305.1 3.5 fusion.117
  308.6 3.5 fusion.118
  313.7 7.1 %fusion.109 = (bf16[768,1024]{1,0:T(8,128)(2,1)S(1)}, f32[768,1024]{1,0:T(8,128)S(1)}) fusion(f32[768,1024]{1,0:T(8,128)} %get-tuple-element.531, bf16[768,1024]{1,0:T(8,128)(2,1)S(1)} %copy-done.5, bf16[1024,1024]{1,0:T(8,128)(2,1)S(1)} %bitcast.307, f32[768,1024]{1,0:T(8,128)} %fusion.118, f32[768,1024]{1,0:T(8,128)} %fusion.117, ...), kind=kOutput, calls=%fused_computation.326 | convolution fusion | flops 1620836352 | bytes 24117248 | tf_op jit(solution)/shard_map/dot_general | solution.py:35
  323.1 13.4 %collective-permute-done.26.got_one = bf16[2,8,64,512]{3,2,1,0:T(8,128)(2,1)S(1)} collective-permute-done((bf16[2,8,64,512]{3,2,1,0:T(8,128)(2,1)S(1)}, bf16[2,8,64,512]{3,2,1,0:T(8,128)(2,1)S(1)}, u32[]{:S(2)}, u32[]{:S(2)}) %collective-permute-start.26) | collective-permute-done | bytes 1048608 | tf_op jit(solution)/shard_map/ppermute | solution.py:90
  339.1 6.9 %collective-permute-start.30 = (bf16[2,96,768]{2,1,0:T(8,128)(2,1)S(1)}, bf16[2,96,768]{2,1,0:T(8,128)(2,1)S(1)}, u32[]{:S(2)}, u32[]{:S(2)}) collective-permute-start(bf16[2,96,768]{2,1,0:T(8,128)(2,1)S(1)} %get-tuple-element.255), channel_id=1, source_target_pairs={{0,1},{1,2},{2,3},{3,0},{4,5},{5,6},{6,7},{7,4},{8,9},{9,10},{10,1... | collective-permute-start | bytes 884744 | tf_op jit(solution)/shard_map/ppermute | solution.py:94
  346.0 4.9 collective-permute-start.31
  352.8 11.2 %shard_map.398 = (bf16[4,8,160,512]{3,2,1,0:T(8,128)(2,1)}, bf16[4,8,160,512]{3,2,1,0:T(8,128)(2,1)}, f32[6,1024]{1,0:T(8,128)S(1)}) custom-call(s32[1]{0:T(128)} %bitcast.84.at, bf16[768,1024]{1,0:T(8,128)(2,1)S(1)} %copy-done.7, bf16[8,1024]{1,0:T(8,128)(2,1)S(1)} %get-tuple-element.528.refs_1_, bf16[768,768]{1,0:T(8,128)(2,1)S(1)} %copy-done.23, ...), custom_call_target="tpu_custom_call" | custom-call | flops 1000000 | bytes 100000 | tf_op jit(solution)/shard_map/pallas_call | solution.py:421
  363.9 6.5 %collective-permute-done.31 = bf16[2,96,768]{2,1,0:T(8,128)(2,1)S(1)} collective-permute-done((bf16[2,96,768]{2,1,0:T(8,128)(2,1)S(1)}, bf16[2,96,768]{2,1,0:T(8,128)(2,1)S(1)}, u32[]{:S(2)}, u32[]{:S(2)}) %collective-permute-start.31) | collective-permute-done | bytes 294944 | tf_op jit(solution)/shard_map/ppermute | solution.py:94
  370.4 5.2 collective-permute-done.32
  377.7 3.3 pad_maximum_fusion.up_ref
  386.4 6.7 %shard_map.399 = (bf16[2,8,96,512]{3,2,1,0:T(8,128)(2,1)}, bf16[2,8,96,512]{3,2,1,0:T(8,128)(2,1)S(1)}, bf16[2,8,64,512]{3,2,1,0:T(8,128)(2,1)}, bf16[2,8,64,512]{3,2,1,0:T(8,128)(2,1)S(1)}) custom-call(s32[2]{0:T(128)S(1)} %get-tuple-element.541.at, bf16[4,8,160,512]{3,2,1,0:T(8,128)(2,1)} %get-tuple-element.258.keep_ref, ...), custom_call_target="tpu_custom_call" | custom-call | flops 1000000 | bytes 100000 | tf_op jit(solution)/shard_map/pallas_call | solution.py:128
  399.7 2.2 copy-done.3
  403.8 2.6 shard_map.400
  406.4 8.7 %collective-permute-done.34 = bf16[2,96,768]{2,1,0:T(8,128)(2,1)S(1)} collective-permute-done((bf16[2,96,768]{2,1,0:T(8,128)(2,1)}, bf16[2,96,768]{2,1,0:T(8,128)(2,1)S(1)}, u32[]{:S(2)}, u32[]{:S(2)}) %collective-permute-start.34) | collective-permute-done | bytes 294944 | tf_op jit(solution)/shard_map/ppermute | solution.py:94
  422.4 2.3 copy-done.11
  424.7 12.0 %shard_map.402 = (bf16[768,3072]{1,0:T(8,128)(2,1)S(1)}, f32[8,3072]{1,0:T(8,128)S(1)}, f32[768,768]{1,0:T(8,128)S(1)}) custom-call(bf16[768,768]{1,0:T(8,128)(2,1)S(1)} %bitcast.273, bf16[768,3072]{1,0:T(8,128)(2,1)S(1)} %copy-done.11, bf16[768,3072]{1,0:T(8,128)(2,1)S(1)} %pad_maximum_fusion.up_ref, bf16[3072,768]{1,0:T(8,128)(2,1)S(1)} %bitcast.272), custom_call_target="tpu_custom_call" | custom-call | flops 1000000 | bytes 100000 | tf_op jit(solution)/shard_map/pallas_call | solution.py:588
  438.4 3.2 shard_map.403
  441.5 2.7 convert_reduce_fusion.2
  446.6 2.6 concatenate.91
  450.6 3.3 shard_map.404
  455.6 2.9 collective-permute-start.39
  461.0 3.9 collective-permute-start.47
  468.8 2.9 convert.27
  481.4 22.6 %shard_map.405 = (bf16[768,768]{1,0:T(8,128)(2,1)S(1)}, bf16[768,768]{1,0:T(8,128)(2,1)S(1)}, bf16[768,768]{1,0:T(8,128)(2,1)S(1)}) custom-call(s32[768,1]{1,0:T(8,128)S(1)} %bitcast.276, s32[2,1,384]{2,1,0:T(1,128)S(1)} %broadcast_in_dim.11.row_ref, bf16[768,768]{1,0:T(8,128)(2,1)S(1)} %copy-done.17, bf16[768,768]{1,0:T(8,128)(2,1)S(1)} %copy-done.13, ...), custom_call_target="tpu_custom_call" | custom-call | flops 1000000 | bytes 100000 | tf_op jit(solution)/shard_map/pallas_call | solution.py:343
  516.1 2.8 fusion.121
  518.9 4.9 collective-permute-done.41
  524.5 2.2 shard_map.407
  527.4 2.4 shard_map.408
  537.6 2.9 fusion.94
  540.7 3.5 collective-permute-start.49
  548.7 2.5 fusion.38
  568.7 3.1 collective-permute-start.67
  (743 shorter events, 205.4 us)
Async XLA Ops:
  7.3 215.2 %all-gather.3.cloned.1.call-start = ((), (), s32[]{:S(2)}) async-start(), calls=%async_computation | async-start | bytes 20545536 | tf_op jit(solution)/shard_map/all_gather | solution.py:734
  12.8 18.4 %collective-permute-start = (bf16[112,768]{1,0:T(8,128)(2,1)S(1)}, bf16[112,768]{1,0:T(8,128)(2,1)S(1)}, u32[]{:S(2)}, u32[]{:S(2)}) collective-permute-start(bf16[112,768]{1,0:T(8,128)(2,1)S(1)} %constant_dynamic-update-slice_fusion), channel_id=1, source_target_pairs={{0,3},{1,0},{2,1},{3,2},{4,7},{5,4},{6,5},{7,6},{8,11},{9,8},{10,9... | collective-permute-start | bytes 516104 | tf_op jit(solution)/shard_map/ppermute | solution.py:94
  12.8 18.4 %collective-permute-start.1 = (bf16[112,768]{1,0:T(8,128)(2,1)S(1)}, bf16[112,768]{1,0:T(8,128)(2,1)S(1)}, u32[]{:S(2)}, u32[]{:S(2)}) collective-permute-start(bf16[112,768]{1,0:T(8,128)(2,1)S(1)} %constant_dynamic-update-slice_fusion), channel_id=1, source_target_pairs={{0,2},{1,3},{2,0},{3,1},{4,6},{5,7},{6,4},{7,5},{8,10},{9,11},{10,... | collective-permute-start | bytes 516104 | tf_op jit(solution)/shard_map/ppermute | solution.py:94
  15.3 15.9 %collective-permute-start.2 = (bf16[112,768]{1,0:T(8,128)(2,1)S(1)}, bf16[112,768]{1,0:T(8,128)(2,1)S(1)}, u32[]{:S(2)}, u32[]{:S(2)}) collective-permute-start(bf16[112,768]{1,0:T(8,128)(2,1)S(1)} %constant_dynamic-update-slice_fusion), channel_id=1, source_target_pairs={{0,1},{1,2},{2,3},{3,0},{4,5},{5,6},{6,7},{7,4},{8,9},{9,10},{10,1... | collective-permute-start | bytes 516104 | tf_op jit(solution)/shard_map/ppermute | solution.py:94
  31.2 7.0 %collective-permute-start.3 = (bf16[192,768]{1,0:T(8,128)(2,1)S(1)}, bf16[192,768]{1,0:T(8,128)(2,1)S(1)}, u32[]{:S(2)}, u32[]{:S(2)}) collective-permute-start(bf16[192,768]{1,0:T(8,128)(2,1)S(1)} %constant_dynamic-update-slice_fusion.5), channel_id=1, source_target_pairs={{0,3},{1,0},{2,1},{3,2},{4,7},{5,4},{6,5},{7,6},{8,11},{9,8},{10,9... | collective-permute-start | bytes 884744 | tf_op jit(solution)/shard_map/ppermute | solution.py:94
  31.3 21.2 %collective-permute-start.4 = (bf16[192,768]{1,0:T(8,128)(2,1)S(1)}, bf16[192,768]{1,0:T(8,128)(2,1)S(1)}, u32[]{:S(2)}, u32[]{:S(2)}) collective-permute-start(bf16[192,768]{1,0:T(8,128)(2,1)S(1)} %constant_dynamic-update-slice_fusion.5), channel_id=1, source_target_pairs={{0,2},{1,3},{2,0},{3,1},{4,6},{5,7},{6,4},{7,5},{8,10},{9,11},{10,... | collective-permute-start | bytes 884744 | tf_op jit(solution)/shard_map/ppermute | solution.py:94
  33.1 25.7 %collective-permute-start.5 = (bf16[192,768]{1,0:T(8,128)(2,1)S(1)}, bf16[192,768]{1,0:T(8,128)(2,1)S(1)}, u32[]{:S(2)}, u32[]{:S(2)}) collective-permute-start(bf16[192,768]{1,0:T(8,128)(2,1)S(1)} %constant_dynamic-update-slice_fusion.5), channel_id=1, source_target_pairs={{0,1},{1,2},{2,3},{3,0},{4,5},{5,6},{6,7},{7,4},{8,9},{9,10},{10,1... | collective-permute-start | bytes 884744 | tf_op jit(solution)/shard_map/ppermute | solution.py:94
  62.7 8.2 %collective-permute-start.9 = (bf16[4,48,768]{2,1,0:T(8,128)(2,1)S(1)}, bf16[4,48,768]{2,1,0:T(8,128)(2,1)S(1)}, u32[]{:S(2)}, u32[]{:S(2)}) collective-permute-start(bf16[4,48,768]{2,1,0:T(8,128)(2,1)S(1)} %get-tuple-element.486), channel_id=1, source_target_pairs={{0,16},{4,20},{8,24},{12,28},{16,0},{20,4},{24,8},{28,12},{1,17},{... | collective-permute-start | bytes 884744 | tf_op jit(solution)/shard_map/ppermute | solution.py:90
  64.1 12.5 %collective-permute-start.13 = (bf16[4,64,768]{2,1,0:T(8,128)(2,1)S(1)}, bf16[4,64,768]{2,1,0:T(8,128)(2,1)S(1)}, u32[]{:S(2)}, u32[]{:S(2)}) collective-permute-start(bf16[4,64,768]{2,1,0:T(8,128)(2,1)S(1)} %get-tuple-element.460), channel_id=1, source_target_pairs={{0,8},{4,12},{8,0},{12,4},{16,24},{20,28},{24,16},{28,20},{1,9},{5... | collective-permute-start | bytes 1179656 | tf_op jit(solution)/shard_map/ppermute | solution.py:90
  67.4 15.9 %collective-permute-start.6 = (bf16[2,96,768]{2,1,0:T(8,128)(2,1)}, bf16[2,96,768]{2,1,0:T(8,128)(2,1)S(1)}, u32[]{:S(2)}, u32[]{:S(2)}) collective-permute-start(bf16[2,96,768]{2,1,0:T(8,128)(2,1)} %bitcast), channel_id=1, source_target_pairs={{0,3},{1,0},{2,1},{3,2},{4,7},{5,4},{6,5},{7,6},{8,11},{9,8},{10,9... | collective-permute-start | bytes 884744 | tf_op jit(solution)/shard_map/ppermute | solution.py:94
  67.4 32.1 %collective-permute-start.7 = (bf16[2,96,768]{2,1,0:T(8,128)(2,1)}, bf16[2,96,768]{2,1,0:T(8,128)(2,1)S(1)}, u32[]{:S(2)}, u32[]{:S(2)}) collective-permute-start(bf16[2,96,768]{2,1,0:T(8,128)(2,1)} %bitcast), channel_id=1, source_target_pairs={{0,2},{1,3},{2,0},{3,1},{4,6},{5,7},{6,4},{7,5},{8,10},{9,11},{10,... | collective-permute-start | bytes 884744 | tf_op jit(solution)/shard_map/ppermute | solution.py:94
  70.8 35.2 %collective-permute-start.8 = (bf16[2,96,768]{2,1,0:T(8,128)(2,1)}, bf16[2,96,768]{2,1,0:T(8,128)(2,1)S(1)}, u32[]{:S(2)}, u32[]{:S(2)}) collective-permute-start(bf16[2,96,768]{2,1,0:T(8,128)(2,1)} %bitcast), channel_id=1, source_target_pairs={{0,1},{1,2},{2,3},{3,0},{4,5},{5,6},{6,7},{7,4},{8,9},{9,10},{10,1... | collective-permute-start | bytes 884744 | tf_op jit(solution)/shard_map/ppermute | solution.py:94
  71.7 36.2 %collective-permute-start.10 = (bf16[2,4,48,768]{3,2,1,0:T(8,128)(2,1)}, bf16[2,4,48,768]{3,2,1,0:T(8,128)(2,1)}, u32[]{:S(2)}, u32[]{:S(2)}) collective-permute-start(bf16[2,4,48,768]{3,2,1,0:T(8,128)(2,1)} %pad_maximum_fusion.6.refs_0_), channel_id=1, source_target_pairs={{0,8},{4,12},{8,0},{12,4},{16,24},{20,28},{24,16},{28,20},{1,9},{5... | collective-permute-start | bytes 1769480 | tf_op jit(solution)/shard_map/ppermute | solution.py:90
  76.7 31.0 %collective-permute-start.14 = (bf16[2,4,64,768]{3,2,1,0:T(8,128)(2,1)S(1)}, bf16[2,4,64,768]{3,2,1,0:T(8,128)(2,1)}, u32[]{:S(2)}, u32[]{:S(2)}) collective-permute-start(bf16[2,4,64,768]{3,2,1,0:T(8,128)(2,1)S(1)} %pad_maximum_fusion.5.refs_4_), channel_id=1, source_target_pairs={{0,16},{4,20},{8,24},{12,28},{16,0},{20,4},{24,8},{28,12},{1,17},{... | collective-permute-start | bytes 2359304 | tf_op jit(solution)/shard_map/ppermute | solution.py:90
  83.2 25.2 %collective-permute-start.21 = (bf16[4,96,768]{2,1,0:T(8,128)(2,1)S(1)}, bf16[4,96,768]{2,1,0:T(8,128)(2,1)S(1)}, u32[]{:S(2)}, u32[]{:S(2)}) collective-permute-start(bf16[4,96,768]{2,1,0:T(8,128)(2,1)S(1)} %get-tuple-element.452), channel_id=1, source_target_pairs={{0,8},{4,12},{8,0},{12,4},{16,24},{20,28},{24,16},{28,20},{1,9},{5... | collective-permute-start | bytes 1769480 | tf_op jit(solution)/shard_map/ppermute | solution.py:90
  99.5 16.1 %collective-permute-start.17 = (bf16[4,96,768]{2,1,0:T(8,128)(2,1)}, bf16[4,96,768]{2,1,0:T(8,128)(2,1)S(1)}, u32[]{:S(2)}, u32[]{:S(2)}) collective-permute-start(bf16[4,96,768]{2,1,0:T(8,128)(2,1)} %get-tuple-element.454), channel_id=1, source_target_pairs={{0,16},{4,20},{8,24},{12,28},{16,0},{20,4},{24,8},{28,12},{1,17},{... | collective-permute-start | bytes 1769480 | tf_op jit(solution)/shard_map/ppermute | solution.py:90
  106.0 16.7 %collective-permute-start.15 = (bf16[2,4,64,768]{3,2,1,0:T(8,128)(2,1)S(1)}, bf16[2,4,64,768]{3,2,1,0:T(8,128)(2,1)}, u32[]{:S(2)}, u32[]{:S(2)}) collective-permute-start(bf16[2,4,64,768]{3,2,1,0:T(8,128)(2,1)S(1)} %pad_maximum_fusion.5.refs_4_), channel_id=1, source_target_pairs={{0,4},{4,0},{8,12},{12,8},{16,20},{20,16},{24,28},{28,24},{1,5},{5... | collective-permute-start | bytes 2359304 | tf_op jit(solution)/shard_map/ppermute | solution.py:90
  107.8 15.1 %collective-permute-start.16 = (bf16[2,4,64,768]{3,2,1,0:T(8,128)(2,1)}, bf16[2,4,64,768]{3,2,1,0:T(8,128)(2,1)}, u32[]{:S(2)}, u32[]{:S(2)}) collective-permute-start(bf16[2,4,64,768]{3,2,1,0:T(8,128)(2,1)} %collective-permute-done.14.refs_5_), channel_id=1, source_target_pairs={{0,4},{4,0},{8,12},{12,8},{16,20},{20,16},{24,28},{28,24},{1,5},{5... | collective-permute-start | bytes 2359304 | tf_op jit(solution)/shard_map/ppermute | solution.py:90
  107.9 10.0 %collective-permute-start.11 = (bf16[2,4,48,768]{3,2,1,0:T(8,128)(2,1)}, bf16[2,4,48,768]{3,2,1,0:T(8,128)(2,1)}, u32[]{:S(2)}, u32[]{:S(2)}) collective-permute-start(bf16[2,4,48,768]{3,2,1,0:T(8,128)(2,1)} %pad_maximum_fusion.6.refs_0_), channel_id=1, source_target_pairs={{0,4},{4,0},{8,12},{12,8},{16,20},{20,16},{24,28},{28,24},{1,5},{5... | collective-permute-start | bytes 1769480 | tf_op jit(solution)/shard_map/ppermute | solution.py:90
  109.3 13.5 %collective-permute-start.12 = (bf16[2,4,48,768]{3,2,1,0:T(8,128)(2,1)}, bf16[2,4,48,768]{3,2,1,0:T(8,128)(2,1)}, u32[]{:S(2)}, u32[]{:S(2)}) collective-permute-start(bf16[2,4,48,768]{3,2,1,0:T(8,128)(2,1)} %collective-permute-done.10.refs_1_), channel_id=1, source_target_pairs={{0,4},{4,0},{8,12},{12,8},{16,20},{20,16},{24,28},{28,24},{1,5},{5... | collective-permute-start | bytes 1769480 | tf_op jit(solution)/shard_map/ppermute | solution.py:90
  115.7 43.4 %collective-permute-start.22 = (bf16[2,4,96,768]{3,2,1,0:T(8,128)(2,1)S(1)}, bf16[2,4,96,768]{3,2,1,0:T(8,128)(2,1)}, u32[]{:S(2)}, u32[]{:S(2)}) collective-permute-start(bf16[2,4,96,768]{3,2,1,0:T(8,128)(2,1)S(1)} %pad_maximum_fusion.3.refs_4_), channel_id=1, source_target_pairs={{0,16},{4,20},{8,24},{12,28},{16,0},{20,4},{24,8},{28,12},{1,17},{... | collective-permute-start | bytes 3538952 | tf_op jit(solution)/shard_map/ppermute | solution.py:90
  117.9 47.3 %collective-permute-start.23 = (bf16[2,4,96,768]{3,2,1,0:T(8,128)(2,1)S(1)}, bf16[2,4,96,768]{3,2,1,0:T(8,128)(2,1)}, u32[]{:S(2)}, u32[]{:S(2)}) collective-permute-start(bf16[2,4,96,768]{3,2,1,0:T(8,128)(2,1)S(1)} %pad_maximum_fusion.3.refs_4_), channel_id=1, source_target_pairs={{0,4},{4,0},{8,12},{12,8},{16,20},{20,16},{24,28},{28,24},{1,5},{5... | collective-permute-start | bytes 3538952 | tf_op jit(solution)/shard_map/ppermute | solution.py:90
  122.7 36.7 %collective-permute-start.18 = (bf16[2,4,96,768]{3,2,1,0:T(8,128)(2,1)S(1)}, bf16[2,4,96,768]{3,2,1,0:T(8,128)(2,1)}, u32[]{:S(2)}, u32[]{:S(2)}) collective-permute-start(bf16[2,4,96,768]{3,2,1,0:T(8,128)(2,1)S(1)} %pad_maximum_fusion.2.refs_0_), channel_id=1, source_target_pairs={{0,8},{4,12},{8,0},{12,4},{16,24},{20,28},{24,16},{28,20},{1,9},{5... | collective-permute-start | bytes 3538952 | tf_op jit(solution)/shard_map/ppermute | solution.py:90
  122.7 42.4 %collective-permute-start.19 = (bf16[2,4,96,768]{3,2,1,0:T(8,128)(2,1)S(1)}, bf16[2,4,96,768]{3,2,1,0:T(8,128)(2,1)}, u32[]{:S(2)}, u32[]{:S(2)}) collective-permute-start(bf16[2,4,96,768]{3,2,1,0:T(8,128)(2,1)S(1)} %pad_maximum_fusion.2.refs_0_), channel_id=1, source_target_pairs={{0,4},{4,0},{8,12},{12,8},{16,20},{20,16},{24,28},{28,24},{1,5},{5... | collective-permute-start | bytes 3538952 | tf_op jit(solution)/shard_map/ppermute | solution.py:90
  159.0 6.1 %collective-permute-start.24 = (bf16[2,4,96,768]{3,2,1,0:T(8,128)(2,1)}, bf16[2,4,96,768]{3,2,1,0:T(8,128)(2,1)}, u32[]{:S(2)}, u32[]{:S(2)}) collective-permute-start(bf16[2,4,96,768]{3,2,1,0:T(8,128)(2,1)} %collective-permute-done.22.refs_5_), channel_id=1, source_target_pairs={{0,4},{4,0},{8,12},{12,8},{16,20},{20,16},{24,28},{28,24},{1,5},{5... | collective-permute-start | bytes 3538952 | tf_op jit(solution)/shard_map/ppermute | solution.py:90
  282.3 13.0 %collective-permute-start.25 = (bf16[4,8,128,512]{3,2,1,0:T(8,128)(2,1)}, bf16[4,8,128,512]{3,2,1,0:T(8,128)(2,1)}, u32[]{:S(2)}, u32[]{:S(2)}) collective-permute-start(bf16[4,8,128,512]{3,2,1,0:T(8,128)(2,1)} %get-tuple-element.221), channel_id=1, source_target_pairs={{0,4},{4,0},{8,12},{12,8},{16,20},{20,16},{24,28},{28,24},{1,5},{5... | collective-permute-start | bytes 12582920 | tf_op jit(solution)/shard_map/ppermute | solution.py:90
  312.0 24.5 %collective-permute-start.26 = (bf16[2,8,64,512]{3,2,1,0:T(8,128)(2,1)S(1)}, bf16[2,8,64,512]{3,2,1,0:T(8,128)(2,1)S(1)}, u32[]{:S(2)}, u32[]{:S(2)}) collective-permute-start(bf16[2,8,64,512]{3,2,1,0:T(8,128)(2,1)S(1)} %get-tuple-element.230), channel_id=1, source_target_pairs={{0,16},{4,20},{8,24},{12,28},{16,0},{20,4},{24,8},{28,12},{1,17},{... | collective-permute-start | bytes 3145736 | tf_op jit(solution)/shard_map/ppermute | solution.py:90
  313.0 24.2 %collective-permute-start.27 = (bf16[2,8,64,512]{3,2,1,0:T(8,128)(2,1)S(1)}, bf16[2,8,64,512]{3,2,1,0:T(8,128)(2,1)S(1)}, u32[]{:S(2)}, u32[]{:S(2)}) collective-permute-start(bf16[2,8,64,512]{3,2,1,0:T(8,128)(2,1)S(1)} %get-tuple-element.231), channel_id=1, source_target_pairs={{0,8},{4,12},{8,0},{12,4},{16,24},{20,28},{24,16},{28,20},{1,9},{5... | collective-permute-start | bytes 3145736 | tf_op jit(solution)/shard_map/ppermute | solution.py:90
  339.1 24.8 %collective-permute-start.30 = (bf16[2,96,768]{2,1,0:T(8,128)(2,1)S(1)}, bf16[2,96,768]{2,1,0:T(8,128)(2,1)S(1)}, u32[]{:S(2)}, u32[]{:S(2)}) collective-permute-start(bf16[2,96,768]{2,1,0:T(8,128)(2,1)S(1)} %get-tuple-element.255), channel_id=1, source_target_pairs={{0,1},{1,2},{2,3},{3,0},{4,5},{5,6},{6,7},{7,4},{8,9},{9,10},{10,1... | collective-permute-start | bytes 884744 | tf_op jit(solution)/shard_map/ppermute | solution.py:94
  346.0 24.4 %collective-permute-start.31 = (bf16[2,96,768]{2,1,0:T(8,128)(2,1)S(1)}, bf16[2,96,768]{2,1,0:T(8,128)(2,1)S(1)}, u32[]{:S(2)}, u32[]{:S(2)}) collective-permute-start(bf16[2,96,768]{2,1,0:T(8,128)(2,1)S(1)} %get-tuple-element.256), channel_id=1, source_target_pairs={{0,2},{1,3},{2,0},{3,1},{4,6},{5,7},{6,4},{7,5},{8,10},{9,11},{10,... | collective-permute-start | bytes 884744 | tf_op jit(solution)/shard_map/ppermute | solution.py:94
  350.9 24.8 %collective-permute-start.32 = (bf16[2,96,768]{2,1,0:T(8,128)(2,1)S(1)}, bf16[2,96,768]{2,1,0:T(8,128)(2,1)S(1)}, u32[]{:S(2)}, u32[]{:S(2)}) collective-permute-start(bf16[2,96,768]{2,1,0:T(8,128)(2,1)S(1)} %get-tuple-element.257), channel_id=1, source_target_pairs={{0,3},{1,0},{2,1},{3,2},{4,7},{5,4},{6,5},{7,6},{8,11},{9,8},{10,9... | collective-permute-start | bytes 884744 | tf_op jit(solution)/shard_map/ppermute | solution.py:94
  376.3 10.0 %collective-permute-start.33 = (bf16[4,8,160,512]{3,2,1,0:T(8,128)(2,1)}, bf16[4,8,160,512]{3,2,1,0:T(8,128)(2,1)}, u32[]{:S(2)}, u32[]{:S(2)}) collective-permute-start(bf16[4,8,160,512]{3,2,1,0:T(8,128)(2,1)} %get-tuple-element.259), channel_id=1, source_target_pairs={{0,4},{4,0},{8,12},{12,8},{16,20},{20,16},{24,28},{28,24},{1,5},{5... | collective-permute-start | bytes 15728648 | tf_op jit(solution)/shard_map/ppermute | solution.py:90
  381.0 38.4 %collective-permute-start.28 = (bf16[1,8,64,512]{3,2,1,0:T(8,128)(2,1)}, bf16[1,8,64,512]{3,2,1,0:T(8,128)(2,1)S(1)}, u32[]{:S(2)}, u32[]{:S(2)}) collective-permute-start(bf16[1,8,64,512]{3,2,1,0:T(8,128)(2,1)} %get-tuple-element.248), channel_id=1, source_target_pairs={{0,8},{4,12},{8,0},{12,4},{16,24},{20,28},{24,16},{28,20},{1,9},{5... | collective-permute-start | bytes 1572872 | tf_op jit(solution)/shard_map/ppermute | solution.py:90
  382.3 37.1 %collective-permute-start.29 = (bf16[1,8,64,512]{3,2,1,0:T(8,128)(2,1)}, bf16[1,8,64,512]{3,2,1,0:T(8,128)(2,1)S(1)}, u32[]{:S(2)}, u32[]{:S(2)}) collective-permute-start(bf16[1,8,64,512]{3,2,1,0:T(8,128)(2,1)} %get-tuple-element.249), channel_id=1, source_target_pairs={{0,16},{4,20},{8,24},{12,28},{16,0},{20,4},{24,8},{28,12},{1,17},{... | collective-permute-start | bytes 1572872 | tf_op jit(solution)/shard_map/ppermute | solution.py:90
  394.1 21.1 %collective-permute-start.34 = (bf16[2,96,768]{2,1,0:T(8,128)(2,1)}, bf16[2,96,768]{2,1,0:T(8,128)(2,1)S(1)}, u32[]{:S(2)}, u32[]{:S(2)}) collective-permute-start(bf16[2,96,768]{2,1,0:T(8,128)(2,1)} %add_convert_fusion.6), channel_id=1, source_target_pairs={{0,3},{1,0},{2,1},{3,2},{4,7},{5,4},{6,5},{7,6},{8,11},{9,8},{10,9... | collective-permute-start | bytes 884744 | tf_op jit(solution)/shard_map/ppermute | solution.py:94
  394.1 21.9 %collective-permute-start.35 = (bf16[2,96,768]{2,1,0:T(8,128)(2,1)}, bf16[2,96,768]{2,1,0:T(8,128)(2,1)S(1)}, u32[]{:S(2)}, u32[]{:S(2)}) collective-permute-start(bf16[2,96,768]{2,1,0:T(8,128)(2,1)} %add_convert_fusion.6), channel_id=1, source_target_pairs={{0,2},{1,3},{2,0},{3,1},{4,6},{5,7},{6,4},{7,5},{8,10},{9,11},{10,... | collective-permute-start | bytes 884744 | tf_op jit(solution)/shard_map/ppermute | solution.py:94
  394.5 24.9 %collective-permute-start.36 = (bf16[2,96,768]{2,1,0:T(8,128)(2,1)}, bf16[2,96,768]{2,1,0:T(8,128)(2,1)S(1)}, u32[]{:S(2)}, u32[]{:S(2)}) collective-permute-start(bf16[2,96,768]{2,1,0:T(8,128)(2,1)} %add_convert_fusion.6), channel_id=1, source_target_pairs={{0,1},{1,2},{2,3},{3,0},{4,5},{5,6},{6,7},{7,4},{8,9},{9,10},{10,1... | collective-permute-start | bytes 884744 | tf_op jit(solution)/shard_map/ppermute | solution.py:94
  415.1 34.2 %collective-permute-start.37 = (bf16[2,8,96,512]{3,2,1,0:T(8,128)(2,1)}, bf16[2,8,96,512]{3,2,1,0:T(8,128)(2,1)}, u32[]{:S(2)}, u32[]{:S(2)}) collective-permute-start(bf16[2,8,96,512]{3,2,1,0:T(8,128)(2,1)} %get-tuple-element.297), channel_id=1, source_target_pairs={{0,16},{4,20},{8,24},{12,28},{16,0},{20,4},{24,8},{28,12},{1,17},{... | collective-permute-start | bytes 4718600 | tf_op jit(solution)/shard_map/ppermute | solution.py:90
  415.9 33.2 %collective-permute-start.38 = (bf16[2,8,64,512]{3,2,1,0:T(8,128)(2,1)}, bf16[2,8,64,512]{3,2,1,0:T(8,128)(2,1)}, u32[]{:S(2)}, u32[]{:S(2)}) collective-permute-start(bf16[2,8,64,512]{3,2,1,0:T(8,128)(2,1)} %get-tuple-element.298), channel_id=1, source_target_pairs={{0,8},{4,12},{8,0},{12,4},{16,24},{20,28},{24,16},{28,20},{1,9},{5... | collective-permute-start | bytes 3145736 | tf_op jit(solution)/shard_map/ppermute | solution.py:90
  455.6 9.2 %collective-permute-start.39 = (f32[48,1024]{1,0:T(8,128)}, f32[48,1024]{1,0:T(8,128)S(1)}, u32[]{:S(2)}, u32[]{:S(2)}) collective-permute-start(f32[48,1024]{1,0:T(8,128)} %concatenate.91), channel_id=1, source_target_pairs={{0,4},{4,0},{8,12},{12,8},{16,20},{20,16},{24,28},{28,24},{1,5},{5... | collective-permute-start | bytes 589832 | tf_op jit(solution)/shard_map/ppermute | solution.py:90
  458.6 68.8 %collective-permute-start.43 = (bf16[4,2,192,384]{3,2,1,0:T(8,128)(2,1)}, bf16[4,2,192,384]{3,2,1,0:T(8,128)(2,1)}, u32[]{:S(2)}, u32[]{:S(2)}) collective-permute-start(bf16[4,2,192,384]{3,2,1,0:T(8,128)(2,1)} %get-tuple-element.330), channel_id=1, source_target_pairs={{0,4},{4,0},{8,12},{12,8},{16,20},{20,16},{24,28},{28,24},{1,5},{5... | collective-permute-start | bytes 3538952 | tf_op jit(solution)/shard_map/ppermute | solution.py:90
  460.0 47.6 %collective-permute-start.46 = (bf16[2,128,512]{2,1,0:T(8,128)(2,1)}, bf16[2,128,512]{2,1,0:T(8,128)(2,1)}, u32[]{:S(2)}, u32[]{:S(2)}) collective-permute-start(bf16[2,128,512]{2,1,0:T(8,128)(2,1)} %copy-done.64), channel_id=1, source_target_pairs={{0,1},{1,2},{2,3},{3,0},{4,5},{5,6},{6,7},{7,4},{8,9},{9,10},{10,1... | collective-permute-start | bytes 786440 | tf_op jit(solution)/shard_map/ppermute | solution.py:94
  461.0 47.7 %collective-permute-start.47 = (bf16[2,128,512]{2,1,0:T(8,128)(2,1)}, bf16[2,128,512]{2,1,0:T(8,128)(2,1)}, u32[]{:S(2)}, u32[]{:S(2)}) collective-permute-start(bf16[2,128,512]{2,1,0:T(8,128)(2,1)} %copy-done.63), channel_id=1, source_target_pairs={{0,2},{1,3},{2,0},{3,1},{4,6},{5,7},{6,4},{7,5},{8,10},{9,11},{10,... | collective-permute-start | bytes 786440 | tf_op jit(solution)/shard_map/ppermute | solution.py:94
  465.9 6.5 %collective-permute-start.40 = (f32[48,1024]{1,0:T(8,128)S(1)}, f32[48,1024]{1,0:T(8,128)S(1)}, u32[]{:S(2)}, u32[]{:S(2)}) collective-permute-start(f32[48,1024]{1,0:T(8,128)S(1)} %add.631), channel_id=1, source_target_pairs={{0,8},{4,12},{8,0},{12,4},{16,24},{20,28},{24,16},{28,20},{1,9},{5... | collective-permute-start | bytes 589832 | tf_op jit(solution)/shard_map/ppermute | solution.py:90
  472.3 40.6 %collective-permute-start.48 = (bf16[2,128,512]{2,1,0:T(8,128)(2,1)}, bf16[2,128,512]{2,1,0:T(8,128)(2,1)}, u32[]{:S(2)}, u32[]{:S(2)}) collective-permute-start(bf16[2,128,512]{2,1,0:T(8,128)(2,1)} %get-tuple-element.361), channel_id=1, source_target_pairs={{0,3},{1,0},{2,1},{3,2},{4,7},{5,4},{6,5},{7,6},{8,11},{9,8},{10,9... | collective-permute-start | bytes 786440 | tf_op jit(solution)/shard_map/ppermute | solution.py:94
  472.3 52.1 %collective-permute-start.44 = (bf16[1,8,96,512]{3,2,1,0:T(8,128)(2,1)}, bf16[1,8,96,512]{3,2,1,0:T(8,128)(2,1)}, u32[]{:S(2)}, u32[]{:S(2)}) collective-permute-start(bf16[1,8,96,512]{3,2,1,0:T(8,128)(2,1)} %get-tuple-element.332), channel_id=1, source_target_pairs={{0,8},{4,12},{8,0},{12,4},{16,24},{20,28},{24,16},{28,20},{1,9},{5... | collective-permute-start | bytes 2359304 | tf_op jit(solution)/shard_map/ppermute | solution.py:90
  507.6 16.9 %collective-permute-start.45 = (bf16[1,8,64,512]{3,2,1,0:T(8,128)(2,1)}, bf16[1,8,64,512]{3,2,1,0:T(8,128)(2,1)S(1)}, u32[]{:S(2)}, u32[]{:S(2)}) collective-permute-start(bf16[1,8,64,512]{3,2,1,0:T(8,128)(2,1)} %get-tuple-element.333), channel_id=1, source_target_pairs={{0,16},{4,20},{8,24},{12,28},{16,0},{20,4},{24,8},{28,12},{1,17},{... | collective-permute-start | bytes 1572872 | tf_op jit(solution)/shard_map/ppermute | solution.py:90
  508.6 26.4 %collective-permute-start.42 = (bf16[4,2,96,384]{3,2,1,0:T(8,128)(2,1)}, bf16[4,2,96,384]{3,2,1,0:T(8,128)(2,1)S(1)}, u32[]{:S(2)}, u32[]{:S(2)}) collective-permute-start(bf16[4,2,96,384]{3,2,1,0:T(8,128)(2,1)} %get-tuple-element.328), channel_id=1, source_target_pairs={{0,4},{4,0},{8,12},{12,8},{16,20},{20,16},{24,28},{28,24},{1,5},{5... | collective-permute-start | bytes 1769480 | tf_op jit(solution)/shard_map/ppermute | solution.py:90
  515.6 8.1 %collective-permute-start.41 = (f32[48,1024]{1,0:T(8,128)}, f32[48,1024]{1,0:T(8,128)S(1)}, u32[]{:S(2)}, u32[]{:S(2)}) collective-permute-start(f32[48,1024]{1,0:T(8,128)} %add.632), channel_id=1, source_target_pairs={{0,16},{4,20},{8,24},{12,28},{16,0},{20,4},{24,8},{28,12},{1,17},{... | collective-permute-start | bytes 589832 | tf_op jit(solution)/shard_map/ppermute | solution.py:90
  529.8 29.9 %collective-permute-start.64 = (bf16[2,160,512]{2,1,0:T(8,128)(2,1)}, bf16[2,160,512]{2,1,0:T(8,128)(2,1)S(1)}, u32[]{:S(2)}, u32[]{:S(2)}) collective-permute-start(bf16[2,160,512]{2,1,0:T(8,128)(2,1)} %get-tuple-element.388), channel_id=1, source_target_pairs={{0,1},{1,2},{2,3},{3,0},{4,5},{5,6},{6,7},{7,4},{8,9},{9,10},{10,1... | collective-permute-start | bytes 983048 | tf_op jit(solution)/shard_map/ppermute | solution.py:94
  530.9 29.1 %collective-permute-start.65 = (bf16[2,160,512]{2,1,0:T(8,128)(2,1)}, bf16[2,160,512]{2,1,0:T(8,128)(2,1)}, u32[]{:S(2)}, u32[]{:S(2)}) collective-permute-start(bf16[2,160,512]{2,1,0:T(8,128)(2,1)} %get-tuple-element.389), channel_id=1, source_target_pairs={{0,2},{1,3},{2,0},{3,1},{4,6},{5,7},{6,4},{7,5},{8,10},{9,11},{10,... | collective-permute-start | bytes 983048 | tf_op jit(solution)/shard_map/ppermute | solution.py:94
  533.0 18.2 %collective-permute-start.57 = (bf16[2,2,96,384]{3,2,1,0:T(8,128)(2,1)}, bf16[2,2,96,384]{3,2,1,0:T(8,128)(2,1)}, u32[]{:S(2)}, u32[]{:S(2)}) collective-permute-start(bf16[2,2,96,384]{3,2,1,0:T(8,128)(2,1)} %get-tuple-element.377), channel_id=1, source_target_pairs={{0,16},{4,20},{8,24},{12,28},{16,0},{20,4},{24,8},{28,12},{1,17},{... | collective-permute-start | bytes 884744 | tf_op jit(solution)/shard_map/ppermute | solution.py:90
  534.1 18.4 %collective-permute-start.58 = (bf16[2,2,96,384]{3,2,1,0:T(8,128)(2,1)}, bf16[2,2,96,384]{3,2,1,0:T(8,128)(2,1)}, u32[]{:S(2)}, u32[]{:S(2)}) collective-permute-start(bf16[2,2,96,384]{3,2,1,0:T(8,128)(2,1)} %get-tuple-element.379), channel_id=1, source_target_pairs={{0,8},{4,12},{8,0},{12,4},{16,24},{20,28},{24,16},{28,20},{1,9},{5... | collective-permute-start | bytes 884744 | tf_op jit(solution)/shard_map/ppermute | solution.py:90
  548.7 12.6 %collective-permute-start.66 = (bf16[2,160,512]{2,1,0:T(8,128)(2,1)S(1)}, bf16[2,160,512]{2,1,0:T(8,128)(2,1)S(1)}, u32[]{:S(2)}, u32[]{:S(2)}) collective-permute-start(bf16[2,160,512]{2,1,0:T(8,128)(2,1)S(1)} %copy-done.62), channel_id=1, source_target_pairs={{0,3},{1,0},{2,1},{3,2},{4,7},{5,4},{6,5},{7,6},{8,11},{9,8},{10,9... | collective-permute-start | bytes 983048 | tf_op jit(solution)/shard_map/ppermute | solution.py:94
  551.3 12.3 %collective-permute-start.68 = (bf16[128,512]{1,0:T(8,128)(2,1)S(1)}, bf16[128,512]{1,0:T(8,128)(2,1)S(1)}, u32[]{:S(2)}, u32[]{:S(2)}) collective-permute-start(bf16[128,512]{1,0:T(8,128)(2,1)S(1)} %copy-done.70), channel_id=1, source_target_pairs={{0,4},{4,0},{8,12},{12,8},{16,20},{20,16},{24,28},{28,24},{1,5},{5... | collective-permute-start | bytes 393224 | tf_op jit(solution)/shard_map/ppermute | solution.py:90
  555.8 12.2 %collective-permute-start.62 = (f32[48,1024]{1,0:T(8,128)S(1)}, f32[48,1024]{1,0:T(8,128)S(1)}, u32[]{:S(2)}, u32[]{:S(2)}) collective-permute-start(f32[48,1024]{1,0:T(8,128)S(1)} %copy-done.117), channel_id=1, source_target_pairs={{0,1},{1,0},{2,3},{3,2},{4,5},{5,4},{6,7},{7,6},{8,9},{9,8},{10,11... | collective-permute-start | bytes 589832 | tf_op jit(solution)/shard_map/ppermute | solution.py:98
  559.7 6.6 %collective-permute-start.52 = (bf16[2,2,48,384]{3,2,1,0:T(8,128)(2,1)S(1)}, bf16[2,2,48,384]{3,2,1,0:T(8,128)(2,1)S(1)}, u32[]{:S(2)}, u32[]{:S(2)}) collective-permute-start(bf16[2,2,48,384]{3,2,1,0:T(8,128)(2,1)S(1)} %copy-done.68), channel_id=1, source_target_pairs={{0,16},{4,20},{8,24},{12,28},{16,0},{20,4},{24,8},{28,12},{1,17},{... | collective-permute-start | bytes 442376 | tf_op jit(solution)/shard_map/ppermute | solution.py:90
  560.1 6.2 %collective-permute-start.53 = (bf16[2,2,48,384]{3,2,1,0:T(8,128)(2,1)S(1)}, bf16[2,2,48,384]{3,2,1,0:T(8,128)(2,1)S(1)}, u32[]{:S(2)}, u32[]{:S(2)}) collective-permute-start(bf16[2,2,48,384]{3,2,1,0:T(8,128)(2,1)S(1)} %copy-done.66), channel_id=1, source_target_pairs={{0,8},{4,12},{8,0},{12,4},{16,24},{20,28},{24,16},{28,20},{1,9},{5... | collective-permute-start | bytes 442376 | tf_op jit(solution)/shard_map/ppermute | solution.py:90
  561.3 14.6 %collective-permute-start.59 = (bf16[1,2,96,384]{3,2,1,0:T(8,128)(2,1)S(1)}, bf16[1,2,96,384]{3,2,1,0:T(8,128)(2,1)S(1)}, u32[]{:S(2)}, u32[]{:S(2)}) collective-permute-start(bf16[1,2,96,384]{3,2,1,0:T(8,128)(2,1)S(1)} %get-tuple-element.382), channel_id=1, source_target_pairs={{0,8},{4,12},{8,0},{12,4},{16,24},{20,28},{24,16},{28,20},{1,9},{5... | collective-permute-start | bytes 442376 | tf_op jit(solution)/shard_map/ppermute | solution.py:90
  563.6 12.4 %collective-permute-start.60 = (bf16[1,2,96,384]{3,2,1,0:T(8,128)(2,1)S(1)}, bf16[1,2,96,384]{3,2,1,0:T(8,128)(2,1)S(1)}, u32[]{:S(2)}, u32[]{:S(2)}) collective-permute-start(bf16[1,2,96,384]{3,2,1,0:T(8,128)(2,1)S(1)} %get-tuple-element.383), channel_id=1, source_target_pairs={{0,16},{4,20},{8,24},{12,28},{16,0},{20,4},{24,8},{28,12},{1,17},{... | collective-permute-start | bytes 442376 | tf_op jit(solution)/shard_map/ppermute | solution.py:90
  567.0 5.8 collective-permute-start.54
  567.6 6.7 %collective-permute-start.55 = (bf16[1,2,48,384]{3,2,1,0:T(8,128)(2,1)S(1)}, bf16[1,2,48,384]{3,2,1,0:T(8,128)(2,1)S(1)}, u32[]{:S(2)}, u32[]{:S(2)}) collective-permute-start(bf16[1,2,48,384]{3,2,1,0:T(8,128)(2,1)S(1)} %get-tuple-element.373), channel_id=1, source_target_pairs={{0,16},{4,20},{8,24},{12,28},{16,0},{20,4},{24,8},{28,12},{1,17},{... | collective-permute-start | bytes 221192 | tf_op jit(solution)/shard_map/ppermute | solution.py:90
  568.7 8.9 %collective-permute-start.67 = (bf16[160,512]{1,0:T(8,128)(2,1)S(1)}, bf16[160,512]{1,0:T(8,128)(2,1)S(1)}, u32[]{:S(2)}, u32[]{:S(2)}) collective-permute-start(bf16[160,512]{1,0:T(8,128)(2,1)S(1)} %get-tuple-element.392), channel_id=1, source_target_pairs={{0,4},{4,0},{8,12},{12,8},{16,20},{20,16},{24,28},{28,24},{1,5},{5... | collective-permute-start | bytes 491528 | tf_op jit(solution)/shard_map/ppermute | solution.py:90
  572.7 9.9 %collective-permute-start.63 = (f32[48,1024]{1,0:T(8,128)S(1)}, f32[48,1024]{1,0:T(8,128)S(1)}, u32[]{:S(2)}, u32[]{:S(2)}) collective-permute-start(f32[48,1024]{1,0:T(8,128)S(1)} %add.644), channel_id=1, source_target_pairs={{0,2},{1,3},{2,0},{3,1},{4,6},{5,7},{6,4},{7,5},{8,10},{9,11},{10,... | collective-permute-start | bytes 589832 | tf_op jit(solution)/shard_map/ppermute | solution.py:98
  (195 other events, 1868.3 us)
Sparse Core Ops, SparseCore 0:
  58.9 163.4 all-gather.2

commit v3 on v2

v3 whole, which is shorter than its diff:
```python
import functools
import math

import jax
import jax.numpy as jnp
from jax import lax
from jax.experimental import pallas as pl
from jax.experimental.pallas import tpu as pltpu
from jax.sharding import PartitionSpec as P

D = 768
HEADS = 12
HEAD_DIM = 64
WIDTH = 1024
FREQ = 256
CHANNELS = 16
IMAGES = 4


epsilon = 1e-06
highest = lax.Precision.HIGHEST


def product(left_side, right_side):
    return jnp.dot(left_side, right_side, preferred_element_type=jnp.float32)


def weight_grad(left_side, right_side):
    return lax.dot_general(
        left_side, right_side, (((0,), (0,)), ((), ())), preferred_element_type=jnp.float32
    )


def input_back(gradient, weight):
    return lax.dot_general(
        gradient, weight, (((1,), (1,)), ((), ())), preferred_element_type=jnp.float32
    )


def column_sum(values):
    return jnp.sum(values.astype(jnp.float32), axis=0)


def normalize(values):
    center = values - jnp.mean(values, axis=-1, keepdims=True)
    inverse = lax.rsqrt(jnp.mean(center * center, axis=-1, keepdims=True) + epsilon)
    return (center * inverse, inverse)


def norm_back(gradient, normed, inverse):
    return inverse * (
        gradient
        - jnp.mean(gradient, axis=-1, keepdims=True)
        - normed * jnp.mean(gradient * normed, axis=-1, keepdims=True)
    )


def silu_slope(values):
    sigma = jax.nn.sigmoid(values)
    return sigma * (1.0 + values * (1.0 - sigma))


def gelu_slope(values):
    return 0.5 * (1.0 + lax.erf(values * 2.0 ** (-0.5))) + values * jnp.exp(
        -0.5 * values * values
    ) * (2.0 * math.pi) ** (-0.5)


def sinusoid(step_vals):
    half_width = FREQ // 2
    rates = jnp.exp(-math.log(10000.0) * jnp.arange(half_width, dtype=jnp.float32) / half_width)
    angles = step_vals[:, None] * rates[None, :]
    return jnp.concatenate([jnp.cos(angles), jnp.sin(angles)], axis=1)


def plan(step_vals):
    anchor = math.cos(0.008 / 1.008 * math.pi / 2.0) ** 2
    angle_now = ((step_vals + 1.0) / 1000.0 + 0.008) / 1.008 * (math.pi / 2.0)
    signal = jnp.cos(angle_now) ** 2 / anchor
    return jnp.stack([jnp.sqrt(signal), jnp.sqrt(1.0 - signal)], axis=1)


def tdot(left_side, right_side):
    return lax.dot_general(
        left_side, right_side, (((0,), (0,)), ((), ())), preferred_element_type=jnp.float32
    )


def swap_bit(values, size, bit):
    return lax.ppermute(values, "dp", [(i, i ^ (1 << bit)) for i in range(size)])


def shift_copy(values, size, shift):
    return lax.ppermute(values, "copy", [(i, (i + shift) % size) for i in range(size)])


def swap_copy(values, size, shift):
    return lax.ppermute(values, "copy", [(i, i ^ shift) for i in range(size)])


def pick(values, index, axis):
    return lax.dynamic_index_in_dim(values, index, axis, keepdims=False)


def tie(*values):
    return lax.optimization_barrier(values)


MIB = 1 << 20


LIGHT = pl.CostEstimate(flops=10**6, bytes_accessed=10**5, transcendentals=0)


def dot0(left_side, right_side):
    return lax.dot_general(
        left_side, right_side, (((0,), (0,)), ((), ())), preferred_element_type=jnp.float32
    )


def dot1(left_side, right_side):
    return lax.dot_general(
        left_side, right_side, (((1,), (1,)), ((), ())), preferred_element_type=jnp.float32
    )


def small_call(body, outs, scalars, ins):
    size = sum(math.prod(o.shape) * o.dtype.itemsize for o in outs)
    size += sum(math.prod(v.shape) * v.dtype.itemsize for v in ins)
    return pl.pallas_call(
        body,
        out_shape=outs,
        in_specs=[pl.BlockSpec(memory_space=pltpu.SMEM)]
        + [pl.BlockSpec(memory_space=pltpu.VMEM)] * len(ins),
        out_specs=[pl.BlockSpec(memory_space=pltpu.VMEM)] * len(outs),
        compiler_params=pltpu.CompilerParams(vmem_limit_bytes=60 * MIB),
        cost_estimate=LIGHT,
    )(jnp.stack([jnp.asarray(v, jnp.int32) for v in scalars]), *ins)


def low_shape(*dims):
    return jax.ShapeDtypeStruct(dims, jnp.bfloat16)


def add_up(one, two):
    return one.astype(jnp.float32) + two.astype(jnp.float32)


def cut_first(keeps, gots, rows, bits, kernels):
    count, mids, _, width = keeps[0].shape
    half = count // 2
    sizes = [k.shape[2] for k in keeps]
    total = sum(sizes)

    if not kernels:
        sums = jnp.concatenate([add_up(k, g) for k, g in zip(keeps, gots)], axis=2)
        sums = sums.astype(jnp.bfloat16)
        first = sums[:, :, :rows].reshape(2, half, mids, rows, width)
        second = sums[:, :, rows:].reshape(half, 2, mids, total - rows, width)
        return [
            pick(first, 1 - bits[0], 0),
            pick(first, bits[0], 0),
            pick(second, 1 - bits[1], 1),
            pick(second, bits[1], 1),
        ]

    def body(at, *refs):
        keep_refs, got_refs = refs[: len(keeps)], refs[len(keeps) : 2 * len(keeps)]
        outs = refs[2 * len(keeps) :]
        for out, bit, low in zip(outs, (1 - at[0], at[0], 1 - at[1], at[1]), (0, 0, 1, 1)):
            begin, end = (rows, total) if low else (0, rows)
            at_row = 0
            for keep, got, n in zip(keep_refs, got_refs, sizes):
                top, bottom = max(begin, at_row), min(end, at_row + n)
                if top < bottom:
                    cut = pl.ds(top - at_row, bottom - top)
                    for i in range(half):
                        p = 2 * i + bit if low else bit * half + i
                        value = add_up(keep[p, :, cut], got[p, :, cut]).astype(jnp.bfloat16)
                        out[i, :, top - begin : bottom - begin] = value
                at_row += n

    outs = [low_shape(half, mids, n, width) for n in (rows, rows, total - rows, total - rows)]
    return small_call(body, outs, bits, [*keeps, *gots])


def cut_next(keeps, gots, bits, kernels):
    count, mids, _, width = keeps[0].shape
    half = count // 2
    sizes = [k.shape[2] for k in keeps]
    if not kernels:
        sums = [add_up(k, g).astype(jnp.bfloat16) for k, g in zip(keeps, gots)]
        first = sums[0].reshape(2, half, mids, sizes[0], width)
        second = sums[1].reshape(half, 2, mids, sizes[1], width)
        return [
            pick(first, 1 - bits[0], 0),
            pick(first, bits[0], 0),
            pick(second, 1 - bits[1], 1),
            pick(second, bits[1], 1),
        ]

    def body(at, keep_one, got_one, keep_two, got_two, *outs):
        for out, bit, top in zip(outs, (1 - at[0], at[0], 1 - at[1], at[1]), (0, 0, 1, 1)):
            keep, got = (keep_two, got_two) if top else (keep_one, got_one)
            for i in range(half):
                p = 2 * i + bit if top else bit * half + i
                out[i] = add_up(keep[p], got[p]).astype(jnp.bfloat16)

    outs = [low_shape(half, mids, n, width) for n in (sizes[0], sizes[0], sizes[1], sizes[1])]
    return small_call(body, outs, bits, [keeps[0], gots[0], keeps[1], gots[1]])


def cut_copies(keeps, gots, place, copy_size, kernels):
    _, mids, _, width = keeps[0].shape
    sizes = [k.shape[2] for k in keeps]
    total = sum(sizes)
    if not kernels:
        sums = jnp.concatenate([add_up(k, g)[0] for k, g in zip(keeps, gots)], axis=1)
        sums = sums.astype(jnp.bfloat16).reshape(2, copy_size, total, width)
        return [pick(sums, lax.rem(place + j, copy_size), 1) for j in range(copy_size)]

    def body(at, keep_one, got_one, keep_two, got_two, *outs):
        for j in range(copy_size):
            z = lax.rem(at[0] + j, copy_size)
            for c in range(2):
                m = c * copy_size + z
                top = add_up(keep_one[0, m], got_one[0, m]).astype(jnp.bfloat16)
                low = add_up(keep_two[0, m], got_two[0, m]).astype(jnp.bfloat16)
                outs[j][c, : sizes[0]] = top
                outs[j][c, sizes[0] :] = low

    outs = [low_shape(2, total, width)] * copy_size
    return small_call(body, outs, [place], [keeps[0], gots[0], keeps[1], gots[1]])


def sum_low(parts, kernels):
    if not kernels:
        return sum(p.astype(jnp.float32) for p in parts).astype(jnp.bfloat16)

    def body(at, *refs):
        total = refs[0][...].astype(jnp.float32)
        for ref in refs[1:-1]:
            total = total + ref[...].astype(jnp.float32)
        refs[-1][...] = total.astype(jnp.bfloat16)

    return small_call(body, [low_shape(*parts[0].shape)], [0], parts)[0]


def own_and_other(parts, scalars, kernels):
    place, core = scalars
    count = len(parts)
    _, total, width = parts[0].shape
    if not kernels:
        stacked = jnp.stack(parts).astype(jnp.float32)
        sums = 0.0
        for i in range(count):
            sums = sums + pick(stacked, lax.rem(place + count - i, count), 0)
        sums = sums.astype(jnp.bfloat16)
        return [pick(sums, 1 - core, 0), pick(sums, core, 0)]

    def body(at, *refs):
        for out, c in zip(refs[count:], (1 - at[1], at[1])):
            values = [r[c].astype(jnp.float32) for r in refs[:count]]
            sums = None
            for i in range(count):
                turn = lax.rem(at[0] + count - i, count)
                value = values[0]
                for j in range(1, count):
                    value = jnp.where(turn == j, values[j], value)
                sums = value if sums is None else sums + value
            out[...] = sums.astype(jnp.bfloat16)

    return small_call(body, [low_shape(total, width)] * 2, scalars, parts)


class Reduction:
    def __init__(self, sent, kept, rows, size, kernels):
        self.size, self.rows, self.kernels = size, rows, kernels
        self.left = size.bit_length() - 2
        self.me = lax.axis_index("dp")
        self.sent, self.kept, self.bits = list(sent), list(kept), [0] * len(sent)
        self.first = True

    def receive(self):
        self.got = [swap_bit(v, self.size, bit) for v, bit in zip(self.sent, self.bits)]
        return self

    def advance(self):
        if self.first:
            self.bits = [self.left, 1]
            bits = [(self.me >> b) & 1 for b in self.bits]
            cuts = cut_first(self.kept, self.got, self.rows, bits, self.kernels)
        else:
            self.bits = [self.bits[0] - 1, self.bits[1] + 1]
            bits = [(self.me >> b) & 1 for b in self.bits]
            cuts = cut_next(self.kept, self.got, bits, self.kernels)
        self.first = False
        self.left -= 1
        self.sent, self.kept = [cuts[0], cuts[2]], [cuts[1], cuts[3]]
        return self


def attend(ids_col, ids_row, q, k, lanes, head, scale):
    wanted = (lanes >= HEAD_DIM) if head else (lanes < HEAD_DIM)
    scores = dot1(jnp.where(wanted, q, 0), k) * scale
    scores = jnp.where(ids_col == ids_row, scores, -1e30)
    exps = jnp.exp(scores - jnp.max(scores, axis=-1, keepdims=True))
    return wanted, exps / jnp.sum(exps, axis=-1, keepdims=True)


def attention_specs(micros, length, first=0):
    wide = pl.BlockSpec((length, 2 * HEAD_DIM), lambda m, h: (m + first, h))
    col = pl.BlockSpec((length, 1), lambda m, h: (m + first, 0))
    row = pl.BlockSpec((1, 1, length), lambda m, h: (m + first, 0, 0))
    return wide, col, row


def attention(queries, key_rows, value_rows, ids):
    micros, length = ids.shape
    scale = HEAD_DIM ** (-0.5)
    wide, col, row = attention_specs(micros, length)

    def body(col_ref, row_ref, q_ref, k_ref, v_ref, out_ref):
        lanes = lax.broadcasted_iota(jnp.int32, (1, 2 * HEAD_DIM), 1)
        outs = []
        for head in range(2):
            _, probs = attend(
                col_ref[...], row_ref[0], q_ref[...], k_ref[...], lanes, head, scale
            )
            outs.append(
                jnp.dot(
                    probs.astype(jnp.bfloat16), v_ref[...], preferred_element_type=jnp.float32
                )
            )
        out_ref[...] = jnp.where(lanes < HEAD_DIM, outs[0], outs[1]).astype(jnp.bfloat16)

    return pl.pallas_call(
        body,
        grid=(micros, HEADS // 2),
        out_shape=low_shape(micros * length, D),
        in_specs=[col, row, wide, wide, wide],
        out_specs=wide,
        compiler_params=pltpu.CompilerParams(vmem_limit_bytes=24 * MIB),
        cost_estimate=LIGHT,
    )(ids.reshape(-1, 1), ids[:, None], queries, key_rows, value_rows)


def attention_back(queries, key_rows, value_rows, grad_mixed, ids, which, before):
    micros, length = ids.shape
    scale = HEAD_DIM ** (-0.5)
    wide, col, row = attention_specs(micros, length, which)

    def body(col_ref, row_ref, q_ref, k_ref, v_ref, g_ref, *outs):
        lanes = lax.broadcasted_iota(jnp.int32, (1, 2 * HEAD_DIM), 1)
        q, k, v, g = q_ref[...], k_ref[...], v_ref[...], g_ref[...]
        parts = []
        for head in range(2):
            wanted, probs = attend(col_ref[...], row_ref[0], q, k, lanes, head, scale)
            grad_probs = dot1(jnp.where(wanted, g, 0), v)
            delta = jnp.sum(grad_probs * probs, axis=-1, keepdims=True)
            grad_scores = (probs * (grad_probs - delta)).astype(jnp.bfloat16)
            parts.append(
                (
                    jnp.dot(grad_scores, k, preferred_element_type=jnp.float32) * scale,
                    dot0(grad_scores, q) * scale,
                    dot0(probs.astype(jnp.bfloat16), g),
                )
            )
        for out, one, two in zip(outs[-3:], *parts):
            out[...] = jnp.where(lanes < HEAD_DIM, one, two).astype(jnp.bfloat16)

    return pl.pallas_call(
        body,
        grid=(1, HEADS // 2),
        out_shape=[low_shape(micros * length, D)] * 3,
        in_specs=[col, row, wide, wide, wide, wide]
        + [pl.BlockSpec(memory_space=pl.ANY)] * len(before or ()),
        out_specs=[wide] * 3,
        input_output_aliases={6 + i: i for i in range(len(before or ()))},
        compiler_params=pltpu.CompilerParams(vmem_limit_bytes=60 * MIB),
        cost_estimate=LIGHT,
    )(ids.reshape(-1, 1), ids[:, None], queries, key_rows, value_rows, grad_mixed, *(before or ()))


def pack_head_grads(pairs, core, dp_size, copy_size, kernels, others=(), plan=None):
    world = dp_size * copy_size
    count, mids = dp_size // 2, 2 * copy_size
    width = pairs[0][1].shape[1]
    half = width // 2
    sizes = [p[0].shape[1] // world for p in pairs]
    total = sum(sizes)
    if not kernels:
        packs = []
        for c in (1 - core, core):
            parts = []
            for left_side, right_side in pairs:
                part = lax.dynamic_slice_in_dim(right_side, c * half, half, 1)
                part = weight_grad(left_side, part).astype(jnp.bfloat16)
                parts.append(part.reshape(count, mids, -1, half))
            packs.append(jnp.concatenate(parts, axis=2))
        given = [jnp.stack([column_sum(p[1]) for p in pairs]), *others]
        if plan is None:
            return packs + given
        return packs + [jnp.concatenate([given[i][at : at + n] for i, at, n in plan])]

    lefts, which = [], []
    for left_side, _ in pairs:
        seen = [i for i, other in enumerate(lefts) if other is left_side]
        which.append(seen[0] if seen else len(lefts))
        lefts += [] if seen else [left_side]
    rights = [p[1] for p in pairs]
    narrow = [v.shape[1] // count % 128 == 0 for v in lefts]
    held = [i for i, w in enumerate(which) if not narrow[w]]

    where, height = list(range(len(pairs))), len(pairs)
    if plan is not None:
        at_row = 0
        for source, row, n in plan:
            if not source:
                where[row : row + n] = range(at_row, at_row + n)
            at_row += n
        height = at_row

    def body(at, *refs):
        left_refs = refs[: len(lefts)]
        right_refs = refs[len(lefts) : len(lefts) + len(rights)]
        other_refs, refs = refs[len(lefts) + len(rights) :][: len(others)], refs[len(others) :]
        sent, kept, sums = refs[len(lefts) + len(rights) :][:3]
        scratch = refs[len(lefts) + len(rights) + 3 :]
        first = at[0] == 0
        step = pl.program_id(0)

        @pl.when(step == 0)
        def _():
            for i, right in enumerate(right_refs):
                ones = jnp.ones((8, right.shape[0]), jnp.bfloat16)
                row = jnp.dot(ones, right[...], preferred_element_type=jnp.float32)
                sums[where[i] : where[i] + 1] = row[:1]
            at = 0
            for source, row, n in plan or ():
                if source:
                    sums[at : at + n] = other_refs[source - 1][row : row + n]
                at += n
            for i, buffer in zip(held, scratch):
                buffer[...] = dot0(left_refs[which[i]][...], right_refs[i][...])

        at_row = 0
        for i, n in enumerate(sizes):
            if i in held:
                rows = mids * n
                whole = scratch[held.index(i)][pl.ds(pl.multiple_of(step * rows, 8), rows)]
            else:
                whole = dot0(left_refs[which[i]][...], right_refs[i][...])
            left, right = whole[:, :half], whole[:, half:]
            for out, part in (
                (sent, jnp.where(first, right, left)),
                (kept, jnp.where(first, left, right)),
            ):
                out[0, :, at_row : at_row + n] = part.reshape(mids, n, half).astype(jnp.bfloat16)
            at_row += n

    in_specs = [pl.BlockSpec(memory_space=pltpu.SMEM)]
    for v, cut_up in zip(lefts, narrow):
        if cut_up:
            in_specs.append(pl.BlockSpec((v.shape[0], v.shape[1] // count), lambda p: (0, p)))
        else:
            in_specs.append(pl.BlockSpec(v.shape, lambda p: (0, 0)))
    in_specs += [pl.BlockSpec(v.shape, lambda p: (0, 0)) for v in [*rights, *others]]
    out_spec = pl.BlockSpec((1, mids, total, half), lambda p: (p, 0, 0, 0))
    return pl.pallas_call(
        body,
        grid=(count,),
        out_shape=[low_shape(count, mids, total, half)] * 2
        + [jax.ShapeDtypeStruct((height, width), jnp.float32)],
        in_specs=in_specs,
        out_specs=[out_spec] * 2 + [pl.BlockSpec((height, width), lambda p: (0, 0))],
        scratch_shapes=[
            pltpu.VMEM((lefts[which[i]].shape[1], width), jnp.float32) for i in held
        ],
        compiler_params=pltpu.CompilerParams(vmem_limit_bytes=60 * MIB),
        cost_estimate=LIGHT,
    )(jnp.asarray(core, jnp.int32)[None], *lefts, *rights, *others)


def assemble(pieces, scalars, copy_size, rows):
    width = pieces[0][0].shape[-1]
    total = rows

    def body(at, *refs):
        ins, out, sems = refs[: len(pieces)], refs[len(pieces)], refs[len(pieces) + 1]
        copies = []
        for ref, (value, first, flip, vary) in zip(ins, pieces):
            for d in range(2):
                for j in range(copy_size):
                    dp = at[0] ^ (flip | (vary if d else 0))
                    owner = dp * copy_size + lax.rem(at[1] + j, copy_size)
                    copy = pltpu.make_async_copy(
                        ref.at[d, j],
                        out.at[owner, pl.ds(first, value.shape[2])],
                        sems.at[len(copies)],
                    )
                    copy.start()
                    copies.append(copy)
        for copy in copies:
            copy.wait()

    return pl.pallas_call(
        body,
        out_shape=low_shape(8 * copy_size, total, width),
        in_specs=[pl.BlockSpec(memory_space=pltpu.SMEM)]
        + [pl.BlockSpec(memory_space=pl.ANY)] * len(pieces),
        out_specs=pl.BlockSpec(memory_space=pl.ANY),
        scratch_shapes=[pltpu.SemaphoreType.DMA((len(pieces) * 2 * copy_size,))],
        compiler_params=pltpu.CompilerParams(vmem_limit_bytes=4 * MIB),
        cost_estimate=LIGHT,
    )(jnp.stack([jnp.asarray(v, jnp.int32) for v in scalars]), *[p[0] for p in pieces])


def gather(pack, rows, arrived):
    total = pack.shape[0]
    along = [pack, *arrived]
    pieces = []
    for first, last, bits in ((0, rows, (2, 1)), (rows, total, (1, 2))):
        held = jnp.stack([v[first:last] for v in along])
        held = jnp.stack([held, swap_bit(held, 8, bits[0])])
        got = swap_bit(held, 8, bits[1])
        vary = 1 << bits[0]
        other = 1 << bits[1]
        pieces += [(held, first, 0, vary), (got, first, other, vary)]
        pieces += [
            (swap_bit(held, 8, 0), first, 1, vary),
            (swap_bit(got, 8, 0), first, other | 1, vary),
        ]
    return assemble(pieces, (lax.axis_index("dp"), lax.axis_index("copy")), 4, total)


LANES = 128


def padded_lanes(values):
    return jnp.pad(values, ((0, 0), (0, LANES - values.shape[1]))).reshape(-1)


def spread(packed, sizes):
    world = packed.shape[0]
    total = sum(count for count, _ in sizes)

    def body(packed_ref, *outs):
        at = 0
        for (count, k), out in zip(sizes, outs):
            width = world * k
            column = lax.broadcasted_iota(jnp.int32, (LANES, width), 1)
            row = lax.broadcasted_iota(jnp.int32, (LANES, width), 0)
            tile = (row == column % k).astype(jnp.bfloat16)
            owner = lax.broadcasted_iota(jnp.int32, (world, width), 0)
            own = owner == lax.broadcasted_iota(jnp.int32, (world, width), 1) // k
            for i in range(count):
                block = packed_ref[:, (at + i) * LANES : (at + i + 1) * LANES]
                values = jnp.dot(block, tile, preferred_element_type=jnp.float32)
                out[i : i + 1] = jnp.sum(jnp.where(own, values, 0.0), axis=0, keepdims=True)
            at += count

    return pl.pallas_call(
        body,
        out_shape=[
            jax.ShapeDtypeStruct((count, world * k), jnp.float32) for count, k in sizes
        ],
        in_specs=[pl.BlockSpec(memory_space=pltpu.VMEM)],
        out_specs=[pl.BlockSpec(memory_space=pltpu.VMEM)] * len(sizes),
        compiler_params=pltpu.CompilerParams(vmem_limit_bytes=16 * MIB),
        cost_estimate=LIGHT,
    )(packed[:, : total * LANES])


def head_step(weight, head_bias, gain, out_bias, embedded, values):
    bf16, f32 = jnp.bfloat16, jnp.float32
    condition, noisy, noise, slot = values
    out, sums = {}, {}
    valid = (slot >= 0).astype(f32)
    cond = product(condition, weight("cond")) + head_bias(0)
    chosen = jnp.zeros_like(cond)
    for i in range(embedded.shape[0]):
        chosen = jnp.where(slot == i, embedded[i : i + 1], chosen)
    cond = cond + chosen
    gated = jax.nn.silu(cond).astype(bf16)
    out["gated"] = gated
    entry = product(noisy, weight("input")) + head_bias(3)
    norm_head, inv_head = normalize(entry)
    affine = norm_head * gain + head_bias(4)
    shift = product(gated, weight("shift")) + head_bias(7)
    scale = product(gated, weight("scale")) + head_bias(8)
    mlp_in = (affine * (1.0 + scale) + shift).astype(bf16)
    out["mlp_in"] = mlp_in
    inner_one = product(mlp_in, weight("one")) + head_bias(5)
    inner_act = jax.nn.silu(inner_one).astype(bf16)
    out["inner_act"] = inner_act
    inner_two = product(inner_act, weight("two")) + head_bias(6)
    gate = product(gated, weight("gate")) + head_bias(9)
    residual = entry + gate * inner_two
    fshift = product(gated, weight("fshift")) + head_bias(10)
    fscale = product(gated, weight("fscale")) + head_bias(11)
    norm_final, inv_final = normalize(residual)
    final_in = (norm_final * (1.0 + fscale) + fshift).astype(bf16)
    predicted = input_back(final_in, weight("output")) + out_bias
    grad_pred = ((predicted - noise) * valid).astype(bf16)
    sums["output"] = weight_grad(grad_pred, final_in)
    sums["out_bias"] = jnp.sum(grad_pred.astype(f32), axis=0, keepdims=True)
    grad_final_in = product(grad_pred, weight("output"))
    out["fshift"] = grad_final_in.astype(bf16)
    out["fscale"] = (grad_final_in * norm_final).astype(bf16)
    grad_residual = norm_back(grad_final_in * (1.0 + fscale), norm_final, inv_final)
    out["two"] = (grad_residual * gate).astype(bf16)
    grad_one = input_back(out["two"], weight("two")) * silu_slope(inner_one)
    out["one"] = grad_one.astype(bf16)
    grad_mlp_in = input_back(out["one"], weight("one"))
    out["shift"] = grad_mlp_in.astype(bf16)
    out["scale"] = (grad_mlp_in * affine).astype(bf16)
    out["gate"] = (grad_residual * inner_two).astype(bf16)
    grad_gated = input_back(out["shift"], weight("shift"))
    for name in ("scale", "gate", "fshift", "fscale"):
        grad_gated = grad_gated + input_back(out[name], weight(name))
    grad_cond = grad_gated * silu_slope(cond)
    out["cond"] = grad_cond.astype(bf16)
    out["condition"] = input_back(out["cond"], weight("cond")).astype(bf16)
    grad_affine = grad_mlp_in * (1.0 + scale)
    grad_entry = grad_residual + norm_back(grad_affine * gain, norm_head, inv_head)
    grad_entry = grad_entry.astype(bf16)
    sums["input"] = weight_grad(noisy, grad_entry)
    sums["gain"] = jnp.sum(grad_affine * norm_head, axis=0, keepdims=True)
    sums["entry"] = jnp.sum(grad_entry.astype(f32), axis=0, keepdims=True)
    sums["affine"] = jnp.sum(grad_affine, axis=0, keepdims=True)
    lanes = lax.broadcasted_iota(jnp.int32, (slot.shape[0], embedded.shape[0]), 1)
    onehot = (slot == lanes).astype(bf16)
    low_part = (grad_cond - out["cond"].astype(f32)).astype(bf16)
    sums["embedded"] = weight_grad(onehot, out["cond"]) + weight_grad(onehot, low_part)
    return out, sums


SQUARES = ("shift", "scale", "gate", "time2", "one", "two", "fshift", "fscale")
HEAD_OUT = (
    "gated", "mlp_in", "inner_act", "fshift", "fscale", "two", "one", "shift", "scale", "gate",
    "cond", "condition",
)
HEAD_SUMS = (
    ("input", CHANNELS), ("output", CHANNELS), ("embedded", 8), ("gain", 1), ("entry", 1),
    ("affine", 1), ("out_bias", 1),
)


def head_kernel(pack, w_cond, w_input, w_output, head_bias, gain, out_bias, embedded, values, k):
    rows = values[0].shape[0]
    step = 256
    world = pack.shape[0]
    used = [i for i, name in enumerate(SQUARES) if name != "time2"]
    height = sum(n for _, n in HEAD_SUMS)
    height += -height % 8
    smalls = [w_cond, w_input, w_output, head_bias, gain, out_bias, embedded]

    def body(*refs):
        ins = refs[: len(smalls)]
        pack_ref = refs[len(smalls)]
        tiles = refs[len(smalls) + 1 :][:4]
        outs = refs[len(smalls) + 5 :][: len(HEAD_OUT)]
        sums_ref, buffer, sems = refs[len(smalls) + 5 + len(HEAD_OUT) :]
        first = pl.program_id(0) == 0

        def fetch(n):
            return pltpu.make_async_copy(
                pack_ref.at[:, pl.ds(used[n] * k, k)], buffer.at[n], sems.at[n]
            )

        @pl.when(first)
        def _():
            for n in range(len(used)):
                fetch(n).start()

        ready = set()

        def weight(name):
            if name in ("cond", "input", "output"):
                return ins[("cond", "input", "output").index(name)][...]
            n = used.index(SQUARES.index(name))
            if n not in ready:
                ready.add(n)

                @pl.when(first)
                def _():
                    fetch(n).wait()

            return buffer[n].reshape(WIDTH, WIDTH)

        out, sums = head_step(
            weight,
            lambda i: ins[3][i : i + 1],
            ins[4][...],
            ins[5][...],
            ins[6][...],
            [t[...] for t in tiles],
        )
        for name, ref in zip(HEAD_OUT, outs):
            ref[...] = out[name]

        @pl.when(first)
        def _():
            sums_ref[...] = jnp.zeros((height, WIDTH), jnp.float32)

        at = 0
        for name, n in HEAD_SUMS:
            width = sums[name].shape[1]
            sums_ref[at : at + n, :width] += sums[name]
            at += n

    def tall(width):
        return pl.BlockSpec((step, width), lambda i: (i, 0))

    widths = [D if name == "condition" else WIDTH for name in HEAD_OUT]
    *outs, sums = pl.pallas_call(
        body,
        grid=(rows // step,),
        out_shape=[low_shape(rows, w) for w in widths]
        + [jax.ShapeDtypeStruct((height, WIDTH), jnp.float32)],
        in_specs=[
            pl.BlockSpec(v.shape, lambda i: (0, 0), pipeline_mode=pl.Buffered(1)) for v in smalls
        ]
        + [pl.BlockSpec(memory_space=pl.ANY)]
        + [tall(v.shape[1]) for v in values],
        out_specs=[tall(w) for w in widths]
        + [pl.BlockSpec((height, WIDTH), lambda i: (0, 0))],
        scratch_shapes=[
            pltpu.VMEM((len(used), world, k, WIDTH), jnp.bfloat16),
            pltpu.SemaphoreType.DMA((len(used),)),
        ],
        compiler_params=pltpu.CompilerParams(vmem_limit_bytes=60 * MIB),
        cost_estimate=LIGHT,
    )(*smalls, pack, *values)
    return dict(zip(HEAD_OUT, outs)), sums


def pack_block_grads(pairs, core, dp_size):
    count = dp_size // 2
    half = D // 2
    packs = []
    for c in (1 - core, core):
        parts = []
        for left_side, right_side in pairs:
            for at in range(0, right_side.shape[1], D):
                part = lax.dynamic_slice_in_dim(right_side, at + c * half, half, 1)
                part = weight_grad(left_side, part).astype(jnp.bfloat16)
                parts.append(part.reshape(count, 2, -1, half))
        packs.append(jnp.concatenate(parts, axis=2))
    return packs


def put_halves(first, sent, kept, at_row, whole):
    half = D // 2
    count = sent.shape[0]
    n = whole.shape[0] // (2 * count)
    left, right = whole[:, :half], whole[:, half:]
    for out, part in (
        (sent, jnp.where(first, right, left)),
        (kept, jnp.where(first, left, right)),
    ):
        part = part.reshape(count, 2, n, half).astype(jnp.bfloat16)
        out[:, :, at_row : at_row + n] = part


def feed_forward(second_in, middle, ups, up_bias, w_down, down_bias, place, copy_size, kernels):
    bf16, f32 = jnp.bfloat16, jnp.float32
    rows = middle.shape[0]
    steps = len(ups)

    def step_of(hidden):
        half = 0.5 * (1.0 + lax.erf(hidden * 2.0 ** (-0.5)))
        bell = jnp.exp(-0.5 * hidden * hidden) * (2.0 * math.pi) ** (-0.5)
        return (hidden * half).astype(bf16), (half + hidden * bell).astype(bf16)

    if not kernels:
        hidden = product(second_in, jnp.concatenate(ups, axis=1)) + up_bias
        active, slope = step_of(hidden)
        output = middle + product(active, w_down) + down_bias
        return output.astype(bf16), slope, None, active

    per = w_down.shape[0] // steps
    k = per // (2 * copy_size)
    width = per // copy_size

    def body(at, *refs):
        up_refs, refs = refs[:steps], refs[steps:]
        in_ref, middle_ref, bias_ref, down_ref, down_bias_ref = refs[:5]
        out_ref, slope_ref, chosen_ref, total, hidden = refs[5:]
        step = pl.program_id(0)
        for n in range(steps):

            @pl.when(step == n)
            def _():
                hidden[...] = product(in_ref[...], up_refs[n][...])

        active, slope = step_of(hidden[...] + bias_ref[...])
        slope_ref[...] = slope
        part = product(active, down_ref[...])
        source = lax.broadcasted_iota(jnp.int32, (per, width), 0)
        target = lax.broadcasted_iota(jnp.int32, (per, width), 1)
        wanted = (target // k * copy_size + at[0]) * k + target % k
        one_hot = (source == wanted).astype(bf16)
        chosen_ref[0] = product(active, one_hot).astype(bf16)

        @pl.when(step == 0)
        def _():
            total[...] = middle_ref[...] + down_bias_ref[...] + part

        @pl.when(step > 0)
        def _():
            total[...] += part

        @pl.when(step == steps - 1)
        def _():
            out_ref[...] = total[...].astype(bf16)

    def full(v):
        return pl.BlockSpec(v.shape, lambda j: (0,) * len(v.shape), pipeline_mode=pl.Buffered(1))

    out, slope, chosen = pl.pallas_call(
        body,
        grid=(steps,),
        out_shape=[low_shape(rows, D), low_shape(rows, per * steps), low_shape(steps, rows, width)],
        in_specs=[pl.BlockSpec(memory_space=pltpu.SMEM)]
        + [full(v) for v in (*ups, second_in, middle)]
        + [
            pl.BlockSpec((1, per), lambda j: (0, j)),
            pl.BlockSpec((per, D), lambda j: (j, 0)),
            full(down_bias),
        ],
        out_specs=[
            pl.BlockSpec((rows, D), lambda j: (0, 0)),
            pl.BlockSpec((rows, per), lambda j: (0, j)),
            pl.BlockSpec((1, rows, width), lambda j: (j, 0, 0)),
        ],
        scratch_shapes=[pltpu.VMEM((rows, D), f32), pltpu.VMEM((rows, per), f32)],
        compiler_params=pltpu.CompilerParams(vmem_limit_bytes=48 * MIB),
        cost_estimate=LIGHT,
    )(place[None], *ups, second_in, middle, up_bias, w_down, down_bias)
    return out, slope, chosen, None


def block_back_one(pieces, slope, ups, w_down, w_proj, lefts, norm, inverse, gain, core, dp_size, kernels):
    bf16, f32 = jnp.bfloat16, jnp.float32
    micros, own, _ = pieces[0].shape
    rows = micros * own * len(pieces)
    steps = len(ups)
    k = lefts[0].shape[1] // dp_size
    k_down = w_down.shape[0] // (dp_size * len(pieces))
    if not kernels:
        grad = jnp.stack(pieces, axis=1).reshape(rows, D)
        hidden = (input_back(grad, w_down) * slope.astype(f32)).astype(bf16)
        second = input_back(hidden, jnp.concatenate(ups, axis=1))
        middle = grad.astype(f32) + norm_back(second * gain, norm, inverse)
        low = middle.astype(bf16)
        sums = [jnp.sum(second * norm, axis=0), jnp.sum(second, axis=0)]
        sums = jnp.stack(sums + [column_sum(low), column_sum(grad)])
        packs = pack_block_grads([(lefts[0], hidden), (lefts[1], grad)], core, dp_size)
        mixed = input_back(low, w_proj).astype(bf16)
        return *packs, middle, low, mixed, sums, column_sum(hidden).reshape(steps, 1, D)

    def body(at, *refs):
        piece_refs, refs = refs[: len(pieces)], refs[len(pieces) :]
        up_refs, refs = refs[:steps], refs[steps:]
        slope_ref, down_ref, proj_ref, left_up, left_down, norm_ref, inv_ref, gain_ref = refs[:8]
        sent, kept, middle_ref, low_ref, mixed_ref, sums_ref, hidden_sums, grad, total = refs[8:]
        step = pl.program_id(0)
        first = at[0] == 0

        @pl.when(step == 0)
        def _():
            for m in range(micros):
                for n, ref in enumerate(piece_refs):
                    start = (m * len(pieces) + n) * own
                    grad[start : start + own] = ref[m]
            for n in range(steps):
                here = pl.ds(n * dp_size // (2 * steps), dp_size // (2 * steps))
                part = dot0(left_down[n], grad[...])
                put_halves(first, sent.at[here], kept.at[here], steps * k, part)
            total[...] = jnp.zeros_like(total)

        hidden = dot1(grad[...], down_ref[...]) * slope_ref[...].astype(f32)
        hidden = hidden.astype(bf16)
        ones = jnp.ones((8, rows), bf16)
        hidden_sums[0] = jnp.dot(ones, hidden, preferred_element_type=f32)
        up_grad = dot0(left_up[...], hidden)
        for n in range(steps):

            @pl.when(step == n)
            def _():
                total[...] += dot1(hidden, up_refs[n][...])
                put_halves(first, sent, kept, n * k, up_grad)

        @pl.when(step == steps - 1)
        def _():
            second, norm_now = total[...], norm_ref[...]
            given = grad[...].astype(f32)
            middle = given + norm_back(second * gain_ref[...], norm_now, inv_ref[...])
            low = middle.astype(bf16)
            middle_ref[...] = middle
            low_ref[...] = low
            mixed_ref[...] = dot1(low, proj_ref[...]).astype(bf16)
            for n, values in enumerate((second * norm_now, second, low.astype(f32), given)):
                sums_ref[n : n + 1] = jnp.sum(values, axis=0, keepdims=True)

    def full(v):
        return pl.BlockSpec(v.shape, lambda j: (0,) * len(v.shape), pipeline_mode=pl.Buffered(1))

    pack = low_shape(dp_size // 2, 2, steps * k + k_down, D // 2)
    tall = jax.ShapeDtypeStruct((rows, D), f32)
    outs = [pack, pack, tall, low_shape(rows, D), low_shape(rows, D)]
    outs += [jax.ShapeDtypeStruct((8, D), f32)]
    ins = [*pieces, *ups, slope, w_down, w_proj, *lefts, norm, inverse, gain]
    in_specs = [full(v) for v in ins]
    in_specs[len(pieces) + steps] = pl.BlockSpec((rows, D), lambda j: (0, j))
    in_specs[len(pieces) + steps + 1] = pl.BlockSpec((D, D), lambda j: (j, 0))
    return pl.pallas_call(
        body,
        grid=(steps,),
        out_shape=outs + [jax.ShapeDtypeStruct((steps, 8, D), f32)],
        in_specs=[pl.BlockSpec(memory_space=pltpu.SMEM)] + in_specs,
        out_specs=[pl.BlockSpec(v.shape, lambda j, n=len(v.shape): (0,) * n) for v in outs]
        + [pl.BlockSpec((1, 8, D), lambda j: (j, 0, 0))],
        scratch_shapes=[pltpu.VMEM((rows, D), bf16), pltpu.VMEM((rows, D), f32)],
        compiler_params=pltpu.CompilerParams(vmem_limit_bytes=60 * MIB),
        cost_estimate=LIGHT,
    )(jnp.asarray(core, jnp.int32)[None], *ins)


def block_back_two(grads, weights, lefts, low, middle, norm, inverse, gain, sums, hidden_sums, own, micros, core, dp_size, kernels):
    f32 = jnp.float32
    rows = low.shape[0]
    length = rows // micros
    steps = hidden_sums.shape[0]

    def smalls(first, norm_now, q, v):
        return [
            jnp.sum(first * norm_now, axis=0, keepdims=True),
            None,
            jnp.sum(first, axis=0, keepdims=True),
            jnp.sum(q.astype(f32), axis=0, keepdims=True),
            jnp.sum(v.astype(f32), axis=0, keepdims=True),
        ]

    if not kernels:
        first = sum(input_back(g, w) for g, w in zip(grads, weights))
        input_grad = middle + norm_back(first * gain, norm, inverse)
        input_grad = input_grad.reshape(micros, length, D)[:, :own]
        rows_of = smalls(first, norm, grads[0], grads[2])
        rows_of[1] = sums[:1]
        small = jnp.concatenate([*rows_of, sums[2:3], sums[1:2], sums[3:4], hidden_sums[:, 0]])
        pairs = [(lefts[0], g) for g in grads] + [(lefts[1], low)]
        return *pack_block_grads(pairs, core, dp_size), input_grad, small

    k = lefts[0].shape[1] // dp_size

    def body(at, *refs):
        grad_refs, weight_refs, refs = refs[:3], refs[3:6], refs[6:]
        left_in, left_mixed, low_ref, middle_ref, norm_ref, inv_ref, gain_ref = refs[:7]
        sums_ref, hidden_ref, sent, kept, out_ref, small_ref = refs[7:]
        flag = at[0] == 0
        for n, ref in enumerate(grad_refs):
            put_halves(flag, sent, kept, n * k, dot0(left_in[...], ref[...]))
        put_halves(flag, sent, kept, 3 * k, dot0(left_mixed[...], low_ref[...]))
        first = dot1(grad_refs[0][...], weight_refs[0][...])
        for g, w in zip(grad_refs[1:], weight_refs[1:]):
            first = first + dot1(g[...], w[...])
        for n, value in enumerate(
            smalls(first, norm_ref[...], grad_refs[0][...], grad_refs[2][...])
        ):
            if value is not None:
                small_ref[n : n + 1] = value
        small_ref[1:2] = sums_ref[0:1]
        small_ref[5:6] = sums_ref[2:3]
        small_ref[6:7] = sums_ref[1:2]
        small_ref[7:8] = sums_ref[3:4]
        for n in range(steps):
            small_ref[8 + n : 9 + n] = hidden_ref[n, 0:1]
        for m in range(micros):
            here = pl.ds(m * length, own)
            back = norm_back(
                first[m * length : m * length + own] * gain_ref[...], norm_ref[here], inv_ref[here]
            )
            out_ref[m] = middle_ref[here] + back

    pack = low_shape(dp_size // 2, 2, 4 * k, D // 2)
    outs = [pack, pack, jax.ShapeDtypeStruct((micros, own, D), f32)]
    outs += [jax.ShapeDtypeStruct((8 + steps, D), f32)]
    ins = [*grads, *weights, *lefts, low, middle, norm, inverse, gain, sums, hidden_sums]
    return small_call(body, outs, [core], ins)


def shards(
    block_input,
    image_ids,
    latents,
    noise,
    timesteps,
    norm_gains,
    block_biases,
    w_qkv,
    w_proj,
    w_up,
    up_bias,
    w_down,
    head_gain,
    head_biases,
    w_cond,
    w_time1,
    w_time2,
    w_input,
    w_ada,
    w_mlp1,
    w_mlp2,
    w_final,
    w_output,
    output_bias,
):
    bf16, f32 = jnp.bfloat16, jnp.float32
    dp_size, copy_size = lax.axis_size("dp"), lax.axis_size("copy")
    world = dp_size * copy_size
    place = lax.axis_index("copy")
    micros, _, own, _ = block_input.shape
    length = image_ids.shape[2]
    total = micros * length
    k_d, k_ff, k_w, k_t = D // world, w_down.shape[0], WIDTH // world, w_time1.shape[0]
    ff = k_ff * world
    kernels = k_d % 8 == 0 and k_w % 16 == 0 and k_t % 8 == 0
    score_scale = HEAD_DIM ** (-0.5)

    def cut(matrix, width):
        return [matrix[:, i : i + width] for i in range(0, matrix.shape[1], width)]

    def pad_flat(parts, width):
        flat = jnp.concatenate([padded_lanes(p) for p in parts])
        count = -(-flat.shape[0] // (16 * width)) * 16 * width
        return jnp.pad(flat, (0, count - flat.shape[0])).reshape(-1, width)

    groups = [
        (cut(w_qkv, D) + [w_proj, pad_flat([norm_gains, block_biases, up_bias[None]], D)], 2),
        (cut(w_up, D) + [w_down], 4),
        (
            cut(w_ada, WIDTH)
            + [w_time2, w_mlp1, w_mlp2]
            + cut(w_final, WIDTH)
            + [w_cond, w_time1]
            + [pad_flat([w_input, w_output.T, head_gain[None], head_biases], WIDTH)],
            0,
        ),
    ]

    def everyone(pack):
        return [shift_copy(pack, copy_size, copy_size - j) for j in range(1, copy_size)]

    def unpack(pack, parts):
        out, at = [], 0
        for part in parts:
            out.append(pack[:, at : at + part.shape[0]].reshape(-1, pack.shape[2]))
            at += part.shape[0]
        return out

    own_rows = block_input[:, 0]
    packs = [jnp.concatenate(parts, 0) for parts, _ in groups]
    if kernels and dp_size == 8 and copy_size == 4:
        head_own = packs[2]
        arrived = [everyone(packs[0])]
        *arrived[0], packs[1] = tie(*arrived[0], packs[1])
        arrived.append(everyone(packs[1]))
        *arrived[1], own_rows, head_own = tie(*arrived[1], own_rows, head_own)
        rows_arrived = everyone(own_rows)
        full = [
            gather(pack, sum(p.shape[0] for p in parts[:n]), got)
            for pack, (parts, n), got in zip(packs[:2], groups[:2], arrived[:2])
        ]
        head = lax.all_gather(head_own, ("dp", "copy"), axis=0)
        full.append(head)
    else:
        rows_arrived = everyone(own_rows)
        full = [lax.all_gather(pack, ("dp", "copy"), axis=0) for pack in packs]
    head_pack = full[2]
    full = [unpack(pack, parts) for pack, (parts, _) in zip(full, groups)]

    rows = jnp.stack([own_rows, *rows_arrived], axis=1).reshape(total, D).astype(f32)

    def turned(values):
        twice = jnp.concatenate([values, values], axis=1)
        return lax.dynamic_slice_in_dim(twice, place * own, length, 1)

    ids = turned(image_ids[:, 0])
    latent_rows = turned(latents[:, 0]).reshape(total, CHANNELS)
    noise_rows = turned(noise[:, 0, 0]).reshape(total, CHANNELS)

    w_q, w_k, w_v, w_proj_full, small = full[0]
    w_down_full = full[1][4]
    small = small.reshape(world, -1)
    gains, biases, up_bias_full = spread(small, [(2, k_d), (6, k_d), (1, k_ff)])

    norm_one, inv_one = normalize(rows)
    first_in = (norm_one * gains[0] + biases[0]).astype(bf16)
    queries = (product(first_in, w_q) + biases[1]).astype(bf16)
    key_rows = product(first_in, w_k).astype(bf16)
    value_rows = (product(first_in, w_v) + biases[2]).astype(bf16)
    mixed = attention(queries, key_rows, value_rows, ids)
    middle = rows + product(mixed, w_proj_full) + biases[3]
    norm_two, inv_two = normalize(middle)
    second_in = (norm_two * gains[1] + biases[4]).astype(bf16)
    condition, slope, active_z, active = feed_forward(
        second_in,
        middle,
        full[1][:4],
        up_bias_full,
        w_down_full,
        biases[5:6],
        place,
        copy_size,
        kernels,
    )

    def chosen(values):
        width = values.shape[1]
        k = width // world
        source = jnp.arange(width, dtype=jnp.int32)[:, None]
        target = jnp.arange(dp_size * k, dtype=jnp.int32)[None, :]
        wanted = (target // k * copy_size + place) * k + target % k
        return product(values, (source == wanted).astype(bf16)).astype(bf16)

    condition, first_z, mixed_z, second_z, active_z, slope, norm_one, inv_one, norm_two, inv_two = tie(
        condition,
        chosen(first_in),
        chosen(mixed),
        chosen(second_in),
        chosen(active) if active_z is None else active_z,
        slope,
        norm_one,
        inv_one,
        norm_two,
        inv_two,
    )
    core = lax.axis_index("dp") & 1

    def split_pack(pack, parts):
        out, at = [], 0
        for rows_of in parts:
            out.append(pack[at : at + rows_of])
            at += rows_of
        return out

    def after(first, *values):
        first = list(first)
        return list(tie(*first, *values)[len(first) :])

    def send_after(reduction, first):
        reduction.sent = after(first, *reduction.sent)
        return reduction.receive()

    def form_after(reduction, first):
        reduction.got = after(first, *reduction.got)
        reduction.advance()
        return [*reduction.sent, *reduction.kept]

    def to_copies(reduction, first):
        reduction.got = after(first, *reduction.got)
        chunks = cut_copies(reduction.kept, reduction.got, place, copy_size, kernels)
        arriving = [shift_copy(chunks[j], copy_size, j) for j in range(1, copy_size)]
        return [chunks[0], *arriving]

    def whole(other, mine):
        got = swap_bit(other, dp_size, 0)
        left = jnp.where(core == 0, mine, got)
        right = jnp.where(core == 0, got, mine)
        return jnp.concatenate([left, right], axis=1).astype(f32)

    def finish(reduction):
        while reduction.left:
            reduction.advance().receive()
        parts = [
            jnp.concatenate([v[0] for v in values], axis=1)
            for values in (reduction.kept, reduction.got)
        ]
        return whole(*own_and_other(parts, (0, core), kernels))

    squares = dict(zip(SQUARES, full[2][:8]))
    w_cond_full, w_time1_full, small = full[2][8:]
    w_time2_full = squares["time2"]
    small = small.reshape(world, -1)
    w_input_full, w_output_t, head_gain_f, head_bias = spread(
        small, [(CHANNELS, k_w), (CHANNELS, k_w), (1, k_w), (12, k_w)]
    )
    w_input_full, w_output_t = w_input_full.astype(bf16), w_output_t.astype(bf16)

    row_slot = ids + IMAGES * jnp.arange(micros, dtype=jnp.int32)[:, None]
    row_slot = jnp.where(ids >= 0, row_slot, -1).reshape(total, 1)
    step_vals = timesteps[:, 0, 0].reshape(micros * IMAGES).astype(f32)
    sinusoid_in = sinusoid(step_vals).astype(bf16)
    time_one = product(sinusoid_in, w_time1_full) + head_bias[1]
    time_act = jax.nn.silu(time_one).astype(bf16)
    embedded = product(time_act, w_time2_full) + head_bias[2]
    factors = plan(step_vals)
    slots = jnp.arange(micros * IMAGES, dtype=jnp.int32)[None, :]
    mixing = [
        jnp.sum(jnp.where(row_slot == slots, factors[None, :, i], 0.0), axis=1, keepdims=True)
        for i in range(2)
    ]
    noisy = (latent_rows * mixing[0] + noise_rows * mixing[1]).astype(bf16)
    values = (condition, noisy, noise_rows, row_slot)
    out_bias = output_bias.astype(f32)[None]
    if kernels:
        out, sums = head_kernel(
            head_pack,
            w_cond_full,
            w_input_full,
            w_output_t,
            head_bias,
            head_gain_f,
            out_bias,
            embedded,
            values,
            k_w,
        )
    else:
        others = {"cond": w_cond_full, "input": w_input_full, "output": w_output_t, **squares}
        out, sums = head_step(
            others.get,
            lambda i: head_bias[i : i + 1],
            head_gain_f,
            out_bias,
            embedded,
            values,
        )
        sums = [jnp.pad(sums[n], ((0, 0), (0, WIDTH - sums[n].shape[1]))) for n, _ in HEAD_SUMS]
        sums = jnp.concatenate(sums)
        sums = jnp.pad(sums, ((0, -sums.shape[0] % 8), (0, 0)))
    chunks = out["condition"].reshape(micros, copy_size, own, D)
    chunks = [chunks[:, j] for j in range(copy_size)]
    at_embedded = 2 * CHANNELS
    grad_embedded = sums[at_embedded : at_embedded + micros * IMAGES].astype(bf16)
    grad_time_one = (input_back(grad_embedded, w_time2_full) * silu_slope(time_one)).astype(bf16)
    arriving = [shift_copy(chunks[j], copy_size, j) for j in range(1, copy_size)]
    (gated,) = after(chunks, out["gated"])
    send, keep, sums_one = pack_head_grads(
        [
            (gated, out["fshift"]),
            (gated, out["fscale"]),
            (out["inner_act"], out["two"]),
            (out["mlp_in"], out["one"]),
        ],
        core,
        dp_size,
        copy_size,
        kernels,
    )
    pack_one = Reduction([send], [keep], 2 * k_w, dp_size, kernels)
    arriving = after([keep], *arriving)
    grad_z_own = sum_low([chunks[0], *arriving], kernels)
    arriving = [shift_copy(grad_z_own, copy_size, copy_size - j) for j in range(1, copy_size)]
    send_after(pack_one, [grad_z_own])
    (gated,) = after([grad_z_own], gated)
    of_head = 2 * CHANNELS + 8
    send, keep, small_grads = pack_head_grads(
        [
            (gated, out["shift"]),
            (gated, out["scale"]),
            (gated, out["gate"]),
            (time_act, grad_embedded),
            (condition, out["cond"]),
            (sinusoid_in, grad_time_one),
        ],
        core,
        dp_size,
        copy_size,
        kernels,
        (sums_one, sums),
        (
            (2, 0, 2 * CHANNELS),
            (2, of_head, 1),
            (0, 4, 2),
            (0, 3, 1),
            (2, of_head + 1, 2),
            (1, 3, 1),
            (1, 2, 1),
            (0, 0, 3),
            (1, 0, 2),
            (2, of_head + 3, 1),
            (2, of_head + 4, 2),
        ),
    )
    pack_two = Reduction([send], [keep], 3 * k_w, dp_size, kernels)
    formed = form_after(pack_one, [keep])
    arriving = after(formed, *arriving)
    send_after(pack_one, arriving)
    send_after(pack_two, arriving)

    def swap_copies(values, shift, first):
        return values + after(first, swap_copy(values, copy_size, shift))[0]

    send, keep, grad_middle, grad_branch, grad_mixed, block_sums, hidden_sums = block_back_one(
        [grad_z_own, *arriving],
        slope,
        full[1][:4],
        w_down_full,
        w_proj_full,
        (second_z, active_z),
        norm_two,
        inv_two,
        gains[1:2],
        core,
        dp_size,
        kernels,
    )
    sent, kept = [send], [keep]
    small_grads = swap_copies(small_grads, 1, [grad_mixed])
    formed = form_after(pack_two, [small_grads])
    send_after(pack_two, formed)
    formed = form_after(pack_one, formed)
    send_after(pack_one, formed)
    (grad_mixed,) = after(formed, grad_mixed)
    back = None
    for m in range(micros):
        back = attention_back(queries, key_rows, value_rows, grad_mixed, ids, m, back)
    small_grads = swap_copies(small_grads, 2, back)
    formed = form_after(pack_two, [small_grads])
    send_after(pack_two, formed)
    one_parts = to_copies(pack_one, formed)
    back = after([one_parts[0]], *back)
    send, keep, input_grad, block_small = block_back_two(
        back,
        (w_q, w_k, w_v),
        (first_z, mixed_z),
        grad_branch,
        grad_middle,
        norm_one,
        inv_one,
        gains[:1],
        block_sums,
        hidden_sums,
        own,
        micros,
        core,
        dp_size,
        kernels,
    )
    one_parts = after([keep], *one_parts)
    own_one_parts = own_and_other(one_parts, (place, core), kernels)
    sent, kept = sent + [send], kept + [keep]
    pack_three = Reduction(sent, kept, 6 * k_d, dp_size, kernels)
    send_after(pack_three, own_one_parts)
    head_rows = small_grads.shape[0]
    block_small = jnp.pad(block_small, ((0, -block_small.shape[0] % 8), (0, WIDTH - D)))
    small_grads = jnp.concatenate([small_grads, block_small], axis=0)
    everywhere = lax.all_gather(small_grads, "dp", axis=0)
    small_grads = everywhere[0]
    for n in range(1, dp_size):
        small_grads = small_grads + everywhere[n]
    block_small = small_grads[head_rows:, :D]
    formed = form_after(pack_three, own_one_parts)
    send_after(pack_three, formed)
    two_parts = to_copies(pack_two, formed)
    while pack_three.left:
        formed = form_after(pack_three, [two_parts[0]])
        send_after(pack_three, formed)
    two_parts = after(formed, *two_parts)
    own_two_parts = own_and_other(two_parts, (place, core), kernels)
    own_all = finish(pack_three)
    own_up = jnp.concatenate(split_pack(own_all, [k_d] * 4), axis=1)
    own_down = own_all[4 * k_d : 4 * k_d + k_ff]
    own_four = own_all[4 * k_d + k_ff :]
    own_q, own_k, own_v, own_proj = split_pack(own_four, [k_d] * 4)
    own_fshift, own_fscale, own_two, own_one = split_pack(
        whole(*own_one_parts), [k_w] * 4
    )
    own_shift, own_scale, own_gate, own_time2, own_cond, own_time1 = split_pack(
        whole(*own_two_parts), [k_w] * 4 + [k_d, k_t]
    )
    me = lax.axis_index("dp") * copy_size + place
    own_rest = lax.dynamic_slice_in_dim(block_small[:8], me * k_d, k_d, 1)
    own_gains, own_biases = own_rest[:2], own_rest[2:]
    own_up_bias = lax.dynamic_slice_in_dim(block_small[8 : 8 + ff // D].reshape(ff), me * k_ff, k_ff)
    own_small = lax.dynamic_slice_in_dim(small_grads, me * k_w, k_w, 1)
    own_w_input = own_small[:CHANNELS]
    own_w_output = own_small[CHANNELS : 2 * CHANNELS].T
    own_head_gain = own_small[2 * CHANNELS]
    own_head_biases = own_small[2 * CHANNELS + 1 : 2 * CHANNELS + 13]
    grad_out_bias = small_grads[2 * CHANNELS + 13, :CHANNELS]

    input_grad = input_grad.reshape(micros, 1, own, D)
    block_output = condition.reshape(micros, length, D)[:, :own].reshape(micros, 1, own, D)
    return (
        block_output,
        input_grad,
        own_gains,
        own_biases,
        jnp.concatenate([own_q, own_k, own_v], axis=1),
        own_proj,
        own_up,
        own_up_bias,
        own_down,
        own_head_gain,
        own_head_biases,
        own_cond,
        own_time1,
        own_time2,
        own_w_input,
        jnp.concatenate([own_shift, own_scale, own_gate], axis=1),
        own_one,
        own_two,
        jnp.concatenate([own_fshift, own_fscale], axis=1),
        own_w_output,
        grad_out_bias,
    )


def solution(mesh):
    in_specs = (
        P(None, "dp", "copy", None),
        P(None, "dp", None),
        P(None, "dp", None, None),
        P(None, "copy", "dp", None, None),
        P(None, "copy", "dp", None),
        P(None, ("dp", "copy")),
        P(None, ("dp", "copy")),
        P(("dp", "copy"), None),
        P(("dp", "copy"), None),
        P(("dp", "copy"), None),
        P(("dp", "copy")),
        P(("dp", "copy"), None),
        P(("dp", "copy")),
        P(None, ("dp", "copy")),
        P(("dp", "copy"), None),
        P(("dp", "copy"), None),
        P(("dp", "copy"), None),
        P(None, ("dp", "copy")),
        P(("dp", "copy"), None),
        P(("dp", "copy"), None),
        P(("dp", "copy"), None),
        P(("dp", "copy"), None),
        P(("dp", "copy"), None),
        P(),
    )
    out_specs = (
        P(None, "dp", "copy", None),
        P(None, "dp", "copy", None),
        P(None, ("dp", "copy")),
        P(None, ("dp", "copy")),
        P(("dp", "copy"), None),
        P(("dp", "copy"), None),
        P(("dp", "copy"), None),
        P(("dp", "copy")),
        P(("dp", "copy"), None),
        P(("dp", "copy")),
        P(None, ("dp", "copy")),
        P(("dp", "copy"), None),
        P(("dp", "copy"), None),
        P(("dp", "copy"), None),
        P(None, ("dp", "copy")),
        P(("dp", "copy"), None),
        P(("dp", "copy"), None),
        P(("dp", "copy"), None),
        P(("dp", "copy"), None),
        P(("dp", "copy"), None),
        P(),
    )
    return jax.shard_map(shards, mesh=mesh, in_specs=in_specs, out_specs=out_specs, check_vma=False)
```

time: 603 us -> 546 us (0.905)
  Pallas kernels: 120 us -> 231 us
  matrix products: 116 us -> 12.8 us
  local copies, waits for them, and re-layouts: 93.4 us -> 47.4 us
  waiting for transfers between devices: 112 us -> 148 us
  starting transfers between devices: 79.4 us -> 52.8 us
  other arithmetic: 55.6 us -> 31.4 us
    pallas_call x4 -> x7, Pallas kernels: 38.4 us -> 114 us  [the longest x1 44.9 us: head_kernel(): pl.pallas_call(body, grid=(rows // step,), out_shape=[low_shape(rows, w)...]
    dot_general x22 -> x9, matrix products: 67.4 us -> 10.8 us  [product(): return jnp.dot(left_side, right_side, preferred_element_type=jnp.float32)]
    dot_general x14 -> x1, matrix products: 41.8 us -> 2.02 us  [input_back(): lax.dot_general(gradient, weight, (((1,), (1,)), ((), ())), preferred_ele...]
    unnamed x398 -> x150, local copies, waits for them, and re-layouts: 44.2 us -> 19 us
    pallas_call x16 -> x13, Pallas kernels: 32.5 us -> 52.3 us  [small_call(): pl.pallas_call(body, out_shape=outs, in_specs=[pl.BlockSpec(memory_space=...]
    ppermute x21, waiting for transfers between devices: 71.8 us -> 89.2 us  [shift_copy(): lax.ppermute(values, 'copy', [(i, (i + shift) % size) for i in range(size)])]
    ppermute x46 -> x35, starting transfers between devices: 43.1 us -> 27.4 us  [swap_bit(): return lax.ppermute(values, 'dp', [(i, i ^ 1 << bit) for i in range(size)])]
    all_gather x1, waiting for transfers between devices: 8.6 us -> 20.6 us  [shards(): head = lax.all_gather(head_own, ('dp', 'copy'), axis=0)]
  transfers between devices with their start and end apart: 70 -> 60, of which waited for: 22 -> 25; matrix products, arithmetic and copies ran while one was open for 29% -> 11% of each run, Pallas kernels for 17% -> 33%
where the time goes in v3:
time: 546 us; the launch traced here: 540 us
  Pallas kernels  231 us (42%)
  waiting for transfers between devices  148 us (27%)
  starting transfers between devices  52.8 us (10%)
  local copies, waits for them, and re-layouts  47.4 us (9%)
  other arithmetic  31.4 us (6%)
  between operations  15.8 us (3%)
  matrix products  12.8 us (2%)
    ppermute x21, waiting for transfers between devices, shift_copy(): lax.ppermute(values, 'copy', [(i, (i + shift) % size) for i in range(size)])  89.2 us
    pallas_call x13, Pallas kernels, small_call(): pl.pallas_call(body, out_shape=outs, in_specs=[pl.BlockSpec(memory_space=...  52.3 us
    pallas_call x1, Pallas kernels, head_kernel(): pl.pallas_call(body, grid=(rows // step,), out_shape=[low_shape(rows, w)...  44.9 us
    ppermute x35, waiting for transfers between devices, swap_bit(): return lax.ppermute(values, 'dp', [(i, i ^ 1 << bit) for i in range(size)])  38.6 us
    pallas_call x2, Pallas kernels, pack_head_grads(): pl.pallas_call(body, grid=(count,), out_shape=[low_shape(count, mids, tot...  27.5 us
    ppermute x35, starting transfers between devices, swap_bit(): return lax.ppermute(values, 'dp', [(i, i ^ 1 << bit) for i in range(size)])  27.4 us
    pallas_call x2, Pallas kernels, attention_back(): pl.pallas_call(body, grid=(1, HEADS // 2), out_shape=[low_shape(micros *...  25 us
    pallas_call x1, Pallas kernels, block_back_one(): pl.pallas_call(body, grid=(steps,), out_shape=outs + [jax.ShapeDtypeStruc...  23.9 us
  transfers between devices with their start and end apart: 60, of which 25 were waited for; matrix products, arithmetic and copies ran while one was open for 11% of the time, Pallas kernels for 33%

profile of v3, /device:TPU:9, one launch (start us, length us, event | category | flops | bytes accessed | tf_op | source)
XLA Modules:
  0.0 539.6 jit_solution(2434494237904062508)
XLA Ops:
  12.7 2.5 collective-permute-start.1
  15.2 2.2 collective-permute-start.2
  26.2 3.4 collective-permute-done.2
  30.9 2.1 collective-permute-start.4
  33.0 4.8 collective-permute-done.3
  37.8 12.2 %collective-permute-done.4 = bf16[192,768]{1,0:T(8,128)(2,1)S(1)} collective-permute-done((bf16[192,768]{1,0:T(8,128)(2,1)S(1)}, bf16[192,768]{1,0:T(8,128)(2,1)S(1)}, u32[]{:S(2)}, u32[]{:S(2)}) %collective-permute-start.4) | collective-permute-done | bytes 294944 | tf_op jit(solution)/shard_map/ppermute | solution.py:94
  50.0 6.3 %collective-permute-done.5 = bf16[192,768]{1,0:T(8,128)(2,1)S(1)} collective-permute-done((bf16[192,768]{1,0:T(8,128)(2,1)S(1)}, bf16[192,768]{1,0:T(8,128)(2,1)S(1)}, u32[]{:S(2)}, u32[]{:S(2)}) %collective-permute-start.5) | collective-permute-done | bytes 294944 | tf_op jit(solution)/shard_map/ppermute | solution.py:94
  64.8 1.8 collective-permute-start.15
  66.5 2.0 collective-permute-done.17
  70.0 4.5 collective-permute-done.21
  76.9 2.1 collective-permute-start.10
  79.0 17.7 %collective-permute-done.15 = bf16[2,96,768]{2,1,0:T(8,128)(2,1)S(1)} collective-permute-done((bf16[2,96,768]{2,1,0:T(8,128)(2,1)S(1)}, bf16[2,96,768]{2,1,0:T(8,128)(2,1)S(1)}, u32[]{:S(2)}, u32[]{:S(2)}) %collective-permute-start.15) | collective-permute-done | bytes 294944 | tf_op jit(solution)/shard_map/ppermute | solution.py:94
  96.9 6.6 %collective-permute-done.16 = bf16[2,96,768]{2,1,0:T(8,128)(2,1)S(1)} collective-permute-done((bf16[2,96,768]{2,1,0:T(8,128)(2,1)S(1)}, bf16[2,96,768]{2,1,0:T(8,128)(2,1)S(1)}, u32[]{:S(2)}, u32[]{:S(2)}) %collective-permute-start.16) | collective-permute-done | bytes 294944 | tf_op jit(solution)/shard_map/ppermute | solution.py:94
  105.3 1.7 fusion.2
  108.0 1.7 fusion.7.refs_10_
  109.7 1.7 pad_maximum_fusion.1.refs_4_
  111.4 1.7 collective-permute-done.6
  114.3 4.4 collective-permute-start.12
  118.9 8.4 %shard_map.392 = bf16[32,112,768]{2,1,0:T(8,128)(2,1)S(1)} custom-call(s32[2]{0:T(128)S(1)} %pad_add_fusion.at, bf16[2,4,48,768]{3,2,1,0:T(8,128)(2,1)S(1)} %pad_maximum_fusion.6.refs_0_, bf16[2,4,48,768]{3,2,1,0:T(8,128)(2,1)} %collective-permute-done.18.refs_1_, bf16[2,4,48,768]{3,2,1,0:T(8,128)(2,1)S(1)} %collective-permute-done.19.refs_2_, ...), custom_call_target="tpu_custom_call" | custom-call | flops 1000000 | bytes 100000 | tf_op jit(solution)/shard_map/pallas_call | solution.py:507
  133.6 15.3 %shard_map.394 = bf16[768,768]{1,0:T(8,128)(2,1)S(1)} custom-call(s32[768,1]{1,0:T(8,128)S(1)} %bitcast.193, s32[2,1,384]{2,1,0:T(1,128)S(1)} %broadcast_in_dim.63.row_ref, bf16[768,768]{1,0:T(8,128)(2,1)S(1)} %add_convert_fusion.3.q_ref, bf16[768,768]{1,0:T(8,128)(2,1)S(1)} %convolution_convert_fusion.k_ref, bf16[768,768]{1,0:T(8,128)(2,1)S(1)} %add_convert_fusion.2.v_ref), custom_call_target="tpu_custom_call" | custom-call | flops 1000000 | bytes 100000 | tf_op jit(solution)/shard_map/pallas_call | solution.py:337
  151.1 3.9 collective-permute-done.7.refs_1_
  161.4 13.9 %shard_map.391 = bf16[32,192,768]{2,1,0:T(8,128)(2,1)S(1)} custom-call(s32[2]{0:T(128)S(1)} %pad_add_fusion.at, bf16[2,4,96,768]{3,2,1,0:T(8,128)(2,1)S(1)} %pad_maximum_fusion.refs_0_, bf16[2,4,96,768]{3,2,1,0:T(8,128)(2,1)S(1)} %collective-permute-done.7.refs_1_, bf16[2,4,96,768]{3,2,1,0:T(8,128)(2,1)S(1)} %collective-permute-done.8.refs_2_, ...), custom_call_target="tpu_custom_call" | custom-call | flops 1000000 | bytes 100000 | tf_op jit(solution)/shard_map/pallas_call | solution.py:507
  175.2 2.6 slice.413
  178.2 18.3 %shard_map.395 = (bf16[768,768]{1,0:T(8,128)(2,1)S(1)}, bf16[768,3072]{1,0:T(8,128)(2,1)}, bf16[4,768,192]{2,1,0:T(8,128)(2,1)}) custom-call(s32[1]{0:T(128)} %bitcast.at, bf16[768,768]{1,0:T(8,128)(2,1)S(1)} %bitcast.191, bf16[768,768]{1,0:T(8,128)(2,1)S(1)} %bitcast.189, bf16[768,768]{1,0:T(8,128)(2,1)S(1)} %bitcast.187, bf16[768,768]{1,0:T(8,128)(2,1)S(1)} %bitcast.185, ...), custom_call_target="tpu_custom_call" | custom-call | flops 1000000 | bytes 100000 | tf_op jit(solution)/shard_map/pallas_call | solution.py:822
  197.5 20.6 %all-gather.5.cloned.1.call-done = bf16[9728,1024]{1,0:T(8,128)(2,1)} async-done(((bf16[304,1024]{1,0:T(8,128)(2,1)}), bf16[9728,1024]{1,0:T(8,128)(2,1)}) %all-gather.5.cloned.1.call-update) | async-done | bytes 19922960 | tf_op jit(solution)/shard_map/all_gather | solution.py:1077
  219.4 1.8 slice.419
  221.2 2.7 slice.415
  229.0 44.9 %shard_map.397 = (bf16[768,1024]{1,0:T(8,128)(2,1)}, bf16[768,1024]{1,0:T(8,128)(2,1)}, bf16[768,1024]{1,0:T(8,128)(2,1)}, bf16[768,1024]{1,0:T(8,128)(2,1)}, bf...) custom-call(bf16[768,1024]{1,0:T(8,128)(2,1)} %bitcast.206, ...), custom_call_target="tpu_custom_call" | custom-call | flops 1000000 | bytes 100000 | tf_op jit(solution)/shard_map/pallas_call | solution.py:717
  274.0 2.0 slice_bitcast_fusion.2
  277.5 13.4 %shard_map.398 = (bf16[4,8,128,512]{3,2,1,0:T(8,128)(2,1)}, bf16[4,8,128,512]{3,2,1,0:T(8,128)(2,1)}, f32[4,1024]{1,0:T(4,128)}) custom-call(s32[1]{0:T(128)} %bitcast.57.at, bf16[768,1024]{1,0:T(8,128)(2,1)} %get-tuple-element.209.refs_0_, bf16[768,1024]{1,0:T(8,128)(2,1)} %get-tuple-element.199.refs_1_, bf16[768,1024]{1,0:T(8,128)(2,1)} %get-tuple-element.200.refs_2_, ...), custom_call_target="tpu_custom_call" | custom-call | flops 1000000 | bytes 100000 | tf_op jit(solution)/shard_map/pallas_call | solution.py:470
  290.9 10.5 %collective-permute-done.26.refs_2_ = bf16[2,96,768]{2,1,0:T(8,128)(2,1)} collective-permute-done((bf16[2,96,768]{2,1,0:T(8,128)(2,1)S(1)}, bf16[2,96,768]{2,1,0:T(8,128)(2,1)}, u32[]{:S(2)}, u32[]{:S(2)}) %collective-permute-start.26) | collective-permute-done | bytes 294944 | tf_op jit(solution)/shard_map/ppermute | solution.py:94
  302.6 2.1 shard_map.399.refs_0_
  305.8 2.3 collective-permute-start.30
  308.1 2.4 collective-permute-start.31
  312.4 2.0 fusion.10.refs_9_
  314.4 14.0 %shard_map.400 = (bf16[4,8,160,512]{3,2,1,0:T(8,128)(2,1)}, bf16[4,8,160,512]{3,2,1,0:T(8,128)(2,1)}, f32[48,1024]{1,0:T(8,128)}) custom-call(s32[1]{0:T(128)} %bitcast.57.at, bf16[768,1024]{1,0:T(8,128)(2,1)} %get-tuple-element.209.refs_0_, bf16[8,1024]{1,0:T(8,128)(2,1)} %copy-done.50, bf16[768,768]{1,0:T(8,128)(2,1)} %copy-done.8, ...), custom_call_target="tpu_custom_call" | custom-call | flops 1000000 | bytes 100000 | tf_op jit(solution)/shard_map/pallas_call | solution.py:470
  328.5 6.4 %shard_map.401 = (bf16[2,8,64,512]{3,2,1,0:T(8,128)(2,1)}, bf16[2,8,64,512]{3,2,1,0:T(8,128)(2,1)}, bf16[2,8,64,512]{3,2,1,0:T(8,128)(2,1)}, bf16[2,8,64,512]{3,2,1,0:T(8,128)(2,1)}) custom-call(s32[2]{0:T(128)} %get-tuple-element.479.at, bf16[4,8,128,512]{3,2,1,0:T(8,128)(2,1)} %get-tuple-element.205.refs_0_, ...), custom_call_target="tpu_custom_call" | custom-call | flops 1000000 | bytes 100000 | tf_op jit(solution)/shard_map/pallas_call | solution.py:130
  338.5 23.9 %shard_map.402 = (bf16[4,2,192,384]{3,2,1,0:T(8,128)(2,1)}, bf16[4,2,192,384]{3,2,1,0:T(8,128)(2,1)}, f32[768,768]{1,0:T(8,128)}, bf16[768,768]{1,0:T(8,128)(2,1...) custom-call(s32[1]{0:T(128)} %bitcast.57.at, bf16[2,96,768]{2,1,0:T(8,128)(2,1)} %shard_map.399.refs_0_, ...), custom_call_target="tpu_custom_call" | custom-call | flops 1000000 | bytes 100000 | tf_op jit(solution)/shard_map/pallas_call | solution.py:919
  362.4 7.4 %shard_map.403 = (bf16[2,8,96,512]{3,2,1,0:T(8,128)(2,1)}, bf16[2,8,96,512]{3,2,1,0:T(8,128)(2,1)}, bf16[2,8,64,512]{3,2,1,0:T(8,128)(2,1)}, bf16[2,8,64,512]{3,2,1,0:T(8,128)(2,1)}) custom-call(s32[2]{0:T(128)} %get-tuple-element.479.at, bf16[4,8,160,512]{3,2,1,0:T(8,128)(2,1)} %get-tuple-element.216.refs_0_, ...), custom_call_target="tpu_custom_call" | custom-call | flops 1000000 | bytes 100000 | tf_op jit(solution)/shard_map/pallas_call | solution.py:130
  372.4 3.9 shard_map.404
  378.0 2.2 collective-permute-start.36
  380.2 12.3 %shard_map.405 = (bf16[768,768]{1,0:T(8,128)(2,1)}, bf16[768,768]{1,0:T(8,128)(2,1)}, bf16[768,768]{1,0:T(8,128)(2,1)}) custom-call(s32[768,1]{1,0:T(8,128)} %bitcast.194, s32[2,1,384]{2,1,0:T(1,128)} %copy-done.10, bf16[768,768]{1,0:T(8,128)(2,1)} %copy-done.5, bf16[768,768]{1,0:T(8,128)(2,1)} %copy-done.6, bf16[768,768]{1,0:T(8,128)(2,1)} %copy-done.4, ...), custom_call_target="tpu_custom_call" | custom-call | flops 1000000 | bytes 100000 | tf_op jit(solution)/shard_map/pallas_call | solution.py:372
  392.5 12.6 %shard_map.406 = (bf16[768,768]{1,0:T(8,128)(2,1)}, bf16[768,768]{1,0:T(8,128)(2,1)}, bf16[768,768]{1,0:T(8,128)(2,1)}) custom-call(s32[768,1]{1,0:T(8,128)} %bitcast.195, s32[2,1,384]{2,1,0:T(1,128)} %copy-done.10, bf16[768,768]{1,0:T(8,128)(2,1)} %copy-done.5, ...), custom_call_target="tpu_custom_call", output_to_operand_aliasing={{0}: (6, {}), {1}: (7, {}), {2}: (8, {})} | custom-call | flops 1000000 | bytes 100000 | tf_op jit(solution)/shard_map/pallas_call | solution.py:372
  406.6 4.5 shard_map.407
  411.1 5.6 %collective-permute-done.40.got_two = bf16[1,8,64,512]{3,2,1,0:T(8,128)(2,1)S(1)} collective-permute-done((bf16[1,8,64,512]{3,2,1,0:T(8,128)(2,1)}, bf16[1,8,64,512]{3,2,1,0:T(8,128)(2,1)S(1)}, u32[]{:S(2)}, u32[]{:S(2)}) %collective-permute-start.40) | collective-permute-done | bytes 524320 | tf_op jit(solution)/shard_map/ppermute | solution.py:90
  417.4 2.6 shard_map.408
  420.9 2.4 collective-permute-start.42
  425.0 10.1 %shard_map.409 = (bf16[4,2,96,384]{3,2,1,0:T(8,128)(2,1)}, bf16[4,2,96,384]{3,2,1,0:T(8,128)(2,1)}, f32[2,96,768]{2,1,0:T(8,128)}, f32[12,768]{1,0:T(8,128)}) custom-call(s32[1]{0:T(128)} %bitcast.57.at, bf16[768,768]{1,0:T(8,128)(2,1)} %get-tuple-element.271.refs_0_, bf16[768,768]{1,0:T(8,128)(2,1)} %get-tuple-element.272.refs_1_, ...), custom_call_target="tpu_custom_call" | custom-call | flops 1000000 | bytes 100000 | tf_op jit(solution)/shard_map/pallas_call | solution.py:130
  435.1 6.9 %collective-permute-done.42.refs_2_ = bf16[2,128,512]{2,1,0:T(8,128)(2,1)S(1)} collective-permute-done((bf16[2,128,512]{2,1,0:T(8,128)(2,1)}, bf16[2,128,512]{2,1,0:T(8,128)(2,1)S(1)}, u32[]{:S(2)}, u32[]{:S(2)}) %collective-permute-start.42) | collective-permute-done | bytes 262176 | tf_op jit(solution)/shard_map/ppermute | solution.py:94
  442.0 4.0 collective-permute-done.43.refs_3_
  446.6 2.2 shard_map.410
  454.3 1.7 slice_bitcast_fusion.6
  457.2 3.4 shard_map.411
  462.6 5.5 %collective-permute-done.47.got_two = bf16[1,8,64,512]{3,2,1,0:T(8,128)(2,1)S(1)} collective-permute-done((bf16[1,8,64,512]{3,2,1,0:T(8,128)(2,1)}, bf16[1,8,64,512]{3,2,1,0:T(8,128)(2,1)S(1)}, u32[]{:S(2)}, u32[]{:S(2)}) %collective-permute-start.47) | collective-permute-done | bytes 524320 | tf_op jit(solution)/shard_map/ppermute | solution.py:90
  468.1 3.5 collective-permute-done.46.got_one
  472.5 2.9 shard_map.412
  478.2 2.6 collective-permute-done.48.got_one
  480.8 5.9 %collective-permute-done.49.got_two = bf16[2,2,144,384]{3,2,1,0:T(8,128)(2,1)S(1)} collective-permute-done((bf16[2,2,144,384]{3,2,1,0:T(8,128)(2,1)}, bf16[2,2,144,384]{3,2,1,0:T(8,128)(2,1)S(1)}, u32[]{:S(2)}, u32[]{:S(2)}) %collective-permute-start.49) | collective-permute-done | bytes 442400 | tf_op jit(solution)/shard_map/ppermute | solution.py:90
  487.5 2.4 shard_map.413
  489.9 11.8 %collective-permute-done.54.refs_2_ = bf16[2,160,512]{2,1,0:T(8,128)(2,1)S(1)} collective-permute-done((bf16[2,160,512]{2,1,0:T(8,128)(2,1)}, bf16[2,160,512]{2,1,0:T(8,128)(2,1)S(1)}, u32[]{:S(2)}, u32[]{:S(2)}) %collective-permute-start.54) | collective-permute-done | bytes 327712 | tf_op jit(solution)/shard_map/ppermute | solution.py:94
  501.7 3.7 collective-permute-done.55.refs_3_
  506.2 2.4 shard_map.415
  514.3 2.5 collective-permute-done.50
  518.3 2.0 shard_map.414
  (362 shorter events, 106.0 us)
Async XLA Ops:
  7.3 49.2 %copy-start.58 = (s32[2,1,384]{2,1,0:T(1,128)S(1)}, s32[2,1,384]{2,1,0:T(1,128)}, u32[]{:S(2)}) copy-start(s32[2,1,384]{2,1,0:T(1,128)} %param.25) | copy-start | bytes 9220
  7.3 210.8 %all-gather.5.cloned.1.call-start = ((), (), s32[]{:S(2)}) async-start(), calls=%async_computation | async-start | bytes 20545536 | tf_op jit(solution)/shard_map/all_gather | solution.py:1077
  12.6 13.5 %collective-permute-start = (bf16[112,768]{1,0:T(8,128)(2,1)S(1)}, bf16[112,768]{1,0:T(8,128)(2,1)S(1)}, u32[]{:S(2)}, u32[]{:S(2)}) collective-permute-start(bf16[112,768]{1,0:T(8,128)(2,1)S(1)} %constant_dynamic-update-slice_fusion), channel_id=1, source_target_pairs={{0,3},{1,0},{2,1},{3,2},{4,7},{5,4},{6,5},{7,6},{8,11},{9,8},{10,9... | collective-permute-start | bytes 516104 | tf_op jit(solution)/shard_map/ppermute | solution.py:94
  12.7 13.5 %collective-permute-start.1 = (bf16[112,768]{1,0:T(8,128)(2,1)S(1)}, bf16[112,768]{1,0:T(8,128)(2,1)S(1)}, u32[]{:S(2)}, u32[]{:S(2)}) collective-permute-start(bf16[112,768]{1,0:T(8,128)(2,1)S(1)} %constant_dynamic-update-slice_fusion), channel_id=1, source_target_pairs={{0,2},{1,3},{2,0},{3,1},{4,6},{5,7},{6,4},{7,5},{8,10},{9,11},{10,... | collective-permute-start | bytes 516104 | tf_op jit(solution)/shard_map/ppermute | solution.py:94
  15.2 14.4 %collective-permute-start.2 = (bf16[112,768]{1,0:T(8,128)(2,1)S(1)}, bf16[112,768]{1,0:T(8,128)(2,1)S(1)}, u32[]{:S(2)}, u32[]{:S(2)}) collective-permute-start(bf16[112,768]{1,0:T(8,128)(2,1)S(1)} %constant_dynamic-update-slice_fusion), channel_id=1, source_target_pairs={{0,1},{1,2},{2,3},{3,0},{4,5},{5,6},{6,7},{7,4},{8,9},{9,10},{10,1... | collective-permute-start | bytes 516104 | tf_op jit(solution)/shard_map/ppermute | solution.py:94
  29.6 8.2 %collective-permute-start.3 = (bf16[192,768]{1,0:T(8,128)(2,1)S(1)}, bf16[192,768]{1,0:T(8,128)(2,1)S(1)}, u32[]{:S(2)}, u32[]{:S(2)}) collective-permute-start(bf16[192,768]{1,0:T(8,128)(2,1)S(1)} %constant_dynamic-update-slice_fusion.5), channel_id=1, source_target_pairs={{0,3},{1,0},{2,1},{3,2},{4,7},{5,4},{6,5},{7,6},{8,11},{9,8},{10,9... | collective-permute-start | bytes 884744 | tf_op jit(solution)/shard_map/ppermute | solution.py:94
  30.9 19.1 %collective-permute-start.4 = (bf16[192,768]{1,0:T(8,128)(2,1)S(1)}, bf16[192,768]{1,0:T(8,128)(2,1)S(1)}, u32[]{:S(2)}, u32[]{:S(2)}) collective-permute-start(bf16[192,768]{1,0:T(8,128)(2,1)S(1)} %constant_dynamic-update-slice_fusion.5), channel_id=1, source_target_pairs={{0,2},{1,3},{2,0},{3,1},{4,6},{5,7},{6,4},{7,5},{8,10},{9,11},{10,... | collective-permute-start | bytes 884744 | tf_op jit(solution)/shard_map/ppermute | solution.py:94
  33.0 23.4 %collective-permute-start.5 = (bf16[192,768]{1,0:T(8,128)(2,1)S(1)}, bf16[192,768]{1,0:T(8,128)(2,1)S(1)}, u32[]{:S(2)}, u32[]{:S(2)}) collective-permute-start(bf16[192,768]{1,0:T(8,128)(2,1)S(1)} %constant_dynamic-update-slice_fusion.5), channel_id=1, source_target_pairs={{0,1},{1,2},{2,3},{3,0},{4,5},{5,6},{6,7},{7,4},{8,9},{9,10},{10,1... | collective-permute-start | bytes 884744 | tf_op jit(solution)/shard_map/ppermute | solution.py:94
  56.4 470.2 %all-gather.7.cloned.1.call-start = ((), (), s32[]{:S(2)}) async-start(), calls=%async_computation.1 | async-start | bytes 2359296 | tf_op jit(solution)/shard_map/all_gather | solution.py:1352
  56.6 77.0 %copy-start.10 = (s32[2,1,384]{2,1,0:T(1,128)}, s32[2,1,384]{2,1,0:T(1,128)S(1)}, u32[]{:S(2)}) copy-start(s32[2,1,384]{2,1,0:T(1,128)S(1)} %broadcast_in_dim.63.row_ref) | copy-start | bytes 9220
  56.8 76.8 %copy-start.7 = (s32[1,768]{0,1:T(8,128)}, s32[1,768]{0,1:T(8,128)S(1)}, u32[]{:S(2)}) copy-start(s32[1,768]{0,1:T(8,128)S(1)} %copy.109) | copy-start | bytes 9220
  60.4 8.2 %collective-permute-start.17 = (bf16[4,48,768]{2,1,0:T(8,128)(2,1)S(1)}, bf16[4,48,768]{2,1,0:T(8,128)(2,1)S(1)}, u32[]{:S(2)}, u32[]{:S(2)}) collective-permute-start(bf16[4,48,768]{2,1,0:T(8,128)(2,1)S(1)} %get-tuple-element.450), channel_id=1, source_target_pairs={{0,16},{4,20},{8,24},{12,28},{16,0},{20,4},{24,8},{28,12},{1,17},{... | collective-permute-start | bytes 884744 | tf_op jit(solution)/shard_map/ppermute | solution.py:90
  61.8 12.6 %collective-permute-start.21 = (bf16[4,64,768]{2,1,0:T(8,128)(2,1)S(1)}, bf16[4,64,768]{2,1,0:T(8,128)(2,1)S(1)}, u32[]{:S(2)}, u32[]{:S(2)}) collective-permute-start(bf16[4,64,768]{2,1,0:T(8,128)(2,1)S(1)} %get-tuple-element.442), channel_id=1, source_target_pairs={{0,8},{4,12},{8,0},{12,4},{16,24},{20,28},{24,16},{28,20},{1,9},{5... | collective-permute-start | bytes 1179656 | tf_op jit(solution)/shard_map/ppermute | solution.py:90
  63.1 13.8 %collective-permute-start.14 = (bf16[2,96,768]{2,1,0:T(8,128)(2,1)S(1)}, bf16[2,96,768]{2,1,0:T(8,128)(2,1)S(1)}, u32[]{:S(2)}, u32[]{:S(2)}) collective-permute-start(bf16[2,96,768]{2,1,0:T(8,128)(2,1)S(1)} %bitcast.226), channel_id=1, source_target_pairs={{0,3},{1,0},{2,1},{3,2},{4,7},{5,4},{6,5},{7,6},{8,11},{9,8},{10,9... | collective-permute-start | bytes 884744 | tf_op jit(solution)/shard_map/ppermute | solution.py:94
  64.8 32.0 %collective-permute-start.15 = (bf16[2,96,768]{2,1,0:T(8,128)(2,1)S(1)}, bf16[2,96,768]{2,1,0:T(8,128)(2,1)S(1)}, u32[]{:S(2)}, u32[]{:S(2)}) collective-permute-start(bf16[2,96,768]{2,1,0:T(8,128)(2,1)S(1)} %bitcast.227), channel_id=1, source_target_pairs={{0,2},{1,3},{2,0},{3,1},{4,6},{5,7},{6,4},{7,5},{8,10},{9,11},{10,... | collective-permute-start | bytes 884744 | tf_op jit(solution)/shard_map/ppermute | solution.py:94
  66.5 37.0 %collective-permute-start.16 = (bf16[2,96,768]{2,1,0:T(8,128)(2,1)S(1)}, bf16[2,96,768]{2,1,0:T(8,128)(2,1)S(1)}, u32[]{:S(2)}, u32[]{:S(2)}) collective-permute-start(bf16[2,96,768]{2,1,0:T(8,128)(2,1)S(1)} %bitcast.228), channel_id=1, source_target_pairs={{0,1},{1,2},{2,3},{3,0},{4,5},{5,6},{6,7},{7,4},{8,9},{9,10},{10,1... | collective-permute-start | bytes 884744 | tf_op jit(solution)/shard_map/ppermute | solution.py:94
  68.6 38.7 %collective-permute-start.18 = (bf16[2,4,48,768]{3,2,1,0:T(8,128)(2,1)S(1)}, bf16[2,4,48,768]{3,2,1,0:T(8,128)(2,1)}, u32[]{:S(2)}, u32[]{:S(2)}) collective-permute-start(bf16[2,4,48,768]{3,2,1,0:T(8,128)(2,1)S(1)} %pad_maximum_fusion.6.refs_0_), channel_id=1, source_target_pairs={{0,8},{4,12},{8,0},{12,4},{16,24},{20,28},{24,16},{28,20},{1,9},{5... | collective-permute-start | bytes 1769480 | tf_op jit(solution)/shard_map/ppermute | solution.py:90
  74.5 32.5 %collective-permute-start.22 = (bf16[2,4,64,768]{3,2,1,0:T(8,128)(2,1)S(1)}, bf16[2,4,64,768]{3,2,1,0:T(8,128)(2,1)S(1)}, u32[]{:S(2)}, u32[]{:S(2)}) collective-permute-start(bf16[2,4,64,768]{3,2,1,0:T(8,128)(2,1)S(1)} %pad_maximum_fusion.3.refs_4_), channel_id=1, source_target_pairs={{0,16},{4,20},{8,24},{12,28},{16,0},{20,4},{24,8},{28,12},{1,17},{... | collective-permute-start | bytes 2359304 | tf_op jit(solution)/shard_map/ppermute | solution.py:90
  76.9 31.0 %collective-permute-start.10 = (bf16[4,96,768]{2,1,0:T(8,128)(2,1)}, bf16[4,96,768]{2,1,0:T(8,128)(2,1)}, u32[]{:S(2)}, u32[]{:S(2)}) collective-permute-start(bf16[4,96,768]{2,1,0:T(8,128)(2,1)} %get-tuple-element.424), channel_id=1, source_target_pairs={{0,8},{4,12},{8,0},{12,4},{16,24},{20,28},{24,16},{28,20},{1,9},{5... | collective-permute-start | bytes 1769480 | tf_op jit(solution)/shard_map/ppermute | solution.py:90
  96.8 16.4 %collective-permute-start.6 = (bf16[4,96,768]{2,1,0:T(8,128)(2,1)}, bf16[4,96,768]{2,1,0:T(8,128)(2,1)}, u32[]{:S(2)}, u32[]{:S(2)}) collective-permute-start(bf16[4,96,768]{2,1,0:T(8,128)(2,1)} %get-tuple-element.426), channel_id=1, source_target_pairs={{0,16},{4,20},{8,24},{12,28},{16,0},{20,4},{24,8},{28,12},{1,17},{... | collective-permute-start | bytes 1769480 | tf_op jit(solution)/shard_map/ppermute | solution.py:90
  103.5 15.2 %collective-permute-start.23 = (bf16[2,4,64,768]{3,2,1,0:T(8,128)(2,1)S(1)}, bf16[2,4,64,768]{3,2,1,0:T(8,128)(2,1)S(1)}, u32[]{:S(2)}, u32[]{:S(2)}) collective-permute-start(bf16[2,4,64,768]{3,2,1,0:T(8,128)(2,1)S(1)} %pad_maximum_fusion.3.refs_4_), channel_id=1, source_target_pairs={{0,4},{4,0},{8,12},{12,8},{16,20},{20,16},{24,28},{28,24},{1,5},{5... | collective-permute-start | bytes 2359304 | tf_op jit(solution)/shard_map/ppermute | solution.py:90
  107.0 11.9 %collective-permute-start.24 = (bf16[2,4,64,768]{3,2,1,0:T(8,128)(2,1)S(1)}, bf16[2,4,64,768]{3,2,1,0:T(8,128)(2,1)}, u32[]{:S(2)}, u32[]{:S(2)}) collective-permute-start(bf16[2,4,64,768]{3,2,1,0:T(8,128)(2,1)S(1)} %collective-permute-done.22.refs_5_), channel_id=1, source_target_pairs={{0,4},{4,0},{8,12},{12,8},{16,20},{20,16},{24,28},{28,24},{1,5},{5... | collective-permute-start | bytes 2359304 | tf_op jit(solution)/shard_map/ppermute | solution.py:90
  107.3 7.0 %collective-permute-start.19 = (bf16[2,4,48,768]{3,2,1,0:T(8,128)(2,1)S(1)}, bf16[2,4,48,768]{3,2,1,0:T(8,128)(2,1)S(1)}, u32[]{:S(2)}, u32[]{:S(2)}) collective-permute-start(bf16[2,4,48,768]{3,2,1,0:T(8,128)(2,1)S(1)} %pad_maximum_fusion.6.refs_0_), channel_id=1, source_target_pairs={{0,4},{4,0},{8,12},{12,8},{16,20},{20,16},{24,28},{28,24},{1,5},{5... | collective-permute-start | bytes 1769480 | tf_op jit(solution)/shard_map/ppermute | solution.py:90
  107.9 10.9 %collective-permute-start.20 = (bf16[2,4,48,768]{3,2,1,0:T(8,128)(2,1)}, bf16[2,4,48,768]{3,2,1,0:T(8,128)(2,1)S(1)}, u32[]{:S(2)}, u32[]{:S(2)}) collective-permute-start(bf16[2,4,48,768]{3,2,1,0:T(8,128)(2,1)} %collective-permute-done.18.refs_1_), channel_id=1, source_target_pairs={{0,4},{4,0},{8,12},{12,8},{16,20},{20,16},{24,28},{28,24},{1,5},{5... | collective-permute-start | bytes 1769480 | tf_op jit(solution)/shard_map/ppermute | solution.py:90
  109.7 50.4 %copy-start.15 = (f32[768,768]{1,0:T(8,128)}, f32[768,768]{1,0:T(8,128)S(1)}, u32[]{:S(2)}) copy-start(f32[768,768]{1,0:T(8,128)S(1)} %fusion.7.refs_10_) | copy-start | bytes 7077892
  113.1 37.4 %collective-permute-start.11 = (bf16[2,4,96,768]{3,2,1,0:T(8,128)(2,1)S(1)}, bf16[2,4,96,768]{3,2,1,0:T(8,128)(2,1)S(1)}, u32[]{:S(2)}, u32[]{:S(2)}) collective-permute-start(bf16[2,4,96,768]{3,2,1,0:T(8,128)(2,1)S(1)} %pad_maximum_fusion.1.refs_4_), channel_id=1, source_target_pairs={{0,16},{4,20},{8,24},{12,28},{16,0},{20,4},{24,8},{28,12},{1,17},{... | collective-permute-start | bytes 3538952 | tf_op jit(solution)/shard_map/ppermute | solution.py:90
  114.3 47.0 %collective-permute-start.12 = (bf16[2,4,96,768]{3,2,1,0:T(8,128)(2,1)S(1)}, bf16[2,4,96,768]{3,2,1,0:T(8,128)(2,1)S(1)}, u32[]{:S(2)}, u32[]{:S(2)}) collective-permute-start(bf16[2,4,96,768]{3,2,1,0:T(8,128)(2,1)S(1)} %pad_maximum_fusion.1.refs_4_), channel_id=1, source_target_pairs={{0,4},{4,0},{8,12},{12,8},{16,20},{20,16},{24,28},{28,24},{1,5},{5... | collective-permute-start | bytes 3538952 | tf_op jit(solution)/shard_map/ppermute | solution.py:90
  118.8 36.1 %collective-permute-start.7 = (bf16[2,4,96,768]{3,2,1,0:T(8,128)(2,1)S(1)}, bf16[2,4,96,768]{3,2,1,0:T(8,128)(2,1)S(1)}, u32[]{:S(2)}, u32[]{:S(2)}) collective-permute-start(bf16[2,4,96,768]{3,2,1,0:T(8,128)(2,1)S(1)} %pad_maximum_fusion.refs_0_), channel_id=1, source_target_pairs={{0,8},{4,12},{8,0},{12,4},{16,24},{20,28},{24,16},{28,20},{1,9},{5... | collective-permute-start | bytes 3538952 | tf_op jit(solution)/shard_map/ppermute | solution.py:90
  118.8 42.6 %collective-permute-start.8 = (bf16[2,4,96,768]{3,2,1,0:T(8,128)(2,1)S(1)}, bf16[2,4,96,768]{3,2,1,0:T(8,128)(2,1)S(1)}, u32[]{:S(2)}, u32[]{:S(2)}) collective-permute-start(bf16[2,4,96,768]{3,2,1,0:T(8,128)(2,1)S(1)} %pad_maximum_fusion.refs_0_), channel_id=1, source_target_pairs={{0,4},{4,0},{8,12},{12,8},{16,20},{20,16},{24,28},{28,24},{1,5},{5... | collective-permute-start | bytes 3538952 | tf_op jit(solution)/shard_map/ppermute | solution.py:90
  150.6 10.8 %collective-permute-start.13 = (bf16[2,4,96,768]{3,2,1,0:T(8,128)(2,1)S(1)}, bf16[2,4,96,768]{3,2,1,0:T(8,128)(2,1)S(1)}, u32[]{:S(2)}, u32[]{:S(2)}) collective-permute-start(bf16[2,4,96,768]{3,2,1,0:T(8,128)(2,1)S(1)} %collective-permute-done.11.refs_5_), channel_id=1, source_target_pairs={{0,4},{4,0},{8,12},{12,8},{16,20},{20,16},{24,28},{28,24},{1,5},{5... | collective-permute-start | bytes 3538952 | tf_op jit(solution)/shard_map/ppermute | solution.py:90
  154.9 6.4 %collective-permute-start.9 = (bf16[2,4,96,768]{3,2,1,0:T(8,128)(2,1)S(1)}, bf16[2,4,96,768]{3,2,1,0:T(8,128)(2,1)S(1)}, u32[]{:S(2)}, u32[]{:S(2)}) collective-permute-start(bf16[2,4,96,768]{3,2,1,0:T(8,128)(2,1)S(1)} %collective-permute-done.7.refs_1_), channel_id=1, source_target_pairs={{0,4},{4,0},{8,12},{12,8},{16,20},{20,16},{24,28},{28,24},{1,5},{5... | collective-permute-start | bytes 3538952 | tf_op jit(solution)/shard_map/ppermute | solution.py:90
  276.0 14.9 %collective-permute-start.25 = (bf16[2,96,768]{2,1,0:T(8,128)(2,1)S(1)}, bf16[2,96,768]{2,1,0:T(8,128)(2,1)S(1)}, u32[]{:S(2)}, u32[]{:S(2)}) collective-permute-start(bf16[2,96,768]{2,1,0:T(8,128)(2,1)S(1)} %get-tuple-element.421), channel_id=1, source_target_pairs={{0,1},{1,2},{2,3},{3,0},{4,5},{5,6},{6,7},{7,4},{8,9},{9,10},{10,1... | collective-permute-start | bytes 884744 | tf_op jit(solution)/shard_map/ppermute | solution.py:94
  276.0 25.4 %collective-permute-start.26 = (bf16[2,96,768]{2,1,0:T(8,128)(2,1)S(1)}, bf16[2,96,768]{2,1,0:T(8,128)(2,1)}, u32[]{:S(2)}, u32[]{:S(2)}) collective-permute-start(bf16[2,96,768]{2,1,0:T(8,128)(2,1)S(1)} %get-tuple-element.420), channel_id=1, source_target_pairs={{0,2},{1,3},{2,0},{3,1},{4,6},{5,7},{6,4},{7,5},{8,10},{9,11},{10,... | collective-permute-start | bytes 884744 | tf_op jit(solution)/shard_map/ppermute | solution.py:94
  276.0 26.6 %collective-permute-start.27 = (bf16[2,96,768]{2,1,0:T(8,128)(2,1)S(1)}, bf16[2,96,768]{2,1,0:T(8,128)(2,1)}, u32[]{:S(2)}, u32[]{:S(2)}) collective-permute-start(bf16[2,96,768]{2,1,0:T(8,128)(2,1)S(1)} %get-tuple-element.419), channel_id=1, source_target_pairs={{0,3},{1,0},{2,1},{3,2},{4,7},{5,4},{6,5},{7,6},{8,11},{9,8},{10,9... | collective-permute-start | bytes 884744 | tf_op jit(solution)/shard_map/ppermute | solution.py:94
  304.7 23.8 %collective-permute-start.28 = (bf16[4,8,128,512]{3,2,1,0:T(8,128)(2,1)}, bf16[4,8,128,512]{3,2,1,0:T(8,128)(2,1)}, u32[]{:S(2)}, u32[]{:S(2)}) collective-permute-start(bf16[4,8,128,512]{3,2,1,0:T(8,128)(2,1)} %get-tuple-element.218), channel_id=1, source_target_pairs={{0,4},{4,0},{8,12},{12,8},{16,20},{20,16},{24,28},{28,24},{1,5},{5... | collective-permute-start | bytes 12582920 | tf_op jit(solution)/shard_map/ppermute | solution.py:90
  305.8 29.1 %collective-permute-start.29 = (bf16[2,96,768]{2,1,0:T(8,128)(2,1)}, bf16[2,96,768]{2,1,0:T(8,128)(2,1)S(1)}, u32[]{:S(2)}, u32[]{:S(2)}) collective-permute-start(bf16[2,96,768]{2,1,0:T(8,128)(2,1)} %shard_map.399.refs_0_), channel_id=1, source_target_pairs={{0,3},{1,0},{2,1},{3,2},{4,7},{5,4},{6,5},{7,6},{8,11},{9,8},{10,9... | collective-permute-start | bytes 884744 | tf_op jit(solution)/shard_map/ppermute | solution.py:94
  305.8 29.1 %collective-permute-start.30 = (bf16[2,96,768]{2,1,0:T(8,128)(2,1)}, bf16[2,96,768]{2,1,0:T(8,128)(2,1)}, u32[]{:S(2)}, u32[]{:S(2)}) collective-permute-start(bf16[2,96,768]{2,1,0:T(8,128)(2,1)} %shard_map.399.refs_0_), channel_id=1, source_target_pairs={{0,2},{1,3},{2,0},{3,1},{4,6},{5,7},{6,4},{7,5},{8,10},{9,11},{10,... | collective-permute-start | bytes 884744 | tf_op jit(solution)/shard_map/ppermute | solution.py:94
  308.1 26.8 %collective-permute-start.31 = (bf16[2,96,768]{2,1,0:T(8,128)(2,1)}, bf16[2,96,768]{2,1,0:T(8,128)(2,1)}, u32[]{:S(2)}, u32[]{:S(2)}) collective-permute-start(bf16[2,96,768]{2,1,0:T(8,128)(2,1)} %shard_map.399.refs_0_), channel_id=1, source_target_pairs={{0,1},{1,2},{2,3},{3,0},{4,5},{5,6},{6,7},{7,4},{8,9},{9,10},{10,1... | collective-permute-start | bytes 884744 | tf_op jit(solution)/shard_map/ppermute | solution.py:94
  334.9 27.5 %collective-permute-start.33 = (bf16[4,8,160,512]{3,2,1,0:T(8,128)(2,1)}, bf16[4,8,160,512]{3,2,1,0:T(8,128)(2,1)}, u32[]{:S(2)}, u32[]{:S(2)}) collective-permute-start(bf16[4,8,160,512]{3,2,1,0:T(8,128)(2,1)} %get-tuple-element.236), channel_id=1, source_target_pairs={{0,4},{4,0},{8,12},{12,8},{16,20},{20,16},{24,28},{28,24},{1,5},{5... | collective-permute-start | bytes 15728648 | tf_op jit(solution)/shard_map/ppermute | solution.py:90
  335.8 26.6 %collective-permute-start.32 = (f32[48,1024]{1,0:T(8,128)S(1)}, f32[48,1024]{1,0:T(8,128)S(1)}, u32[]{:S(2)}, u32[]{:S(2)}) collective-permute-start(f32[48,1024]{1,0:T(8,128)S(1)} %copy-done.46), channel_id=1, source_target_pairs={{0,1},{1,0},{2,3},{3,2},{4,5},{5,4},{6,7},{7,6},{8,9},{9,8},{10,11... | collective-permute-start | bytes 589832 | tf_op jit(solution)/shard_map/ppermute | solution.py:98
  336.8 34.3 %collective-permute-start.34 = (bf16[2,8,64,512]{3,2,1,0:T(8,128)(2,1)}, bf16[2,8,64,512]{3,2,1,0:T(8,128)(2,1)S(1)}, u32[]{:S(2)}, u32[]{:S(2)}) collective-permute-start(bf16[2,8,64,512]{3,2,1,0:T(8,128)(2,1)} %get-tuple-element.242), channel_id=1, source_target_pairs={{0,16},{4,20},{8,24},{12,28},{16,0},{20,4},{24,8},{28,12},{1,17},{... | collective-permute-start | bytes 3145736 | tf_op jit(solution)/shard_map/ppermute | solution.py:90
  338.0 33.1 %collective-permute-start.35 = (bf16[2,8,64,512]{3,2,1,0:T(8,128)(2,1)}, bf16[2,8,64,512]{3,2,1,0:T(8,128)(2,1)S(1)}, u32[]{:S(2)}, u32[]{:S(2)}) collective-permute-start(bf16[2,8,64,512]{3,2,1,0:T(8,128)(2,1)} %get-tuple-element.243), channel_id=1, source_target_pairs={{0,8},{4,12},{8,0},{12,4},{16,24},{20,28},{24,16},{28,20},{1,9},{5... | collective-permute-start | bytes 3145736 | tf_op jit(solution)/shard_map/ppermute | solution.py:90
  369.9 35.5 %collective-permute-start.37 = (bf16[2,8,96,512]{3,2,1,0:T(8,128)(2,1)}, bf16[2,8,96,512]{3,2,1,0:T(8,128)(2,1)S(1)}, u32[]{:S(2)}, u32[]{:S(2)}) collective-permute-start(bf16[2,8,96,512]{3,2,1,0:T(8,128)(2,1)} %get-tuple-element.258), channel_id=1, source_target_pairs={{0,16},{4,20},{8,24},{12,28},{16,0},{20,4},{24,8},{28,12},{1,17},{... | collective-permute-start | bytes 4718600 | tf_op jit(solution)/shard_map/ppermute | solution.py:90
  370.0 35.2 %collective-permute-start.38 = (bf16[2,8,64,512]{3,2,1,0:T(8,128)(2,1)}, bf16[2,8,64,512]{3,2,1,0:T(8,128)(2,1)}, u32[]{:S(2)}, u32[]{:S(2)}) collective-permute-start(bf16[2,8,64,512]{3,2,1,0:T(8,128)(2,1)} %get-tuple-element.259), channel_id=1, source_target_pairs={{0,8},{4,12},{8,0},{12,4},{16,24},{20,28},{24,16},{28,20},{1,9},{5... | collective-permute-start | bytes 3145736 | tf_op jit(solution)/shard_map/ppermute | solution.py:90
  376.3 34.8 %collective-permute-start.39 = (bf16[1,8,64,512]{3,2,1,0:T(8,128)(2,1)}, bf16[1,8,64,512]{3,2,1,0:T(8,128)(2,1)S(1)}, u32[]{:S(2)}, u32[]{:S(2)}) collective-permute-start(bf16[1,8,64,512]{3,2,1,0:T(8,128)(2,1)} %get-tuple-element.266), channel_id=1, source_target_pairs={{0,8},{4,12},{8,0},{12,4},{16,24},{20,28},{24,16},{28,20},{1,9},{5... | collective-permute-start | bytes 1572872 | tf_op jit(solution)/shard_map/ppermute | solution.py:90
  376.7 39.9 %collective-permute-start.40 = (bf16[1,8,64,512]{3,2,1,0:T(8,128)(2,1)}, bf16[1,8,64,512]{3,2,1,0:T(8,128)(2,1)S(1)}, u32[]{:S(2)}, u32[]{:S(2)}) collective-permute-start(bf16[1,8,64,512]{3,2,1,0:T(8,128)(2,1)} %get-tuple-element.267), channel_id=1, source_target_pairs={{0,16},{4,20},{8,24},{12,28},{16,0},{20,4},{24,8},{28,12},{1,17},{... | collective-permute-start | bytes 1572872 | tf_op jit(solution)/shard_map/ppermute | solution.py:90
  378.0 27.1 %collective-permute-start.36 = (f32[48,1024]{1,0:T(8,128)S(1)}, f32[48,1024]{1,0:T(8,128)S(1)}, u32[]{:S(2)}, u32[]{:S(2)}) collective-permute-start(f32[48,1024]{1,0:T(8,128)S(1)} %add.313), channel_id=1, source_target_pairs={{0,2},{1,3},{2,0},{3,1},{4,6},{5,7},{6,4},{7,5},{8,10},{9,11},{10,... | collective-permute-start | bytes 589832 | tf_op jit(solution)/shard_map/ppermute | solution.py:98
  420.1 15.0 %collective-permute-start.41 = (bf16[2,128,512]{2,1,0:T(8,128)(2,1)}, bf16[2,128,512]{2,1,0:T(8,128)(2,1)S(1)}, u32[]{:S(2)}, u32[]{:S(2)}) collective-permute-start(bf16[2,128,512]{2,1,0:T(8,128)(2,1)} %get-tuple-element.286), channel_id=1, source_target_pairs={{0,1},{1,2},{2,3},{3,0},{4,5},{5,6},{6,7},{7,4},{8,9},{9,10},{10,1... | collective-permute-start | bytes 786440 | tf_op jit(solution)/shard_map/ppermute | solution.py:94
  420.9 21.1 %collective-permute-start.42 = (bf16[2,128,512]{2,1,0:T(8,128)(2,1)}, bf16[2,128,512]{2,1,0:T(8,128)(2,1)S(1)}, u32[]{:S(2)}, u32[]{:S(2)}) collective-permute-start(bf16[2,128,512]{2,1,0:T(8,128)(2,1)} %get-tuple-element.287), channel_id=1, source_target_pairs={{0,2},{1,3},{2,0},{3,1},{4,6},{5,7},{6,4},{7,5},{8,10},{9,11},{10,... | collective-permute-start | bytes 786440 | tf_op jit(solution)/shard_map/ppermute | solution.py:94
  423.3 22.6 %collective-permute-start.43 = (bf16[2,128,512]{2,1,0:T(8,128)(2,1)}, bf16[2,128,512]{2,1,0:T(8,128)(2,1)S(1)}, u32[]{:S(2)}, u32[]{:S(2)}) collective-permute-start(bf16[2,128,512]{2,1,0:T(8,128)(2,1)} %get-tuple-element.288), channel_id=1, source_target_pairs={{0,3},{1,0},{2,1},{3,2},{4,7},{5,4},{6,5},{7,6},{8,11},{9,8},{10,9... | collective-permute-start | bytes 786440 | tf_op jit(solution)/shard_map/ppermute | solution.py:94
  448.8 7.1 %collective-permute-start.44 = (bf16[4,2,192,384]{3,2,1,0:T(8,128)(2,1)}, bf16[4,2,192,384]{3,2,1,0:T(8,128)(2,1)S(1)}, u32[]{:S(2)}, u32[]{:S(2)}) collective-permute-start(bf16[4,2,192,384]{3,2,1,0:T(8,128)(2,1)} %get-tuple-element.297), channel_id=1, source_target_pairs={{0,4},{4,0},{8,12},{12,8},{16,20},{20,16},{24,28},{28,24},{1,5},{5... | collective-permute-start | bytes 3538952 | tf_op jit(solution)/shard_map/ppermute | solution.py:90
  450.0 6.0 %collective-permute-start.45 = (bf16[4,2,96,384]{3,2,1,0:T(8,128)(2,1)}, bf16[4,2,96,384]{3,2,1,0:T(8,128)(2,1)S(1)}, u32[]{:S(2)}, u32[]{:S(2)}) collective-permute-start(bf16[4,2,96,384]{3,2,1,0:T(8,128)(2,1)} %get-tuple-element.298), channel_id=1, source_target_pairs={{0,4},{4,0},{8,12},{12,8},{16,20},{20,16},{24,28},{28,24},{1,5},{5... | collective-permute-start | bytes 1769480 | tf_op jit(solution)/shard_map/ppermute | solution.py:90
  450.0 21.6 %collective-permute-start.46 = (bf16[1,8,96,512]{3,2,1,0:T(8,128)(2,1)}, bf16[1,8,96,512]{3,2,1,0:T(8,128)(2,1)S(1)}, u32[]{:S(2)}, u32[]{:S(2)}) collective-permute-start(bf16[1,8,96,512]{3,2,1,0:T(8,128)(2,1)} %get-tuple-element.305), channel_id=1, source_target_pairs={{0,8},{4,12},{8,0},{12,4},{16,24},{20,28},{24,16},{28,20},{1,9},{5... | collective-permute-start | bytes 2359304 | tf_op jit(solution)/shard_map/ppermute | solution.py:90
  452.4 15.7 %collective-permute-start.47 = (bf16[1,8,64,512]{3,2,1,0:T(8,128)(2,1)}, bf16[1,8,64,512]{3,2,1,0:T(8,128)(2,1)S(1)}, u32[]{:S(2)}, u32[]{:S(2)}) collective-permute-start(bf16[1,8,64,512]{3,2,1,0:T(8,128)(2,1)} %get-tuple-element.306), channel_id=1, source_target_pairs={{0,16},{4,20},{8,24},{12,28},{16,0},{20,4},{24,8},{28,12},{1,17},{... | collective-permute-start | bytes 1572872 | tf_op jit(solution)/shard_map/ppermute | solution.py:90
  453.2 9.4 %collective-permute-start.57 = (bf16[128,512]{1,0:T(8,128)(2,1)}, bf16[128,512]{1,0:T(8,128)(2,1)S(1)}, u32[]{:S(2)}, u32[]{:S(2)}) collective-permute-start(bf16[128,512]{1,0:T(8,128)(2,1)} %get-tuple-element.293), channel_id=1, source_target_pairs={{0,4},{4,0},{8,12},{12,8},{16,20},{20,16},{24,28},{28,24},{1,5},{5... | collective-permute-start | bytes 393224 | tf_op jit(solution)/shard_map/ppermute | solution.py:90
  460.7 20.1 %collective-permute-start.48 = (bf16[2,2,144,384]{3,2,1,0:T(8,128)(2,1)}, bf16[2,2,144,384]{3,2,1,0:T(8,128)(2,1)S(1)}, u32[]{:S(2)}, u32[]{:S(2)}) collective-permute-start(bf16[2,2,144,384]{3,2,1,0:T(8,128)(2,1)} %get-tuple-element.310), channel_id=1, source_target_pairs={{0,16},{4,20},{8,24},{12,28},{16,0},{20,4},{24,8},{28,12},{1,17},{... | collective-permute-start | bytes 1327112 | tf_op jit(solution)/shard_map/ppermute | solution.py:90
  462.0 24.7 %collective-permute-start.49 = (bf16[2,2,144,384]{3,2,1,0:T(8,128)(2,1)}, bf16[2,2,144,384]{3,2,1,0:T(8,128)(2,1)S(1)}, u32[]{:S(2)}, u32[]{:S(2)}) collective-permute-start(bf16[2,2,144,384]{3,2,1,0:T(8,128)(2,1)} %get-tuple-element.311), channel_id=1, source_target_pairs={{0,8},{4,12},{8,0},{12,4},{16,24},{20,28},{24,16},{28,20},{1,9},{5... | collective-permute-start | bytes 1327112 | tf_op jit(solution)/shard_map/ppermute | solution.py:90
  475.4 14.5 %collective-permute-start.53 = (bf16[2,160,512]{2,1,0:T(8,128)(2,1)}, bf16[2,160,512]{2,1,0:T(8,128)(2,1)S(1)}, u32[]{:S(2)}, u32[]{:S(2)}) collective-permute-start(bf16[2,160,512]{2,1,0:T(8,128)(2,1)} %get-tuple-element.322), channel_id=1, source_target_pairs={{0,1},{1,2},{2,3},{3,0},{4,5},{5,6},{6,7},{7,4},{8,9},{9,10},{10,1... | collective-permute-start | bytes 983048 | tf_op jit(solution)/shard_map/ppermute | solution.py:94
  475.4 26.3 %collective-permute-start.54 = (bf16[2,160,512]{2,1,0:T(8,128)(2,1)}, bf16[2,160,512]{2,1,0:T(8,128)(2,1)S(1)}, u32[]{:S(2)}, u32[]{:S(2)}) collective-permute-start(bf16[2,160,512]{2,1,0:T(8,128)(2,1)} %get-tuple-element.323), channel_id=1, source_target_pairs={{0,2},{1,3},{2,0},{3,1},{4,6},{5,7},{6,4},{7,5},{8,10},{9,11},{10,... | collective-permute-start | bytes 983048 | tf_op jit(solution)/shard_map/ppermute | solution.py:94
  476.0 29.5 %collective-permute-start.55 = (bf16[2,160,512]{2,1,0:T(8,128)(2,1)}, bf16[2,160,512]{2,1,0:T(8,128)(2,1)S(1)}, u32[]{:S(2)}, u32[]{:S(2)}) collective-permute-start(bf16[2,160,512]{2,1,0:T(8,128)(2,1)} %get-tuple-element.324), channel_id=1, source_target_pairs={{0,3},{1,0},{2,1},{3,2},{4,7},{5,4},{6,5},{7,6},{8,11},{9,8},{10,9... | collective-permute-start | bytes 983048 | tf_op jit(solution)/shard_map/ppermute | solution.py:94
  508.5 3.3 collective-permute-start.56
  509.8 7.0 %collective-permute-start.50 = (bf16[1,2,144,384]{3,2,1,0:T(8,128)(2,1)S(1)}, bf16[1,2,144,384]{3,2,1,0:T(8,128)(2,1)S(1)}, u32[]{:S(2)}, u32[]{:S(2)}) collective-permute-start(bf16[1,2,144,384]{3,2,1,0:T(8,128)(2,1)S(1)} %copy-done.61), channel_id=1, source_target_pairs={{0,8},{4,12},{8,0},{12,4},{16,24},{20,28},{24,16},{28,20},{1,9},{5... | collective-permute-start | bytes 663560 | tf_op jit(solution)/shard_map/ppermute | solution.py:90
  510.7 6.7 %collective-permute-start.51 = (bf16[1,2,144,384]{3,2,1,0:T(8,128)(2,1)S(1)}, bf16[1,2,144,384]{3,2,1,0:T(8,128)(2,1)S(1)}, u32[]{:S(2)}, u32[]{:S(2)}) collective-permute-start(bf16[1,2,144,384]{3,2,1,0:T(8,128)(2,1)S(1)} %copy-done.60), channel_id=1, source_target_pairs={{0,16},{4,20},{8,24},{12,28},{16,0},{20,4},{24,8},{28,12},{1,17},{... | collective-permute-start | bytes 663560 | tf_op jit(solution)/shard_map/ppermute | solution.py:90
  520.3 2.4 collective-permute-start.52
  (59 other events, 709.1 us)
Sparse Core Ops, SparseCore 0:
  56.5 161.5 all-gather.4
  452.5 34.8 all-gather.6

commit v4 on v3

--- a/solution.py
+++ b/solution.py
@@ -109,7 +109,10 @@
 MIB = 1 << 20
 
 
-LIGHT = pl.CostEstimate(flops=10**6, bytes_accessed=10**5, transcendentals=0)
+def cost(microseconds):
+    return pl.CostEstimate(
+        flops=int(microseconds * 10**9), bytes_accessed=10**5, transcendentals=0
+    )
 
 
 def dot0(left_side, right_side):
@@ -134,7 +137,7 @@
         + [pl.BlockSpec(memory_space=pltpu.VMEM)] * len(ins),
         out_specs=[pl.BlockSpec(memory_space=pltpu.VMEM)] * len(outs),
         compiler_params=pltpu.CompilerParams(vmem_limit_bytes=60 * MIB),
-        cost_estimate=LIGHT,
+        cost_estimate=cost(size / 2.2e6),
     )(jnp.stack([jnp.asarray(v, jnp.int32) for v in scalars]), *ins)
 
 
@@ -246,6 +249,45 @@
     return small_call(body, [low_shape(*parts[0].shape)], [0], parts)[0]
 
 
+def cut_copy_halves(keeps, gots, place, copy_size, kernels):
+    _, mids, _, width = keeps[0].shape
+    sizes = [k.shape[2] for k in keeps]
+    total, half = sum(sizes), copy_size // 2
+    if not kernels:
+        sums = jnp.concatenate([add_up(k, g)[0] for k, g in zip(keeps, gots)], axis=1)
+        sums = sums.astype(jnp.bfloat16).reshape(2, 2, half, total, width)
+        top = place // half
+        return [pick(sums, 1 - top, 1), pick(sums, top, 1)]
+
+    def body(at, keep_one, got_one, keep_two, got_two, *outs):
+        top = at[0] // half
+        for out, bit in zip(outs, (1 - top, top)):
+            for c in range(2):
+                for j in range(half):
+                    m = c * copy_size + bit * half + j
+                    first = add_up(keep_one[0, m], got_one[0, m]).astype(jnp.bfloat16)
+                    second = add_up(keep_two[0, m], got_two[0, m]).astype(jnp.bfloat16)
+                    out[c, j, : sizes[0]] = first
+                    out[c, j, sizes[0] :] = second
+
+    outs = [low_shape(2, half, total, width)] * 2
+    return small_call(body, outs, [place], [keeps[0], gots[0], keeps[1], gots[1]])
+
+
+def cut_copy_last(keep, got, place, kernels):
+    if not kernels:
+        sums = add_up(keep, got).astype(jnp.bfloat16)
+        return [pick(sums, 1 - place % 2, 1), pick(sums, place % 2, 1)]
+
+    def body(at, keep_ref, got_ref, *outs):
+        low = lax.rem(at[0], 2)
+        for out, bit in zip(outs, (1 - low, low)):
+            for c in range(2):
+                out[c] = add_up(keep_ref[c, bit], got_ref[c, bit]).astype(jnp.bfloat16)
+
+    return small_call(body, [low_shape(2, *keep.shape[2:])] * 2, [place], [keep, got])
+
+
 def own_and_other(parts, scalars, kernels):
     place, core = scalars
     count = len(parts)
@@ -341,7 +383,7 @@
         in_specs=[col, row, wide, wide, wide],
         out_specs=wide,
         compiler_params=pltpu.CompilerParams(vmem_limit_bytes=24 * MIB),
-        cost_estimate=LIGHT,
+        cost_estimate=cost(15.0),
     )(ids.reshape(-1, 1), ids[:, None], queries, key_rows, value_rows)
 
 
@@ -378,7 +420,7 @@
         out_specs=[wide] * 3,
         input_output_aliases={6 + i: i for i in range(len(before or ()))},
         compiler_params=pltpu.CompilerParams(vmem_limit_bytes=60 * MIB),
-        cost_estimate=LIGHT,
+        cost_estimate=cost(12.0),
     )(ids.reshape(-1, 1), ids[:, None], queries, key_rows, value_rows, grad_mixed, *(before or ()))
 
 
@@ -478,7 +520,7 @@
             pltpu.VMEM((lefts[which[i]].shape[1], width), jnp.float32) for i in held
         ],
         compiler_params=pltpu.CompilerParams(vmem_limit_bytes=60 * MIB),
-        cost_estimate=LIGHT,
+        cost_estimate=cost(13.0),
     )(jnp.asarray(core, jnp.int32)[None], *lefts, *rights, *others)
 
 
@@ -512,7 +554,7 @@
         out_specs=pl.BlockSpec(memory_space=pl.ANY),
         scratch_shapes=[pltpu.SemaphoreType.DMA((len(pieces) * 2 * copy_size,))],
         compiler_params=pltpu.CompilerParams(vmem_limit_bytes=4 * MIB),
-        cost_estimate=LIGHT,
+        cost_estimate=cost(8.0),
     )(jnp.stack([jnp.asarray(v, jnp.int32) for v in scalars]), *[p[0] for p in pieces])
 
 
@@ -541,6 +583,41 @@
     return jnp.pad(values, ((0, 0), (0, LANES - values.shape[1]))).reshape(-1)
 
 
+def lay(ins, shape, plan, vectors):
+    height, width = shape
+    start = max(p[5] + p[3] for p in plan)
+
+    def body(*refs):
+        out = refs[-1]
+        for which, row, column, rows, columns, there in plan:
+            out[there : there + rows] = refs[which][row : row + rows, column : column + columns]
+        values = []
+        for which, turned in vectors:
+            value = refs[which][...].astype(jnp.float32)
+            value = value.T if turned else value
+            values += [value[i : i + 1] for i in range(value.shape[0])]
+        zero = jnp.zeros((1, LANES), jnp.float32)
+        values = [
+            jnp.concatenate([v, zero[:, : LANES - v.shape[1]]], axis=1) for v in values
+        ]
+        values += [zero] * ((height - start) * width // LANES - len(values))
+        per = width // LANES
+        lines = [
+            jnp.concatenate(values[i : i + per], axis=1) for i in range(0, len(values), per)
+        ]
+        if lines:
+            out[start:] = jnp.concatenate(lines, axis=0).astype(jnp.bfloat16)
+
+    return pl.pallas_call(
+        body,
+        out_shape=low_shape(height, width),
+        in_specs=[pl.BlockSpec(memory_space=pltpu.VMEM)] * len(ins),
+        out_specs=pl.BlockSpec(memory_space=pltpu.VMEM),
+        compiler_params=pltpu.CompilerParams(vmem_limit_bytes=16 * MIB),
+        cost_estimate=cost(2.0),
+    )(*ins)
+
+
 def spread(packed, sizes):
     world = packed.shape[0]
     total = sum(count for count, _ in sizes)
@@ -568,7 +645,7 @@
         in_specs=[pl.BlockSpec(memory_space=pltpu.VMEM)],
         out_specs=[pl.BlockSpec(memory_space=pltpu.VMEM)] * len(sizes),
         compiler_params=pltpu.CompilerParams(vmem_limit_bytes=16 * MIB),
-        cost_estimate=LIGHT,
+        cost_estimate=cost(0.7),
     )(packed[:, : total * LANES])
 
 
@@ -731,7 +808,7 @@
             pltpu.SemaphoreType.DMA((len(used),)),
         ],
         compiler_params=pltpu.CompilerParams(vmem_limit_bytes=60 * MIB),
-        cost_estimate=LIGHT,
+        cost_estimate=cost(45.0),
     )(*smalls, pack, *values)
     return dict(zip(HEAD_OUT, outs)), sums
 
@@ -837,7 +914,7 @@
         ],
         scratch_shapes=[pltpu.VMEM((rows, D), f32), pltpu.VMEM((rows, per), f32)],
         compiler_params=pltpu.CompilerParams(vmem_limit_bytes=48 * MIB),
-        cost_estimate=LIGHT,
+        cost_estimate=cost(18.0),
     )(place[None], *ups, second_in, middle, up_bias, w_down, down_bias)
     return out, slope, chosen, None
 
@@ -925,7 +1002,7 @@
         + [pl.BlockSpec((1, 8, D), lambda j: (j, 0, 0))],
         scratch_shapes=[pltpu.VMEM((rows, D), bf16), pltpu.VMEM((rows, D), f32)],
         compiler_params=pltpu.CompilerParams(vmem_limit_bytes=60 * MIB),
-        cost_estimate=LIGHT,
+        cost_estimate=cost(24.0),
     )(jnp.asarray(core, jnp.int32)[None], *ins)
 
 
@@ -1062,7 +1139,35 @@
         return out
 
     own_rows = block_input[:, 0]
-    packs = [jnp.concatenate(parts, 0) for parts, _ in groups]
+    if kernels:
+        square = range(3)
+        packs = [
+            lay(
+                [w_qkv, w_proj, norm_gains, block_biases, up_bias[None]],
+                (4 * k_d + 16, D),
+                [(0, 0, i * D, k_d, D, i * k_d) for i in square] + [(1, 0, 0, k_d, D, 3 * k_d)],
+                [(2, False), (3, False), (4, False)],
+            ),
+            lay(
+                [w_up, w_down],
+                (ff // D * k_d + k_ff, D),
+                [(0, 0, i * D, k_d, D, i * k_d) for i in range(ff // D)]
+                + [(1, 0, 0, k_ff, D, ff // D * k_d)],
+                [],
+            ),
+            lay(
+                [w_ada, w_time2, w_mlp1, w_mlp2, w_final, w_cond, w_time1]
+                + [w_input, w_output, head_gain[None], head_biases],
+                (8 * k_w + k_d + k_t + 16, WIDTH),
+                [(0, 0, i * WIDTH, k_w, WIDTH, i * k_w) for i in square]
+                + [(i, 0, 0, k_w, WIDTH, (2 + i) * k_w) for i in (1, 2, 3)]
+                + [(4, 0, i * WIDTH, k_w, WIDTH, (6 + i) * k_w) for i in range(2)]
+                + [(5, 0, 0, k_d, WIDTH, 8 * k_w), (6, 0, 0, k_t, WIDTH, 8 * k_w + k_d)],
+                [(7, False), (8, True), (9, False), (10, False)],
+            ),
+        ]
+    else:
+        packs = [jnp.concatenate(parts, 0) for parts, _ in groups]
     if kernels and dp_size == 8 and copy_size == 4:
         head_own = packs[2]
         arrived = [everyone(packs[0])]
@@ -1310,20 +1415,26 @@
         kernels,
     )
     sent, kept = [send], [keep]
-    small_grads = swap_copies(small_grads, 1, [grad_mixed])
+    formed = form_after(pack_one, [grad_mixed])
+    send_after(pack_one, formed)
+    small_grads = swap_copies(small_grads, 1, formed)
     formed = form_after(pack_two, [small_grads])
     send_after(pack_two, formed)
-    formed = form_after(pack_one, formed)
-    send_after(pack_one, formed)
     (grad_mixed,) = after(formed, grad_mixed)
-    back = None
-    for m in range(micros):
+    back = attention_back(queries, key_rows, value_rows, grad_mixed, ids, 0, None)
+    pack_one.got = after(back, *pack_one.got)
+    send, one_half = cut_copy_halves(pack_one.kept, pack_one.got, place, copy_size, kernels)
+    one_got = swap_copy(send, copy_size, copy_size // 2)
+    small_grads = swap_copies(small_grads, 2, [one_half])
+    (grad_mixed,) = after([small_grads], grad_mixed)
+    for m in range(1, micros):
         back = attention_back(queries, key_rows, value_rows, grad_mixed, ids, m, back)
-    small_grads = swap_copies(small_grads, 2, back)
-    formed = form_after(pack_two, [small_grads])
+    formed = form_after(pack_two, back)
     send_after(pack_two, formed)
-    one_parts = to_copies(pack_one, formed)
-    back = after([one_parts[0]], *back)
+    (one_got,) = after(formed, one_got)
+    send, one_last = cut_copy_last(one_half, one_got, place, kernels)
+    one_got = swap_copy(send, copy_size, 1)
+    back = after([one_last], *back)
     send, keep, input_grad, block_small = block_back_two(
         back,
         (w_q, w_k, w_v),
@@ -1341,10 +1452,11 @@
         dp_size,
         kernels,
     )
-    one_parts = after([keep], *one_parts)
-    own_one_parts = own_and_other(one_parts, (place, core), kernels)
     sent, kept = sent + [send], kept + [keep]
     pack_three = Reduction(sent, kept, 6 * k_d, dp_size, kernels)
+    two_parts = to_copies(pack_two, [keep])
+    (one_got,) = after([two_parts[0]], one_got)
+    own_one_parts = own_and_other([one_last, one_got], (0, core), kernels)
     send_after(pack_three, own_one_parts)
     head_rows = small_grads.shape[0]
     block_small = jnp.pad(block_small, ((0, -block_small.shape[0] % 8), (0, WIDTH - D)))
@@ -1356,7 +1468,6 @@
     block_small = small_grads[head_rows:, :D]
     formed = form_after(pack_three, own_one_parts)
     send_after(pack_three, formed)
-    two_parts = to_copies(pack_two, formed)
     while pack_three.left:
         formed = form_after(pack_three, [two_parts[0]])
         send_after(pack_three, formed)

time: 546 us -> 525 us (0.962)
  waiting for transfers between devices: 148 us -> 133 us
  local copies, waits for them, and re-layouts: 47.4 us -> 39.2 us
    ppermute x35, waiting for transfers between devices: 38.6 us -> 30.7 us  [swap_bit(): return lax.ppermute(values, 'dp', [(i, i ^ 1 << bit) for i in range(size)])]
    ppermute x21 -> x18, waiting for transfers between devices: 89.2 us -> 82 us  [shift_copy(): lax.ppermute(values, 'copy', [(i, (i + shift) % size) for i in range(size)])]
    unnamed x150 -> x164, local copies, waits for them, and re-layouts: 19 us -> 16.2 us
    pallas_call x13 -> x14, Pallas kernels: 52.3 us -> 54.3 us  [small_call(): pl.pallas_call(body, out_shape=outs, in_specs=[pl.BlockSpec(memory_space=...]
    ppermute x21 -> x18, starting transfers between devices: 23.1 us -> 22.6 us  [shift_copy(): lax.ppermute(values, 'copy', [(i, (i + shift) % size) for i in range(size)])]
  transfers between devices with their start and end apart: 60 -> 59, of which waited for: 25 -> 23; matrix products, arithmetic and copies ran while one was open for 11% -> 10% of each run, Pallas kernels for 33% -> 36%
where the time goes in v4:
time: 525 us; the launch traced here: 519 us
  Pallas kernels  234 us (45%)
  waiting for transfers between devices  133 us (25%)
  starting transfers between devices  53.7 us (10%)
  local copies, waits for them, and re-layouts  39.2 us (7%)
  other arithmetic  30.4 us (6%)
  between operations  15.5 us (3%)
  matrix products  12.8 us (2%)
    ppermute x18, waiting for transfers between devices, shift_copy(): lax.ppermute(values, 'copy', [(i, (i + shift) % size) for i in range(size)])  82 us
    pallas_call x14, Pallas kernels, small_call(): pl.pallas_call(body, out_shape=outs, in_specs=[pl.BlockSpec(memory_space=...  54.3 us
    pallas_call x1, Pallas kernels, head_kernel(): pl.pallas_call(body, grid=(rows // step,), out_shape=[low_shape(rows, w)...  44.7 us
    ppermute x35, waiting for transfers between devices, swap_bit(): return lax.ppermute(values, 'dp', [(i, i ^ 1 << bit) for i in range(size)])  30.7 us
    pallas_call x2, Pallas kernels, pack_head_grads(): pl.pallas_call(body, grid=(count,), out_shape=[low_shape(count, mids, tot...  27.5 us
    ppermute x35, starting transfers between devices, swap_bit(): return lax.ppermute(values, 'dp', [(i, i ^ 1 << bit) for i in range(size)])  26.3 us
    pallas_call x2, Pallas kernels, attention_back(): pl.pallas_call(body, grid=(1, HEADS // 2), out_shape=[low_shape(micros *...  24.8 us
    pallas_call x1, Pallas kernels, block_back_one(): pl.pallas_call(body, grid=(steps,), out_shape=outs + [jax.ShapeDtypeStruc...  24.3 us
  transfers between devices with their start and end apart: 59, of which 23 were waited for; matrix products, arithmetic and copies ran while one was open for 10% of the time, Pallas kernels for 36%

profile of v4, /device:TPU:9, one launch (start us, length us, event | category | flops | bytes accessed | tf_op | source)
XLA Modules:
  0.0 519.0 jit_solution(9645919372203196094)
XLA Ops:
  11.1 2.5 collective-permute-start.1
  13.6 2.2 collective-permute-start.2
  16.4 8.0 %collective-permute-done.1 = bf16[112,768]{1,0:T(8,128)(2,1)S(1)} collective-permute-done((bf16[112,768]{1,0:T(8,128)(2,1)S(1)}, bf16[112,768]{1,0:T(8,128)(2,1)S(1)}, u32[]{:S(2)}, u32[]{:S(2)}) %collective-permute-start.1) | collective-permute-done | bytes 172064 | tf_op jit(solution)/shard_map/ppermute | solution.py:94
  24.3 3.7 collective-permute-done.2
  29.3 2.1 collective-permute-start.4
  32.5 3.7 collective-permute-done.3
  36.3 12.2 %collective-permute-done.4 = bf16[192,768]{1,0:T(8,128)(2,1)S(1)} collective-permute-done((bf16[192,768]{1,0:T(8,128)(2,1)S(1)}, bf16[192,768]{1,0:T(8,128)(2,1)S(1)}, u32[]{:S(2)}, u32[]{:S(2)}) %collective-permute-start.4) | collective-permute-done | bytes 294944 | tf_op jit(solution)/shard_map/ppermute | solution.py:94
  48.5 6.3 %collective-permute-done.5 = bf16[192,768]{1,0:T(8,128)(2,1)S(1)} collective-permute-done((bf16[192,768]{1,0:T(8,128)(2,1)S(1)}, bf16[192,768]{1,0:T(8,128)(2,1)S(1)}, u32[]{:S(2)}, u32[]{:S(2)}) %collective-permute-start.5) | collective-permute-done | bytes 294944 | tf_op jit(solution)/shard_map/ppermute | solution.py:94
  61.5 1.7 collective-permute-start.14
  63.2 1.8 collective-permute-start.15
  64.9 2.0 collective-permute-done.17
  68.3 4.4 collective-permute-done.21
  75.1 2.1 collective-permute-start.10
  77.3 17.9 %collective-permute-done.15 = bf16[2,96,768]{2,1,0:T(8,128)(2,1)S(1)} collective-permute-done((bf16[2,96,768]{2,1,0:T(8,128)(2,1)S(1)}, bf16[2,96,768]{2,1,0:T(8,128)(2,1)S(1)}, u32[]{:S(2)}, u32[]{:S(2)}) %collective-permute-start.15) | collective-permute-done | bytes 294944 | tf_op jit(solution)/shard_map/ppermute | solution.py:94
  95.3 6.6 %collective-permute-done.16 = bf16[2,96,768]{2,1,0:T(8,128)(2,1)S(1)} collective-permute-done((bf16[2,96,768]{2,1,0:T(8,128)(2,1)S(1)}, bf16[2,96,768]{2,1,0:T(8,128)(2,1)S(1)}, u32[]{:S(2)}, u32[]{:S(2)}) %collective-permute-start.16) | collective-permute-done | bytes 294944 | tf_op jit(solution)/shard_map/ppermute | solution.py:94
  103.7 1.7 fusion.2
  106.8 1.6 fusion.7.refs_10_
  108.5 1.7 pad_maximum_fusion.1.refs_4_
  112.6 4.5 collective-permute-start.12
  117.4 8.6 %shard_map.395 = bf16[32,112,768]{2,1,0:T(8,128)(2,1)S(1)} custom-call(s32[2]{0:T(128)S(1)} %pad_add_fusion.at, bf16[2,4,48,768]{3,2,1,0:T(8,128)(2,1)S(1)} %pad_maximum_fusion.6.refs_0_, bf16[2,4,48,768]{3,2,1,0:T(8,128)(2,1)} %collective-permute-done.18.refs_1_, bf16[2,4,48,768]{3,2,1,0:T(8,128)(2,1)S(1)} %collective-permute-done.19.refs_2_, ...), custom_call_target="tpu_custom_call" | custom-call | flops 8000000000 | bytes 100000 | tf_op jit(solution)/shard_map/pallas_call | solution.py:549
  132.1 15.2 %shard_map.397 = bf16[768,768]{1,0:T(8,128)(2,1)S(1)} custom-call(s32[768,1]{1,0:T(8,128)S(1)} %bitcast.178, s32[2,1,384]{2,1,0:T(1,128)S(1)} %broadcast_in_dim.63.row_ref, bf16[768,768]{1,0:T(8,128)(2,1)S(1)} %add_convert_fusion.3.q_ref, bf16[768,768]{1,0:T(8,128)(2,1)S(1)} %convolution_convert_fusion.k_ref, bf16[768,768]{1,0:T(8,128)(2,1)S(1)} %add_convert_fusion.2.v_ref), custom_call_target="tpu_custom_call" | custom-call | flops 15000000512 | bytes 100000 | tf_op jit(solution)/shard_map/pallas_call | solution.py:379
  149.4 3.9 collective-permute-done.7.refs_1_
  159.8 13.9 %shard_map.394 = bf16[32,192,768]{2,1,0:T(8,128)(2,1)S(1)} custom-call(s32[2]{0:T(128)S(1)} %pad_add_fusion.at, bf16[2,4,96,768]{3,2,1,0:T(8,128)(2,1)S(1)} %pad_maximum_fusion.refs_0_, bf16[2,4,96,768]{3,2,1,0:T(8,128)(2,1)S(1)} %collective-permute-done.7.refs_1_, bf16[2,4,96,768]{3,2,1,0:T(8,128)(2,1)S(1)} %collective-permute-done.8.refs_2_, ...), custom_call_target="tpu_custom_call" | custom-call | flops 8000000000 | bytes 100000 | tf_op jit(solution)/shard_map/pallas_call | solution.py:549
  173.6 2.6 slice.371
  176.6 18.3 %shard_map.398 = (bf16[768,768]{1,0:T(8,128)(2,1)S(1)}, bf16[768,3072]{1,0:T(8,128)(2,1)}, bf16[4,768,192]{2,1,0:T(8,128)(2,1)}) custom-call(s32[1]{0:T(128)} %bitcast.at, bf16[768,768]{1,0:T(8,128)(2,1)S(1)} %bitcast.176, bf16[768,768]{1,0:T(8,128)(2,1)S(1)} %bitcast.174, bf16[768,768]{1,0:T(8,128)(2,1)S(1)} %bitcast.172, bf16[768,768]{1,0:T(8,128)(2,1)S(1)} %bitcast.170, ...), custom_call_target="tpu_custom_call" | custom-call | flops 17999998976 | bytes 100000 | tf_op jit(solution)/shard_map/pallas_call | solution.py:899
  196.0 20.5 %all-gather.5.cloned.1.call-done = bf16[9728,1024]{1,0:T(8,128)(2,1)} async-done(((bf16[304,1024]{1,0:T(8,128)(2,1)}), bf16[9728,1024]{1,0:T(8,128)(2,1)}) %all-gather.5.cloned.1.call-update) | async-done | bytes 19922960 | tf_op jit(solution)/shard_map/all_gather | solution.py:1182
  217.8 1.8 slice.377
  219.6 2.7 slice.373
  227.4 44.7 %shard_map.400 = (bf16[768,1024]{1,0:T(8,128)(2,1)}, bf16[768,1024]{1,0:T(8,128)(2,1)}, bf16[768,1024]{1,0:T(8,128)(2,1)}, bf16[768,1024]{1,0:T(8,128)(2,1)}, bf...) custom-call(bf16[768,1024]{1,0:T(8,128)(2,1)} %bitcast.191, ...), custom_call_target="tpu_custom_call" | custom-call | flops 44999999488 | bytes 100000 | tf_op jit(solution)/shard_map/pallas_call | solution.py:794
  272.1 2.0 slice_bitcast_fusion.2
  275.6 13.5 %shard_map.401 = (bf16[4,8,128,512]{3,2,1,0:T(8,128)(2,1)}, bf16[4,8,128,512]{3,2,1,0:T(8,128)(2,1)}, f32[4,1024]{1,0:T(4,128)}) custom-call(s32[1]{0:T(128)} %bitcast.49.at, bf16[768,1024]{1,0:T(8,128)(2,1)} %get-tuple-element.208.refs_0_, bf16[768,1024]{1,0:T(8,128)(2,1)} %get-tuple-element.198.refs_1_, bf16[768,1024]{1,0:T(8,128)(2,1)} %get-tuple-element.199.refs_2_, ...), custom_call_target="tpu_custom_call" | custom-call | flops 12999999488 | bytes 100000 | tf_op jit(solution)/shard_map/pallas_call | solution.py:512
  289.1 10.5 %collective-permute-done.26.refs_2_ = bf16[2,96,768]{2,1,0:T(8,128)(2,1)S(1)} collective-permute-done((bf16[2,96,768]{2,1,0:T(8,128)(2,1)S(1)}, bf16[2,96,768]{2,1,0:T(8,128)(2,1)S(1)}, u32[]{:S(2)}, u32[]{:S(2)}) %collective-permute-start.26) | collective-permute-done | bytes 294944 | tf_op jit(solution)/shard_map/ppermute | solution.py:94
  300.8 2.1 shard_map.402.refs_0_
  305.9 2.0 fusion.10.refs_9_
  308.0 2.9 collective-permute-start.30
  310.9 2.4 collective-permute-start.31
  313.2 14.1 %shard_map.403 = (bf16[4,8,160,512]{3,2,1,0:T(8,128)(2,1)}, bf16[4,8,160,512]{3,2,1,0:T(8,128)(2,1)}, f32[48,1024]{1,0:T(8,128)}) custom-call(s32[1]{0:T(128)} %bitcast.49.at, bf16[768,1024]{1,0:T(8,128)(2,1)} %get-tuple-element.208.refs_0_, bf16[8,1024]{1,0:T(8,128)(2,1)} %copy-done.48, bf16[768,768]{1,0:T(8,128)(2,1)} %copy-done.5, ...), custom_call_target="tpu_custom_call" | custom-call | flops 12999999488 | bytes 100000 | tf_op jit(solution)/shard_map/pallas_call | solution.py:512
  327.3 6.4 %shard_map.404 = (bf16[2,8,64,512]{3,2,1,0:T(8,128)(2,1)}, bf16[2,8,64,512]{3,2,1,0:T(8,128)(2,1)}, bf16[2,8,64,512]{3,2,1,0:T(8,128)(2,1)}, bf16[2,8,64,512]{3,2,1,0:T(8,128)(2,1)}) custom-call(s32[2]{0:T(128)} %get-tuple-element.473.at, bf16[4,8,128,512]{3,2,1,0:T(8,128)(2,1)} %get-tuple-element.204.refs_0_, ...), custom_call_target="tpu_custom_call" | custom-call | flops 5719505408 | bytes 100000 | tf_op jit(solution)/shard_map/pallas_call | solution.py:133
  333.7 2.6 collective-permute-done.31.refs_3_
  340.1 24.3 %shard_map.405 = (bf16[4,2,192,384]{3,2,1,0:T(8,128)(2,1)}, bf16[4,2,192,384]{3,2,1,0:T(8,128)(2,1)}, f32[768,768]{1,0:T(8,128)}, bf16[768,768]{1,0:T(8,128)(2,1...) custom-call(s32[1]{0:T(128)} %bitcast.49.at, bf16[2,96,768]{2,1,0:T(8,128)(2,1)} %shard_map.402.refs_0_, ...), custom_call_target="tpu_custom_call" | custom-call | flops 24000000000 | bytes 100000 | tf_op jit(solution)/shard_map/pallas_call | solution.py:996
  365.6 3.9 shard_map.406
  371.0 2.9 collective-permute-start.38
  373.9 7.5 %shard_map.407 = (bf16[2,8,96,512]{3,2,1,0:T(8,128)(2,1)}, bf16[2,8,96,512]{3,2,1,0:T(8,128)(2,1)}, bf16[2,8,64,512]{3,2,1,0:T(8,128)(2,1)}, bf16[2,8,64,512]{3,2,1,0:T(8,128)(2,1)}) custom-call(s32[2]{0:T(128)} %get-tuple-element.473.at, bf16[4,8,160,512]{3,2,1,0:T(8,128)(2,1)} %get-tuple-element.215.refs_0_, ...), custom_call_target="tpu_custom_call" | custom-call | flops 7149381632 | bytes 100000 | tf_op jit(solution)/shard_map/pallas_call | solution.py:133
  383.1 12.5 %shard_map.408 = (bf16[768,768]{1,0:T(8,128)(2,1)}, bf16[768,768]{1,0:T(8,128)(2,1)}, bf16[768,768]{1,0:T(8,128)(2,1)}) custom-call(s32[768,1]{1,0:T(8,128)} %bitcast.179, s32[2,1,384]{2,1,0:T(1,128)} %copy-done.6, bf16[768,768]{1,0:T(8,128)(2,1)} %copy-done.27, bf16[768,768]{1,0:T(8,128)(2,1)} %copy-done.25, bf16[768,768]{1,0:T(8,128)(2,1)} %copy-done.26, ...), custom_call_target="tpu_custom_call" | custom-call | flops 12000000000 | bytes 100000 | tf_op jit(solution)/shard_map/pallas_call | solution.py:414
  396.4 2.7 shard_map.409
  399.2 12.4 %shard_map.410 = (bf16[768,768]{1,0:T(8,128)(2,1)}, bf16[768,768]{1,0:T(8,128)(2,1)}, bf16[768,768]{1,0:T(8,128)(2,1)}) custom-call(s32[768,1]{1,0:T(8,128)} %bitcast.180, s32[2,1,384]{2,1,0:T(1,128)} %copy-done.6, bf16[768,768]{1,0:T(8,128)(2,1)} %copy-done.27, ...), custom_call_target="tpu_custom_call", output_to_operand_aliasing={{0}: (6, {}), {1}: (7, {}), {2}: (8, {})} | custom-call | flops 12000000000 | bytes 100000 | tf_op jit(solution)/shard_map/pallas_call | solution.py:414
  411.6 5.4 %collective-permute-done.39.got_one = bf16[2,8,96,512]{3,2,1,0:T(8,128)(2,1)S(1)} collective-permute-done((bf16[2,8,96,512]{3,2,1,0:T(8,128)(2,1)}, bf16[2,8,96,512]{3,2,1,0:T(8,128)(2,1)S(1)}, u32[]{:S(2)}, u32[]{:S(2)}) %collective-permute-start.39) | collective-permute-done | bytes 1572896 | tf_op jit(solution)/shard_map/ppermute | solution.py:90
  418.2 4.5 shard_map.411
  425.5 2.1 shard_map.412
  428.9 10.1 %shard_map.413 = (bf16[4,2,96,384]{3,2,1,0:T(8,128)(2,1)}, bf16[4,2,96,384]{3,2,1,0:T(8,128)(2,1)}, f32[2,96,768]{2,1,0:T(8,128)}, f32[12,768]{1,0:T(8,128)}) custom-call(s32[1]{0:T(128)} %bitcast.49.at, bf16[768,768]{1,0:T(8,128)(2,1)} %get-tuple-element.274.refs_0_, bf16[768,768]{1,0:T(8,128)(2,1)} %get-tuple-element.275.refs_1_, ...), custom_call_target="tpu_custom_call" | custom-call | flops 7046050816 | bytes 100000 | tf_op jit(solution)/shard_map/pallas_call | solution.py:133
  440.9 3.0 shard_map.414
  444.6 1.8 shard_map.415
  446.4 2.9 collective-permute-start.45
  450.7 1.7 slice_bitcast_fusion.6
  452.8 2.0 collective-permute-start.52
  458.2 3.5 shard_map.416
  463.2 9.5 %collective-permute-done.47.got_one = bf16[2,2,144,384]{3,2,1,0:T(8,128)(2,1)S(1)} collective-permute-done((bf16[2,2,144,384]{3,2,1,0:T(8,128)(2,1)}, bf16[2,2,144,384]{3,2,1,0:T(8,128)(2,1)S(1)}, u32[]{:S(2)}, u32[]{:S(2)}) %collective-permute-start.47) | collective-permute-done | bytes 442400 | tf_op jit(solution)/shard_map/ppermute | solution.py:90
  474.3 2.4 shard_map.417
  476.7 6.6 %collective-permute-done.53.refs_2_ = bf16[2,160,512]{2,1,0:T(8,128)(2,1)} collective-permute-done((bf16[2,160,512]{2,1,0:T(8,128)(2,1)}, bf16[2,160,512]{2,1,0:T(8,128)(2,1)}, u32[]{:S(2)}, u32[]{:S(2)}) %collective-permute-start.53) | collective-permute-done | bytes 327712 | tf_op jit(solution)/shard_map/ppermute | solution.py:94
  483.3 2.2 collective-permute-done.54.refs_3_
  486.2 2.4 shard_map.419
  493.8 3.0 collective-permute-done.49
  497.8 2.0 shard_map.418
  506.2 1.6 slice_add_fusion
  (363 shorter events, 93.5 us)
Async XLA Ops:
  7.2 209.3 %all-gather.5.cloned.1.call-start = ((), (), s32[]{:S(2)}) async-start(), calls=%async_computation | async-start | bytes 20545536 | tf_op jit(solution)/shard_map/all_gather | solution.py:1182
  11.1 5.3 %collective-permute-start = (bf16[112,768]{1,0:T(8,128)(2,1)S(1)}, bf16[112,768]{1,0:T(8,128)(2,1)S(1)}, u32[]{:S(2)}, u32[]{:S(2)}) collective-permute-start(bf16[112,768]{1,0:T(8,128)(2,1)S(1)} %shard_map.391), channel_id=1, source_target_pairs={{0,3},{1,0},{2,1},{3,2},{4,7},{5,4},{6,5},{7,6},{8,11},{9,8},{10,9... | collective-permute-start | bytes 516104 | tf_op jit(solution)/shard_map/ppermute | solution.py:94
  11.1 13.2 %collective-permute-start.1 = (bf16[112,768]{1,0:T(8,128)(2,1)S(1)}, bf16[112,768]{1,0:T(8,128)(2,1)S(1)}, u32[]{:S(2)}, u32[]{:S(2)}) collective-permute-start(bf16[112,768]{1,0:T(8,128)(2,1)S(1)} %shard_map.391), channel_id=1, source_target_pairs={{0,2},{1,3},{2,0},{3,1},{4,6},{5,7},{6,4},{7,5},{8,10},{9,11},{10,... | collective-permute-start | bytes 516104 | tf_op jit(solution)/shard_map/ppermute | solution.py:94
  13.6 14.4 %collective-permute-start.2 = (bf16[112,768]{1,0:T(8,128)(2,1)S(1)}, bf16[112,768]{1,0:T(8,128)(2,1)S(1)}, u32[]{:S(2)}, u32[]{:S(2)}) collective-permute-start(bf16[112,768]{1,0:T(8,128)(2,1)S(1)} %shard_map.391), channel_id=1, source_target_pairs={{0,1},{1,2},{2,3},{3,0},{4,5},{5,6},{6,7},{7,4},{8,9},{9,10},{10,1... | collective-permute-start | bytes 516104 | tf_op jit(solution)/shard_map/ppermute | solution.py:94
  28.0 8.2 %collective-permute-start.3 = (bf16[192,768]{1,0:T(8,128)(2,1)S(1)}, bf16[192,768]{1,0:T(8,128)(2,1)S(1)}, u32[]{:S(2)}, u32[]{:S(2)}) collective-permute-start(bf16[192,768]{1,0:T(8,128)(2,1)S(1)} %shard_map.392), channel_id=1, source_target_pairs={{0,3},{1,0},{2,1},{3,2},{4,7},{5,4},{6,5},{7,6},{8,11},{9,8},{10,9... | collective-permute-start | bytes 884744 | tf_op jit(solution)/shard_map/ppermute | solution.py:94
  29.3 19.1 %collective-permute-start.4 = (bf16[192,768]{1,0:T(8,128)(2,1)S(1)}, bf16[192,768]{1,0:T(8,128)(2,1)S(1)}, u32[]{:S(2)}, u32[]{:S(2)}) collective-permute-start(bf16[192,768]{1,0:T(8,128)(2,1)S(1)} %shard_map.392), channel_id=1, source_target_pairs={{0,2},{1,3},{2,0},{3,1},{4,6},{5,7},{6,4},{7,5},{8,10},{9,11},{10,... | collective-permute-start | bytes 884744 | tf_op jit(solution)/shard_map/ppermute | solution.py:94
  31.4 23.4 %collective-permute-start.5 = (bf16[192,768]{1,0:T(8,128)(2,1)S(1)}, bf16[192,768]{1,0:T(8,128)(2,1)S(1)}, u32[]{:S(2)}, u32[]{:S(2)}) collective-permute-start(bf16[192,768]{1,0:T(8,128)(2,1)S(1)} %shard_map.392), channel_id=1, source_target_pairs={{0,1},{1,2},{2,3},{3,0},{4,5},{5,6},{6,7},{7,4},{8,9},{9,10},{10,1... | collective-permute-start | bytes 884744 | tf_op jit(solution)/shard_map/ppermute | solution.py:94
  32.5 24.5 %copy-start.77 = (bf16[16]{0:T(256)(128)(2,1)S(1)}, bf16[16]{0:T(256)(128)(2,1)}, u32[]{:S(2)}) copy-start(bf16[16]{0:T(256)(128)(2,1)} %param.47) | copy-start | bytes 100
  54.8 451.3 %all-gather.7.cloned.1.call-start = ((), (), s32[]{:S(2)}) async-start(), calls=%async_computation.1 | async-start | bytes 2359296 | tf_op jit(solution)/shard_map/all_gather | solution.py:1464
  55.0 77.0 %copy-start.6 = (s32[2,1,384]{2,1,0:T(1,128)}, s32[2,1,384]{2,1,0:T(1,128)S(1)}, u32[]{:S(2)}) copy-start(s32[2,1,384]{2,1,0:T(1,128)S(1)} %broadcast_in_dim.63.row_ref) | copy-start | bytes 9220
  55.2 76.8 %copy-start.4 = (s32[1,768]{0,1:T(8,128)}, s32[1,768]{0,1:T(8,128)S(1)}, u32[]{:S(2)}) copy-start(s32[1,768]{0,1:T(8,128)S(1)} %copy.112) | copy-start | bytes 9220
  58.8 8.2 %collective-permute-start.17 = (bf16[4,48,768]{2,1,0:T(8,128)(2,1)S(1)}, bf16[4,48,768]{2,1,0:T(8,128)(2,1)S(1)}, u32[]{:S(2)}, u32[]{:S(2)}) collective-permute-start(bf16[4,48,768]{2,1,0:T(8,128)(2,1)S(1)} %get-tuple-element.448), channel_id=1, source_target_pairs={{0,16},{4,20},{8,24},{12,28},{16,0},{20,4},{24,8},{28,12},{1,17},{... | collective-permute-start | bytes 884744 | tf_op jit(solution)/shard_map/ppermute | solution.py:90
  60.2 12.6 %collective-permute-start.21 = (bf16[4,64,768]{2,1,0:T(8,128)(2,1)S(1)}, bf16[4,64,768]{2,1,0:T(8,128)(2,1)S(1)}, u32[]{:S(2)}, u32[]{:S(2)}) collective-permute-start(bf16[4,64,768]{2,1,0:T(8,128)(2,1)S(1)} %get-tuple-element.440), channel_id=1, source_target_pairs={{0,8},{4,12},{8,0},{12,4},{16,24},{20,28},{24,16},{28,20},{1,9},{5... | collective-permute-start | bytes 1179656 | tf_op jit(solution)/shard_map/ppermute | solution.py:90
  61.5 13.6 %collective-permute-start.14 = (bf16[2,96,768]{2,1,0:T(8,128)(2,1)S(1)}, bf16[2,96,768]{2,1,0:T(8,128)(2,1)S(1)}, u32[]{:S(2)}, u32[]{:S(2)}) collective-permute-start(bf16[2,96,768]{2,1,0:T(8,128)(2,1)S(1)} %bitcast.213), channel_id=1, source_target_pairs={{0,3},{1,0},{2,1},{3,2},{4,7},{5,4},{6,5},{7,6},{8,11},{9,8},{10,9... | collective-permute-start | bytes 884744 | tf_op jit(solution)/shard_map/ppermute | solution.py:94
  63.2 32.0 %collective-permute-start.15 = (bf16[2,96,768]{2,1,0:T(8,128)(2,1)S(1)}, bf16[2,96,768]{2,1,0:T(8,128)(2,1)S(1)}, u32[]{:S(2)}, u32[]{:S(2)}) collective-permute-start(bf16[2,96,768]{2,1,0:T(8,128)(2,1)S(1)} %bitcast.214), channel_id=1, source_target_pairs={{0,2},{1,3},{2,0},{3,1},{4,6},{5,7},{6,4},{7,5},{8,10},{9,11},{10,... | collective-permute-start | bytes 884744 | tf_op jit(solution)/shard_map/ppermute | solution.py:94
  64.9 37.0 %collective-permute-start.16 = (bf16[2,96,768]{2,1,0:T(8,128)(2,1)S(1)}, bf16[2,96,768]{2,1,0:T(8,128)(2,1)S(1)}, u32[]{:S(2)}, u32[]{:S(2)}) collective-permute-start(bf16[2,96,768]{2,1,0:T(8,128)(2,1)S(1)} %bitcast.215), channel_id=1, source_target_pairs={{0,1},{1,2},{2,3},{3,0},{4,5},{5,6},{6,7},{7,4},{8,9},{9,10},{10,1... | collective-permute-start | bytes 884744 | tf_op jit(solution)/shard_map/ppermute | solution.py:94
  67.0 39.3 %collective-permute-start.18 = (bf16[2,4,48,768]{3,2,1,0:T(8,128)(2,1)S(1)}, bf16[2,4,48,768]{3,2,1,0:T(8,128)(2,1)}, u32[]{:S(2)}, u32[]{:S(2)}) collective-permute-start(bf16[2,4,48,768]{3,2,1,0:T(8,128)(2,1)S(1)} %pad_maximum_fusion.6.refs_0_), channel_id=1, source_target_pairs={{0,8},{4,12},{8,0},{12,4},{16,24},{20,28},{24,16},{28,20},{1,9},{5... | collective-permute-start | bytes 1769480 | tf_op jit(solution)/shard_map/ppermute | solution.py:90
  72.9 32.6 %collective-permute-start.22 = (bf16[2,4,64,768]{3,2,1,0:T(8,128)(2,1)S(1)}, bf16[2,4,64,768]{3,2,1,0:T(8,128)(2,1)S(1)}, u32[]{:S(2)}, u32[]{:S(2)}) collective-permute-start(bf16[2,4,64,768]{3,2,1,0:T(8,128)(2,1)S(1)} %pad_maximum_fusion.3.refs_4_), channel_id=1, source_target_pairs={{0,16},{4,20},{8,24},{12,28},{16,0},{20,4},{24,8},{28,12},{1,17},{... | collective-permute-start | bytes 2359304 | tf_op jit(solution)/shard_map/ppermute | solution.py:90
  75.1 31.6 %collective-permute-start.10 = (bf16[4,96,768]{2,1,0:T(8,128)(2,1)}, bf16[4,96,768]{2,1,0:T(8,128)(2,1)}, u32[]{:S(2)}, u32[]{:S(2)}) collective-permute-start(bf16[4,96,768]{2,1,0:T(8,128)(2,1)} %get-tuple-element.422), channel_id=1, source_target_pairs={{0,8},{4,12},{8,0},{12,4},{16,24},{20,28},{24,16},{28,20},{1,9},{5... | collective-permute-start | bytes 1769480 | tf_op jit(solution)/shard_map/ppermute | solution.py:90
  95.1 16.3 %collective-permute-start.6 = (bf16[4,96,768]{2,1,0:T(8,128)(2,1)}, bf16[4,96,768]{2,1,0:T(8,128)(2,1)}, u32[]{:S(2)}, u32[]{:S(2)}) collective-permute-start(bf16[4,96,768]{2,1,0:T(8,128)(2,1)} %get-tuple-element.424), channel_id=1, source_target_pairs={{0,16},{4,20},{8,24},{12,28},{16,0},{20,4},{24,8},{28,12},{1,17},{... | collective-permute-start | bytes 1769480 | tf_op jit(solution)/shard_map/ppermute | solution.py:90
  101.9 15.3 %collective-permute-start.23 = (bf16[2,4,64,768]{3,2,1,0:T(8,128)(2,1)S(1)}, bf16[2,4,64,768]{3,2,1,0:T(8,128)(2,1)S(1)}, u32[]{:S(2)}, u32[]{:S(2)}) collective-permute-start(bf16[2,4,64,768]{3,2,1,0:T(8,128)(2,1)S(1)} %pad_maximum_fusion.3.refs_4_), channel_id=1, source_target_pairs={{0,4},{4,0},{8,12},{12,8},{16,20},{20,16},{24,28},{28,24},{1,5},{5... | collective-permute-start | bytes 2359304 | tf_op jit(solution)/shard_map/ppermute | solution.py:90
  105.4 12.0 %collective-permute-start.24 = (bf16[2,4,64,768]{3,2,1,0:T(8,128)(2,1)S(1)}, bf16[2,4,64,768]{3,2,1,0:T(8,128)(2,1)}, u32[]{:S(2)}, u32[]{:S(2)}) collective-permute-start(bf16[2,4,64,768]{3,2,1,0:T(8,128)(2,1)S(1)} %collective-permute-done.22.refs_5_), channel_id=1, source_target_pairs={{0,4},{4,0},{8,12},{12,8},{16,20},{20,16},{24,28},{28,24},{1,5},{5... | collective-permute-start | bytes 2359304 | tf_op jit(solution)/shard_map/ppermute | solution.py:90
  106.3 6.3 %collective-permute-start.19 = (bf16[2,4,48,768]{3,2,1,0:T(8,128)(2,1)S(1)}, bf16[2,4,48,768]{3,2,1,0:T(8,128)(2,1)S(1)}, u32[]{:S(2)}, u32[]{:S(2)}) collective-permute-start(bf16[2,4,48,768]{3,2,1,0:T(8,128)(2,1)S(1)} %pad_maximum_fusion.6.refs_0_), channel_id=1, source_target_pairs={{0,4},{4,0},{8,12},{12,8},{16,20},{20,16},{24,28},{28,24},{1,5},{5... | collective-permute-start | bytes 1769480 | tf_op jit(solution)/shard_map/ppermute | solution.py:90
  106.8 10.4 %collective-permute-start.20 = (bf16[2,4,48,768]{3,2,1,0:T(8,128)(2,1)}, bf16[2,4,48,768]{3,2,1,0:T(8,128)(2,1)S(1)}, u32[]{:S(2)}, u32[]{:S(2)}) collective-permute-start(bf16[2,4,48,768]{3,2,1,0:T(8,128)(2,1)} %collective-permute-done.18.refs_1_), channel_id=1, source_target_pairs={{0,4},{4,0},{8,12},{12,8},{16,20},{20,16},{24,28},{28,24},{1,5},{5... | collective-permute-start | bytes 1769480 | tf_op jit(solution)/shard_map/ppermute | solution.py:90
  108.5 49.9 %copy-start.31 = (f32[768,768]{1,0:T(8,128)}, f32[768,768]{1,0:T(8,128)S(1)}, u32[]{:S(2)}) copy-start(f32[768,768]{1,0:T(8,128)S(1)} %fusion.7.refs_10_) | copy-start | bytes 7077892
  111.4 37.5 %collective-permute-start.11 = (bf16[2,4,96,768]{3,2,1,0:T(8,128)(2,1)S(1)}, bf16[2,4,96,768]{3,2,1,0:T(8,128)(2,1)S(1)}, u32[]{:S(2)}, u32[]{:S(2)}) collective-permute-start(bf16[2,4,96,768]{3,2,1,0:T(8,128)(2,1)S(1)} %pad_maximum_fusion.1.refs_4_), channel_id=1, source_target_pairs={{0,16},{4,20},{8,24},{12,28},{16,0},{20,4},{24,8},{28,12},{1,17},{... | collective-permute-start | bytes 3538952 | tf_op jit(solution)/shard_map/ppermute | solution.py:90
  112.6 47.1 %collective-permute-start.12 = (bf16[2,4,96,768]{3,2,1,0:T(8,128)(2,1)S(1)}, bf16[2,4,96,768]{3,2,1,0:T(8,128)(2,1)S(1)}, u32[]{:S(2)}, u32[]{:S(2)}) collective-permute-start(bf16[2,4,96,768]{3,2,1,0:T(8,128)(2,1)S(1)} %pad_maximum_fusion.1.refs_4_), channel_id=1, source_target_pairs={{0,4},{4,0},{8,12},{12,8},{16,20},{20,16},{24,28},{28,24},{1,5},{5... | collective-permute-start | bytes 3538952 | tf_op jit(solution)/shard_map/ppermute | solution.py:90
  117.2 36.1 %collective-permute-start.7 = (bf16[2,4,96,768]{3,2,1,0:T(8,128)(2,1)S(1)}, bf16[2,4,96,768]{3,2,1,0:T(8,128)(2,1)S(1)}, u32[]{:S(2)}, u32[]{:S(2)}) collective-permute-start(bf16[2,4,96,768]{3,2,1,0:T(8,128)(2,1)S(1)} %pad_maximum_fusion.refs_0_), channel_id=1, source_target_pairs={{0,8},{4,12},{8,0},{12,4},{16,24},{20,28},{24,16},{28,20},{1,9},{5... | collective-permute-start | bytes 3538952 | tf_op jit(solution)/shard_map/ppermute | solution.py:90
  117.2 42.5 %collective-permute-start.8 = (bf16[2,4,96,768]{3,2,1,0:T(8,128)(2,1)S(1)}, bf16[2,4,96,768]{3,2,1,0:T(8,128)(2,1)S(1)}, u32[]{:S(2)}, u32[]{:S(2)}) collective-permute-start(bf16[2,4,96,768]{3,2,1,0:T(8,128)(2,1)S(1)} %pad_maximum_fusion.refs_0_), channel_id=1, source_target_pairs={{0,4},{4,0},{8,12},{12,8},{16,20},{20,16},{24,28},{28,24},{1,5},{5... | collective-permute-start | bytes 3538952 | tf_op jit(solution)/shard_map/ppermute | solution.py:90
  149.0 10.8 %collective-permute-start.13 = (bf16[2,4,96,768]{3,2,1,0:T(8,128)(2,1)S(1)}, bf16[2,4,96,768]{3,2,1,0:T(8,128)(2,1)S(1)}, u32[]{:S(2)}, u32[]{:S(2)}) collective-permute-start(bf16[2,4,96,768]{3,2,1,0:T(8,128)(2,1)S(1)} %collective-permute-done.11.refs_5_), channel_id=1, source_target_pairs={{0,4},{4,0},{8,12},{12,8},{16,20},{20,16},{24,28},{28,24},{1,5},{5... | collective-permute-start | bytes 3538952 | tf_op jit(solution)/shard_map/ppermute | solution.py:90
  153.3 6.4 %collective-permute-start.9 = (bf16[2,4,96,768]{3,2,1,0:T(8,128)(2,1)S(1)}, bf16[2,4,96,768]{3,2,1,0:T(8,128)(2,1)S(1)}, u32[]{:S(2)}, u32[]{:S(2)}) collective-permute-start(bf16[2,4,96,768]{3,2,1,0:T(8,128)(2,1)S(1)} %collective-permute-done.7.refs_1_), channel_id=1, source_target_pairs={{0,4},{4,0},{8,12},{12,8},{16,20},{20,16},{24,28},{28,24},{1,5},{5... | collective-permute-start | bytes 3538952 | tf_op jit(solution)/shard_map/ppermute | solution.py:90
  226.4 45.7 %copy-start.48 = (bf16[8,1024]{1,0:T(8,128)(2,1)}, bf16[8,1024]{1,0:T(8,128)(2,1)S(1)}, u32[]{:S(2)}) copy-start(bf16[8,1024]{1,0:T(8,128)(2,1)S(1)} %get-tuple-element.470.refs_1_) | copy-start | bytes 49156
  274.2 14.9 %collective-permute-start.25 = (bf16[2,96,768]{2,1,0:T(8,128)(2,1)S(1)}, bf16[2,96,768]{2,1,0:T(8,128)(2,1)S(1)}, u32[]{:S(2)}, u32[]{:S(2)}) collective-permute-start(bf16[2,96,768]{2,1,0:T(8,128)(2,1)S(1)} %get-tuple-element.419), channel_id=1, source_target_pairs={{0,1},{1,2},{2,3},{3,0},{4,5},{5,6},{6,7},{7,4},{8,9},{9,10},{10,1... | collective-permute-start | bytes 884744 | tf_op jit(solution)/shard_map/ppermute | solution.py:94
  274.2 25.4 %collective-permute-start.26 = (bf16[2,96,768]{2,1,0:T(8,128)(2,1)S(1)}, bf16[2,96,768]{2,1,0:T(8,128)(2,1)S(1)}, u32[]{:S(2)}, u32[]{:S(2)}) collective-permute-start(bf16[2,96,768]{2,1,0:T(8,128)(2,1)S(1)} %get-tuple-element.418), channel_id=1, source_target_pairs={{0,2},{1,3},{2,0},{3,1},{4,6},{5,7},{6,4},{7,5},{8,10},{9,11},{10,... | collective-permute-start | bytes 884744 | tf_op jit(solution)/shard_map/ppermute | solution.py:94
  274.2 26.6 %collective-permute-start.27 = (bf16[2,96,768]{2,1,0:T(8,128)(2,1)S(1)}, bf16[2,96,768]{2,1,0:T(8,128)(2,1)}, u32[]{:S(2)}, u32[]{:S(2)}) collective-permute-start(bf16[2,96,768]{2,1,0:T(8,128)(2,1)S(1)} %get-tuple-element.417), channel_id=1, source_target_pairs={{0,3},{1,0},{2,1},{3,2},{4,7},{5,4},{6,5},{7,6},{8,11},{9,8},{10,9... | collective-permute-start | bytes 884744 | tf_op jit(solution)/shard_map/ppermute | solution.py:94
  302.9 24.4 %collective-permute-start.28 = (bf16[4,8,128,512]{3,2,1,0:T(8,128)(2,1)}, bf16[4,8,128,512]{3,2,1,0:T(8,128)(2,1)}, u32[]{:S(2)}, u32[]{:S(2)}) collective-permute-start(bf16[4,8,128,512]{3,2,1,0:T(8,128)(2,1)} %get-tuple-element.217), channel_id=1, source_target_pairs={{0,4},{4,0},{8,12},{12,8},{16,20},{20,16},{24,28},{28,24},{1,5},{5... | collective-permute-start | bytes 12582920 | tf_op jit(solution)/shard_map/ppermute | solution.py:90
  308.0 25.7 %collective-permute-start.29 = (bf16[2,96,768]{2,1,0:T(8,128)(2,1)S(1)}, bf16[2,96,768]{2,1,0:T(8,128)(2,1)S(1)}, u32[]{:S(2)}, u32[]{:S(2)}) collective-permute-start(bf16[2,96,768]{2,1,0:T(8,128)(2,1)S(1)} %copy-done.68), channel_id=1, source_target_pairs={{0,3},{1,0},{2,1},{3,2},{4,7},{5,4},{6,5},{7,6},{8,11},{9,8},{10,9... | collective-permute-start | bytes 884744 | tf_op jit(solution)/shard_map/ppermute | solution.py:94
  308.0 25.7 %collective-permute-start.30 = (bf16[2,96,768]{2,1,0:T(8,128)(2,1)S(1)}, bf16[2,96,768]{2,1,0:T(8,128)(2,1)S(1)}, u32[]{:S(2)}, u32[]{:S(2)}) collective-permute-start(bf16[2,96,768]{2,1,0:T(8,128)(2,1)S(1)} %copy-done.68), channel_id=1, source_target_pairs={{0,2},{1,3},{2,0},{3,1},{4,6},{5,7},{6,4},{7,5},{8,10},{9,11},{10,... | collective-permute-start | bytes 884744 | tf_op jit(solution)/shard_map/ppermute | solution.py:94
  310.9 25.4 %collective-permute-start.31 = (bf16[2,96,768]{2,1,0:T(8,128)(2,1)S(1)}, bf16[2,96,768]{2,1,0:T(8,128)(2,1)S(1)}, u32[]{:S(2)}, u32[]{:S(2)}) collective-permute-start(bf16[2,96,768]{2,1,0:T(8,128)(2,1)S(1)} %copy-done.68), channel_id=1, source_target_pairs={{0,1},{1,2},{2,3},{3,0},{4,5},{5,6},{6,7},{7,4},{8,9},{9,10},{10,1... | collective-permute-start | bytes 884744 | tf_op jit(solution)/shard_map/ppermute | solution.py:94
  336.3 37.6 %collective-permute-start.35 = (bf16[4,8,160,512]{3,2,1,0:T(8,128)(2,1)}, bf16[4,8,160,512]{3,2,1,0:T(8,128)(2,1)}, u32[]{:S(2)}, u32[]{:S(2)}) collective-permute-start(bf16[4,8,160,512]{3,2,1,0:T(8,128)(2,1)} %get-tuple-element.243), channel_id=1, source_target_pairs={{0,4},{4,0},{8,12},{12,8},{16,20},{20,16},{24,28},{28,24},{1,5},{5... | collective-permute-start | bytes 15728648 | tf_op jit(solution)/shard_map/ppermute | solution.py:90
  338.0 31.5 %collective-permute-start.34 = (f32[48,1024]{1,0:T(8,128)S(1)}, f32[48,1024]{1,0:T(8,128)S(1)}, u32[]{:S(2)}, u32[]{:S(2)}) collective-permute-start(f32[48,1024]{1,0:T(8,128)S(1)} %copy-done.43), channel_id=1, source_target_pairs={{0,1},{1,0},{2,3},{3,2},{4,5},{5,4},{6,7},{7,6},{8,9},{9,8},{10,11... | collective-permute-start | bytes 589832 | tf_op jit(solution)/shard_map/ppermute | solution.py:98
  338.5 25.8 %collective-permute-start.32 = (bf16[2,8,64,512]{3,2,1,0:T(8,128)(2,1)}, bf16[2,8,64,512]{3,2,1,0:T(8,128)(2,1)S(1)}, u32[]{:S(2)}, u32[]{:S(2)}) collective-permute-start(bf16[2,8,64,512]{3,2,1,0:T(8,128)(2,1)} %get-tuple-element.232), channel_id=1, source_target_pairs={{0,16},{4,20},{8,24},{12,28},{16,0},{20,4},{24,8},{28,12},{1,17},{... | collective-permute-start | bytes 3145736 | tf_op jit(solution)/shard_map/ppermute | solution.py:90
  339.7 24.6 %collective-permute-start.33 = (bf16[2,8,64,512]{3,2,1,0:T(8,128)(2,1)}, bf16[2,8,64,512]{3,2,1,0:T(8,128)(2,1)S(1)}, u32[]{:S(2)}, u32[]{:S(2)}) collective-permute-start(bf16[2,8,64,512]{3,2,1,0:T(8,128)(2,1)} %get-tuple-element.233), channel_id=1, source_target_pairs={{0,8},{4,12},{8,0},{12,4},{16,24},{20,28},{24,16},{28,20},{1,9},{5... | collective-permute-start | bytes 3145736 | tf_op jit(solution)/shard_map/ppermute | solution.py:90
  369.6 26.0 %collective-permute-start.36 = (bf16[1,8,64,512]{3,2,1,0:T(8,128)(2,1)}, bf16[1,8,64,512]{3,2,1,0:T(8,128)(2,1)S(1)}, u32[]{:S(2)}, u32[]{:S(2)}) collective-permute-start(bf16[1,8,64,512]{3,2,1,0:T(8,128)(2,1)} %get-tuple-element.253), channel_id=1, source_target_pairs={{0,8},{4,12},{8,0},{12,4},{16,24},{20,28},{24,16},{28,20},{1,9},{5... | collective-permute-start | bytes 1572872 | tf_op jit(solution)/shard_map/ppermute | solution.py:90
  370.8 24.8 %collective-permute-start.37 = (bf16[1,8,64,512]{3,2,1,0:T(8,128)(2,1)}, bf16[1,8,64,512]{3,2,1,0:T(8,128)(2,1)}, u32[]{:S(2)}, u32[]{:S(2)}) collective-permute-start(bf16[1,8,64,512]{3,2,1,0:T(8,128)(2,1)} %get-tuple-element.254), channel_id=1, source_target_pairs={{0,16},{4,20},{8,24},{12,28},{16,0},{20,4},{24,8},{28,12},{1,17},{... | collective-permute-start | bytes 1572872 | tf_op jit(solution)/shard_map/ppermute | solution.py:90
  371.0 28.1 %collective-permute-start.38 = (f32[48,1024]{1,0:T(8,128)S(1)}, f32[48,1024]{1,0:T(8,128)S(1)}, u32[]{:S(2)}, u32[]{:S(2)}) collective-permute-start(f32[48,1024]{1,0:T(8,128)S(1)} %add.295), channel_id=1, source_target_pairs={{0,2},{1,3},{2,0},{3,1},{4,6},{5,7},{6,4},{7,5},{8,10},{9,11},{10,... | collective-permute-start | bytes 589832 | tf_op jit(solution)/shard_map/ppermute | solution.py:98
  381.4 35.7 %collective-permute-start.39 = (bf16[2,8,96,512]{3,2,1,0:T(8,128)(2,1)}, bf16[2,8,96,512]{3,2,1,0:T(8,128)(2,1)S(1)}, u32[]{:S(2)}, u32[]{:S(2)}) collective-permute-start(bf16[2,8,96,512]{3,2,1,0:T(8,128)(2,1)} %get-tuple-element.263), channel_id=1, source_target_pairs={{0,16},{4,20},{8,24},{12,28},{16,0},{20,4},{24,8},{28,12},{1,17},{... | collective-permute-start | bytes 4718600 | tf_op jit(solution)/shard_map/ppermute | solution.py:90
  382.6 29.0 %collective-permute-start.40 = (bf16[2,8,64,512]{3,2,1,0:T(8,128)(2,1)}, bf16[2,8,64,512]{3,2,1,0:T(8,128)(2,1)S(1)}, u32[]{:S(2)}, u32[]{:S(2)}) collective-permute-start(bf16[2,8,64,512]{3,2,1,0:T(8,128)(2,1)} %get-tuple-element.264), channel_id=1, source_target_pairs={{0,8},{4,12},{8,0},{12,4},{16,24},{20,28},{24,16},{28,20},{1,9},{5... | collective-permute-start | bytes 3145736 | tf_op jit(solution)/shard_map/ppermute | solution.py:90
  399.1 25.6 %collective-permute-start.41 = (bf16[2,2,128,512]{3,2,1,0:T(8,128)(2,1)}, bf16[2,2,128,512]{3,2,1,0:T(8,128)(2,1)S(1)}, u32[]{:S(2)}, u32[]{:S(2)}) collective-permute-start(bf16[2,2,128,512]{3,2,1,0:T(8,128)(2,1)} %get-tuple-element.271), channel_id=1, source_target_pairs={{0,2},{1,3},{2,0},{3,1},{4,6},{5,7},{6,4},{7,5},{8,10},{9,11},{10,... | collective-permute-start | bytes 1572872 | tf_op jit(solution)/shard_map/ppermute | solution.py:98
  422.7 17.3 %collective-permute-start.42 = (bf16[1,8,96,512]{3,2,1,0:T(8,128)(2,1)}, bf16[1,8,96,512]{3,2,1,0:T(8,128)(2,1)S(1)}, u32[]{:S(2)}, u32[]{:S(2)}) collective-permute-start(bf16[1,8,96,512]{3,2,1,0:T(8,128)(2,1)} %get-tuple-element.289), channel_id=1, source_target_pairs={{0,8},{4,12},{8,0},{12,4},{16,24},{20,28},{24,16},{28,20},{1,9},{5... | collective-permute-start | bytes 2359304 | tf_op jit(solution)/shard_map/ppermute | solution.py:90
  424.4 14.6 %collective-permute-start.43 = (bf16[1,8,64,512]{3,2,1,0:T(8,128)(2,1)}, bf16[1,8,64,512]{3,2,1,0:T(8,128)(2,1)S(1)}, u32[]{:S(2)}, u32[]{:S(2)}) collective-permute-start(bf16[1,8,64,512]{3,2,1,0:T(8,128)(2,1)} %get-tuple-element.290), channel_id=1, source_target_pairs={{0,16},{4,20},{8,24},{12,28},{16,0},{20,4},{24,8},{28,12},{1,17},{... | collective-permute-start | bytes 1572872 | tf_op jit(solution)/shard_map/ppermute | solution.py:90
  427.6 16.3 %collective-permute-start.44 = (bf16[2,128,512]{2,1,0:T(8,128)(2,1)}, bf16[2,128,512]{2,1,0:T(8,128)(2,1)S(1)}, u32[]{:S(2)}, u32[]{:S(2)}) collective-permute-start(bf16[2,128,512]{2,1,0:T(8,128)(2,1)} %get-tuple-element.294), channel_id=1, source_target_pairs={{0,1},{1,0},{2,3},{3,2},{4,5},{5,4},{6,7},{7,6},{8,9},{9,8},{10,11... | collective-permute-start | bytes 786440 | tf_op jit(solution)/shard_map/ppermute | solution.py:98
  446.4 10.8 %collective-permute-start.45 = (bf16[4,2,192,384]{3,2,1,0:T(8,128)(2,1)S(1)}, bf16[4,2,192,384]{3,2,1,0:T(8,128)(2,1)S(1)}, u32[]{:S(2)}, u32[]{:S(2)}) collective-permute-start(bf16[4,2,192,384]{3,2,1,0:T(8,128)(2,1)S(1)} %copy-done.54), channel_id=1, source_target_pairs={{0,4},{4,0},{8,12},{12,8},{16,20},{20,16},{24,28},{28,24},{1,5},{5... | collective-permute-start | bytes 3538952 | tf_op jit(solution)/shard_map/ppermute | solution.py:90
  449.3 6.6 %collective-permute-start.46 = (bf16[4,2,96,384]{3,2,1,0:T(8,128)(2,1)S(1)}, bf16[4,2,96,384]{3,2,1,0:T(8,128)(2,1)}, u32[]{:S(2)}, u32[]{:S(2)}) collective-permute-start(bf16[4,2,96,384]{3,2,1,0:T(8,128)(2,1)S(1)} %copy-done.60), channel_id=1, source_target_pairs={{0,4},{4,0},{8,12},{12,8},{16,20},{20,16},{24,28},{28,24},{1,5},{5... | collective-permute-start | bytes 1769480 | tf_op jit(solution)/shard_map/ppermute | solution.py:90
  452.4 9.5 %collective-permute-start.56 = (bf16[128,512]{1,0:T(8,128)(2,1)}, bf16[128,512]{1,0:T(8,128)(2,1)S(1)}, u32[]{:S(2)}, u32[]{:S(2)}) collective-permute-start(bf16[128,512]{1,0:T(8,128)(2,1)} %get-tuple-element.296), channel_id=1, source_target_pairs={{0,4},{4,0},{8,12},{12,8},{16,20},{20,16},{24,28},{28,24},{1,5},{5... | collective-permute-start | bytes 393224 | tf_op jit(solution)/shard_map/ppermute | solution.py:90
  452.8 23.8 %collective-permute-start.52 = (bf16[2,160,512]{2,1,0:T(8,128)(2,1)}, bf16[2,160,512]{2,1,0:T(8,128)(2,1)}, u32[]{:S(2)}, u32[]{:S(2)}) collective-permute-start(bf16[2,160,512]{2,1,0:T(8,128)(2,1)} %get-tuple-element.320), channel_id=1, source_target_pairs={{0,1},{1,2},{2,3},{3,0},{4,5},{5,6},{6,7},{7,4},{8,9},{9,10},{10,1... | collective-permute-start | bytes 983048 | tf_op jit(solution)/shard_map/ppermute | solution.py:94
  454.8 28.4 %collective-permute-start.53 = (bf16[2,160,512]{2,1,0:T(8,128)(2,1)}, bf16[2,160,512]{2,1,0:T(8,128)(2,1)}, u32[]{:S(2)}, u32[]{:S(2)}) collective-permute-start(bf16[2,160,512]{2,1,0:T(8,128)(2,1)} %get-tuple-element.321), channel_id=1, source_target_pairs={{0,2},{1,3},{2,0},{3,1},{4,6},{5,7},{6,4},{7,5},{8,10},{9,11},{10,... | collective-permute-start | bytes 983048 | tf_op jit(solution)/shard_map/ppermute | solution.py:94
  455.9 29.5 %collective-permute-start.54 = (bf16[2,160,512]{2,1,0:T(8,128)(2,1)S(1)}, bf16[2,160,512]{2,1,0:T(8,128)(2,1)S(1)}, u32[]{:S(2)}, u32[]{:S(2)}) collective-permute-start(bf16[2,160,512]{2,1,0:T(8,128)(2,1)S(1)} %copy-done.66), channel_id=1, source_target_pairs={{0,3},{1,0},{2,1},{3,2},{4,7},{5,4},{6,5},{7,6},{8,11},{9,8},{10,9... | collective-permute-start | bytes 983048 | tf_op jit(solution)/shard_map/ppermute | solution.py:94
  461.7 11.0 %collective-permute-start.47 = (bf16[2,2,144,384]{3,2,1,0:T(8,128)(2,1)}, bf16[2,2,144,384]{3,2,1,0:T(8,128)(2,1)S(1)}, u32[]{:S(2)}, u32[]{:S(2)}) collective-permute-start(bf16[2,2,144,384]{3,2,1,0:T(8,128)(2,1)} %get-tuple-element.308), channel_id=1, source_target_pairs={{0,16},{4,20},{8,24},{12,28},{16,0},{20,4},{24,8},{28,12},{1,17},{... | collective-permute-start | bytes 1327112 | tf_op jit(solution)/shard_map/ppermute | solution.py:90
  461.9 10.8 %collective-permute-start.48 = (bf16[2,2,144,384]{3,2,1,0:T(8,128)(2,1)}, bf16[2,2,144,384]{3,2,1,0:T(8,128)(2,1)S(1)}, u32[]{:S(2)}, u32[]{:S(2)}) collective-permute-start(bf16[2,2,144,384]{3,2,1,0:T(8,128)(2,1)} %get-tuple-element.309), channel_id=1, source_target_pairs={{0,8},{4,12},{8,0},{12,4},{16,24},{20,28},{24,16},{28,20},{1,9},{5... | collective-permute-start | bytes 1327112 | tf_op jit(solution)/shard_map/ppermute | solution.py:90
  488.6 2.7 collective-permute-start.55
  489.8 7.0 %collective-permute-start.49 = (bf16[1,2,144,384]{3,2,1,0:T(8,128)(2,1)S(1)}, bf16[1,2,144,384]{3,2,1,0:T(8,128)(2,1)S(1)}, u32[]{:S(2)}, u32[]{:S(2)}) collective-permute-start(bf16[1,2,144,384]{3,2,1,0:T(8,128)(2,1)S(1)} %copy-done.76), channel_id=1, source_target_pairs={{0,8},{4,12},{8,0},{12,4},{16,24},{20,28},{24,16},{28,20},{1,9},{5... | collective-permute-start | bytes 663560 | tf_op jit(solution)/shard_map/ppermute | solution.py:90
  490.3 6.7 %collective-permute-start.50 = (bf16[1,2,144,384]{3,2,1,0:T(8,128)(2,1)S(1)}, bf16[1,2,144,384]{3,2,1,0:T(8,128)(2,1)S(1)}, u32[]{:S(2)}, u32[]{:S(2)}) collective-permute-start(bf16[1,2,144,384]{3,2,1,0:T(8,128)(2,1)S(1)} %copy-done.75), channel_id=1, source_target_pairs={{0,16},{4,20},{8,24},{12,28},{16,0},{20,4},{24,8},{28,12},{1,17},{... | collective-permute-start | bytes 663560 | tf_op jit(solution)/shard_map/ppermute | solution.py:90
  499.8 2.5 collective-permute-start.51
  (73 other events, 600.2 us)
Sparse Core Ops, SparseCore 0:
  54.9 161.5 all-gather.4
  450.8 30.7 all-gather.6

commit v5 on v4

--- a/solution.py
+++ b/solution.py
@@ -716,7 +716,7 @@
 SQUARES = ("shift", "scale", "gate", "time2", "one", "two", "fshift", "fscale")
 HEAD_OUT = (
     "gated", "mlp_in", "inner_act", "fshift", "fscale", "two", "one", "shift", "scale", "gate",
-    "cond", "condition",
+    "cond",
 )
 HEAD_SUMS = (
     ("input", CHANNELS), ("output", CHANNELS), ("embedded", 8), ("gain", 1), ("entry", 1),
@@ -724,9 +724,10 @@
 )
 
 
-def head_kernel(pack, w_cond, w_input, w_output, head_bias, gain, out_bias, embedded, values, k):
+def head_kernel(pack, w_cond, w_input, w_output, head_bias, gain, out_bias, embedded, values, k, cut):
     rows = values[0].shape[0]
-    step = 256
+    micros, own = cut
+    step = rows // micros
     world = pack.shape[0]
     used = [i for i, name in enumerate(SQUARES) if name != "time2"]
     height = sum(n for _, n in HEAD_SUMS)
@@ -738,7 +739,8 @@
         pack_ref = refs[len(smalls)]
         tiles = refs[len(smalls) + 1 :][:4]
         outs = refs[len(smalls) + 5 :][: len(HEAD_OUT)]
-        sums_ref, buffer, sems = refs[len(smalls) + 5 + len(HEAD_OUT) :]
+        rest = refs[len(smalls) + 5 + len(HEAD_OUT) :]
+        chunks, (sums_ref, buffer, sems) = rest[:-3], rest[-3:]
         first = pl.program_id(0) == 0
 
         def fetch(n):
@@ -776,6 +778,8 @@
         )
         for name, ref in zip(HEAD_OUT, outs):
             ref[...] = out[name]
+        for n, ref in enumerate(chunks):
+            ref[0] = out["condition"][n * own : (n + 1) * own]
 
         @pl.when(first)
         def _():
@@ -790,18 +794,20 @@
     def tall(width):
         return pl.BlockSpec((step, width), lambda i: (i, 0))
 
-    widths = [D if name == "condition" else WIDTH for name in HEAD_OUT]
+    count = step // own
     *outs, sums = pl.pallas_call(
         body,
         grid=(rows // step,),
-        out_shape=[low_shape(rows, w) for w in widths]
+        out_shape=[low_shape(rows, WIDTH)] * len(HEAD_OUT)
+        + [low_shape(micros, own, D)] * count
         + [jax.ShapeDtypeStruct((height, WIDTH), jnp.float32)],
         in_specs=[
             pl.BlockSpec(v.shape, lambda i: (0, 0), pipeline_mode=pl.Buffered(1)) for v in smalls
         ]
         + [pl.BlockSpec(memory_space=pl.ANY)]
         + [tall(v.shape[1]) for v in values],
-        out_specs=[tall(w) for w in widths]
+        out_specs=[tall(WIDTH)] * len(HEAD_OUT)
+        + [pl.BlockSpec((1, own, D), lambda i: (i, 0, 0))] * count
         + [pl.BlockSpec((height, WIDTH), lambda i: (0, 0))],
         scratch_shapes=[
             pltpu.VMEM((len(used), world, k, WIDTH), jnp.bfloat16),
@@ -810,7 +816,7 @@
         compiler_params=pltpu.CompilerParams(vmem_limit_bytes=60 * MIB),
         cost_estimate=cost(45.0),
     )(*smalls, pack, *values)
-    return dict(zip(HEAD_OUT, outs)), sums
+    return dict(zip(HEAD_OUT, outs)), outs[len(HEAD_OUT) :], sums
 
 
 def pack_block_grads(pairs, core, dp_size):
@@ -822,7 +828,7 @@
         for left_side, right_side in pairs:
             for at in range(0, right_side.shape[1], D):
                 part = lax.dynamic_slice_in_dim(right_side, at + c * half, half, 1)
-                part = weight_grad(left_side, part).astype(jnp.bfloat16)
+                part = product(left_side, part).astype(jnp.bfloat16)
                 parts.append(part.reshape(count, 2, -1, half))
         packs.append(jnp.concatenate(parts, axis=2))
     return packs
@@ -875,11 +881,11 @@
         active, slope = step_of(hidden[...] + bias_ref[...])
         slope_ref[...] = slope
         part = product(active, down_ref[...])
-        source = lax.broadcasted_iota(jnp.int32, (per, width), 0)
-        target = lax.broadcasted_iota(jnp.int32, (per, width), 1)
+        source = lax.broadcasted_iota(jnp.int32, (width, per), 1)
+        target = lax.broadcasted_iota(jnp.int32, (width, per), 0)
         wanted = (target // k * copy_size + at[0]) * k + target % k
         one_hot = (source == wanted).astype(bf16)
-        chosen_ref[0] = product(active, one_hot).astype(bf16)
+        chosen_ref[0] = dot1(one_hot, active).astype(bf16)
 
         @pl.when(step == 0)
         def _():
@@ -899,7 +905,7 @@
     out, slope, chosen = pl.pallas_call(
         body,
         grid=(steps,),
-        out_shape=[low_shape(rows, D), low_shape(rows, per * steps), low_shape(steps, rows, width)],
+        out_shape=[low_shape(rows, D), low_shape(rows, per * steps), low_shape(steps, width, rows)],
         in_specs=[pl.BlockSpec(memory_space=pltpu.SMEM)]
         + [full(v) for v in (*ups, second_in, middle)]
         + [
@@ -910,7 +916,7 @@
         out_specs=[
             pl.BlockSpec((rows, D), lambda j: (0, 0)),
             pl.BlockSpec((rows, per), lambda j: (0, j)),
-            pl.BlockSpec((1, rows, width), lambda j: (j, 0, 0)),
+            pl.BlockSpec((1, width, rows), lambda j: (j, 0, 0)),
         ],
         scratch_shapes=[pltpu.VMEM((rows, D), f32), pltpu.VMEM((rows, per), f32)],
         compiler_params=pltpu.CompilerParams(vmem_limit_bytes=48 * MIB),
@@ -924,7 +930,7 @@
     micros, own, _ = pieces[0].shape
     rows = micros * own * len(pieces)
     steps = len(ups)
-    k = lefts[0].shape[1] // dp_size
+    k = lefts[0].shape[0] // dp_size
     k_down = w_down.shape[0] // (dp_size * len(pieces))
     if not kernels:
         grad = jnp.stack(pieces, axis=1).reshape(rows, D)
@@ -954,7 +960,7 @@
                     grad[start : start + own] = ref[m]
             for n in range(steps):
                 here = pl.ds(n * dp_size // (2 * steps), dp_size // (2 * steps))
-                part = dot0(left_down[n], grad[...])
+                part = product(left_down[n], grad[...])
                 put_halves(first, sent.at[here], kept.at[here], steps * k, part)
             total[...] = jnp.zeros_like(total)
 
@@ -962,7 +968,7 @@
         hidden = hidden.astype(bf16)
         ones = jnp.ones((8, rows), bf16)
         hidden_sums[0] = jnp.dot(ones, hidden, preferred_element_type=f32)
-        up_grad = dot0(left_up[...], hidden)
+        up_grad = product(left_up[...], hidden)
         for n in range(steps):
 
             @pl.when(step == n)
@@ -1031,7 +1037,7 @@
         pairs = [(lefts[0], g) for g in grads] + [(lefts[1], low)]
         return *pack_block_grads(pairs, core, dp_size), input_grad, small
 
-    k = lefts[0].shape[1] // dp_size
+    k = lefts[0].shape[0] // dp_size
 
     def body(at, *refs):
         grad_refs, weight_refs, refs = refs[:3], refs[3:6], refs[6:]
@@ -1039,8 +1045,8 @@
         sums_ref, hidden_ref, sent, kept, out_ref, small_ref = refs[7:]
         flag = at[0] == 0
         for n, ref in enumerate(grad_refs):
-            put_halves(flag, sent, kept, n * k, dot0(left_in[...], ref[...]))
-        put_halves(flag, sent, kept, 3 * k, dot0(left_mixed[...], low_ref[...]))
+            put_halves(flag, sent, kept, n * k, product(left_in[...], ref[...]))
+        put_halves(flag, sent, kept, 3 * k, product(left_mixed[...], low_ref[...]))
         first = dot1(grad_refs[0][...], weight_refs[0][...])
         for g, w in zip(grad_refs[1:], weight_refs[1:]):
             first = first + dot1(g[...], w[...])
@@ -1226,10 +1232,10 @@
     def chosen(values):
         width = values.shape[1]
         k = width // world
-        source = jnp.arange(width, dtype=jnp.int32)[:, None]
-        target = jnp.arange(dp_size * k, dtype=jnp.int32)[None, :]
+        source = jnp.arange(width, dtype=jnp.int32)[None, :]
+        target = jnp.arange(dp_size * k, dtype=jnp.int32)[:, None]
         wanted = (target // k * copy_size + place) * k + target % k
-        return product(values, (source == wanted).astype(bf16)).astype(bf16)
+        return input_back((source == wanted).astype(bf16), values).astype(bf16)
 
     condition, first_z, mixed_z, second_z, active_z, slope, norm_one, inv_one, norm_two, inv_two = tie(
         condition,
@@ -1312,7 +1318,7 @@
     values = (condition, noisy, noise_rows, row_slot)
     out_bias = output_bias.astype(f32)[None]
     if kernels:
-        out, sums = head_kernel(
+        out, chunks, sums = head_kernel(
             head_pack,
             w_cond_full,
             w_input_full,
@@ -1323,6 +1329,7 @@
             embedded,
             values,
             k_w,
+            (micros, own),
         )
     else:
         others = {"cond": w_cond_full, "input": w_input_full, "output": w_output_t, **squares}
@@ -1334,11 +1341,11 @@
             embedded,
             values,
         )
+        chunks = out["condition"].reshape(micros, copy_size, own, D)
+        chunks = [chunks[:, j] for j in range(copy_size)]
         sums = [jnp.pad(sums[n], ((0, 0), (0, WIDTH - sums[n].shape[1]))) for n, _ in HEAD_SUMS]
         sums = jnp.concatenate(sums)
         sums = jnp.pad(sums, ((0, -sums.shape[0] % 8), (0, 0)))
-    chunks = out["condition"].reshape(micros, copy_size, own, D)
-    chunks = [chunks[:, j] for j in range(copy_size)]
     at_embedded = 2 * CHANNELS
     grad_embedded = sums[at_embedded : at_embedded + micros * IMAGES].astype(bf16)
     grad_time_one = (input_back(grad_embedded, w_time2_full) * silu_slope(time_one)).astype(bf16)

time: 525 us -> 522 us (level)
    dot_general x9 -> x6, matrix products: 10.8 us -> 6.7 us  [product(): return jnp.dot(left_side, right_side, preferred_element_type=jnp.float32)]
    unnamed x164 -> x166, local copies, waits for them, and re-layouts: 16.2 us -> 18 us
where the time goes in v5:
time: 522 us; the launch traced here: 516 us
  Pallas kernels  232 us (44%)
  waiting for transfers between devices  135 us (26%)
  starting transfers between devices  50.1 us (10%)
  local copies, waits for them, and re-layouts  39.9 us (8%)
  other arithmetic  30.4 us (6%)
  between operations  15.4 us (3%)
  matrix products  12.8 us (2%)
    ppermute x18, waiting for transfers between devices, shift_copy(): lax.ppermute(values, 'copy', [(i, (i + shift) % size) for i in range(size)])  82.2 us
    pallas_call x14, Pallas kernels, small_call(): pl.pallas_call(body, out_shape=outs, in_specs=[pl.BlockSpec(memory_space=...  54.2 us
    pallas_call x1, Pallas kernels, head_kernel(): pl.pallas_call(body, grid=(rows // step,), out_shape=[low_shape(rows, WID...  43.4 us
    ppermute x35, waiting for transfers between devices, swap_bit(): return lax.ppermute(values, 'dp', [(i, i ^ 1 << bit) for i in range(size)])  34 us
    pallas_call x2, Pallas kernels, pack_head_grads(): pl.pallas_call(body, grid=(count,), out_shape=[low_shape(count, mids, tot...  27.3 us
    pallas_call x2, Pallas kernels, attention_back(): pl.pallas_call(body, grid=(1, HEADS // 2), out_shape=[low_shape(micros *...  24.8 us
    ppermute x35, starting transfers between devices, swap_bit(): return lax.ppermute(values, 'dp', [(i, i ^ 1 << bit) for i in range(size)])  24.8 us
    pallas_call x1, Pallas kernels, block_back_one(): pl.pallas_call(body, grid=(steps,), out_shape=outs + [jax.ShapeDtypeStruc...  24 us
  transfers between devices with their start and end apart: 59, of which 23 were waited for; matrix products, arithmetic and copies ran while one was open for 10% of the time, Pallas kernels for 36%

profile of v5, /device:TPU:9, one launch (start us, length us, event | category | flops | bytes accessed | tf_op | source)
XLA Modules:
  0.0 516.0 jit_solution(6858214684686541384)
XLA Ops:
  11.1 2.5 collective-permute-start.1
  13.6 2.2 collective-permute-start.2
  16.4 8.0 %collective-permute-done.1 = bf16[112,768]{1,0:T(8,128)(2,1)S(1)} collective-permute-done((bf16[112,768]{1,0:T(8,128)(2,1)S(1)}, bf16[112,768]{1,0:T(8,128)(2,1)S(1)}, u32[]{:S(2)}, u32[]{:S(2)}) %collective-permute-start.1) | collective-permute-done | bytes 172064 | tf_op jit(solution)/shard_map/ppermute | solution.py:94
  24.3 3.7 collective-permute-done.2
  29.3 2.1 collective-permute-start.4
  32.5 3.7 collective-permute-done.3
  36.3 12.2 %collective-permute-done.4 = bf16[192,768]{1,0:T(8,128)(2,1)S(1)} collective-permute-done((bf16[192,768]{1,0:T(8,128)(2,1)S(1)}, bf16[192,768]{1,0:T(8,128)(2,1)S(1)}, u32[]{:S(2)}, u32[]{:S(2)}) %collective-permute-start.4) | collective-permute-done | bytes 294944 | tf_op jit(solution)/shard_map/ppermute | solution.py:94
  48.5 6.3 %collective-permute-done.5 = bf16[192,768]{1,0:T(8,128)(2,1)S(1)} collective-permute-done((bf16[192,768]{1,0:T(8,128)(2,1)S(1)}, bf16[192,768]{1,0:T(8,128)(2,1)S(1)}, u32[]{:S(2)}, u32[]{:S(2)}) %collective-permute-start.5) | collective-permute-done | bytes 294944 | tf_op jit(solution)/shard_map/ppermute | solution.py:94
  61.5 1.7 collective-permute-start.14
  63.2 1.8 collective-permute-start.15
  65.0 2.0 collective-permute-done.17
  68.4 4.5 collective-permute-done.21
  75.2 2.1 collective-permute-start.10
  77.3 17.8 %collective-permute-done.15 = bf16[2,96,768]{2,1,0:T(8,128)(2,1)S(1)} collective-permute-done((bf16[2,96,768]{2,1,0:T(8,128)(2,1)S(1)}, bf16[2,96,768]{2,1,0:T(8,128)(2,1)S(1)}, u32[]{:S(2)}, u32[]{:S(2)}) %collective-permute-start.15) | collective-permute-done | bytes 294944 | tf_op jit(solution)/shard_map/ppermute | solution.py:94
  95.3 6.6 %collective-permute-done.16 = bf16[2,96,768]{2,1,0:T(8,128)(2,1)S(1)} collective-permute-done((bf16[2,96,768]{2,1,0:T(8,128)(2,1)S(1)}, bf16[2,96,768]{2,1,0:T(8,128)(2,1)S(1)}, u32[]{:S(2)}, u32[]{:S(2)}) %collective-permute-start.16) | collective-permute-done | bytes 294944 | tf_op jit(solution)/shard_map/ppermute | solution.py:94
  103.7 1.7 fusion.2
  106.9 1.6 fusion.7.refs_10_
  108.6 1.7 pad_maximum_fusion.1.refs_4_
  112.8 4.4 collective-permute-start.12
  117.4 8.6 %shard_map.395 = bf16[32,112,768]{2,1,0:T(8,128)(2,1)S(1)} custom-call(s32[2]{0:T(128)S(1)} %pad_add_fusion.at, bf16[2,4,48,768]{3,2,1,0:T(8,128)(2,1)S(1)} %pad_maximum_fusion.6.refs_0_, bf16[2,4,48,768]{3,2,1,0:T(8,128)(2,1)} %collective-permute-done.18.refs_1_, bf16[2,4,48,768]{3,2,1,0:T(8,128)(2,1)S(1)} %collective-permute-done.19.refs_2_, ...), custom_call_target="tpu_custom_call" | custom-call | flops 8000000000 | bytes 100000 | tf_op jit(solution)/shard_map/pallas_call | solution.py:549
  132.1 15.2 %shard_map.397 = bf16[768,768]{1,0:T(8,128)(2,1)S(1)} custom-call(s32[768,1]{1,0:T(8,128)S(1)} %bitcast.159, s32[2,1,384]{2,1,0:T(1,128)S(1)} %broadcast_in_dim.63.row_ref, bf16[768,768]{1,0:T(8,128)(2,1)S(1)} %add_convert_fusion.3.q_ref, bf16[768,768]{1,0:T(8,128)(2,1)S(1)} %convolution_convert_fusion.k_ref, bf16[768,768]{1,0:T(8,128)(2,1)S(1)} %add_convert_fusion.2.v_ref), custom_call_target="tpu_custom_call" | custom-call | flops 15000000512 | bytes 100000 | tf_op jit(solution)/shard_map/pallas_call | solution.py:379
  149.5 3.8 collective-permute-done.7.refs_1_
  155.5 1.5 add_convert_fusion.1
  159.8 13.9 %shard_map.394 = bf16[32,192,768]{2,1,0:T(8,128)(2,1)S(1)} custom-call(s32[2]{0:T(128)S(1)} %pad_add_fusion.at, bf16[2,4,96,768]{3,2,1,0:T(8,128)(2,1)S(1)} %pad_maximum_fusion.refs_0_, bf16[2,4,96,768]{3,2,1,0:T(8,128)(2,1)S(1)} %collective-permute-done.7.refs_1_, bf16[2,4,96,768]{3,2,1,0:T(8,128)(2,1)S(1)} %collective-permute-done.8.refs_2_, ...), custom_call_target="tpu_custom_call" | custom-call | flops 8000000000 | bytes 100000 | tf_op jit(solution)/shard_map/pallas_call | solution.py:549
  173.7 2.6 slice.355
  177.6 18.1 %shard_map.398 = (bf16[768,768]{1,0:T(8,128)(2,1)S(1)}, bf16[768,3072]{1,0:T(8,128)(2,1)}, bf16[4,192,768]{2,1,0:T(8,128)(2,1)S(1)}) custom-call(s32[1]{0:T(128)} %bitcast.at, bf16[768,768]{1,0:T(8,128)(2,1)S(1)} %bitcast.157, bf16[768,768]{1,0:T(8,128)(2,1)S(1)} %bitcast.155, bf16[768,768]{1,0:T(8,128)(2,1)S(1)} %bitcast.153, bf16[768,768]{1,0:T(8,128)(2,1)} %bitcast.182, ...), custom_call_target="tpu_custom_call" | custom-call | flops 17999998976 | bytes 100000 | tf_op jit(solution)/shard_map/pallas_call | solution.py:905
  197.8 18.8 %all-gather.5.cloned.1.call-done = bf16[9728,1024]{1,0:T(8,128)(2,1)} async-done(((bf16[304,1024]{1,0:T(8,128)(2,1)}), bf16[9728,1024]{1,0:T(8,128)(2,1)}) %all-gather.5.cloned.1.call-update) | async-done | bytes 19922960 | tf_op jit(solution)/shard_map/all_gather | solution.py:1188
  217.8 1.8 slice.361
  219.7 2.7 slice.357
  227.4 43.4 %shard_map.400 = (bf16[768,1024]{1,0:T(8,128)(2,1)}, bf16[768,1024]{1,0:T(8,128)(2,1)}, bf16[768,1024]{1,0:T(8,128)(2,1)}, bf16[768,1024]{1,0:T(8,128)(2,1)}, bf...) custom-call(bf16[768,1024]{1,0:T(8,128)(2,1)} %bitcast.172, ...), custom_call_target="tpu_custom_call" | custom-call | flops 44999999488 | bytes 100000 | tf_op jit(solution)/shard_map/pallas_call | solution.py:798
  272.4 13.2 %shard_map.401 = (bf16[4,8,128,512]{3,2,1,0:T(8,128)(2,1)}, bf16[4,8,128,512]{3,2,1,0:T(8,128)(2,1)}, f32[4,1024]{1,0:T(4,128)}) custom-call(s32[1]{0:T(128)} %bitcast.49.at, bf16[768,1024]{1,0:T(8,128)(2,1)} %get-tuple-element.214.refs_0_, bf16[768,1024]{1,0:T(8,128)(2,1)} %get-tuple-element.204.refs_1_, bf16[768,1024]{1,0:T(8,128)(2,1)} %get-tuple-element.205.refs_2_, ...), custom_call_target="tpu_custom_call" | custom-call | flops 12999999488 | bytes 100000 | tf_op jit(solution)/shard_map/pallas_call | solution.py:512
  285.7 11.0 %collective-permute-done.26.refs_2_ = bf16[2,96,768]{2,1,0:T(8,128)(2,1)S(1)} collective-permute-done((bf16[2,96,768]{2,1,0:T(8,128)(2,1)}, bf16[2,96,768]{2,1,0:T(8,128)(2,1)S(1)}, u32[]{:S(2)}, u32[]{:S(2)}) %collective-permute-start.26) | collective-permute-done | bytes 294944 | tf_op jit(solution)/shard_map/ppermute | solution.py:94
  298.3 2.1 shard_map.402.refs_0_
  303.6 2.0 fusion.10.refs_9_
  305.6 2.4 collective-permute-start.30
  308.0 2.4 collective-permute-start.31
  310.3 14.1 %shard_map.403 = (bf16[4,8,160,512]{3,2,1,0:T(8,128)(2,1)}, bf16[4,8,160,512]{3,2,1,0:T(8,128)(2,1)}, f32[48,1024]{1,0:T(8,128)}) custom-call(s32[1]{0:T(128)} %bitcast.49.at, bf16[768,1024]{1,0:T(8,128)(2,1)} %get-tuple-element.214.refs_0_, bf16[8,1024]{1,0:T(8,128)(2,1)} %copy-done.48, bf16[768,768]{1,0:T(8,128)(2,1)} %copy-done.4, ...), custom_call_target="tpu_custom_call" | custom-call | flops 12999999488 | bytes 100000 | tf_op jit(solution)/shard_map/pallas_call | solution.py:512
  324.5 6.4 %shard_map.404 = (bf16[2,8,64,512]{3,2,1,0:T(8,128)(2,1)}, bf16[2,8,64,512]{3,2,1,0:T(8,128)(2,1)}, bf16[2,8,64,512]{3,2,1,0:T(8,128)(2,1)}, bf16[2,8,64,512]{3,2,1,0:T(8,128)(2,1)}) custom-call(s32[2]{0:T(128)} %get-tuple-element.475.at, bf16[4,8,128,512]{3,2,1,0:T(8,128)(2,1)} %get-tuple-element.210.refs_0_, ...), custom_call_target="tpu_custom_call" | custom-call | flops 5719505408 | bytes 100000 | tf_op jit(solution)/shard_map/pallas_call | solution.py:133
  330.9 2.6 collective-permute-done.31.refs_3_
  337.7 24.0 %shard_map.405 = (bf16[4,2,192,384]{3,2,1,0:T(8,128)(2,1)}, bf16[4,2,192,384]{3,2,1,0:T(8,128)(2,1)}, f32[768,768]{1,0:T(8,128)}, bf16[768,768]{1,0:T(8,128)(2,1...) custom-call(s32[1]{0:T(128)} %bitcast.49.at, bf16[2,96,768]{2,1,0:T(8,128)(2,1)} %shard_map.402.refs_0_, ...), custom_call_target="tpu_custom_call" | custom-call | flops 24000000000 | bytes 100000 | tf_op jit(solution)/shard_map/pallas_call | solution.py:1002
  363.0 3.9 shard_map.406
  368.4 2.4 collective-permute-start.38
  370.8 7.5 %shard_map.407 = (bf16[2,8,96,512]{3,2,1,0:T(8,128)(2,1)}, bf16[2,8,96,512]{3,2,1,0:T(8,128)(2,1)}, bf16[2,8,64,512]{3,2,1,0:T(8,128)(2,1)}, bf16[2,8,64,512]{3,2,1,0:T(8,128)(2,1)}) custom-call(s32[2]{0:T(128)} %get-tuple-element.475.at, bf16[4,8,160,512]{3,2,1,0:T(8,128)(2,1)} %get-tuple-element.221.refs_0_, ...), custom_call_target="tpu_custom_call" | custom-call | flops 7149381632 | bytes 100000 | tf_op jit(solution)/shard_map/pallas_call | solution.py:133
  380.0 12.5 %shard_map.408 = (bf16[768,768]{1,0:T(8,128)(2,1)}, bf16[768,768]{1,0:T(8,128)(2,1)}, bf16[768,768]{1,0:T(8,128)(2,1)}) custom-call(s32[768,1]{1,0:T(8,128)} %bitcast.160, s32[2,1,384]{2,1,0:T(1,128)} %copy-done.5, bf16[768,768]{1,0:T(8,128)(2,1)} %copy-done.26, bf16[768,768]{1,0:T(8,128)(2,1)} %copy-done.24, bf16[768,768]{1,0:T(8,128)(2,1)} %copy-done.25, ...), custom_call_target="tpu_custom_call" | custom-call | flops 12000000000 | bytes 100000 | tf_op jit(solution)/shard_map/pallas_call | solution.py:414
  393.3 2.7 shard_map.409
  396.1 12.4 %shard_map.410 = (bf16[768,768]{1,0:T(8,128)(2,1)}, bf16[768,768]{1,0:T(8,128)(2,1)}, bf16[768,768]{1,0:T(8,128)(2,1)}) custom-call(s32[768,1]{1,0:T(8,128)} %bitcast.161, s32[2,1,384]{2,1,0:T(1,128)} %copy-done.5, bf16[768,768]{1,0:T(8,128)(2,1)} %copy-done.26, ...), custom_call_target="tpu_custom_call", output_to_operand_aliasing={{0}: (6, {}), {1}: (7, {}), {2}: (8, {})} | custom-call | flops 12000000000 | bytes 100000 | tf_op jit(solution)/shard_map/pallas_call | solution.py:414
  408.5 6.5 %collective-permute-done.39.got_one = bf16[2,8,96,512]{3,2,1,0:T(8,128)(2,1)S(1)} collective-permute-done((bf16[2,8,96,512]{3,2,1,0:T(8,128)(2,1)}, bf16[2,8,96,512]{3,2,1,0:T(8,128)(2,1)S(1)}, u32[]{:S(2)}, u32[]{:S(2)}) %collective-permute-start.39) | collective-permute-done | bytes 1572896 | tf_op jit(solution)/shard_map/ppermute | solution.py:90
  416.1 4.5 shard_map.411
  423.0 2.1 shard_map.412
  425.8 10.0 %shard_map.413 = (bf16[4,2,96,384]{3,2,1,0:T(8,128)(2,1)}, bf16[4,2,96,384]{3,2,1,0:T(8,128)(2,1)}, f32[2,96,768]{2,1,0:T(8,128)}, f32[12,768]{1,0:T(8,128)}) custom-call(s32[1]{0:T(128)} %bitcast.49.at, bf16[768,768]{1,0:T(8,128)(2,1)} %get-tuple-element.280.refs_0_, bf16[768,768]{1,0:T(8,128)(2,1)} %get-tuple-element.281.refs_1_, ...), custom_call_target="tpu_custom_call" | custom-call | flops 7046050816 | bytes 100000 | tf_op jit(solution)/shard_map/pallas_call | solution.py:133
  435.8 2.7 collective-permute-done.42.got_one
  439.4 3.0 shard_map.414
  443.1 1.8 shard_map.415
  444.9 2.4 collective-permute-start.45
  448.6 1.7 slice_bitcast_fusion.2
  455.1 3.4 shard_map.416
  459.8 9.8 %collective-permute-done.47.got_one = bf16[2,2,144,384]{3,2,1,0:T(8,128)(2,1)S(1)} collective-permute-done((bf16[2,2,144,384]{3,2,1,0:T(8,128)(2,1)}, bf16[2,2,144,384]{3,2,1,0:T(8,128)(2,1)S(1)}, u32[]{:S(2)}, u32[]{:S(2)}) %collective-permute-start.47) | collective-permute-done | bytes 442400 | tf_op jit(solution)/shard_map/ppermute | solution.py:90
  471.2 2.4 shard_map.417
  473.6 6.6 %collective-permute-done.53.refs_2_ = bf16[2,160,512]{2,1,0:T(8,128)(2,1)} collective-permute-done((bf16[2,160,512]{2,1,0:T(8,128)(2,1)}, bf16[2,160,512]{2,1,0:T(8,128)(2,1)}, u32[]{:S(2)}, u32[]{:S(2)}) %collective-permute-start.53) | collective-permute-done | bytes 327712 | tf_op jit(solution)/shard_map/ppermute | solution.py:94
  480.2 2.2 collective-permute-done.54.refs_3_
  483.1 2.4 shard_map.419
  490.7 3.1 collective-permute-done.49
  494.9 2.0 shard_map.418
  503.1 1.6 slice_add_fusion
  (364 shorter events, 93.9 us)
Async XLA Ops:
  7.2 209.3 %all-gather.5.cloned.1.call-start = ((), (), s32[]{:S(2)}) async-start(), calls=%async_computation | async-start | bytes 20545536 | tf_op jit(solution)/shard_map/all_gather | solution.py:1188
  11.1 5.3 %collective-permute-start = (bf16[112,768]{1,0:T(8,128)(2,1)S(1)}, bf16[112,768]{1,0:T(8,128)(2,1)S(1)}, u32[]{:S(2)}, u32[]{:S(2)}) collective-permute-start(bf16[112,768]{1,0:T(8,128)(2,1)S(1)} %shard_map.391), channel_id=1, source_target_pairs={{0,3},{1,0},{2,1},{3,2},{4,7},{5,4},{6,5},{7,6},{8,11},{9,8},{10,9... | collective-permute-start | bytes 516104 | tf_op jit(solution)/shard_map/ppermute | solution.py:94
  11.1 13.2 %collective-permute-start.1 = (bf16[112,768]{1,0:T(8,128)(2,1)S(1)}, bf16[112,768]{1,0:T(8,128)(2,1)S(1)}, u32[]{:S(2)}, u32[]{:S(2)}) collective-permute-start(bf16[112,768]{1,0:T(8,128)(2,1)S(1)} %shard_map.391), channel_id=1, source_target_pairs={{0,2},{1,3},{2,0},{3,1},{4,6},{5,7},{6,4},{7,5},{8,10},{9,11},{10,... | collective-permute-start | bytes 516104 | tf_op jit(solution)/shard_map/ppermute | solution.py:94
  13.6 14.4 %collective-permute-start.2 = (bf16[112,768]{1,0:T(8,128)(2,1)S(1)}, bf16[112,768]{1,0:T(8,128)(2,1)S(1)}, u32[]{:S(2)}, u32[]{:S(2)}) collective-permute-start(bf16[112,768]{1,0:T(8,128)(2,1)S(1)} %shard_map.391), channel_id=1, source_target_pairs={{0,1},{1,2},{2,3},{3,0},{4,5},{5,6},{6,7},{7,4},{8,9},{9,10},{10,1... | collective-permute-start | bytes 516104 | tf_op jit(solution)/shard_map/ppermute | solution.py:94
  28.0 8.2 %collective-permute-start.3 = (bf16[192,768]{1,0:T(8,128)(2,1)S(1)}, bf16[192,768]{1,0:T(8,128)(2,1)S(1)}, u32[]{:S(2)}, u32[]{:S(2)}) collective-permute-start(bf16[192,768]{1,0:T(8,128)(2,1)S(1)} %shard_map.392), channel_id=1, source_target_pairs={{0,3},{1,0},{2,1},{3,2},{4,7},{5,4},{6,5},{7,6},{8,11},{9,8},{10,9... | collective-permute-start | bytes 884744 | tf_op jit(solution)/shard_map/ppermute | solution.py:94
  29.3 19.1 %collective-permute-start.4 = (bf16[192,768]{1,0:T(8,128)(2,1)S(1)}, bf16[192,768]{1,0:T(8,128)(2,1)S(1)}, u32[]{:S(2)}, u32[]{:S(2)}) collective-permute-start(bf16[192,768]{1,0:T(8,128)(2,1)S(1)} %shard_map.392), channel_id=1, source_target_pairs={{0,2},{1,3},{2,0},{3,1},{4,6},{5,7},{6,4},{7,5},{8,10},{9,11},{10,... | collective-permute-start | bytes 884744 | tf_op jit(solution)/shard_map/ppermute | solution.py:94
  31.4 23.4 %collective-permute-start.5 = (bf16[192,768]{1,0:T(8,128)(2,1)S(1)}, bf16[192,768]{1,0:T(8,128)(2,1)S(1)}, u32[]{:S(2)}, u32[]{:S(2)}) collective-permute-start(bf16[192,768]{1,0:T(8,128)(2,1)S(1)} %shard_map.392), channel_id=1, source_target_pairs={{0,1},{1,2},{2,3},{3,0},{4,5},{5,6},{6,7},{7,4},{8,9},{9,10},{10,1... | collective-permute-start | bytes 884744 | tf_op jit(solution)/shard_map/ppermute | solution.py:94
  32.5 24.6 %copy-start.78 = (bf16[16]{0:T(256)(128)(2,1)S(1)}, bf16[16]{0:T(256)(128)(2,1)}, u32[]{:S(2)}) copy-start(bf16[16]{0:T(256)(128)(2,1)} %param.47) | copy-start | bytes 100
  54.8 448.3 %all-gather.7.cloned.1.call-start = ((), (), s32[]{:S(2)}) async-start(), calls=%async_computation.1 | async-start | bytes 2359296 | tf_op jit(solution)/shard_map/all_gather | solution.py:1471
  55.0 77.1 %copy-start.5 = (s32[2,1,384]{2,1,0:T(1,128)}, s32[2,1,384]{2,1,0:T(1,128)S(1)}, u32[]{:S(2)}) copy-start(s32[2,1,384]{2,1,0:T(1,128)S(1)} %broadcast_in_dim.63.row_ref) | copy-start | bytes 9220
  55.2 76.9 %copy-start.3 = (s32[1,768]{0,1:T(8,128)}, s32[1,768]{0,1:T(8,128)S(1)}, u32[]{:S(2)}) copy-start(s32[1,768]{0,1:T(8,128)S(1)} %copy.88) | copy-start | bytes 9220
  58.8 8.2 %collective-permute-start.17 = (bf16[4,48,768]{2,1,0:T(8,128)(2,1)S(1)}, bf16[4,48,768]{2,1,0:T(8,128)(2,1)S(1)}, u32[]{:S(2)}, u32[]{:S(2)}) collective-permute-start(bf16[4,48,768]{2,1,0:T(8,128)(2,1)S(1)} %get-tuple-element.450), channel_id=1, source_target_pairs={{0,16},{4,20},{8,24},{12,28},{16,0},{20,4},{24,8},{28,12},{1,17},{... | collective-permute-start | bytes 884744 | tf_op jit(solution)/shard_map/ppermute | solution.py:90
  60.2 12.6 %collective-permute-start.21 = (bf16[4,64,768]{2,1,0:T(8,128)(2,1)S(1)}, bf16[4,64,768]{2,1,0:T(8,128)(2,1)S(1)}, u32[]{:S(2)}, u32[]{:S(2)}) collective-permute-start(bf16[4,64,768]{2,1,0:T(8,128)(2,1)S(1)} %get-tuple-element.442), channel_id=1, source_target_pairs={{0,8},{4,12},{8,0},{12,4},{16,24},{20,28},{24,16},{28,20},{1,9},{5... | collective-permute-start | bytes 1179656 | tf_op jit(solution)/shard_map/ppermute | solution.py:90
  61.5 13.7 %collective-permute-start.14 = (bf16[2,96,768]{2,1,0:T(8,128)(2,1)S(1)}, bf16[2,96,768]{2,1,0:T(8,128)(2,1)S(1)}, u32[]{:S(2)}, u32[]{:S(2)}) collective-permute-start(bf16[2,96,768]{2,1,0:T(8,128)(2,1)S(1)} %bitcast.195), channel_id=1, source_target_pairs={{0,3},{1,0},{2,1},{3,2},{4,7},{5,4},{6,5},{7,6},{8,11},{9,8},{10,9... | collective-permute-start | bytes 884744 | tf_op jit(solution)/shard_map/ppermute | solution.py:94
  63.2 32.0 %collective-permute-start.15 = (bf16[2,96,768]{2,1,0:T(8,128)(2,1)S(1)}, bf16[2,96,768]{2,1,0:T(8,128)(2,1)S(1)}, u32[]{:S(2)}, u32[]{:S(2)}) collective-permute-start(bf16[2,96,768]{2,1,0:T(8,128)(2,1)S(1)} %bitcast.196), channel_id=1, source_target_pairs={{0,2},{1,3},{2,0},{3,1},{4,6},{5,7},{6,4},{7,5},{8,10},{9,11},{10,... | collective-permute-start | bytes 884744 | tf_op jit(solution)/shard_map/ppermute | solution.py:94
  65.0 37.0 %collective-permute-start.16 = (bf16[2,96,768]{2,1,0:T(8,128)(2,1)S(1)}, bf16[2,96,768]{2,1,0:T(8,128)(2,1)S(1)}, u32[]{:S(2)}, u32[]{:S(2)}) collective-permute-start(bf16[2,96,768]{2,1,0:T(8,128)(2,1)S(1)} %bitcast.197), channel_id=1, source_target_pairs={{0,1},{1,2},{2,3},{3,0},{4,5},{5,6},{6,7},{7,4},{8,9},{9,10},{10,1... | collective-permute-start | bytes 884744 | tf_op jit(solution)/shard_map/ppermute | solution.py:94
  67.0 39.3 %collective-permute-start.18 = (bf16[2,4,48,768]{3,2,1,0:T(8,128)(2,1)S(1)}, bf16[2,4,48,768]{3,2,1,0:T(8,128)(2,1)}, u32[]{:S(2)}, u32[]{:S(2)}) collective-permute-start(bf16[2,4,48,768]{3,2,1,0:T(8,128)(2,1)S(1)} %pad_maximum_fusion.6.refs_0_), channel_id=1, source_target_pairs={{0,8},{4,12},{8,0},{12,4},{16,24},{20,28},{24,16},{28,20},{1,9},{5... | collective-permute-start | bytes 1769480 | tf_op jit(solution)/shard_map/ppermute | solution.py:90
  72.9 32.5 %collective-permute-start.22 = (bf16[2,4,64,768]{3,2,1,0:T(8,128)(2,1)S(1)}, bf16[2,4,64,768]{3,2,1,0:T(8,128)(2,1)S(1)}, u32[]{:S(2)}, u32[]{:S(2)}) collective-permute-start(bf16[2,4,64,768]{3,2,1,0:T(8,128)(2,1)S(1)} %pad_maximum_fusion.3.refs_4_), channel_id=1, source_target_pairs={{0,16},{4,20},{8,24},{12,28},{16,0},{20,4},{24,8},{28,12},{1,17},{... | collective-permute-start | bytes 2359304 | tf_op jit(solution)/shard_map/ppermute | solution.py:90
  75.2 31.6 %collective-permute-start.10 = (bf16[4,96,768]{2,1,0:T(8,128)(2,1)}, bf16[4,96,768]{2,1,0:T(8,128)(2,1)}, u32[]{:S(2)}, u32[]{:S(2)}) collective-permute-start(bf16[4,96,768]{2,1,0:T(8,128)(2,1)} %get-tuple-element.424), channel_id=1, source_target_pairs={{0,8},{4,12},{8,0},{12,4},{16,24},{20,28},{24,16},{28,20},{1,9},{5... | collective-permute-start | bytes 1769480 | tf_op jit(solution)/shard_map/ppermute | solution.py:90
  95.2 16.4 %collective-permute-start.6 = (bf16[4,96,768]{2,1,0:T(8,128)(2,1)}, bf16[4,96,768]{2,1,0:T(8,128)(2,1)}, u32[]{:S(2)}, u32[]{:S(2)}) collective-permute-start(bf16[4,96,768]{2,1,0:T(8,128)(2,1)} %get-tuple-element.426), channel_id=1, source_target_pairs={{0,16},{4,20},{8,24},{12,28},{16,0},{20,4},{24,8},{28,12},{1,17},{... | collective-permute-start | bytes 1769480 | tf_op jit(solution)/shard_map/ppermute | solution.py:90
  101.9 15.2 %collective-permute-start.23 = (bf16[2,4,64,768]{3,2,1,0:T(8,128)(2,1)S(1)}, bf16[2,4,64,768]{3,2,1,0:T(8,128)(2,1)S(1)}, u32[]{:S(2)}, u32[]{:S(2)}) collective-permute-start(bf16[2,4,64,768]{3,2,1,0:T(8,128)(2,1)S(1)} %pad_maximum_fusion.3.refs_4_), channel_id=1, source_target_pairs={{0,4},{4,0},{8,12},{12,8},{16,20},{20,16},{24,28},{28,24},{1,5},{5... | collective-permute-start | bytes 2359304 | tf_op jit(solution)/shard_map/ppermute | solution.py:90
  105.5 11.9 %collective-permute-start.24 = (bf16[2,4,64,768]{3,2,1,0:T(8,128)(2,1)S(1)}, bf16[2,4,64,768]{3,2,1,0:T(8,128)(2,1)}, u32[]{:S(2)}, u32[]{:S(2)}) collective-permute-start(bf16[2,4,64,768]{3,2,1,0:T(8,128)(2,1)S(1)} %collective-permute-done.22.refs_5_), channel_id=1, source_target_pairs={{0,4},{4,0},{8,12},{12,8},{16,20},{20,16},{24,28},{28,24},{1,5},{5... | collective-permute-start | bytes 2359304 | tf_op jit(solution)/shard_map/ppermute | solution.py:90
  106.3 6.4 %collective-permute-start.19 = (bf16[2,4,48,768]{3,2,1,0:T(8,128)(2,1)S(1)}, bf16[2,4,48,768]{3,2,1,0:T(8,128)(2,1)S(1)}, u32[]{:S(2)}, u32[]{:S(2)}) collective-permute-start(bf16[2,4,48,768]{3,2,1,0:T(8,128)(2,1)S(1)} %pad_maximum_fusion.6.refs_0_), channel_id=1, source_target_pairs={{0,4},{4,0},{8,12},{12,8},{16,20},{20,16},{24,28},{28,24},{1,5},{5... | collective-permute-start | bytes 1769480 | tf_op jit(solution)/shard_map/ppermute | solution.py:90
  106.8 10.4 %collective-permute-start.20 = (bf16[2,4,48,768]{3,2,1,0:T(8,128)(2,1)}, bf16[2,4,48,768]{3,2,1,0:T(8,128)(2,1)S(1)}, u32[]{:S(2)}, u32[]{:S(2)}) collective-permute-start(bf16[2,4,48,768]{3,2,1,0:T(8,128)(2,1)} %collective-permute-done.18.refs_1_), channel_id=1, source_target_pairs={{0,4},{4,0},{8,12},{12,8},{16,20},{20,16},{24,28},{28,24},{1,5},{5... | collective-permute-start | bytes 1769480 | tf_op jit(solution)/shard_map/ppermute | solution.py:90
  108.5 49.9 %copy-start.30 = (f32[768,768]{1,0:T(8,128)}, f32[768,768]{1,0:T(8,128)S(1)}, u32[]{:S(2)}) copy-start(f32[768,768]{1,0:T(8,128)S(1)} %fusion.7.refs_10_) | copy-start | bytes 7077892
  111.6 37.5 %collective-permute-start.11 = (bf16[2,4,96,768]{3,2,1,0:T(8,128)(2,1)S(1)}, bf16[2,4,96,768]{3,2,1,0:T(8,128)(2,1)S(1)}, u32[]{:S(2)}, u32[]{:S(2)}) collective-permute-start(bf16[2,4,96,768]{3,2,1,0:T(8,128)(2,1)S(1)} %pad_maximum_fusion.1.refs_4_), channel_id=1, source_target_pairs={{0,16},{4,20},{8,24},{12,28},{16,0},{20,4},{24,8},{28,12},{1,17},{... | collective-permute-start | bytes 3538952 | tf_op jit(solution)/shard_map/ppermute | solution.py:90
  112.8 47.0 %collective-permute-start.12 = (bf16[2,4,96,768]{3,2,1,0:T(8,128)(2,1)S(1)}, bf16[2,4,96,768]{3,2,1,0:T(8,128)(2,1)S(1)}, u32[]{:S(2)}, u32[]{:S(2)}) collective-permute-start(bf16[2,4,96,768]{3,2,1,0:T(8,128)(2,1)S(1)} %pad_maximum_fusion.1.refs_4_), channel_id=1, source_target_pairs={{0,4},{4,0},{8,12},{12,8},{16,20},{20,16},{24,28},{28,24},{1,5},{5... | collective-permute-start | bytes 3538952 | tf_op jit(solution)/shard_map/ppermute | solution.py:90
  117.2 36.2 %collective-permute-start.7 = (bf16[2,4,96,768]{3,2,1,0:T(8,128)(2,1)S(1)}, bf16[2,4,96,768]{3,2,1,0:T(8,128)(2,1)S(1)}, u32[]{:S(2)}, u32[]{:S(2)}) collective-permute-start(bf16[2,4,96,768]{3,2,1,0:T(8,128)(2,1)S(1)} %pad_maximum_fusion.refs_0_), channel_id=1, source_target_pairs={{0,8},{4,12},{8,0},{12,4},{16,24},{20,28},{24,16},{28,20},{1,9},{5... | collective-permute-start | bytes 3538952 | tf_op jit(solution)/shard_map/ppermute | solution.py:90
  117.2 42.6 %collective-permute-start.8 = (bf16[2,4,96,768]{3,2,1,0:T(8,128)(2,1)S(1)}, bf16[2,4,96,768]{3,2,1,0:T(8,128)(2,1)S(1)}, u32[]{:S(2)}, u32[]{:S(2)}) collective-permute-start(bf16[2,4,96,768]{3,2,1,0:T(8,128)(2,1)S(1)} %pad_maximum_fusion.refs_0_), channel_id=1, source_target_pairs={{0,4},{4,0},{8,12},{12,8},{16,20},{20,16},{24,28},{28,24},{1,5},{5... | collective-permute-start | bytes 3538952 | tf_op jit(solution)/shard_map/ppermute | solution.py:90
  149.0 10.7 %collective-permute-start.13 = (bf16[2,4,96,768]{3,2,1,0:T(8,128)(2,1)S(1)}, bf16[2,4,96,768]{3,2,1,0:T(8,128)(2,1)S(1)}, u32[]{:S(2)}, u32[]{:S(2)}) collective-permute-start(bf16[2,4,96,768]{3,2,1,0:T(8,128)(2,1)S(1)} %collective-permute-done.11.refs_5_), channel_id=1, source_target_pairs={{0,4},{4,0},{8,12},{12,8},{16,20},{20,16},{24,28},{28,24},{1,5},{5... | collective-permute-start | bytes 3538952 | tf_op jit(solution)/shard_map/ppermute | solution.py:90
  153.4 6.4 %collective-permute-start.9 = (bf16[2,4,96,768]{3,2,1,0:T(8,128)(2,1)S(1)}, bf16[2,4,96,768]{3,2,1,0:T(8,128)(2,1)S(1)}, u32[]{:S(2)}, u32[]{:S(2)}) collective-permute-start(bf16[2,4,96,768]{3,2,1,0:T(8,128)(2,1)S(1)} %collective-permute-done.7.refs_1_), channel_id=1, source_target_pairs={{0,4},{4,0},{8,12},{12,8},{16,20},{20,16},{24,28},{28,24},{1,5},{5... | collective-permute-start | bytes 3538952 | tf_op jit(solution)/shard_map/ppermute | solution.py:90
  226.4 44.4 %copy-start.48 = (bf16[8,1024]{1,0:T(8,128)(2,1)}, bf16[8,1024]{1,0:T(8,128)(2,1)S(1)}, u32[]{:S(2)}) copy-start(bf16[8,1024]{1,0:T(8,128)(2,1)S(1)} %get-tuple-element.472.refs_1_) | copy-start | bytes 49156
  270.9 14.8 %collective-permute-start.25 = (bf16[2,96,768]{2,1,0:T(8,128)(2,1)}, bf16[2,96,768]{2,1,0:T(8,128)(2,1)S(1)}, u32[]{:S(2)}, u32[]{:S(2)}) collective-permute-start(bf16[2,96,768]{2,1,0:T(8,128)(2,1)} %get-tuple-element.199), channel_id=1, source_target_pairs={{0,1},{1,2},{2,3},{3,0},{4,5},{5,6},{6,7},{7,4},{8,9},{9,10},{10,1... | collective-permute-start | bytes 884744 | tf_op jit(solution)/shard_map/ppermute | solution.py:94
  270.9 25.7 %collective-permute-start.26 = (bf16[2,96,768]{2,1,0:T(8,128)(2,1)}, bf16[2,96,768]{2,1,0:T(8,128)(2,1)S(1)}, u32[]{:S(2)}, u32[]{:S(2)}) collective-permute-start(bf16[2,96,768]{2,1,0:T(8,128)(2,1)} %get-tuple-element.200), channel_id=1, source_target_pairs={{0,2},{1,3},{2,0},{3,1},{4,6},{5,7},{6,4},{7,5},{8,10},{9,11},{10,... | collective-permute-start | bytes 884744 | tf_op jit(solution)/shard_map/ppermute | solution.py:94
  271.0 26.6 %collective-permute-start.27 = (bf16[2,96,768]{2,1,0:T(8,128)(2,1)}, bf16[2,96,768]{2,1,0:T(8,128)(2,1)S(1)}, u32[]{:S(2)}, u32[]{:S(2)}) collective-permute-start(bf16[2,96,768]{2,1,0:T(8,128)(2,1)} %get-tuple-element.201), channel_id=1, source_target_pairs={{0,3},{1,0},{2,1},{3,2},{4,7},{5,4},{6,5},{7,6},{8,11},{9,8},{10,9... | collective-permute-start | bytes 884744 | tf_op jit(solution)/shard_map/ppermute | solution.py:94
  300.4 24.0 %collective-permute-start.28 = (bf16[4,8,128,512]{3,2,1,0:T(8,128)(2,1)}, bf16[4,8,128,512]{3,2,1,0:T(8,128)(2,1)}, u32[]{:S(2)}, u32[]{:S(2)}) collective-permute-start(bf16[4,8,128,512]{3,2,1,0:T(8,128)(2,1)} %get-tuple-element.223), channel_id=1, source_target_pairs={{0,4},{4,0},{8,12},{12,8},{16,20},{20,16},{24,28},{28,24},{1,5},{5... | collective-permute-start | bytes 12582920 | tf_op jit(solution)/shard_map/ppermute | solution.py:90
  305.6 25.2 %collective-permute-start.29 = (bf16[2,96,768]{2,1,0:T(8,128)(2,1)S(1)}, bf16[2,96,768]{2,1,0:T(8,128)(2,1)S(1)}, u32[]{:S(2)}, u32[]{:S(2)}) collective-permute-start(bf16[2,96,768]{2,1,0:T(8,128)(2,1)S(1)} %copy-done.68), channel_id=1, source_target_pairs={{0,3},{1,0},{2,1},{3,2},{4,7},{5,4},{6,5},{7,6},{8,11},{9,8},{10,9... | collective-permute-start | bytes 884744 | tf_op jit(solution)/shard_map/ppermute | solution.py:94
  305.6 25.3 %collective-permute-start.30 = (bf16[2,96,768]{2,1,0:T(8,128)(2,1)S(1)}, bf16[2,96,768]{2,1,0:T(8,128)(2,1)S(1)}, u32[]{:S(2)}, u32[]{:S(2)}) collective-permute-start(bf16[2,96,768]{2,1,0:T(8,128)(2,1)S(1)} %copy-done.68), channel_id=1, source_target_pairs={{0,2},{1,3},{2,0},{3,1},{4,6},{5,7},{6,4},{7,5},{8,10},{9,11},{10,... | collective-permute-start | bytes 884744 | tf_op jit(solution)/shard_map/ppermute | solution.py:94
  308.0 25.4 %collective-permute-start.31 = (bf16[2,96,768]{2,1,0:T(8,128)(2,1)S(1)}, bf16[2,96,768]{2,1,0:T(8,128)(2,1)S(1)}, u32[]{:S(2)}, u32[]{:S(2)}) collective-permute-start(bf16[2,96,768]{2,1,0:T(8,128)(2,1)S(1)} %copy-done.68), channel_id=1, source_target_pairs={{0,1},{1,2},{2,3},{3,0},{4,5},{5,6},{6,7},{7,4},{8,9},{9,10},{10,1... | collective-permute-start | bytes 884744 | tf_op jit(solution)/shard_map/ppermute | solution.py:94
  333.4 37.4 %collective-permute-start.35 = (bf16[4,8,160,512]{3,2,1,0:T(8,128)(2,1)}, bf16[4,8,160,512]{3,2,1,0:T(8,128)(2,1)}, u32[]{:S(2)}, u32[]{:S(2)}) collective-permute-start(bf16[4,8,160,512]{3,2,1,0:T(8,128)(2,1)} %get-tuple-element.249), channel_id=1, source_target_pairs={{0,4},{4,0},{8,12},{12,8},{16,20},{20,16},{24,28},{28,24},{1,5},{5... | collective-permute-start | bytes 15728648 | tf_op jit(solution)/shard_map/ppermute | solution.py:90
  335.2 31.8 %collective-permute-start.34 = (f32[48,1024]{1,0:T(8,128)S(1)}, f32[48,1024]{1,0:T(8,128)S(1)}, u32[]{:S(2)}, u32[]{:S(2)}) collective-permute-start(f32[48,1024]{1,0:T(8,128)S(1)} %copy-done.43), channel_id=1, source_target_pairs={{0,1},{1,0},{2,3},{3,2},{4,5},{5,4},{6,7},{7,6},{8,9},{9,8},{10,11... | collective-permute-start | bytes 589832 | tf_op jit(solution)/shard_map/ppermute | solution.py:98
  336.2 25.5 %collective-permute-start.32 = (bf16[2,8,64,512]{3,2,1,0:T(8,128)(2,1)}, bf16[2,8,64,512]{3,2,1,0:T(8,128)(2,1)S(1)}, u32[]{:S(2)}, u32[]{:S(2)}) collective-permute-start(bf16[2,8,64,512]{3,2,1,0:T(8,128)(2,1)} %get-tuple-element.238), channel_id=1, source_target_pairs={{0,16},{4,20},{8,24},{12,28},{16,0},{20,4},{24,8},{28,12},{1,17},{... | collective-permute-start | bytes 3145736 | tf_op jit(solution)/shard_map/ppermute | solution.py:90
  337.4 24.4 %collective-permute-start.33 = (bf16[2,8,64,512]{3,2,1,0:T(8,128)(2,1)}, bf16[2,8,64,512]{3,2,1,0:T(8,128)(2,1)S(1)}, u32[]{:S(2)}, u32[]{:S(2)}) collective-permute-start(bf16[2,8,64,512]{3,2,1,0:T(8,128)(2,1)} %get-tuple-element.239), channel_id=1, source_target_pairs={{0,8},{4,12},{8,0},{12,4},{16,24},{20,28},{24,16},{28,20},{1,9},{5... | collective-permute-start | bytes 3145736 | tf_op jit(solution)/shard_map/ppermute | solution.py:90
  366.9 25.6 %collective-permute-start.36 = (bf16[1,8,64,512]{3,2,1,0:T(8,128)(2,1)}, bf16[1,8,64,512]{3,2,1,0:T(8,128)(2,1)S(1)}, u32[]{:S(2)}, u32[]{:S(2)}) collective-permute-start(bf16[1,8,64,512]{3,2,1,0:T(8,128)(2,1)} %get-tuple-element.259), channel_id=1, source_target_pairs={{0,8},{4,12},{8,0},{12,4},{16,24},{20,28},{24,16},{28,20},{1,9},{5... | collective-permute-start | bytes 1572872 | tf_op jit(solution)/shard_map/ppermute | solution.py:90
  368.2 24.3 %collective-permute-start.37 = (bf16[1,8,64,512]{3,2,1,0:T(8,128)(2,1)}, bf16[1,8,64,512]{3,2,1,0:T(8,128)(2,1)}, u32[]{:S(2)}, u32[]{:S(2)}) collective-permute-start(bf16[1,8,64,512]{3,2,1,0:T(8,128)(2,1)} %get-tuple-element.260), channel_id=1, source_target_pairs={{0,16},{4,20},{8,24},{12,28},{16,0},{20,4},{24,8},{28,12},{1,17},{... | collective-permute-start | bytes 1572872 | tf_op jit(solution)/shard_map/ppermute | solution.py:90
  368.4 27.6 %collective-permute-start.38 = (f32[48,1024]{1,0:T(8,128)S(1)}, f32[48,1024]{1,0:T(8,128)S(1)}, u32[]{:S(2)}, u32[]{:S(2)}) collective-permute-start(f32[48,1024]{1,0:T(8,128)S(1)} %add.295), channel_id=1, source_target_pairs={{0,2},{1,3},{2,0},{3,1},{4,6},{5,7},{6,4},{7,5},{8,10},{9,11},{10,... | collective-permute-start | bytes 589832 | tf_op jit(solution)/shard_map/ppermute | solution.py:98
  378.3 36.7 %collective-permute-start.39 = (bf16[2,8,96,512]{3,2,1,0:T(8,128)(2,1)}, bf16[2,8,96,512]{3,2,1,0:T(8,128)(2,1)S(1)}, u32[]{:S(2)}, u32[]{:S(2)}) collective-permute-start(bf16[2,8,96,512]{3,2,1,0:T(8,128)(2,1)} %get-tuple-element.269), channel_id=1, source_target_pairs={{0,16},{4,20},{8,24},{12,28},{16,0},{20,4},{24,8},{28,12},{1,17},{... | collective-permute-start | bytes 4718600 | tf_op jit(solution)/shard_map/ppermute | solution.py:90
  379.5 29.0 %collective-permute-start.40 = (bf16[2,8,64,512]{3,2,1,0:T(8,128)(2,1)}, bf16[2,8,64,512]{3,2,1,0:T(8,128)(2,1)S(1)}, u32[]{:S(2)}, u32[]{:S(2)}) collective-permute-start(bf16[2,8,64,512]{3,2,1,0:T(8,128)(2,1)} %get-tuple-element.270), channel_id=1, source_target_pairs={{0,8},{4,12},{8,0},{12,4},{16,24},{20,28},{24,16},{28,20},{1,9},{5... | collective-permute-start | bytes 3145736 | tf_op jit(solution)/shard_map/ppermute | solution.py:90
  396.1 26.1 %collective-permute-start.41 = (bf16[2,2,128,512]{3,2,1,0:T(8,128)(2,1)}, bf16[2,2,128,512]{3,2,1,0:T(8,128)(2,1)S(1)}, u32[]{:S(2)}, u32[]{:S(2)}) collective-permute-start(bf16[2,2,128,512]{3,2,1,0:T(8,128)(2,1)} %get-tuple-element.277), channel_id=1, source_target_pairs={{0,2},{1,3},{2,0},{3,1},{4,6},{5,7},{6,4},{7,5},{8,10},{9,11},{10,... | collective-permute-start | bytes 1572872 | tf_op jit(solution)/shard_map/ppermute | solution.py:98
  420.7 17.8 %collective-permute-start.42 = (bf16[1,8,96,512]{3,2,1,0:T(8,128)(2,1)}, bf16[1,8,96,512]{3,2,1,0:T(8,128)(2,1)S(1)}, u32[]{:S(2)}, u32[]{:S(2)}) collective-permute-start(bf16[1,8,96,512]{3,2,1,0:T(8,128)(2,1)} %get-tuple-element.295), channel_id=1, source_target_pairs={{0,8},{4,12},{8,0},{12,4},{16,24},{20,28},{24,16},{28,20},{1,9},{5... | collective-permute-start | bytes 2359304 | tf_op jit(solution)/shard_map/ppermute | solution.py:90
  422.2 13.6 %collective-permute-start.43 = (bf16[1,8,64,512]{3,2,1,0:T(8,128)(2,1)}, bf16[1,8,64,512]{3,2,1,0:T(8,128)(2,1)S(1)}, u32[]{:S(2)}, u32[]{:S(2)}) collective-permute-start(bf16[1,8,64,512]{3,2,1,0:T(8,128)(2,1)} %get-tuple-element.296), channel_id=1, source_target_pairs={{0,16},{4,20},{8,24},{12,28},{16,0},{20,4},{24,8},{28,12},{1,17},{... | collective-permute-start | bytes 1572872 | tf_op jit(solution)/shard_map/ppermute | solution.py:90
  425.0 17.3 %collective-permute-start.44 = (bf16[2,128,512]{2,1,0:T(8,128)(2,1)}, bf16[2,128,512]{2,1,0:T(8,128)(2,1)S(1)}, u32[]{:S(2)}, u32[]{:S(2)}) collective-permute-start(bf16[2,128,512]{2,1,0:T(8,128)(2,1)} %get-tuple-element.300), channel_id=1, source_target_pairs={{0,1},{1,0},{2,3},{3,2},{4,5},{5,4},{6,7},{7,6},{8,9},{9,8},{10,11... | collective-permute-start | bytes 786440 | tf_op jit(solution)/shard_map/ppermute | solution.py:98
  444.9 9.2 %collective-permute-start.45 = (bf16[4,2,192,384]{3,2,1,0:T(8,128)(2,1)S(1)}, bf16[4,2,192,384]{3,2,1,0:T(8,128)(2,1)S(1)}, u32[]{:S(2)}, u32[]{:S(2)}) collective-permute-start(bf16[4,2,192,384]{3,2,1,0:T(8,128)(2,1)S(1)} %copy-done.54), channel_id=1, source_target_pairs={{0,4},{4,0},{8,12},{12,8},{16,20},{20,16},{24,28},{28,24},{1,5},{5... | collective-permute-start | bytes 3538952 | tf_op jit(solution)/shard_map/ppermute | solution.py:90
  447.2 5.6 %collective-permute-start.46 = (bf16[4,2,96,384]{3,2,1,0:T(8,128)(2,1)S(1)}, bf16[4,2,96,384]{3,2,1,0:T(8,128)(2,1)}, u32[]{:S(2)}, u32[]{:S(2)}) collective-permute-start(bf16[4,2,96,384]{3,2,1,0:T(8,128)(2,1)S(1)} %copy-done.60), channel_id=1, source_target_pairs={{0,4},{4,0},{8,12},{12,8},{16,20},{20,16},{24,28},{28,24},{1,5},{5... | collective-permute-start | bytes 1769480 | tf_op jit(solution)/shard_map/ppermute | solution.py:90
  450.3 8.5 %collective-permute-start.56 = (bf16[128,512]{1,0:T(8,128)(2,1)}, bf16[128,512]{1,0:T(8,128)(2,1)S(1)}, u32[]{:S(2)}, u32[]{:S(2)}) collective-permute-start(bf16[128,512]{1,0:T(8,128)(2,1)} %get-tuple-element.302), channel_id=1, source_target_pairs={{0,4},{4,0},{8,12},{12,8},{16,20},{20,16},{24,28},{28,24},{1,5},{5... | collective-permute-start | bytes 393224 | tf_op jit(solution)/shard_map/ppermute | solution.py:90
  450.8 22.8 %collective-permute-start.52 = (bf16[2,160,512]{2,1,0:T(8,128)(2,1)}, bf16[2,160,512]{2,1,0:T(8,128)(2,1)}, u32[]{:S(2)}, u32[]{:S(2)}) collective-permute-start(bf16[2,160,512]{2,1,0:T(8,128)(2,1)} %get-tuple-element.326), channel_id=1, source_target_pairs={{0,1},{1,2},{2,3},{3,0},{4,5},{5,6},{6,7},{7,4},{8,9},{9,10},{10,1... | collective-permute-start | bytes 983048 | tf_op jit(solution)/shard_map/ppermute | solution.py:94
  451.7 28.4 %collective-permute-start.53 = (bf16[2,160,512]{2,1,0:T(8,128)(2,1)}, bf16[2,160,512]{2,1,0:T(8,128)(2,1)}, u32[]{:S(2)}, u32[]{:S(2)}) collective-permute-start(bf16[2,160,512]{2,1,0:T(8,128)(2,1)} %get-tuple-element.327), channel_id=1, source_target_pairs={{0,2},{1,3},{2,0},{3,1},{4,6},{5,7},{6,4},{7,5},{8,10},{9,11},{10,... | collective-permute-start | bytes 983048 | tf_op jit(solution)/shard_map/ppermute | solution.py:94
  452.9 29.5 %collective-permute-start.54 = (bf16[2,160,512]{2,1,0:T(8,128)(2,1)S(1)}, bf16[2,160,512]{2,1,0:T(8,128)(2,1)S(1)}, u32[]{:S(2)}, u32[]{:S(2)}) collective-permute-start(bf16[2,160,512]{2,1,0:T(8,128)(2,1)S(1)} %copy-done.66), channel_id=1, source_target_pairs={{0,3},{1,0},{2,1},{3,2},{4,7},{5,4},{6,5},{7,6},{8,11},{9,8},{10,9... | collective-permute-start | bytes 983048 | tf_op jit(solution)/shard_map/ppermute | solution.py:94
  458.6 11.1 %collective-permute-start.47 = (bf16[2,2,144,384]{3,2,1,0:T(8,128)(2,1)}, bf16[2,2,144,384]{3,2,1,0:T(8,128)(2,1)S(1)}, u32[]{:S(2)}, u32[]{:S(2)}) collective-permute-start(bf16[2,2,144,384]{3,2,1,0:T(8,128)(2,1)} %get-tuple-element.314), channel_id=1, source_target_pairs={{0,16},{4,20},{8,24},{12,28},{16,0},{20,4},{24,8},{28,12},{1,17},{... | collective-permute-start | bytes 1327112 | tf_op jit(solution)/shard_map/ppermute | solution.py:90
  458.8 10.8 %collective-permute-start.48 = (bf16[2,2,144,384]{3,2,1,0:T(8,128)(2,1)}, bf16[2,2,144,384]{3,2,1,0:T(8,128)(2,1)S(1)}, u32[]{:S(2)}, u32[]{:S(2)}) collective-permute-start(bf16[2,2,144,384]{3,2,1,0:T(8,128)(2,1)} %get-tuple-element.315), channel_id=1, source_target_pairs={{0,8},{4,12},{8,0},{12,4},{16,24},{20,28},{24,16},{28,20},{1,9},{5... | collective-permute-start | bytes 1327112 | tf_op jit(solution)/shard_map/ppermute | solution.py:90
  485.6 2.7 collective-permute-start.55
  486.7 7.0 %collective-permute-start.49 = (bf16[1,2,144,384]{3,2,1,0:T(8,128)(2,1)S(1)}, bf16[1,2,144,384]{3,2,1,0:T(8,128)(2,1)S(1)}, u32[]{:S(2)}, u32[]{:S(2)}) collective-permute-start(bf16[1,2,144,384]{3,2,1,0:T(8,128)(2,1)S(1)} %copy-done.77), channel_id=1, source_target_pairs={{0,8},{4,12},{8,0},{12,4},{16,24},{20,28},{24,16},{28,20},{1,9},{5... | collective-permute-start | bytes 663560 | tf_op jit(solution)/shard_map/ppermute | solution.py:90
  487.3 6.7 %collective-permute-start.50 = (bf16[1,2,144,384]{3,2,1,0:T(8,128)(2,1)S(1)}, bf16[1,2,144,384]{3,2,1,0:T(8,128)(2,1)S(1)}, u32[]{:S(2)}, u32[]{:S(2)}) collective-permute-start(bf16[1,2,144,384]{3,2,1,0:T(8,128)(2,1)S(1)} %copy-done.76), channel_id=1, source_target_pairs={{0,16},{4,20},{8,24},{12,28},{16,0},{20,4},{24,8},{28,12},{1,17},{... | collective-permute-start | bytes 663560 | tf_op jit(solution)/shard_map/ppermute | solution.py:90
  496.9 2.4 collective-permute-start.51
  (74 other events, 584.5 us)
Sparse Core Ops, SparseCore 0:
  54.9 161.5 all-gather.4
  448.8 29.7 all-gather.6

commit v6 on v5

--- a/solution.py
+++ b/solution.py
@@ -136,7 +136,7 @@
         in_specs=[pl.BlockSpec(memory_space=pltpu.SMEM)]
         + [pl.BlockSpec(memory_space=pltpu.VMEM)] * len(ins),
         out_specs=[pl.BlockSpec(memory_space=pltpu.VMEM)] * len(outs),
-        compiler_params=pltpu.CompilerParams(vmem_limit_bytes=60 * MIB),
+        compiler_params=pltpu.CompilerParams(vmem_limit_bytes=2 * size + 16 * MIB),
         cost_estimate=cost(size / 2.2e6),
     )(jnp.stack([jnp.asarray(v, jnp.int32) for v in scalars]), *ins)
 
@@ -519,7 +519,7 @@
         scratch_shapes=[
             pltpu.VMEM((lefts[which[i]].shape[1], width), jnp.float32) for i in held
         ],
-        compiler_params=pltpu.CompilerParams(vmem_limit_bytes=60 * MIB),
+        compiler_params=pltpu.CompilerParams(vmem_limit_bytes=40 * MIB),
         cost_estimate=cost(13.0),
     )(jnp.asarray(core, jnp.int32)[None], *lefts, *rights, *others)
 

time: 522 us -> 516 us (0.989)
  local copies, waits for them, and re-layouts: 39.9 us -> 71.7 us
  Pallas kernels: 232 us -> 203 us
  waiting for transfers between devices: 135 us -> 125 us
    unnamed x166 -> x214, local copies, waits for them, and re-layouts: 18 us -> 49.9 us
    pallas_call x14, Pallas kernels: 54.2 us -> 32 us  [small_call(): pl.pallas_call(body, out_shape=outs, in_specs=[pl.BlockSpec(memory_space=...]
    ppermute x35, starting transfers between devices: 24.8 us -> 31.1 us  [swap_bit(): return lax.ppermute(values, 'dp', [(i, i ^ 1 << bit) for i in range(size)])]
    pallas_call x2, Pallas kernels: 27.3 us -> 21.3 us  [pack_head_grads(): pl.pallas_call(body, grid=(count,), out_shape=[low_shape(count, mids, tot...]
    ppermute x18, waiting for transfers between devices: 82.2 us -> 76.3 us  [shift_copy(): lax.ppermute(values, 'copy', [(i, (i + shift) % size) for i in range(size)])]
  transfers between devices with their start and end apart: 59 -> 59, of which waited for: 23 -> 21; matrix products, arithmetic and copies ran while one was open for 10% -> 9% of each run, Pallas kernels for 36% -> 31%
where the time goes in v6:
time: 516 us; the launch traced here: 509 us
  Pallas kernels  203 us (39%)
  waiting for transfers between devices  125 us (24%)
  local copies, waits for them, and re-layouts  71.7 us (14%)
  starting transfers between devices  54.9 us (11%)
  other arithmetic  26.6 us (5%)
  between operations  15.6 us (3%)
  matrix products  12.3 us (2%)
    ppermute x18, waiting for transfers between devices, shift_copy(): lax.ppermute(values, 'copy', [(i, (i + shift) % size) for i in range(size)])  76.3 us
    unnamed x214, local copies, waits for them, and re-layouts  49.9 us
    pallas_call x1, Pallas kernels, head_kernel(): pl.pallas_call(body, grid=(rows // step,), out_shape=[low_shape(rows, WID...  43.4 us
    pallas_call x14, Pallas kernels, small_call(): pl.pallas_call(body, out_shape=outs, in_specs=[pl.BlockSpec(memory_space=...  32 us
    ppermute x35, starting transfers between devices, swap_bit(): return lax.ppermute(values, 'dp', [(i, i ^ 1 << bit) for i in range(size)])  31.1 us
    ppermute x35, waiting for transfers between devices, swap_bit(): return lax.ppermute(values, 'dp', [(i, i ^ 1 << bit) for i in range(size)])  30.3 us
    pallas_call x2, Pallas kernels, attention_back(): pl.pallas_call(body, grid=(1, HEADS // 2), out_shape=[low_shape(micros *...  24.8 us
    pallas_call x1, Pallas kernels, block_back_one(): pl.pallas_call(body, grid=(steps,), out_shape=outs + [jax.ShapeDtypeStruc...  24 us
  transfers between devices with their start and end apart: 59, of which 21 were waited for; matrix products, arithmetic and copies ran while one was open for 9% of the time, Pallas kernels for 31%

profile of v6, /device:TPU:9, one launch (start us, length us, event | category | flops | bytes accessed | tf_op | source)
XLA Modules:
  0.0 509.4 jit_solution(3595443578043362895)
XLA Ops:
  11.1 2.5 collective-permute-start.1
  13.6 2.2 collective-permute-start.2
  16.4 8.0 %collective-permute-done.1 = bf16[112,768]{1,0:T(8,128)(2,1)S(1)} collective-permute-done((bf16[112,768]{1,0:T(8,128)(2,1)S(1)}, bf16[112,768]{1,0:T(8,128)(2,1)S(1)}, u32[]{:S(2)}, u32[]{:S(2)}) %collective-permute-start.1) | collective-permute-done | bytes 172064 | tf_op jit(solution)/shard_map/ppermute | solution.py:94
  24.3 3.7 collective-permute-done.2
  29.3 2.1 collective-permute-start.4
  32.6 3.7 collective-permute-done.3
  36.3 12.2 %collective-permute-done.4 = bf16[192,768]{1,0:T(8,128)(2,1)S(1)} collective-permute-done((bf16[192,768]{1,0:T(8,128)(2,1)S(1)}, bf16[192,768]{1,0:T(8,128)(2,1)S(1)}, u32[]{:S(2)}, u32[]{:S(2)}) %collective-permute-start.4) | collective-permute-done | bytes 294944 | tf_op jit(solution)/shard_map/ppermute | solution.py:94
  48.5 6.3 %collective-permute-done.5 = bf16[192,768]{1,0:T(8,128)(2,1)S(1)} collective-permute-done((bf16[192,768]{1,0:T(8,128)(2,1)S(1)}, bf16[192,768]{1,0:T(8,128)(2,1)S(1)}, u32[]{:S(2)}, u32[]{:S(2)}) %collective-permute-start.5) | collective-permute-done | bytes 294944 | tf_op jit(solution)/shard_map/ppermute | solution.py:94
  62.7 1.7 collective-permute-start.14
  64.3 1.8 collective-permute-start.15
  66.1 2.4 collective-permute-done.17
  69.9 5.2 %collective-permute-done.21 = bf16[4,64,768]{2,1,0:T(8,128)(2,1)S(1)} collective-permute-done((bf16[4,64,768]{2,1,0:T(8,128)(2,1)S(1)}, bf16[4,64,768]{2,1,0:T(8,128)(2,1)S(1)}, u32[]{:S(2)}, u32[]{:S(2)}) %collective-permute-start.21) | collective-permute-done | bytes 393248 | tf_op jit(solution)/shard_map/ppermute | solution.py:90
  77.6 2.0 collective-permute-start.10
  79.5 16.8 %collective-permute-done.15 = bf16[2,96,768]{2,1,0:T(8,128)(2,1)S(1)} collective-permute-done((bf16[2,96,768]{2,1,0:T(8,128)(2,1)S(1)}, bf16[2,96,768]{2,1,0:T(8,128)(2,1)S(1)}, u32[]{:S(2)}, u32[]{:S(2)}) %collective-permute-start.15) | collective-permute-done | bytes 294944 | tf_op jit(solution)/shard_map/ppermute | solution.py:94
  96.6 6.4 %collective-permute-done.16 = bf16[2,96,768]{2,1,0:T(8,128)(2,1)S(1)} collective-permute-done((bf16[2,96,768]{2,1,0:T(8,128)(2,1)S(1)}, bf16[2,96,768]{2,1,0:T(8,128)(2,1)S(1)}, u32[]{:S(2)}, u32[]{:S(2)}) %collective-permute-start.16) | collective-permute-done | bytes 294944 | tf_op jit(solution)/shard_map/ppermute | solution.py:94
  108.1 1.7 pad_maximum_fusion.1.refs_4_
  109.8 2.9 collective-permute-done.6
  112.7 1.4 collective-permute-start.11
  115.4 4.5 collective-permute-start.12
  120.9 7.5 %shard_map.395 = bf16[32,112,768]{2,1,0:T(8,128)(2,1)S(1)} custom-call(s32[2]{0:T(128)S(1)} %pad_add_fusion.at, bf16[2,4,48,768]{3,2,1,0:T(8,128)(2,1)S(1)} %pad_maximum_fusion.6.refs_0_, bf16[2,4,48,768]{3,2,1,0:T(8,128)(2,1)S(1)} %collective-permute-done.18.refs_1_, bf16[2,4,48,768]{3,2,1,0:T(8,128)(2,1)S(1)} %collective-permute-done.19.refs_2_, ...), custom_call_target="tpu_custom_call" | custom-call | flops 8000000000 | bytes 100000 | tf_op jit(solution)/shard_map/pallas_call | solution.py:549
  134.5 15.3 %shard_map.397 = bf16[768,768]{1,0:T(8,128)(2,1)S(1)} custom-call(s32[768,1]{1,0:T(8,128)S(1)} %bitcast.163, s32[2,1,384]{2,1,0:T(1,128)S(1)} %broadcast_in_dim.63.row_ref, bf16[768,768]{1,0:T(8,128)(2,1)S(1)} %add_convert_fusion.3.q_ref, bf16[768,768]{1,0:T(8,128)(2,1)S(1)} %convolution_convert_fusion.k_ref, bf16[768,768]{1,0:T(8,128)(2,1)S(1)} %add_convert_fusion.2.v_ref), custom_call_target="tpu_custom_call" | custom-call | flops 15000000512 | bytes 100000 | tf_op jit(solution)/shard_map/pallas_call | solution.py:379
  151.7 3.7 collective-permute-done.7.refs_1_
  156.8 1.5 add_convert_fusion.1
  158.3 1.5 convolution_convert_fusion.1.refs_11_
  161.1 13.9 %shard_map.394 = bf16[32,192,768]{2,1,0:T(8,128)(2,1)S(1)} custom-call(s32[2]{0:T(128)S(1)} %pad_add_fusion.at, bf16[2,4,96,768]{3,2,1,0:T(8,128)(2,1)S(1)} %pad_maximum_fusion.refs_0_, bf16[2,4,96,768]{3,2,1,0:T(8,128)(2,1)S(1)} %collective-permute-done.7.refs_1_, bf16[2,4,96,768]{3,2,1,0:T(8,128)(2,1)S(1)} %collective-permute-done.8.refs_2_, ...), custom_call_target="tpu_custom_call" | custom-call | flops 8000000000 | bytes 100000 | tf_op jit(solution)/shard_map/pallas_call | solution.py:549
  175.0 2.6 slice.355
  179.0 18.1 %shard_map.398 = (bf16[768,768]{1,0:T(8,128)(2,1)S(1)}, bf16[768,3072]{1,0:T(8,128)(2,1)}, bf16[4,192,768]{2,1,0:T(8,128)(2,1)S(1)}) custom-call(s32[1]{0:T(128)} %bitcast.at, bf16[768,768]{1,0:T(8,128)(2,1)S(1)} %bitcast.161, bf16[768,768]{1,0:T(8,128)(2,1)S(1)} %bitcast.159, bf16[768,768]{1,0:T(8,128)(2,1)S(1)} %bitcast.157, bf16[768,768]{1,0:T(8,128)(2,1)} %bitcast.184, ...), custom_call_target="tpu_custom_call" | custom-call | flops 17999998976 | bytes 100000 | tf_op jit(solution)/shard_map/pallas_call | solution.py:905
  199.1 18.6 %all-gather.5.cloned.1.call-done = bf16[9728,1024]{1,0:T(8,128)(2,1)} async-done(((bf16[304,1024]{1,0:T(8,128)(2,1)}), bf16[9728,1024]{1,0:T(8,128)(2,1)}) %all-gather.5.cloned.1.call-update) | async-done | bytes 19922960 | tf_op jit(solution)/shard_map/all_gather | solution.py:1188
  219.0 1.8 slice.361
  220.8 3.4 slice.357
  229.3 43.4 %shard_map.400 = (bf16[768,1024]{1,0:T(8,128)(2,1)}, bf16[768,1024]{1,0:T(8,128)(2,1)}, bf16[768,1024]{1,0:T(8,128)(2,1)}, bf16[768,1024]{1,0:T(8,128)(2,1)}, bf...) custom-call(bf16[768,1024]{1,0:T(8,128)(2,1)} %bitcast.178, ...), custom_call_target="tpu_custom_call" | custom-call | flops 44999999488 | bytes 100000 | tf_op jit(solution)/shard_map/pallas_call | solution.py:798
  278.5 1.4 copy-done.66
  279.9 1.4 copy-done.67
  284.1 10.4 %shard_map.401 = (bf16[4,8,128,512]{3,2,1,0:T(8,128)(2,1)}, bf16[4,8,128,512]{3,2,1,0:T(8,128)(2,1)}, f32[4,1024]{1,0:T(4,128)S(1)}) custom-call(s32[1]{0:T(128)} %bitcast.49.at, bf16[768,1024]{1,0:T(8,128)(2,1)S(1)} %copy-done.62, bf16[768,1024]{1,0:T(8,128)(2,1)S(1)} %copy-done.65, bf16[768,1024]{1,0:T(8,128)(2,1)S(1)} %copy-done.64, ...), custom_call_target="tpu_custom_call" | custom-call | flops 12999999488 | bytes 100000 | tf_op jit(solution)/shard_map/pallas_call | solution.py:512
  294.5 4.1 collective-permute-done.26.refs_2_
  298.5 1.9 collective-permute-done.27.refs_3_
  301.2 2.2 fusion.10.refs_9_
  304.9 2.3 collective-permute-start.31
  307.2 1.4 copy-done.63
  314.3 11.0 %shard_map.403 = (bf16[4,8,160,512]{3,2,1,0:T(8,128)(2,1)}, bf16[4,8,160,512]{3,2,1,0:T(8,128)(2,1)}, f32[48,1024]{1,0:T(8,128)S(1)}) custom-call(s32[1]{0:T(128)} %bitcast.49.at, bf16[768,1024]{1,0:T(8,128)(2,1)S(1)} %copy-done.63, bf16[8,1024]{1,0:T(8,128)(2,1)S(1)} %get-tuple-element.472.refs_1_, bf16[768,768]{1,0:T(8,128)(2,1)S(1)} %copy-done.10, ...), custom_call_target="tpu_custom_call" | custom-call | flops 12999999488 | bytes 100000 | tf_op jit(solution)/shard_map/pallas_call | solution.py:512
  325.2 3.2 shard_map.404
  333.9 1.6 collective-permute-start.34
  336.9 24.0 %shard_map.405 = (bf16[4,2,192,384]{3,2,1,0:T(8,128)(2,1)}, bf16[4,2,192,384]{3,2,1,0:T(8,128)(2,1)}, f32[768,768]{1,0:T(8,128)}, bf16[768,768]{1,0:T(8,128)(2,1...) custom-call(s32[1]{0:T(128)} %bitcast.49.at, bf16[2,96,768]{2,1,0:T(8,128)(2,1)} %copy-done.15, ...), custom_call_target="tpu_custom_call" | custom-call | flops 24000000000 | bytes 100000 | tf_op jit(solution)/shard_map/pallas_call | solution.py:1002
  363.4 2.7 shard_map.406
  369.9 6.2 %shard_map.407 = (bf16[2,8,96,512]{3,2,1,0:T(8,128)(2,1)S(1)}, bf16[2,8,96,512]{3,2,1,0:T(8,128)(2,1)S(1)}, bf16[2,8,64,512]{3,2,1,0:T(8,128)(2,1)}, bf16[2,8,64,512]{3,2,1,0:T(8,128)(2,1)S(1)}) custom-call(s32[2]{0:T(128)S(1)} %get-tuple-element.475.at, bf16[4,8,160,512]{3,2,1,0:T(8,128)(2,1)} %get-tuple-element.221.refs_0_, ...), custom_call_target="tpu_custom_call" | custom-call | flops 7149381632 | bytes 100000 | tf_op jit(solution)/shard_map/pallas_call | solution.py:133
  379.8 12.5 %shard_map.408 = (bf16[768,768]{1,0:T(8,128)(2,1)}, bf16[768,768]{1,0:T(8,128)(2,1)}, bf16[768,768]{1,0:T(8,128)(2,1)}) custom-call(s32[768,1]{1,0:T(8,128)} %bitcast.164, s32[2,1,384]{2,1,0:T(1,128)} %copy-done.12, bf16[768,768]{1,0:T(8,128)(2,1)} %copy-done.47, bf16[768,768]{1,0:T(8,128)(2,1)} %copy-done.36, bf16[768,768]{1,0:T(8,128)(2,1)} %copy-done.46, ...), custom_call_target="tpu_custom_call" | custom-call | flops 12000000000 | bytes 100000 | tf_op jit(solution)/shard_map/pallas_call | solution.py:414
  394.3 2.2 shard_map.409
  397.3 1.7 add.296
  399.0 1.7 collective-permute-start.41
  400.7 12.4 %shard_map.410 = (bf16[768,768]{1,0:T(8,128)(2,1)}, bf16[768,768]{1,0:T(8,128)(2,1)}, bf16[768,768]{1,0:T(8,128)(2,1)}) custom-call(s32[768,1]{1,0:T(8,128)} %bitcast.165, s32[2,1,384]{2,1,0:T(1,128)} %copy-done.12, bf16[768,768]{1,0:T(8,128)(2,1)} %copy-done.47, ...), custom_call_target="tpu_custom_call", output_to_operand_aliasing={{0}: (6, {}), {1}: (7, {}), {2}: (8, {})} | custom-call | flops 12000000000 | bytes 100000 | tf_op jit(solution)/shard_map/pallas_call | solution.py:414
  413.1 1.9 collective-permute-done.39.got_one
  415.0 1.4 copy-done.54
  417.6 2.7 shard_map.411
  431.3 8.2 %shard_map.413 = (bf16[4,2,96,384]{3,2,1,0:T(8,128)(2,1)}, bf16[4,2,96,384]{3,2,1,0:T(8,128)(2,1)S(1)}, f32[2,96,768]{2,1,0:T(8,128)}, f32[12,768]{1,0:T(8,128)S(1)}) custom-call(s32[1]{0:T(128)} %bitcast.49.at, bf16[768,768]{1,0:T(8,128)(2,1)S(1)} %copy-done.59, bf16[768,768]{1,0:T(8,128)(2,1)S(1)} %copy-done.60, bf16[768,768]{1,0:T(8,128)(2,1)S(1)} %copy-done.61, ...), custom_call_target="tpu_custom_call" | custom-call | flops 7046050816 | bytes 100000 | tf_op jit(solution)/shard_map/pallas_call | solution.py:133
  440.1 1.4 shard_map.414
  442.2 3.0 collective-permute-start.45
  445.4 1.6 select_maximum_fusion
  447.1 1.7 slice_bitcast_fusion.2
  449.4 2.4 collective-permute-start.53
  458.3 9.4 %collective-permute-done.47.got_one = bf16[2,2,144,384]{3,2,1,0:T(8,128)(2,1)S(1)} collective-permute-done((bf16[2,2,144,384]{3,2,1,0:T(8,128)(2,1)S(1)}, bf16[2,2,144,384]{3,2,1,0:T(8,128)(2,1)S(1)}, u32[]{:S(2)}, u32[]{:S(2)}) %collective-permute-start.47) | collective-permute-done | bytes 442400 | tf_op jit(solution)/shard_map/ppermute | solution.py:90
  468.4 9.2 %collective-permute-done.53.refs_2_ = bf16[2,160,512]{2,1,0:T(8,128)(2,1)S(1)} collective-permute-done((bf16[2,160,512]{2,1,0:T(8,128)(2,1)S(1)}, bf16[2,160,512]{2,1,0:T(8,128)(2,1)S(1)}, u32[]{:S(2)}, u32[]{:S(2)}) %collective-permute-start.53) | collective-permute-done | bytes 327712 | tf_op jit(solution)/shard_map/ppermute | solution.py:94
  477.6 3.6 collective-permute-done.54.refs_3_
  486.2 4.3 collective-permute-done.49
  496.5 1.6 slice_add_fusion
  (412 shorter events, 118.6 us)
Async XLA Ops:
  7.2 210.5 %all-gather.5.cloned.1.call-start = ((), (), s32[]{:S(2)}) async-start(), calls=%async_computation | async-start | bytes 20545536 | tf_op jit(solution)/shard_map/all_gather | solution.py:1188
  11.1 5.3 %collective-permute-start = (bf16[112,768]{1,0:T(8,128)(2,1)S(1)}, bf16[112,768]{1,0:T(8,128)(2,1)S(1)}, u32[]{:S(2)}, u32[]{:S(2)}) collective-permute-start(bf16[112,768]{1,0:T(8,128)(2,1)S(1)} %shard_map.391), channel_id=1, source_target_pairs={{0,3},{1,0},{2,1},{3,2},{4,7},{5,4},{6,5},{7,6},{8,11},{9,8},{10,9... | collective-permute-start | bytes 516104 | tf_op jit(solution)/shard_map/ppermute | solution.py:94
  11.1 13.2 %collective-permute-start.1 = (bf16[112,768]{1,0:T(8,128)(2,1)S(1)}, bf16[112,768]{1,0:T(8,128)(2,1)S(1)}, u32[]{:S(2)}, u32[]{:S(2)}) collective-permute-start(bf16[112,768]{1,0:T(8,128)(2,1)S(1)} %shard_map.391), channel_id=1, source_target_pairs={{0,2},{1,3},{2,0},{3,1},{4,6},{5,7},{6,4},{7,5},{8,10},{9,11},{10,... | collective-permute-start | bytes 516104 | tf_op jit(solution)/shard_map/ppermute | solution.py:94
  13.6 14.4 %collective-permute-start.2 = (bf16[112,768]{1,0:T(8,128)(2,1)S(1)}, bf16[112,768]{1,0:T(8,128)(2,1)S(1)}, u32[]{:S(2)}, u32[]{:S(2)}) collective-permute-start(bf16[112,768]{1,0:T(8,128)(2,1)S(1)} %shard_map.391), channel_id=1, source_target_pairs={{0,1},{1,2},{2,3},{3,0},{4,5},{5,6},{6,7},{7,4},{8,9},{9,10},{10,1... | collective-permute-start | bytes 516104 | tf_op jit(solution)/shard_map/ppermute | solution.py:94
  28.0 8.2 %collective-permute-start.3 = (bf16[192,768]{1,0:T(8,128)(2,1)S(1)}, bf16[192,768]{1,0:T(8,128)(2,1)S(1)}, u32[]{:S(2)}, u32[]{:S(2)}) collective-permute-start(bf16[192,768]{1,0:T(8,128)(2,1)S(1)} %shard_map.392), channel_id=1, source_target_pairs={{0,3},{1,0},{2,1},{3,2},{4,7},{5,4},{6,5},{7,6},{8,11},{9,8},{10,9... | collective-permute-start | bytes 884744 | tf_op jit(solution)/shard_map/ppermute | solution.py:94
  29.3 19.1 %collective-permute-start.4 = (bf16[192,768]{1,0:T(8,128)(2,1)S(1)}, bf16[192,768]{1,0:T(8,128)(2,1)S(1)}, u32[]{:S(2)}, u32[]{:S(2)}) collective-permute-start(bf16[192,768]{1,0:T(8,128)(2,1)S(1)} %shard_map.392), channel_id=1, source_target_pairs={{0,2},{1,3},{2,0},{3,1},{4,6},{5,7},{6,4},{7,5},{8,10},{9,11},{10,... | collective-permute-start | bytes 884744 | tf_op jit(solution)/shard_map/ppermute | solution.py:94
  31.4 23.4 %collective-permute-start.5 = (bf16[192,768]{1,0:T(8,128)(2,1)S(1)}, bf16[192,768]{1,0:T(8,128)(2,1)S(1)}, u32[]{:S(2)}, u32[]{:S(2)}) collective-permute-start(bf16[192,768]{1,0:T(8,128)(2,1)S(1)} %shard_map.392), channel_id=1, source_target_pairs={{0,1},{1,2},{2,3},{3,0},{4,5},{5,6},{6,7},{7,4},{8,9},{9,10},{10,1... | collective-permute-start | bytes 884744 | tf_op jit(solution)/shard_map/ppermute | solution.py:94
  32.5 25.1 %copy-start.102 = (bf16[16]{0:T(256)(128)(2,1)S(1)}, bf16[16]{0:T(256)(128)(2,1)}, u32[]{:S(2)}) copy-start(bf16[16]{0:T(256)(128)(2,1)} %param.47) | copy-start | bytes 100
  54.8 441.7 %all-gather.7.cloned.1.call-start = ((), (), s32[]{:S(2)}) async-start(), calls=%async_computation.1 | async-start | bytes 2359296 | tf_op jit(solution)/shard_map/all_gather | solution.py:1471
  55.0 79.4 %copy-start.12 = (s32[2,1,384]{2,1,0:T(1,128)}, s32[2,1,384]{2,1,0:T(1,128)S(1)}, u32[]{:S(2)}) copy-start(s32[2,1,384]{2,1,0:T(1,128)S(1)} %broadcast_in_dim.63.row_ref) | copy-start | bytes 9220
  55.2 79.2 %copy-start.7 = (s32[1,768]{0,1:T(8,128)}, s32[1,768]{0,1:T(8,128)S(1)}, u32[]{:S(2)}) copy-start(s32[1,768]{0,1:T(8,128)S(1)} %copy.88) | copy-start | bytes 9220
  59.9 8.5 %collective-permute-start.17 = (bf16[4,48,768]{2,1,0:T(8,128)(2,1)S(1)}, bf16[4,48,768]{2,1,0:T(8,128)(2,1)S(1)}, u32[]{:S(2)}, u32[]{:S(2)}) collective-permute-start(bf16[4,48,768]{2,1,0:T(8,128)(2,1)S(1)} %get-tuple-element.450), channel_id=1, source_target_pairs={{0,16},{4,20},{8,24},{12,28},{16,0},{20,4},{24,8},{28,12},{1,17},{... | collective-permute-start | bytes 884744 | tf_op jit(solution)/shard_map/ppermute | solution.py:90
  61.3 13.7 %collective-permute-start.21 = (bf16[4,64,768]{2,1,0:T(8,128)(2,1)S(1)}, bf16[4,64,768]{2,1,0:T(8,128)(2,1)S(1)}, u32[]{:S(2)}, u32[]{:S(2)}) collective-permute-start(bf16[4,64,768]{2,1,0:T(8,128)(2,1)S(1)} %get-tuple-element.442), channel_id=1, source_target_pairs={{0,8},{4,12},{8,0},{12,4},{16,24},{20,28},{24,16},{28,20},{1,9},{5... | collective-permute-start | bytes 1179656 | tf_op jit(solution)/shard_map/ppermute | solution.py:90
  62.7 14.9 %collective-permute-start.14 = (bf16[2,96,768]{2,1,0:T(8,128)(2,1)S(1)}, bf16[2,96,768]{2,1,0:T(8,128)(2,1)S(1)}, u32[]{:S(2)}, u32[]{:S(2)}) collective-permute-start(bf16[2,96,768]{2,1,0:T(8,128)(2,1)S(1)} %bitcast.197), channel_id=1, source_target_pairs={{0,3},{1,0},{2,1},{3,2},{4,7},{5,4},{6,5},{7,6},{8,11},{9,8},{10,9... | collective-permute-start | bytes 884744 | tf_op jit(solution)/shard_map/ppermute | solution.py:94
  64.3 32.0 %collective-permute-start.15 = (bf16[2,96,768]{2,1,0:T(8,128)(2,1)S(1)}, bf16[2,96,768]{2,1,0:T(8,128)(2,1)S(1)}, u32[]{:S(2)}, u32[]{:S(2)}) collective-permute-start(bf16[2,96,768]{2,1,0:T(8,128)(2,1)S(1)} %bitcast.198), channel_id=1, source_target_pairs={{0,2},{1,3},{2,0},{3,1},{4,6},{5,7},{6,4},{7,5},{8,10},{9,11},{10,... | collective-permute-start | bytes 884744 | tf_op jit(solution)/shard_map/ppermute | solution.py:94
  66.1 36.9 %collective-permute-start.16 = (bf16[2,96,768]{2,1,0:T(8,128)(2,1)S(1)}, bf16[2,96,768]{2,1,0:T(8,128)(2,1)S(1)}, u32[]{:S(2)}, u32[]{:S(2)}) collective-permute-start(bf16[2,96,768]{2,1,0:T(8,128)(2,1)S(1)} %bitcast.199), channel_id=1, source_target_pairs={{0,1},{1,2},{2,3},{3,0},{4,5},{5,6},{6,7},{7,4},{8,9},{9,10},{10,1... | collective-permute-start | bytes 884744 | tf_op jit(solution)/shard_map/ppermute | solution.py:94
  68.5 37.9 %collective-permute-start.18 = (bf16[2,4,48,768]{3,2,1,0:T(8,128)(2,1)S(1)}, bf16[2,4,48,768]{3,2,1,0:T(8,128)(2,1)S(1)}, u32[]{:S(2)}, u32[]{:S(2)}) collective-permute-start(bf16[2,4,48,768]{3,2,1,0:T(8,128)(2,1)S(1)} %pad_maximum_fusion.6.refs_0_), channel_id=1, source_target_pairs={{0,8},{4,12},{8,0},{12,4},{16,24},{20,28},{24,16},{28,20},{1,9},{5... | collective-permute-start | bytes 1769480 | tf_op jit(solution)/shard_map/ppermute | solution.py:90
  75.2 29.8 %collective-permute-start.22 = (bf16[2,4,64,768]{3,2,1,0:T(8,128)(2,1)S(1)}, bf16[2,4,64,768]{3,2,1,0:T(8,128)(2,1)}, u32[]{:S(2)}, u32[]{:S(2)}) collective-permute-start(bf16[2,4,64,768]{3,2,1,0:T(8,128)(2,1)S(1)} %pad_maximum_fusion.3.refs_4_), channel_id=1, source_target_pairs={{0,16},{4,20},{8,24},{12,28},{16,0},{20,4},{24,8},{28,12},{1,17},{... | collective-permute-start | bytes 2359304 | tf_op jit(solution)/shard_map/ppermute | solution.py:90
  77.6 29.3 %collective-permute-start.10 = (bf16[4,96,768]{2,1,0:T(8,128)(2,1)}, bf16[4,96,768]{2,1,0:T(8,128)(2,1)}, u32[]{:S(2)}, u32[]{:S(2)}) collective-permute-start(bf16[4,96,768]{2,1,0:T(8,128)(2,1)} %get-tuple-element.424), channel_id=1, source_target_pairs={{0,8},{4,12},{8,0},{12,4},{16,24},{20,28},{24,16},{28,20},{1,9},{5... | collective-permute-start | bytes 1769480 | tf_op jit(solution)/shard_map/ppermute | solution.py:90
  96.3 16.4 %collective-permute-start.6 = (bf16[4,96,768]{2,1,0:T(8,128)(2,1)}, bf16[4,96,768]{2,1,0:T(8,128)(2,1)}, u32[]{:S(2)}, u32[]{:S(2)}) collective-permute-start(bf16[4,96,768]{2,1,0:T(8,128)(2,1)} %get-tuple-element.426), channel_id=1, source_target_pairs={{0,16},{4,20},{8,24},{12,28},{16,0},{20,4},{24,8},{28,12},{1,17},{... | collective-permute-start | bytes 1769480 | tf_op jit(solution)/shard_map/ppermute | solution.py:90
  103.0 16.9 %collective-permute-start.23 = (bf16[2,4,64,768]{3,2,1,0:T(8,128)(2,1)S(1)}, bf16[2,4,64,768]{3,2,1,0:T(8,128)(2,1)}, u32[]{:S(2)}, u32[]{:S(2)}) collective-permute-start(bf16[2,4,64,768]{3,2,1,0:T(8,128)(2,1)S(1)} %pad_maximum_fusion.3.refs_4_), channel_id=1, source_target_pairs={{0,4},{4,0},{8,12},{12,8},{16,20},{20,16},{24,28},{28,24},{1,5},{5... | collective-permute-start | bytes 2359304 | tf_op jit(solution)/shard_map/ppermute | solution.py:90
  105.0 15.9 %collective-permute-start.24 = (bf16[2,4,64,768]{3,2,1,0:T(8,128)(2,1)}, bf16[2,4,64,768]{3,2,1,0:T(8,128)(2,1)}, u32[]{:S(2)}, u32[]{:S(2)}) collective-permute-start(bf16[2,4,64,768]{3,2,1,0:T(8,128)(2,1)} %collective-permute-done.22.refs_5_), channel_id=1, source_target_pairs={{0,4},{4,0},{8,12},{12,8},{16,20},{20,16},{24,28},{28,24},{1,5},{5... | collective-permute-start | bytes 2359304 | tf_op jit(solution)/shard_map/ppermute | solution.py:90
  106.4 9.0 %collective-permute-start.19 = (bf16[2,4,48,768]{3,2,1,0:T(8,128)(2,1)S(1)}, bf16[2,4,48,768]{3,2,1,0:T(8,128)(2,1)S(1)}, u32[]{:S(2)}, u32[]{:S(2)}) collective-permute-start(bf16[2,4,48,768]{3,2,1,0:T(8,128)(2,1)S(1)} %pad_maximum_fusion.6.refs_0_), channel_id=1, source_target_pairs={{0,4},{4,0},{8,12},{12,8},{16,20},{20,16},{24,28},{28,24},{1,5},{5... | collective-permute-start | bytes 1769480 | tf_op jit(solution)/shard_map/ppermute | solution.py:90
  106.9 13.6 %collective-permute-start.20 = (bf16[2,4,48,768]{3,2,1,0:T(8,128)(2,1)S(1)}, bf16[2,4,48,768]{3,2,1,0:T(8,128)(2,1)S(1)}, u32[]{:S(2)}, u32[]{:S(2)}) collective-permute-start(bf16[2,4,48,768]{3,2,1,0:T(8,128)(2,1)S(1)} %collective-permute-done.18.refs_1_), channel_id=1, source_target_pairs={{0,4},{4,0},{8,12},{12,8},{16,20},{20,16},{24,28},{28,24},{1,5},{5... | collective-permute-start | bytes 1769480 | tf_op jit(solution)/shard_map/ppermute | solution.py:90
  108.1 51.7 %copy-start.79 = (f32[768,768]{1,0:T(8,128)}, f32[768,768]{1,0:T(8,128)S(1)}, u32[]{:S(2)}) copy-start(f32[768,768]{1,0:T(8,128)S(1)} %fusion.7.refs_10_) | copy-start | bytes 7077892
  112.7 38.8 %collective-permute-start.11 = (bf16[2,4,96,768]{3,2,1,0:T(8,128)(2,1)S(1)}, bf16[2,4,96,768]{3,2,1,0:T(8,128)(2,1)S(1)}, u32[]{:S(2)}, u32[]{:S(2)}) collective-permute-start(bf16[2,4,96,768]{3,2,1,0:T(8,128)(2,1)S(1)} %pad_maximum_fusion.1.refs_4_), channel_id=1, source_target_pairs={{0,16},{4,20},{8,24},{12,28},{16,0},{20,4},{24,8},{28,12},{1,17},{... | collective-permute-start | bytes 3538952 | tf_op jit(solution)/shard_map/ppermute | solution.py:90
  115.4 45.7 %collective-permute-start.12 = (bf16[2,4,96,768]{3,2,1,0:T(8,128)(2,1)S(1)}, bf16[2,4,96,768]{3,2,1,0:T(8,128)(2,1)S(1)}, u32[]{:S(2)}, u32[]{:S(2)}) collective-permute-start(bf16[2,4,96,768]{3,2,1,0:T(8,128)(2,1)S(1)} %pad_maximum_fusion.1.refs_4_), channel_id=1, source_target_pairs={{0,4},{4,0},{8,12},{12,8},{16,20},{20,16},{24,28},{28,24},{1,5},{5... | collective-permute-start | bytes 3538952 | tf_op jit(solution)/shard_map/ppermute | solution.py:90
  119.9 35.5 %collective-permute-start.7 = (bf16[2,4,96,768]{3,2,1,0:T(8,128)(2,1)S(1)}, bf16[2,4,96,768]{3,2,1,0:T(8,128)(2,1)S(1)}, u32[]{:S(2)}, u32[]{:S(2)}) collective-permute-start(bf16[2,4,96,768]{3,2,1,0:T(8,128)(2,1)S(1)} %pad_maximum_fusion.refs_0_), channel_id=1, source_target_pairs={{0,8},{4,12},{8,0},{12,4},{16,24},{20,28},{24,16},{28,20},{1,9},{5... | collective-permute-start | bytes 3538952 | tf_op jit(solution)/shard_map/ppermute | solution.py:90
  120.5 40.6 %collective-permute-start.8 = (bf16[2,4,96,768]{3,2,1,0:T(8,128)(2,1)S(1)}, bf16[2,4,96,768]{3,2,1,0:T(8,128)(2,1)S(1)}, u32[]{:S(2)}, u32[]{:S(2)}) collective-permute-start(bf16[2,4,96,768]{3,2,1,0:T(8,128)(2,1)S(1)} %pad_maximum_fusion.refs_0_), channel_id=1, source_target_pairs={{0,4},{4,0},{8,12},{12,8},{16,20},{20,16},{24,28},{28,24},{1,5},{5... | collective-permute-start | bytes 3538952 | tf_op jit(solution)/shard_map/ppermute | solution.py:90
  151.5 9.6 %collective-permute-start.13 = (bf16[2,4,96,768]{3,2,1,0:T(8,128)(2,1)S(1)}, bf16[2,4,96,768]{3,2,1,0:T(8,128)(2,1)S(1)}, u32[]{:S(2)}, u32[]{:S(2)}) collective-permute-start(bf16[2,4,96,768]{3,2,1,0:T(8,128)(2,1)S(1)} %collective-permute-done.11.refs_5_), channel_id=1, source_target_pairs={{0,4},{4,0},{8,12},{12,8},{16,20},{20,16},{24,28},{28,24},{1,5},{5... | collective-permute-start | bytes 3538952 | tf_op jit(solution)/shard_map/ppermute | solution.py:90
  155.4 5.7 %collective-permute-start.9 = (bf16[2,4,96,768]{3,2,1,0:T(8,128)(2,1)S(1)}, bf16[2,4,96,768]{3,2,1,0:T(8,128)(2,1)S(1)}, u32[]{:S(2)}, u32[]{:S(2)}) collective-permute-start(bf16[2,4,96,768]{3,2,1,0:T(8,128)(2,1)S(1)} %collective-permute-done.7.refs_1_), channel_id=1, source_target_pairs={{0,4},{4,0},{8,12},{12,8},{16,20},{20,16},{24,28},{28,24},{1,5},{5... | collective-permute-start | bytes 3538952 | tf_op jit(solution)/shard_map/ppermute | solution.py:90
  272.7 21.8 %collective-permute-start.25 = (bf16[2,96,768]{2,1,0:T(8,128)(2,1)}, bf16[2,96,768]{2,1,0:T(8,128)(2,1)S(1)}, u32[]{:S(2)}, u32[]{:S(2)}) collective-permute-start(bf16[2,96,768]{2,1,0:T(8,128)(2,1)} %get-tuple-element.199), channel_id=1, source_target_pairs={{0,1},{1,2},{2,3},{3,0},{4,5},{5,6},{6,7},{7,4},{8,9},{9,10},{10,1... | collective-permute-start | bytes 884744 | tf_op jit(solution)/shard_map/ppermute | solution.py:94
  272.8 25.7 %collective-permute-start.26 = (bf16[2,96,768]{2,1,0:T(8,128)(2,1)}, bf16[2,96,768]{2,1,0:T(8,128)(2,1)S(1)}, u32[]{:S(2)}, u32[]{:S(2)}) collective-permute-start(bf16[2,96,768]{2,1,0:T(8,128)(2,1)} %get-tuple-element.200), channel_id=1, source_target_pairs={{0,2},{1,3},{2,0},{3,1},{4,6},{5,7},{6,4},{7,5},{8,10},{9,11},{10,... | collective-permute-start | bytes 884744 | tf_op jit(solution)/shard_map/ppermute | solution.py:94
  273.7 26.7 %collective-permute-start.27 = (bf16[2,96,768]{2,1,0:T(8,128)(2,1)}, bf16[2,96,768]{2,1,0:T(8,128)(2,1)S(1)}, u32[]{:S(2)}, u32[]{:S(2)}) collective-permute-start(bf16[2,96,768]{2,1,0:T(8,128)(2,1)} %get-tuple-element.201), channel_id=1, source_target_pairs={{0,3},{1,0},{2,1},{3,2},{4,7},{5,4},{6,5},{7,6},{8,11},{9,8},{10,9... | collective-permute-start | bytes 884744 | tf_op jit(solution)/shard_map/ppermute | solution.py:94
  300.6 24.7 %copy-start.15 = (bf16[2,96,768]{2,1,0:T(8,128)(2,1)}, bf16[2,96,768]{2,1,0:T(8,128)(2,1)S(1)}, u32[]{:S(2)}) copy-start(bf16[2,96,768]{2,1,0:T(8,128)(2,1)S(1)} %shard_map.402.refs_0_) | copy-start | bytes 884740
  300.6 24.6 %collective-permute-start.28 = (bf16[4,8,128,512]{3,2,1,0:T(8,128)(2,1)}, bf16[4,8,128,512]{3,2,1,0:T(8,128)(2,1)}, u32[]{:S(2)}, u32[]{:S(2)}) collective-permute-start(bf16[4,8,128,512]{3,2,1,0:T(8,128)(2,1)} %get-tuple-element.223), channel_id=1, source_target_pairs={{0,4},{4,0},{8,12},{12,8},{16,20},{20,16},{24,28},{28,24},{1,5},{5... | collective-permute-start | bytes 12582920 | tf_op jit(solution)/shard_map/ppermute | solution.py:90
  303.5 26.9 %collective-permute-start.29 = (bf16[2,96,768]{2,1,0:T(8,128)(2,1)S(1)}, bf16[2,96,768]{2,1,0:T(8,128)(2,1)S(1)}, u32[]{:S(2)}, u32[]{:S(2)}) collective-permute-start(bf16[2,96,768]{2,1,0:T(8,128)(2,1)S(1)} %shard_map.402.refs_0_), channel_id=1, source_target_pairs={{0,3},{1,0},{2,1},{3,2},{4,7},{5,4},{6,5},{7,6},{8,11},{9,8},{10,9... | collective-permute-start | bytes 884744 | tf_op jit(solution)/shard_map/ppermute | solution.py:94
  303.5 26.9 %collective-permute-start.30 = (bf16[2,96,768]{2,1,0:T(8,128)(2,1)S(1)}, bf16[2,96,768]{2,1,0:T(8,128)(2,1)S(1)}, u32[]{:S(2)}, u32[]{:S(2)}) collective-permute-start(bf16[2,96,768]{2,1,0:T(8,128)(2,1)S(1)} %shard_map.402.refs_0_), channel_id=1, source_target_pairs={{0,2},{1,3},{2,0},{3,1},{4,6},{5,7},{6,4},{7,5},{8,10},{9,11},{10,... | collective-permute-start | bytes 884744 | tf_op jit(solution)/shard_map/ppermute | solution.py:94
  304.9 25.5 %collective-permute-start.31 = (bf16[2,96,768]{2,1,0:T(8,128)(2,1)S(1)}, bf16[2,96,768]{2,1,0:T(8,128)(2,1)S(1)}, u32[]{:S(2)}, u32[]{:S(2)}) collective-permute-start(bf16[2,96,768]{2,1,0:T(8,128)(2,1)S(1)} %shard_map.402.refs_0_), channel_id=1, source_target_pairs={{0,1},{1,2},{2,3},{3,0},{4,5},{5,6},{6,7},{7,4},{8,9},{9,10},{10,1... | collective-permute-start | bytes 884744 | tf_op jit(solution)/shard_map/ppermute | solution.py:94
  331.9 38.0 %collective-permute-start.35 = (bf16[4,8,160,512]{3,2,1,0:T(8,128)(2,1)}, bf16[4,8,160,512]{3,2,1,0:T(8,128)(2,1)}, u32[]{:S(2)}, u32[]{:S(2)}) collective-permute-start(bf16[4,8,160,512]{3,2,1,0:T(8,128)(2,1)} %get-tuple-element.249), channel_id=1, source_target_pairs={{0,4},{4,0},{8,12},{12,8},{16,20},{20,16},{24,28},{28,24},{1,5},{5... | collective-permute-start | bytes 15728648 | tf_op jit(solution)/shard_map/ppermute | solution.py:90
  333.9 33.1 %collective-permute-start.34 = (f32[48,1024]{1,0:T(8,128)S(1)}, f32[48,1024]{1,0:T(8,128)S(1)}, u32[]{:S(2)}, u32[]{:S(2)}) collective-permute-start(f32[48,1024]{1,0:T(8,128)S(1)} %get-tuple-element.243), channel_id=1, source_target_pairs={{0,1},{1,0},{2,3},{3,2},{4,5},{5,4},{6,7},{7,6},{8,9},{9,8},{10,11... | collective-permute-start | bytes 589832 | tf_op jit(solution)/shard_map/ppermute | solution.py:98
  335.4 25.5 %collective-permute-start.32 = (bf16[2,8,64,512]{3,2,1,0:T(8,128)(2,1)S(1)}, bf16[2,8,64,512]{3,2,1,0:T(8,128)(2,1)}, u32[]{:S(2)}, u32[]{:S(2)}) collective-permute-start(bf16[2,8,64,512]{3,2,1,0:T(8,128)(2,1)S(1)} %get-tuple-element.238), channel_id=1, source_target_pairs={{0,16},{4,20},{8,24},{12,28},{16,0},{20,4},{24,8},{28,12},{1,17},{... | collective-permute-start | bytes 3145736 | tf_op jit(solution)/shard_map/ppermute | solution.py:90
  336.7 24.3 %collective-permute-start.33 = (bf16[2,8,64,512]{3,2,1,0:T(8,128)(2,1)S(1)}, bf16[2,8,64,512]{3,2,1,0:T(8,128)(2,1)}, u32[]{:S(2)}, u32[]{:S(2)}) collective-permute-start(bf16[2,8,64,512]{3,2,1,0:T(8,128)(2,1)S(1)} %get-tuple-element.239), channel_id=1, source_target_pairs={{0,8},{4,12},{8,0},{12,4},{16,24},{20,28},{24,16},{28,20},{1,9},{5... | collective-permute-start | bytes 3145736 | tf_op jit(solution)/shard_map/ppermute | solution.py:90
  367.8 24.5 %collective-permute-start.36 = (bf16[1,8,64,512]{3,2,1,0:T(8,128)(2,1)}, bf16[1,8,64,512]{3,2,1,0:T(8,128)(2,1)}, u32[]{:S(2)}, u32[]{:S(2)}) collective-permute-start(bf16[1,8,64,512]{3,2,1,0:T(8,128)(2,1)} %get-tuple-element.259), channel_id=1, source_target_pairs={{0,8},{4,12},{8,0},{12,4},{16,24},{20,28},{24,16},{28,20},{1,9},{5... | collective-permute-start | bytes 1572872 | tf_op jit(solution)/shard_map/ppermute | solution.py:90
  369.0 23.3 %collective-permute-start.37 = (bf16[1,8,64,512]{3,2,1,0:T(8,128)(2,1)S(1)}, bf16[1,8,64,512]{3,2,1,0:T(8,128)(2,1)}, u32[]{:S(2)}, u32[]{:S(2)}) collective-permute-start(bf16[1,8,64,512]{3,2,1,0:T(8,128)(2,1)S(1)} %get-tuple-element.260), channel_id=1, source_target_pairs={{0,16},{4,20},{8,24},{12,28},{16,0},{20,4},{24,8},{28,12},{1,17},{... | collective-permute-start | bytes 1572872 | tf_op jit(solution)/shard_map/ppermute | solution.py:90
  369.2 28.1 %collective-permute-start.38 = (f32[48,1024]{1,0:T(8,128)}, f32[48,1024]{1,0:T(8,128)}, u32[]{:S(2)}, u32[]{:S(2)}) collective-permute-start(f32[48,1024]{1,0:T(8,128)} %add.295), channel_id=1, source_target_pairs={{0,2},{1,3},{2,0},{3,1},{4,6},{5,7},{6,4},{7,5},{8,10},{9,11},{10,... | collective-permute-start | bytes 589832 | tf_op jit(solution)/shard_map/ppermute | solution.py:98
  378.3 36.7 %collective-permute-start.39 = (bf16[2,8,96,512]{3,2,1,0:T(8,128)(2,1)S(1)}, bf16[2,8,96,512]{3,2,1,0:T(8,128)(2,1)S(1)}, u32[]{:S(2)}, u32[]{:S(2)}) collective-permute-start(bf16[2,8,96,512]{3,2,1,0:T(8,128)(2,1)S(1)} %get-tuple-element.269), channel_id=1, source_target_pairs={{0,16},{4,20},{8,24},{12,28},{16,0},{20,4},{24,8},{28,12},{1,17},{... | collective-permute-start | bytes 4718600 | tf_op jit(solution)/shard_map/ppermute | solution.py:90
  379.5 33.6 %collective-permute-start.40 = (bf16[2,8,64,512]{3,2,1,0:T(8,128)(2,1)}, bf16[2,8,64,512]{3,2,1,0:T(8,128)(2,1)}, u32[]{:S(2)}, u32[]{:S(2)}) collective-permute-start(bf16[2,8,64,512]{3,2,1,0:T(8,128)(2,1)} %get-tuple-element.270), channel_id=1, source_target_pairs={{0,8},{4,12},{8,0},{12,4},{16,24},{20,28},{24,16},{28,20},{1,9},{5... | collective-permute-start | bytes 3145736 | tf_op jit(solution)/shard_map/ppermute | solution.py:90
  399.0 25.1 %collective-permute-start.41 = (bf16[2,2,128,512]{3,2,1,0:T(8,128)(2,1)}, bf16[2,2,128,512]{3,2,1,0:T(8,128)(2,1)}, u32[]{:S(2)}, u32[]{:S(2)}) collective-permute-start(bf16[2,2,128,512]{3,2,1,0:T(8,128)(2,1)} %get-tuple-element.277), channel_id=1, source_target_pairs={{0,2},{1,3},{2,0},{3,1},{4,6},{5,7},{6,4},{7,5},{8,10},{9,11},{10,... | collective-permute-start | bytes 1572872 | tf_op jit(solution)/shard_map/ppermute | solution.py:98
  422.8 17.3 %collective-permute-start.42 = (bf16[1,8,96,512]{3,2,1,0:T(8,128)(2,1)}, bf16[1,8,96,512]{3,2,1,0:T(8,128)(2,1)}, u32[]{:S(2)}, u32[]{:S(2)}) collective-permute-start(bf16[1,8,96,512]{3,2,1,0:T(8,128)(2,1)} %get-tuple-element.295), channel_id=1, source_target_pairs={{0,8},{4,12},{8,0},{12,4},{16,24},{20,28},{24,16},{28,20},{1,9},{5... | collective-permute-start | bytes 2359304 | tf_op jit(solution)/shard_map/ppermute | solution.py:90
  423.4 16.2 %collective-permute-start.43 = (bf16[1,8,64,512]{3,2,1,0:T(8,128)(2,1)}, bf16[1,8,64,512]{3,2,1,0:T(8,128)(2,1)S(1)}, u32[]{:S(2)}, u32[]{:S(2)}) collective-permute-start(bf16[1,8,64,512]{3,2,1,0:T(8,128)(2,1)} %copy-done.14), channel_id=1, source_target_pairs={{0,16},{4,20},{8,24},{12,28},{16,0},{20,4},{24,8},{28,12},{1,17},{... | collective-permute-start | bytes 1572872 | tf_op jit(solution)/shard_map/ppermute | solution.py:90
  426.4 15.2 %collective-permute-start.44 = (bf16[2,128,512]{2,1,0:T(8,128)(2,1)S(1)}, bf16[2,128,512]{2,1,0:T(8,128)(2,1)S(1)}, u32[]{:S(2)}, u32[]{:S(2)}) collective-permute-start(bf16[2,128,512]{2,1,0:T(8,128)(2,1)S(1)} %get-tuple-element.300), channel_id=1, source_target_pairs={{0,1},{1,0},{2,3},{3,2},{4,5},{5,4},{6,7},{7,6},{8,9},{9,8},{10,11... | collective-permute-start | bytes 786440 | tf_op jit(solution)/shard_map/ppermute | solution.py:98
  442.2 9.6 %collective-permute-start.45 = (bf16[4,2,192,384]{3,2,1,0:T(8,128)(2,1)}, bf16[4,2,192,384]{3,2,1,0:T(8,128)(2,1)S(1)}, u32[]{:S(2)}, u32[]{:S(2)}) collective-permute-start(bf16[4,2,192,384]{3,2,1,0:T(8,128)(2,1)} %get-tuple-element.306), channel_id=1, source_target_pairs={{0,4},{4,0},{8,12},{12,8},{16,20},{20,16},{24,28},{28,24},{1,5},{5... | collective-permute-start | bytes 3538952 | tf_op jit(solution)/shard_map/ppermute | solution.py:90
  445.3 6.6 %collective-permute-start.46 = (bf16[4,2,96,384]{3,2,1,0:T(8,128)(2,1)}, bf16[4,2,96,384]{3,2,1,0:T(8,128)(2,1)S(1)}, u32[]{:S(2)}, u32[]{:S(2)}) collective-permute-start(bf16[4,2,96,384]{3,2,1,0:T(8,128)(2,1)} %get-tuple-element.307), channel_id=1, source_target_pairs={{0,4},{4,0},{8,12},{12,8},{16,20},{20,16},{24,28},{28,24},{1,5},{5... | collective-permute-start | bytes 1769480 | tf_op jit(solution)/shard_map/ppermute | solution.py:90
  448.8 7.4 %collective-permute-start.56 = (bf16[128,512]{1,0:T(8,128)(2,1)S(1)}, bf16[128,512]{1,0:T(8,128)(2,1)S(1)}, u32[]{:S(2)}, u32[]{:S(2)}) collective-permute-start(bf16[128,512]{1,0:T(8,128)(2,1)S(1)} %get-tuple-element.302), channel_id=1, source_target_pairs={{0,4},{4,0},{8,12},{12,8},{16,20},{20,16},{24,28},{28,24},{1,5},{5... | collective-permute-start | bytes 393224 | tf_op jit(solution)/shard_map/ppermute | solution.py:90
  449.2 19.2 %collective-permute-start.52 = (bf16[2,160,512]{2,1,0:T(8,128)(2,1)S(1)}, bf16[2,160,512]{2,1,0:T(8,128)(2,1)S(1)}, u32[]{:S(2)}, u32[]{:S(2)}) collective-permute-start(bf16[2,160,512]{2,1,0:T(8,128)(2,1)S(1)} %get-tuple-element.326), channel_id=1, source_target_pairs={{0,1},{1,2},{2,3},{3,0},{4,5},{5,6},{6,7},{7,4},{8,9},{9,10},{10,1... | collective-permute-start | bytes 983048 | tf_op jit(solution)/shard_map/ppermute | solution.py:94
  449.4 28.1 %collective-permute-start.53 = (bf16[2,160,512]{2,1,0:T(8,128)(2,1)S(1)}, bf16[2,160,512]{2,1,0:T(8,128)(2,1)S(1)}, u32[]{:S(2)}, u32[]{:S(2)}) collective-permute-start(bf16[2,160,512]{2,1,0:T(8,128)(2,1)S(1)} %get-tuple-element.327), channel_id=1, source_target_pairs={{0,2},{1,3},{2,0},{3,1},{4,6},{5,7},{6,4},{7,5},{8,10},{9,11},{10,... | collective-permute-start | bytes 983048 | tf_op jit(solution)/shard_map/ppermute | solution.py:94
  451.9 29.3 %collective-permute-start.54 = (bf16[2,160,512]{2,1,0:T(8,128)(2,1)S(1)}, bf16[2,160,512]{2,1,0:T(8,128)(2,1)S(1)}, u32[]{:S(2)}, u32[]{:S(2)}) collective-permute-start(bf16[2,160,512]{2,1,0:T(8,128)(2,1)S(1)} %get-tuple-element.328), channel_id=1, source_target_pairs={{0,3},{1,0},{2,1},{3,2},{4,7},{5,4},{6,5},{7,6},{8,11},{9,8},{10,9... | collective-permute-start | bytes 983048 | tf_op jit(solution)/shard_map/ppermute | solution.py:94
  455.3 12.4 %collective-permute-start.47 = (bf16[2,2,144,384]{3,2,1,0:T(8,128)(2,1)S(1)}, bf16[2,2,144,384]{3,2,1,0:T(8,128)(2,1)S(1)}, u32[]{:S(2)}, u32[]{:S(2)}) collective-permute-start(bf16[2,2,144,384]{3,2,1,0:T(8,128)(2,1)S(1)} %get-tuple-element.314), channel_id=1, source_target_pairs={{0,16},{4,20},{8,24},{12,28},{16,0},{20,4},{24,8},{28,12},{1,17},{... | collective-permute-start | bytes 1327112 | tf_op jit(solution)/shard_map/ppermute | solution.py:90
  456.2 11.4 %collective-permute-start.48 = (bf16[2,2,144,384]{3,2,1,0:T(8,128)(2,1)S(1)}, bf16[2,2,144,384]{3,2,1,0:T(8,128)(2,1)S(1)}, u32[]{:S(2)}, u32[]{:S(2)}) collective-permute-start(bf16[2,2,144,384]{3,2,1,0:T(8,128)(2,1)S(1)} %get-tuple-element.315), channel_id=1, source_target_pairs={{0,8},{4,12},{8,0},{12,4},{16,24},{20,28},{24,16},{28,20},{1,9},{5... | collective-permute-start | bytes 1327112 | tf_op jit(solution)/shard_map/ppermute | solution.py:90
  482.1 2.5 collective-permute-start.55
  483.4 7.0 %collective-permute-start.49 = (bf16[1,2,144,384]{3,2,1,0:T(8,128)(2,1)S(1)}, bf16[1,2,144,384]{3,2,1,0:T(8,128)(2,1)S(1)}, u32[]{:S(2)}, u32[]{:S(2)}) collective-permute-start(bf16[1,2,144,384]{3,2,1,0:T(8,128)(2,1)S(1)} %get-tuple-element.322), channel_id=1, source_target_pairs={{0,8},{4,12},{8,0},{12,4},{16,24},{20,28},{24,16},{28,20},{1,9},{5... | collective-permute-start | bytes 663560 | tf_op jit(solution)/shard_map/ppermute | solution.py:90
  483.7 6.7 %collective-permute-start.50 = (bf16[1,2,144,384]{3,2,1,0:T(8,128)(2,1)S(1)}, bf16[1,2,144,384]{3,2,1,0:T(8,128)(2,1)S(1)}, u32[]{:S(2)}, u32[]{:S(2)}) collective-permute-start(bf16[1,2,144,384]{3,2,1,0:T(8,128)(2,1)S(1)} %get-tuple-element.323), channel_id=1, source_target_pairs={{0,16},{4,20},{8,24},{12,28},{16,0},{20,4},{24,8},{28,12},{1,17},{... | collective-permute-start | bytes 663560 | tf_op jit(solution)/shard_map/ppermute | solution.py:90
  491.2 2.4 collective-permute-start.51
  (98 other events, 623.1 us)
Sparse Core Ops, SparseCore 0:
  54.9 162.6 all-gather.4
  447.2 29.0 all-gather.6
